TPU v7x, 32 devices: a whole 2x2x4 slice. The times are simulated.
32 devices in a mesh: grp: 2 (over y), dp: 4 (over z), mp: 2 (over x), sub: 2 (over core).
Axes of the slice: x: 2, y: 2, z: 4, core: 2. Of those that a mesh axis runs over, the one named last changes fastest.
Arguments:
- tokens: bfloat16 [4096, 16384], P(('grp', 'dp', 'sub'), 'mp'), parts along dimension 0
- cotangent: bfloat16 [4096, 16384], P(('grp', 'dp', 'sub'), 'mp'), parts along dimension 0, may hold values from -6 to 6
- rms_norm_gain: bfloat16 [16384], P('mp'), may hold values from 0.5 to 1.5
- gate_codes: bfloat16 [128, 128, 256], P('mp', ('dp', 'sub')), may hold values from -6 to 6
- gate_block_scale: bfloat16 [128, 2], P('mp'), may hold values from 0.0039978027 to 0.015991211
- up_codes: bfloat16 [128, 128, 256], P('mp', ('dp', 'sub')), may hold values from -6 to 6
- up_block_scale: bfloat16 [128, 2], P('mp'), may hold values from 0.0039978027 to 0.015991211
- down_codes: bfloat16 [256, 128, 128], P(('dp', 'sub'), 'mp'), may hold values from -6 to 6
- down_block_scale: bfloat16 [2, 128], P(None, 'mp'), may hold values from 0.014953613 to 0.059814453
- up_adapter_in: bfloat16 [32768, 128], P(('grp', 'mp')), parts along dimension 0, may hold values from -0.046875 to 0.046875
- up_adapter_out: bfloat16 [256, 256], P('grp', 'mp'), parts along dimension 0, may hold values from -0.5 to 0.5
- down_adapter_in: bfloat16 [512, 128], P(('grp', 'mp')), parts along dimension 0, may hold values from -0.375 to 0.375
- down_adapter_out: bfloat16 [256, 16384], P('grp', 'mp'), parts along dimension 0, may hold values from -0.5 to 0.5
- sequence_length_list: int32 [16, 2], P(('grp', 'dp', 'sub')), parts along dimension 0, may hold values from 32 to 128, as said below
- slot_sequence_index: int32 [4096], P(('grp', 'dp', 'sub')), parts along dimension 0, may hold values from 0 to 2, as said below
Outputs:
- up_in_gradient: bfloat16 [32768, 128], P(('grp', 'mp')), parts along dimension 0
- up_out_gradient: bfloat16 [256, 256], P('grp', 'mp'), parts along dimension 0
- down_in_gradient: bfloat16 [512, 128], P(('grp', 'mp')), parts along dimension 0
- down_out_gradient: bfloat16 [256, 16384], P('grp', 'mp'), parts along dimension 0
There are 2 independent parts, one for each index of `grp`. A program takes and returns all parts, laid end to end along the dimension named above; an argument that names none is the same for every part. Nothing has to cross between parts.
Inputs may be any that keep to these rules, and one draw needn't show every extreme that they name: `sequence_length_list`: row d holds, in order, the lengths of the 2 sequences packed from the first token slot of data device d on; the rest of its 256 slots are padding. At least one row fills all slots. `slot_sequence_index`: within each data device's 256 slots, the number of the sequence that holds the slot as given by sequence_length_list, and 2 for padding slots; some device has padding.
All inputs are finite; a program needn't handle non-finite values.
Results may differ from a plain program's by a relative error of at most 0.0091.
Values may be sent and summed in bfloat16 or wider, within the bound.
No kernel may reach another device: no remote copies, remote signals or barrier semaphores. Data moves between devices by JAX's collectives and lax.ppermute only.
A program may use at most 128 MiB of HBM per device.

v0:
```python
import math

import jax
import jax.numpy as jnp
from jax import lax
from jax.sharding import PartitionSpec as P

ADAPTER_SCALE = 2.0
EPS = 1e-05


def contract_dims(left, right, left_dim, right_dim):
    return lax.dot_general(
        left, right, (((left_dim,), (right_dim,)), ((), ())), preferred_element_type=jnp.float32
    )


def body(
    tokens,
    cotangent,
    rms_norm_gain,
    gate_codes,
    gate_block_scale,
    up_codes,
    up_block_scale,
    down_codes,
    down_block_scale,
    up_adapter_in,
    up_adapter_out,
    down_adapter_in,
    down_adapter_out,
    sequence_length_list,
    slot_sequence_index,
):
    rows = tokens.shape[0]
    local_width = tokens.shape[1]
    block = gate_block_scale.shape[0] and local_width // gate_codes.shape[0]
    blocks_here = gate_codes.shape[0]
    total_width = local_width * lax.axis_size("mp")
    own_squares = jnp.sum(jnp.square(tokens.astype(jnp.float32)), axis=-1, keepdims=True)
    squares = lax.psum(own_squares, "mp") / total_width
    inv_rms = lax.rsqrt(squares + EPS)
    local_normed_input = (
        tokens.astype(jnp.float32) * inv_rms * rms_norm_gain.astype(jnp.float32)[None, :]
    ).astype(jnp.bfloat16)
    seq_count = sequence_length_list.shape[1]
    longest = rows // seq_count
    total = rows * lax.axis_size("dp") * lax.axis_size("sub")
    ratios = longest / sequence_length_list[0].astype(jnp.float32)
    match = slot_sequence_index[:, None] == jnp.arange(seq_count, dtype=jnp.int32)[None, :]
    token_weight = jnp.sum(jnp.where(match, ratios[None, :], jnp.float32(0.0)), axis=-1)
    token_weight = token_weight * jnp.float32(1.0 / math.sqrt(total))
    local_output = (cotangent.astype(jnp.float32) * token_weight[:, None]).astype(jnp.bfloat16)
    partial_up = jnp.dot(local_normed_input, up_adapter_in, preferred_element_type=jnp.float32)
    partial_output = contract_dims(local_output, down_adapter_out, 1, 1)
    up_adapter_rank, output_adapter_rank = lax.psum((partial_up, partial_output), "mp")
    up_adapter_rank = up_adapter_rank.astype(jnp.bfloat16)
    output_adapter_rank = output_adapter_rank.astype(jnp.bfloat16)
    normed_blocks = local_normed_input.reshape(rows, blocks_here, block)
    out_blocks = local_output.reshape(rows, blocks_here, block)
    wide_gate = jnp.repeat(gate_block_scale.astype(jnp.float32), block, axis=1)[:, None, :]
    wide_up = jnp.repeat(up_block_scale.astype(jnp.float32), block, axis=1)[:, None, :]
    wide_down = jnp.repeat(down_block_scale.astype(jnp.float32), block, axis=0)
    dims_front = (((1, 2), (0, 1)), ((), ()))
    dims_back = (((1, 2), (1, 2)), ((), ()))
    quant_g = lax.all_gather(gate_codes, ("dp", "sub"), axis=1, tiled=True)
    quant_u = lax.all_gather(up_codes, ("dp", "sub"), axis=1, tiled=True)
    weight_g = (quant_g.astype(jnp.float32) * wide_gate).astype(jnp.bfloat16)
    weight_u = (quant_u.astype(jnp.float32) * wide_up).astype(jnp.bfloat16)
    gate_next = lax.dot_general(
        normed_blocks, weight_g, dims_front, preferred_element_type=jnp.float32
    )
    up_next = lax.dot_general(
        normed_blocks, weight_u, dims_front, preferred_element_type=jnp.float32
    )
    gate, base_up_projected = (
        lax.psum_scatter(gate_next, "mp", scatter_dimension=1, tiled=True),
        lax.psum_scatter(up_next, "mp", scatter_dimension=1, tiled=True),
    )
    up_projected = base_up_projected + ADAPTER_SCALE * jnp.dot(
        up_adapter_rank, up_adapter_out, preferred_element_type=jnp.float32
    )
    silu_gate = jax.nn.silu(gate)
    hidden_units = (silu_gate * up_projected).astype(jnp.bfloat16)
    partial_hidden = jnp.dot(hidden_units, down_adapter_in, preferred_element_type=jnp.float32)
    hidden_adapter_rank = lax.psum(partial_hidden, "mp").astype(jnp.bfloat16)
    weight_d = (
        lax.all_gather(down_codes, ("dp", "sub"), axis=0, tiled=True).astype(jnp.float32)
        * wide_down[:, :, None]
    ).astype(jnp.bfloat16)
    back_part = lax.dot_general(out_blocks, weight_d, dims_back, preferred_element_type=jnp.float32)
    base_backward = lax.psum_scatter(back_part, "mp", scatter_dimension=1, tiled=True)
    hidden_gradient = base_backward + ADAPTER_SCALE * contract_dims(
        output_adapter_rank, down_adapter_in, 1, 1
    )
    up_gradient = (hidden_gradient * silu_gate).astype(jnp.bfloat16)
    partial_gradient = contract_dims(up_gradient, up_adapter_out, 1, 1)
    up_adapter_rank_gradient = lax.psum(partial_gradient, "mp").astype(jnp.bfloat16)
    up_in_term = ADAPTER_SCALE * contract_dims(local_normed_input, up_adapter_rank_gradient, 0, 0)
    up_out_term = ADAPTER_SCALE * contract_dims(up_adapter_rank, up_gradient, 0, 0)
    down_in_term = ADAPTER_SCALE * contract_dims(hidden_units, output_adapter_rank, 0, 0)
    down_out_term = ADAPTER_SCALE * contract_dims(hidden_adapter_rank, local_output, 0, 0)
    sum_up_a, sum_up_b, sum_down_a, sum_down_b = lax.psum(
        (up_in_term, up_out_term, down_in_term, down_out_term), ("dp", "sub")
    )
    return (
        sum_up_a.astype(jnp.bfloat16),
        sum_up_b.astype(jnp.bfloat16),
        sum_down_a.astype(jnp.bfloat16),
        sum_down_b.astype(jnp.bfloat16),
    )


def solution(mesh):
    placed = (
        P(("grp", "dp", "sub"), "mp"),
        P(("grp", "dp", "sub"), "mp"),
        P("mp"),
        P("mp", ("dp", "sub"), None),
        P("mp", None),
        P("mp", ("dp", "sub"), None),
        P("mp", None),
        P(("dp", "sub"), "mp", None),
        P(None, "mp"),
        P(("grp", "mp"), None),
        P("grp", "mp"),
        P(("grp", "mp"), None),
        P("grp", "mp"),
        P(("grp", "dp", "sub"), None),
        P(("grp", "dp", "sub")),
    )
    return jax.shard_map(
        body,
        mesh=mesh,
        in_specs=placed,
        out_specs=(P(("grp", "mp"), None), P("grp", "mp"), P(("grp", "mp"), None), P("grp", "mp")),
        check_vma=False,
    )
```

profile of v0, /device:TPU:0, one launch (start us, length us, event | category | flops | bytes accessed | tf_op | source)
XLA Modules:
  0.0 396.0 jit_solution(9186202787149081078)
XLA Ops:
  9.4 0.7 convert_element_type.78
  10.2 0.8 copy.39
  11.1 0.8 copy.41
  12.0 3.1 fusion
  15.1 5.8 %psum.63 = f32[256,1]{0,1:T(1,128)S(1)} all-reduce(f32[256,1]{0,1:T(1,128)S(1)} %bitcast.64), channel_id=1, replica_groups=mesh['grp'=2,'dp'=4,'mp'=2,'sub'=2] {'mp'}, use_global_device_ids=true, to_apply=%region_1.0 | all-reduce | flops 256 | bytes 2048 | tf_op jit(solution)/shard_map/psum | solution.py:41
  21.0 3.7 fusion.41
  25.1 1.3 fusion.39
  26.4 12.4 %all-reduce.6 = (bf16[256,128]{1,0:T(8,128)(2,1)S(1)}, bf16[256,128]{1,0:T(8,128)(2,1)S(1)}) all-reduce(f32[256,128]{1,0:T(8,128)S(1)} %fusion.39, f32[256,128]{1,0:T(8,128)S(1)} %fusion.41), channel_id=1, replica_groups=mesh['grp'=2,'dp'=4,'mp'=2,'sub'=2] {'mp'}, use_global_device_ids=true, to_apply=%region_4.5 | all-reduce | flops 65536 | bytes 393216 | tf_op jit(solution)/shard_map/psum | solution.py:56
  38.8 20.6 %all-gather.6.cloned.1.call-done = bf16[64,128,256]{2,1,0:T(8,128)(2,1)} async-done(((bf16[64,16,256]{2,1,0:T(8,128)(2,1)}), bf16[64,128,256]{2,1,0:T(8,128)(2,1)}) %all-gather.6.cloned.1.call-update) | async-done | bytes 4194320 | tf_op jit(solution)/shard_map/all_gather | solution.py:66
  59.4 5.9 %fusion.23 = f32[256,256]{1,0:T(8,128)} fusion(bf16[64,128,256]{2,1,0:T(8,128)(2,1)} %all-gather.6.cloned.1.call-done, f32[64,256]{1,0:T(8,128)S(1)} %bitcast.63, f32[8192]{0:T(1024)S(1)} %convert_element_type.78, f32[256]{0:T(256)S(1)} %bitcast.66, bf16[256,8192]{1,0:T(8,128)(2,1)} %param.15), kind=kOutput, calls=%fused_computation.25 | convolution fusion | flops 1088421888 | bytes 8750080 | tf_op jit(solution)/shard_map/dot_general | solution.py:70
  65.5 41.5 %all-gather.8.cloned.1.call-done = bf16[64,128,256]{2,1,0:T(8,128)(2,1)} async-done(((bf16[64,16,256]{2,1,0:T(8,128)(2,1)}), bf16[64,128,256]{2,1,0:T(8,128)(2,1)}) %all-gather.8.cloned.1.call-update) | async-done | bytes 4194320 | tf_op jit(solution)/shard_map/all_gather | solution.py:67
  107.0 6.0 %fusion.20 = f32[256,256]{1,0:T(8,128)} fusion(bf16[64,128,256]{2,1,0:T(8,128)(2,1)} %all-gather.8.cloned.1.call-done, f32[64,256]{1,0:T(8,128)S(1)} %bitcast.62, f32[8192]{0:T(1024)S(1)} %convert_element_type.78, f32[256]{0:T(256)S(1)} %bitcast.67, bf16[256,8192]{1,0:T(8,128)(2,1)} %param.15), kind=kOutput, calls=%fused_computation.24 | convolution fusion | flops 1088421888 | bytes 8750080 | tf_op jit(solution)/shard_map/dot_general | solution.py:73
  113.2 41.3 %all-gather.4.cloned.1.call-done = bf16[256,64,128]{2,1,0:T(8,128)(2,1)} async-done(((bf16[32,64,128]{2,1,0:T(8,128)(2,1)}), bf16[256,64,128]{2,1,0:T(8,128)(2,1)}) %all-gather.4.cloned.1.call-update) | async-done | bytes 4194320 | tf_op jit(solution)/shard_map/all_gather | solution.py:88
  154.5 5.4 %multiply_convert_fusion.2 = bf16[256,64,128]{2,1,0:T(8,128)(2,1)S(1)} fusion(bf16[256,64,128]{2,1,0:T(8,128)(2,1)} %all-gather.4.cloned.1.call-done, f32[256,64]{1,0:T(8,128)S(1)} %bitcast.59), kind=kLoop, calls=%fused_computation.9 | loop fusion | flops 6291456 | bytes 8454144 | tf_op jit(solution)/shard_map/convert_element_type | solution.py:90
  160.0 3.5 fusion.15
  163.5 4.1 %reduce-scatter.6.cloned.1.call-done = f32[256,128]{1,0:T(8,128)} async-done(((f32[256,256]{1,0:T(8,128)}), f32[256,128]{1,0:T(8,128)}) %reduce-scatter.6.cloned.1.call-update) | async-done | bytes 131088 | tf_op jit(solution)/shard_map/reduce_scatter | solution.py:77
  167.6 13.9 %reduce-scatter.8.cloned.1.call-done = f32[256,128]{1,0:T(8,128)} async-done(((f32[256,256]{1,0:T(8,128)}), f32[256,128]{1,0:T(8,128)}) %reduce-scatter.8.cloned.1.call-update) | async-done | bytes 131088 | tf_op jit(solution)/shard_map/reduce_scatter | solution.py:78
  181.4 1.1 fusion.31
  182.9 12.9 %reduce-scatter.4.cloned.1.call-done = f32[256,128]{1,0:T(8,128)} async-done(((f32[256,256]{1,0:T(8,128)}), f32[256,128]{1,0:T(8,128)}) %reduce-scatter.4.cloned.1.call-update) | async-done | bytes 131088 | tf_op jit(solution)/shard_map/reduce_scatter | solution.py:92
  195.8 1.1 fusion.30
  197.3 10.5 %all-reduce.7 = (bf16[256,128]{1,0:T(8,128)(2,1)S(1)}, bf16[256,128]{1,0:T(8,128)(2,1)S(1)}) all-reduce(f32[256,128]{1,0:T(8,128)S(1)} %fusion.45, f32[256,128]{1,0:T(8,128)S(1)} %fusion.46), channel_id=1, replica_groups=mesh['grp'=2,'dp'=4,'mp'=2,'sub'=2] {'mp'}, use_global_device_ids=true, to_apply=%region_6.7 | all-reduce | flops 65536 | bytes 393216 | tf_op jit(solution)/shard_map/psum | solution.py:98
  207.8 5.8 %convolution_multiply_fusion.1 = f32[8192,128]{1,0:T(8,128)} fusion(bf16[256,128]{1,0:T(8,128)(2,1)S(1)} %get-tuple-element.8, bf16[256,8192]{1,0:T(8,128)(2,1)} %param.15, f32[8192]{0:T(1024)S(1)} %convert_element_type.78, f32[256]{0:T(256)S(1)} %bitcast.68), kind=kOutput, calls=%fused_computation.3 | convolution fusion | flops 546308096 | bytes 8487936 | tf_op jit(solution)/shard_map/dot_general | solution.py:13
  213.7 3.3 convolution_multiply_fusion
  216.9 172.2 %all-reduce.8 = (bf16[8192,128]{1,0:T(8,128)(2,1)}, bf16[128,128]{1,0:T(8,128)(2,1)}, bf16[128,128]{1,0:T(8,128)(2,1)}, bf16[128,8192]{1,0:T(8,128)(2,1)}) all-reduce(f32[8192,128]{1,0:T(8,128)} %convolution_multiply_fusion.1, ...), channel_id=1, replica_groups=mesh['grp'=2,'dp'=4,'mp'=2,'sub'=2] {'dp','sub'}, use_global_device_ids=true, to_apply=%region_7.8 | all-reduce | flops 2129920 | bytes 12779520 | tf_op jit(solution)/shard_map/psum | solution.py:103
  (45 shorter events, 3.9 us)
Async XLA Ops:
  7.2 13.7 %copy-start = (bf16[8192,128]{1,0:T(8,128)(2,1)S(1)}, bf16[8192,128]{1,0:T(8,128)(2,1)}, u32[]{:S(2)}) copy-start(bf16[8192,128]{1,0:T(8,128)(2,1)} %param.24) | copy-start | bytes 6291460
  7.2 52.3 %all-gather.6.cloned.1.call-start = ((), (), s32[]{:S(2)}) async-start(), calls=%async_computation.5 | async-start | bytes 4718592 | tf_op jit(solution)/shard_map/all_gather | solution.py:66
  7.9 99.1 %all-gather.8.cloned.1.call-start = ((), (), s32[]{:S(2)}) async-start(), calls=%async_computation.7 | async-start | bytes 4718592 | tf_op jit(solution)/shard_map/all_gather | solution.py:67
  8.7 145.8 %all-gather.4.cloned.1.call-start = ((), (), s32[]{:S(2)}) async-start(), calls=%async_computation.3 | async-start | bytes 4718592 | tf_op jit(solution)/shard_map/all_gather | solution.py:88
  9.4 158.2 %reduce-scatter.6.cloned.1.call-start = ((), (), s32[]{:S(2)}) async-start(), calls=%async_computation.6 | async-start | bytes 393216 | tf_op jit(solution)/shard_map/reduce_scatter | solution.py:77
  20.9 3.8 copy-start.9
  20.9 3.8 copy-start.6
  20.9 3.9 copy-start.1
  20.9 4.1 %copy-start.8 = (bf16[128,8192]{1,0:T(8,128)(2,1)S(1)}, bf16[128,8192]{1,0:T(8,128)(2,1)}, u32[]{:S(2)}) copy-start(bf16[128,8192]{1,0:T(8,128)(2,1)} %param.27) | copy-start | bytes 6291460
  65.4 116.0 %reduce-scatter.8.cloned.1.call-start = ((), (), s32[]{:S(2)}) async-start(), calls=%async_computation.8 | async-start | bytes 393216 | tf_op jit(solution)/shard_map/reduce_scatter | solution.py:78
  107.0 47.5 %copy-start.7 = (bf16[2,64]{1,0:T(2,128)(2,1)S(1)}, bf16[2,64]{1,0:T(2,128)(2,1)}, u32[]{:S(2)}) copy-start(bf16[2,64]{1,0:T(2,128)(2,1)} %param.23) | copy-start | bytes 772
  113.0 82.8 %reduce-scatter.4.cloned.1.call-start = ((), (), s32[]{:S(2)}) async-start(), calls=%async_computation.4 | async-start | bytes 393216 | tf_op jit(solution)/shard_map/reduce_scatter | solution.py:92
  154.5 5.4 %copy-start.2 = (bf16[256,8192]{1,0:T(8,128)(2,1)S(1)}, bf16[256,8192]{1,0:T(8,128)(2,1)}, u32[]{:S(2)}) copy-start(bf16[256,8192]{1,0:T(8,128)(2,1)} %param.16) | copy-start | bytes 12582916
  159.9 21.5 %copy-start.5 = (bf16[128,128]{1,0:T(8,128)(2,1)S(1)}, bf16[128,128]{1,0:T(8,128)(2,1)}, u32[]{:S(2)}) copy-start(bf16[128,128]{1,0:T(8,128)(2,1)} %param.25) | copy-start | bytes 98308
  160.0 22.8 %copy-start.4 = (bf16[128,128]{1,0:T(8,128)(2,1)S(1)}, bf16[128,128]{1,0:T(8,128)(2,1)}, u32[]{:S(2)}) copy-start(bf16[128,128]{1,0:T(8,128)(2,1)} %param.26) | copy-start | bytes 98308
  207.8 5.8 %copy-start.3 = (bf16[256,8192]{1,0:T(8,128)(2,1)S(1)}, bf16[256,8192]{1,0:T(8,128)(2,1)}, u32[]{:S(2)}) copy-start(bf16[256,8192]{1,0:T(8,128)(2,1)} %param.16) | copy-start | bytes 12582916
Sparse Core Ops, SparseCore 0:
  9.6 49.7 all-gather.5
  61.0 45.9 all-gather.7
  108.6 45.8 all-gather.3
  157.2 10.3 reduce-scatter.5
  169.7 11.6 reduce-scatter.7
  184.1 11.6 reduce-scatter.3
where the time goes:
time: 396 us
  blocking collectives  201 us (51%)
  waiting for transfers between devices  136 us (34%)
  matrix products  32.5 us (8%)
  between operations  14.3 us (4%)
  other arithmetic  9.33 us (2%)
    psum x1, blocking collectives, body(): lax.psum((up_in_term, up_out_term, down_in_term, down_out_term), ('dp', '...  172 us
    all_gather x1, waiting for transfers between devices, body(): quant_u = lax.all_gather(up_codes, ('dp', 'sub'), axis=1, tiled=True)  41.5 us
    all_gather x1, waiting for transfers between devices, body(): lax.all_gather(down_codes, ('dp', 'sub'), axis=0, tiled=True)  41.3 us
    all_gather x1, waiting for transfers between devices, body(): quant_g = lax.all_gather(gate_codes, ('dp', 'sub'), axis=1, tiled=True)  20.6 us
    reduce_scatter x1, waiting for transfers between devices, body(): lax.psum_scatter(up_next, 'mp', scatter_dimension=1, tiled=True)  13.9 us
    reduce_scatter x1, waiting for transfers between devices, body(): lax.psum_scatter(back_part, 'mp', scatter_dimension=1, tiled=True)  12.9 us
    psum x1, blocking collectives, body(): lax.psum((partial_up, partial_output), 'mp')  12.4 us
    dot_general x7, matrix products, contract_dims(): lax.dot_general(left, right, (((left_dim,), (right_dim,)), ((), ())), pre...  12.1 us
  transfers between devices with their start and end apart: 6, of which 6 were waited for; matrix products, arithmetic and copies ran while one was open for 8% of the time, Pallas kernels for 0%

commit v1 on v0

--- a/solution.py
+++ b/solution.py
@@ -3,19 +3,359 @@
 import jax
 import jax.numpy as jnp
 from jax import lax
+from jax.experimental import pallas as pl
+from jax.experimental.pallas import tpu as pltpu
 from jax.sharding import PartitionSpec as P
 
 ADAPTER_SCALE = 2.0
 EPS = 1e-05
+ROW_TILE = 16
+CHUNKS = 4
+VMEM_LIMIT = 48 * 1024 * 1024
+
+F32 = jnp.float32
+BF16 = jnp.bfloat16
 
 
 def contract_dims(left, right, left_dim, right_dim):
     return lax.dot_general(
-        left, right, (((left_dim,), (right_dim,)), ((), ())), preferred_element_type=jnp.float32
-    )
-
-
-def body(
+        left, right, (((left_dim,), (right_dim,)), ((), ())), preferred_element_type=F32
+    )
+
+
+def vmem_specs(count):
+    return [pl.BlockSpec(memory_space=pltpu.VMEM)] * count
+
+
+def swap(x, axis):
+    return lax.ppermute(x, axis, [(0, 1), (1, 0)])
+
+
+def others(x, axis):
+    n = lax.axis_size(axis)
+    return [lax.ppermute(x, axis, [(i, (i + k) % n) for i in range(n)]) for k in range(1, n)]
+
+
+def ring_order(n):
+    return [0] + list(range(1, n, 2)) + [i for i in reversed(range(2, n)) if i % 2 == 0]
+
+
+def gather_line(own):
+    n = lax.axis_size("dp")
+    order = ring_order(n)
+    ring = [(order[i], order[(i + 1) % n]) for i in range(n)]
+    half = own.shape[0] // 2
+    moving = lax.dynamic_slice_in_dim(own, lax.axis_index("grp") * half, half, 0)
+    steps = []
+    for _ in range(n - 1):
+        moving = lax.ppermute(moving, "dp", ring)
+        steps.append((moving, swap(moving, "grp")))
+    return own, steps
+
+
+def gather_chip(own):
+    mine, steps = gather_line(own)
+    flat = [mine] + [part for step in steps for part in step]
+    return flat + [swap(part, "sub") for part in flat]
+
+
+def line_sum(x, axis):
+    n = lax.axis_size(axis)
+    place = lax.axis_index(axis)
+    half = n // 2
+
+    def add(left, right):
+        return (left.astype(F32) + right.astype(F32)).astype(BF16)
+
+    for s in range(half - 1):
+        x = add(x, lax.ppermute(x, axis, [(s, s + 1), (n - 1 - s, n - 2 - s)]))
+    x = add(x, lax.ppermute(x, axis, [(half - 1, half), (half, half - 1)]))
+    for s in reversed(range(half - 1)):
+        got = lax.ppermute(x, axis, [(s + 1, s), (n - 2 - s, n - 1 - s)])
+        x = jnp.where((place == s) | (place == n - 1 - s), got, x)
+    return x
+
+
+def place_shards(meta, bufs, store):
+    steps = (len(bufs) // 2 - 1) // 2
+    grp, sub = meta[steps + 1], meta[steps + 2]
+    half = bufs[1].shape[0]
+    per_core = 1 + 2 * steps
+    for core in range(2):
+        core_id = sub if core == 0 else 1 - sub
+        own = bufs[core * per_core]
+
+        @pl.loop(0, 2 * half)
+        def _(b, own=own, core_id=core_id):
+            store(b, meta[0] * 2 + core_id, own[b])
+
+        for k in range(steps):
+            shard = meta[k + 1] * 2 + core_id
+            for which in range(2):
+                buf = bufs[core * per_core + 1 + 2 * k + which]
+                first = (grp if which == 0 else 1 - grp) * half
+
+                @pl.loop(0, half)
+                def _(b, buf=buf, first=first, shard=shard):
+                    store(first + b, shard, buf[b])
+
+
+def front_kernel(meta, scale, x_ref, *refs):
+    bufs, (out_ref, send_ref, weight) = refs[:-3], refs[-3:]
+    rows = bufs[0].shape[1]
+    block, units = weight.shape[1], weight.shape[2]
+    groups = scale.shape[1]
+    wide = units // groups
+
+    def store(b, shard, codes):
+        at = pl.ds(pl.multiple_of(shard * rows, ROW_TILE), rows)
+        for g in range(groups):
+            cols = slice(g * wide, (g + 1) * wide)
+            weight[b, at, cols] = (codes[:, cols].astype(F32) * scale[b, g]).astype(BF16)
+
+    place_shards(meta, bufs, store)
+    total = jnp.dot(
+        x_ref[...], weight[...].reshape(-1, units), preferred_element_type=F32
+    )
+    out_ref[...] = total
+    send_ref[...] = total.astype(BF16)
+
+
+def back_kernel(meta, scale, x_ref, *refs):
+    bufs, (out_ref, send_ref, weight) = refs[:-3], refs[-3:]
+    rows, block = bufs[0].shape[1], bufs[0].shape[2]
+    per_group = weight.shape[0] // scale.shape[0]
+
+    def store(b, shard, codes):
+        first = pl.multiple_of(shard * rows, ROW_TILE)
+        at = pl.ds(first, rows)
+        factor = scale[first // per_group, b]
+        weight[at, pl.ds(pl.multiple_of(b * block, block), block)] = (
+            codes.astype(F32) * factor
+        ).astype(BF16)
+
+    place_shards(meta, bufs, store)
+    total = contract_dims(x_ref[...], weight[...], 1, 1)
+    out_ref[...] = total
+    send_ref[...] = total.astype(BF16)
+
+
+def weight_product(kernel, meta, scale, x, bufs, weight_shape, units, name):
+    rows = x.shape[0]
+    return pl.pallas_call(
+        kernel,
+        out_shape=(
+            jax.ShapeDtypeStruct((rows, units), F32),
+            jax.ShapeDtypeStruct((rows, units), BF16),
+        ),
+        in_specs=[pl.BlockSpec(memory_space=pltpu.SMEM)] * 2 + vmem_specs(1 + len(bufs)),
+        out_specs=tuple(vmem_specs(2)),
+        scratch_shapes=[pltpu.VMEM(weight_shape, BF16)],
+        compiler_params=pltpu.CompilerParams(vmem_limit_bytes=VMEM_LIMIT),
+        cost_estimate=pl.CostEstimate(
+            flops=2 * rows * x.shape[1] * units,
+            bytes_accessed=2 * x.size + 2 * x.shape[1] * units,
+            transcendentals=0,
+        ),
+        name=name,
+    )(meta, scale, x, *bufs)
+
+
+def hidden_kernel(
+    count, place, gate_ref, up_ref, low_up_ref, up_out_ref, down_in_ref, low_out_ref, grad_ref, *refs
+):
+    gate_more, up_more = refs[:count], refs[count : 2 * count]
+    silu_ref, keep_ref, send_ref, down_in_grad_ref = refs[2 * count :]
+    gate, up = gate_ref[...], up_ref[...]
+    for ref in gate_more:
+        gate = gate + ref[...].astype(F32)
+    for ref in up_more:
+        up = up + ref[...].astype(F32)
+    up = up + ADAPTER_SCALE * jnp.dot(low_up_ref[...], up_out_ref[...], preferred_element_type=F32)
+    silu = gate * jax.nn.sigmoid(gate)
+    silu_ref[...] = silu
+    hidden_wide = silu * up
+    hidden = hidden_wide.astype(BF16)
+    low_hidden = jnp.dot(hidden, down_in_ref[...], preferred_element_type=F32)
+    low_hidden = (ADAPTER_SCALE * low_hidden.T).astype(BF16)
+    sub, mp = place[0], place[1]
+    half = grad_ref.shape[1] // 2
+    for which, out_ref in ((sub, keep_ref), (1 - sub, send_ref)):
+        cols = pl.ds(pl.multiple_of(which * half, half), half)
+        out_ref[...] = jnp.dot(low_hidden, grad_ref[:, cols], preferred_element_type=F32).astype(BF16)
+    own = down_in_grad_ref.shape[0]
+    full = ADAPTER_SCALE * jnp.dot(
+        hidden_wide.astype(BF16).astype(F32).T.astype(BF16), low_out_ref[...], preferred_element_type=F32
+    )
+    for i in range(full.shape[0] // own):
+
+        @pl.when(mp == i)
+        def _(i=i):
+            down_in_grad_ref[...] = full[i * own : (i + 1) * own].astype(BF16)
+
+
+def gradient_kernel(
+    count, place, back_ref, silu_ref, low_out_ref, down_in_ref, up_out_ref, low_up_ref, x_t_ref, *refs
+):
+    back_more = refs[:count]
+    keep_ref, send_ref, up_out_grad_ref = refs[count:]
+    back = back_ref[...]
+    for ref in back_more:
+        back = back + ref[...].astype(F32)
+    back = back + ADAPTER_SCALE * contract_dims(low_out_ref[...], down_in_ref[...], 1, 1)
+    up_grad = (back * silu_ref[...]).astype(BF16)
+    low = (ADAPTER_SCALE * contract_dims(up_grad, up_out_ref[...], 1, 1)).astype(BF16)
+    sub, mp = place[0], place[1]
+    half = x_t_ref.shape[0] // 2
+    for which, out_ref in ((sub, keep_ref), (1 - sub, send_ref)):
+        at = pl.ds(pl.multiple_of(which * half, half), half)
+        out_ref[...] = jnp.dot(x_t_ref[at, :], low, preferred_element_type=F32).astype(BF16)
+    own = up_out_grad_ref.shape[1]
+    low_up_t = low_up_ref[...].astype(F32).T.astype(BF16)
+    full = ADAPTER_SCALE * jnp.dot(low_up_t, up_grad, preferred_element_type=F32)
+    for i in range(full.shape[1] // own):
+
+        @pl.when(mp == i)
+        def _(i=i):
+            up_out_grad_ref[...] = full[:, i * own : (i + 1) * own].astype(BF16)
+
+
+def small_call(kernel, name, place, args, out_shape):
+    flops = 4 * 256 * 8192 * 128
+    return pl.pallas_call(
+        kernel,
+        out_shape=out_shape,
+        in_specs=[pl.BlockSpec(memory_space=pltpu.SMEM)] + vmem_specs(len(args)),
+        out_specs=tuple(vmem_specs(len(out_shape))),
+        compiler_params=pltpu.CompilerParams(vmem_limit_bytes=VMEM_LIMIT),
+        cost_estimate=pl.CostEstimate(flops=flops, bytes_accessed=6 * 2**20, transcendentals=0),
+        name=name,
+    )(place, *args)
+
+
+def token_weights(sequence_length_list, slot_sequence_index, rows):
+    seq_count = sequence_length_list.shape[1]
+    longest = rows // seq_count
+    total = rows * lax.axis_size("dp") * lax.axis_size("sub")
+    ratios = longest / sequence_length_list[0].astype(F32)
+    match = slot_sequence_index[:, None] == jnp.arange(seq_count, dtype=jnp.int32)[None, :]
+    weight = jnp.sum(jnp.where(match, ratios[None, :], F32(0.0)), axis=-1)
+    return weight * F32(1.0 / math.sqrt(total))
+
+
+def summed_halves(keep, send, axis, extra=None):
+    mine = keep.astype(F32) + swap(send, "sub").astype(F32)
+    mine = mine.astype(BF16)
+    pieces = [line_sum(p, "dp") for p in jnp.split(mine, CHUNKS, axis=axis)]
+    theirs = [swap(p, "sub") for p in pieces]
+    first = lax.axis_index("sub") == 0
+    low = [jnp.where(first, a, b) for a, b in zip(pieces, theirs)]
+    high = [jnp.where(first, b, a) for a, b in zip(pieces, theirs)]
+    return jnp.concatenate(low + high, axis=axis)
+
+
+def fast_body(
+    tokens,
+    cotangent,
+    rms_norm_gain,
+    gate_codes,
+    gate_block_scale,
+    up_codes,
+    up_block_scale,
+    down_codes,
+    down_block_scale,
+    up_adapter_in,
+    up_adapter_out,
+    down_adapter_in,
+    down_adapter_out,
+    sequence_length_list,
+    slot_sequence_index,
+):
+    rows, local_width = tokens.shape
+    blocks, _, units = gate_codes.shape
+    block = local_width // blocks
+    total_width = local_width * lax.axis_size("mp")
+    line = lax.axis_size("dp")
+    sub, mp, grp, dp = (lax.axis_index(a) for a in ("sub", "mp", "grp", "dp"))
+
+    order = ring_order(line)
+    sources = [[order[(order.index(d) - k) % line] for k in range(line)] for d in range(line)]
+    meta = jnp.concatenate(
+        [jnp.array(sources, jnp.int32)[dp], jnp.stack([grp, sub]).astype(jnp.int32)]
+    )
+    place = jnp.stack([sub, mp]).astype(jnp.int32)
+
+    gate_bufs = gather_chip(gate_codes)
+    up_bufs = gather_chip(up_codes)
+    down_bufs = gather_chip(jnp.swapaxes(down_codes, 0, 1))
+
+    own_squares = jnp.sum(jnp.square(tokens.astype(F32)), axis=-1)
+    squares = sum(others(own_squares, "mp"), own_squares) / total_width
+    inv_rms = lax.rsqrt(squares + EPS)[:, None]
+    normed = (tokens.astype(F32) * inv_rms * rms_norm_gain.astype(F32)[None, :]).astype(BF16)
+    weight = token_weights(sequence_length_list, slot_sequence_index, rows)
+    out_grad = (cotangent.astype(F32) * weight[:, None]).astype(BF16)
+    low_up = jnp.dot(normed, up_adapter_in, preferred_element_type=F32)
+    low_out = contract_dims(out_grad, down_adapter_out, 1, 1)
+    low_up = sum(others(low_up, "mp"), low_up).astype(BF16)
+    low_out = sum(others(low_out, "mp"), low_out).astype(BF16)
+    up_out = lax.all_gather(up_adapter_out, "mp", axis=1, tiled=True)
+    down_in = lax.all_gather(down_adapter_in, "mp", axis=0, tiled=True)
+    normed_t = normed.T
+
+    gate, gate_send = weight_product(
+        front_kernel, meta, gate_block_scale.astype(F32), normed, gate_bufs,
+        (blocks, block, units), units, "gate_product",
+    )
+    gate_more = others(gate_send, "mp")
+    up, up_send = weight_product(
+        front_kernel, meta, up_block_scale.astype(F32), normed, up_bufs,
+        (blocks, block, units), units, "up_product",
+    )
+    up_more = others(up_send, "mp")
+    count = len(up_more)
+
+    own_units = up_adapter_out.shape[1]
+    rank = up_adapter_out.shape[0]
+    half = local_width // 2
+    silu, down_keep, down_send, down_in_term = small_call(
+        lambda *refs: hidden_kernel(count, *refs),
+        "hidden_units",
+        place,
+        [gate, up, low_up, up_out, down_in, low_out, out_grad, *gate_more, *up_more],
+        (
+            jax.ShapeDtypeStruct((rows, units), F32),
+            jax.ShapeDtypeStruct((rank, half), BF16),
+            jax.ShapeDtypeStruct((rank, half), BF16),
+            jax.ShapeDtypeStruct((own_units, rank), BF16),
+        ),
+    )
+    down_out_gradient = summed_halves(down_keep, down_send, 1)
+
+    back, back_send = weight_product(
+        back_kernel, meta, down_block_scale.astype(F32), out_grad, down_bufs,
+        (units, local_width), units, "hidden_gradient",
+    )
+    up_keep, up_send_grad, up_out_term = small_call(
+        lambda *refs: gradient_kernel(count, *refs),
+        "up_gradient",
+        place,
+        [back, silu, low_out, down_in, up_out, low_up, normed_t, *others(back_send, "mp")],
+        (
+            jax.ShapeDtypeStruct((half, rank), BF16),
+            jax.ShapeDtypeStruct((half, rank), BF16),
+            jax.ShapeDtypeStruct((rank, own_units), BF16),
+        ),
+    )
+    up_in_gradient = summed_halves(up_keep, up_send_grad, 0)
+
+    small = jnp.stack([up_out_term, down_in_term])
+    small = (small.astype(F32) + swap(small, "sub").astype(F32)).astype(BF16)
+    small = line_sum(small, "dp")
+    return up_in_gradient, small[0], small[1], down_out_gradient
+
+
+def general_body(
     tokens,
     cotangent,
     rms_norm_gain,
@@ -111,6 +451,12 @@
     )
 
 
+def body(tokens, cotangent, rms_norm_gain, gate_codes, *rest):
+    whole_tiles = gate_codes.shape[1] % ROW_TILE == 0
+    form = fast_body if whole_tiles else general_body
+    return form(tokens, cotangent, rms_norm_gain, gate_codes, *rest)
+
+
 def solution(mesh):
     placed = (
         P(("grp", "dp", "sub"), "mp"),

time: 396 us -> 282 us (0.71)
  blocking collectives: 201 us -> 9.6 us
  starting transfers between devices: 0.42 us -> 75.2 us
  Pallas kernels: 0 us -> 35.9 us
  waiting for transfers between devices: 136 us -> 104 us
  matrix products: 32.5 us -> 5.48 us
  local copies, waits for them, and re-layouts: 2.07 us -> 25.1 us
  other arithmetic: 9.33 us -> 23.5 us
  between operations: 14.3 us -> 1.67 us
    psum x4 -> x0, blocking collectives: 201 us -> none  [the longest x1 172 us: body(): lax.psum((up_in_term, up_out_term, down_in_term, down_out_term), ('dp', '...]
    ppermute x0 -> x83, waiting for transfers between devices: none -> 104 us  [the longest x9 54.2 us: line_sum(): got = lax.ppermute(x, axis, [(s + 1, s), (n - 2 - s, n - 1 - s)])]
    all_gather x3 -> x0, waiting for transfers between devices: 103 us -> none  [the longest x1 41.5 us: body(): quant_u = lax.all_gather(up_codes, ('dp', 'sub'), axis=1, tiled=True)]
    ppermute x0 -> x83, starting transfers between devices: none -> 75.2 us  [the longest x41 22.4 us: swap(): return lax.ppermute(x, axis, [(0, 1), (1, 0)])]
    pallas_call x0 -> x5, Pallas kernels: none -> 35.9 us  [the longest x3 27.8 us: weight_product(): pl.pallas_call(kernel, out_shape=(jax.ShapeDtypeStruct((rows, units), F32...]
    reduce_scatter x3 -> x0, waiting for transfers between devices: 30.9 us -> none  [the longest x1 13.9 us: body(): lax.psum_scatter(up_next, 'mp', scatter_dimension=1, tiled=True)]
    dot_general x6 -> x1, matrix products: 20.4 us -> 4.19 us  [fast_body(): low_up = jnp.dot(normed, up_adapter_in, preferred_element_type=F32)]
    unnamed x22 -> x58, local copies, waits for them, and re-layouts: 0.32 us -> 13.1 us
  transfers between devices with their start and end apart: 6 -> 83, of which waited for: 6 -> 29; matrix products, arithmetic and copies ran while one was open for 8% -> 16% of each run, Pallas kernels for 0% -> 11%
where the time goes in v1:
time: 282 us; the launch traced here: 281 us
  waiting for transfers between devices  104 us (37%)
  starting transfers between devices  75.2 us (27%)
  Pallas kernels  35.9 us (13%)
  local copies, waits for them, and re-layouts  25.1 us (9%)
  other arithmetic  23.5 us (8%)
  blocking collectives  9.6 us (3%)
  matrix products  5.48 us (2%)
    ppermute x9, waiting for transfers between devices, line_sum(): got = lax.ppermute(x, axis, [(s + 1, s), (n - 2 - s, n - 1 - s)])  54.2 us
    pallas_call x3, Pallas kernels, weight_product(): pl.pallas_call(kernel, out_shape=(jax.ShapeDtypeStruct((rows, units), F32...  27.8 us
    ppermute x9, waiting for transfers between devices, line_sum(): x = add(x, lax.ppermute(x, axis, [(s, s + 1), (n - 1 - s, n - 2 - s)]))  23.5 us
    ppermute x41, starting transfers between devices, swap(): return lax.ppermute(x, axis, [(0, 1), (1, 0)])  22.4 us
    ppermute x9, starting transfers between devices, line_sum(): x = add(x, lax.ppermute(x, axis, [(s, s + 1), (n - 1 - s, n - 2 - s)]))  21.3 us
    ppermute x9, waiting for transfers between devices, gather_line(): moving = lax.ppermute(moving, 'dp', ring)  13.8 us
    unnamed x58, local copies, waits for them, and re-layouts  13.1 us
    ppermute x9, starting transfers between devices, line_sum(): got = lax.ppermute(x, axis, [(s + 1, s), (n - 2 - s, n - 1 - s)])  11.6 us
  transfers between devices with their start and end apart: 83, of which 29 were waited for; matrix products, arithmetic and copies ran while one was open for 16% of the time, Pallas kernels for 11%

profile of v1, /device:TPU:0, one launch (start us, length us, event | category | flops | bytes accessed | tf_op | source)
XLA Modules:
  0.0 280.6 jit_solution(12144252115413439805)
XLA Ops:
  16.7 6.4 %copy.36 = bf16[256,8192]{0,1:T(8,128)(2,1)} copy(bf16[256,8192]{1,0:T(8,128)(2,1)} %param.16) | data formatting | bytes 8388608 | tf_op args[0]
  36.5 4.6 %collective-permute-done.29.refs_3_ = bf16[32,16,256]{2,1,0:T(8,128)(2,1)} collective-permute-done((bf16[32,16,256]{2,1,0:T(8,128)(2,1)S(1)}, bf16[32,16,256]{2,1,0:T(8,128)(2,1)}, u32[]{:S(2)}, u32[]{:S(2)}) %collective-permute-start.29) | collective-permute-done | bytes 262176 | tf_op jit(solution)/shard_map/ppermute | solution.py:51
  44.8 5.3 %collective-permute-done.16.refs_3_ = bf16[32,16,256]{2,1,0:T(8,128)(2,1)} collective-permute-done((bf16[32,16,256]{2,1,0:T(8,128)(2,1)S(1)}, bf16[32,16,256]{2,1,0:T(8,128)(2,1)}, u32[]{:S(2)}, u32[]{:S(2)}) %collective-permute-start.16) | collective-permute-done | bytes 262176 | tf_op jit(solution)/shard_map/ppermute | solution.py:51
  62.2 4.8 %all_gather.6.refs_4_.refs_5_ = bf16[128,256]{1,0:T(8,128)(2,1)S(1)} all-gather(bf16[128,128]{1,0:T(8,128)(2,1)} %param.26), channel_id=1, replica_groups=mesh['grp'=2,'dp'=4,'mp'=2,'sub'=2] {'mp'}, dimensions={1}, use_global_device_ids=true | all-gather | bytes 98304 | tf_op jit(solution)/shard_map/all_gather | solution.py:302
  67.1 4.8 %all_gather.7.refs_5_.refs_4_ = bf16[256,128]{1,0:T(8,128)(2,1)S(1)} all-gather(bf16[128,128]{1,0:T(8,128)(2,1)} %param.27), channel_id=1, replica_groups=mesh['grp'=2,'dp'=4,'mp'=2,'sub'=2] {'mp'}, dimensions={0}, use_global_device_ids=true | all-gather | bytes 98304 | tf_op jit(solution)/shard_map/all_gather | solution.py:303
  75.8 4.4 %fusion.2 = bf16[256,8192]{0,1:T(8,128)(2,1)} fusion(bf16[256,8192]{0,1:T(8,128)(2,1)} %copy.36, f32[8192]{0:T(1024)} %convert_element_type.230, f32[256]{0:T(256)S(1)} %add_rsqrt_fusion), kind=kLoop, calls=%fused_computation.4 | loop fusion | flops 8388608 | bytes 8422400 | tf_op jit(solution)/shard_map/convert_element_type | solution.py:295
  80.2 5.2 %collective-permute-start.3 = (bf16[32,32,128]{2,1,0:T(8,128)(2,1)}, bf16[32,32,128]{2,1,0:T(8,128)(2,1)}, u32[]{:S(2)}, u32[]{:S(2)}) collective-permute-start(bf16[32,32,128]{2,1,0:T(8,128)(2,1)} %collective-permute-done.2.refs_3_), channel_id=1, source_target_pairs={{0,16},{16,0},{1,17},{17,1},{2,18},{18,2},{3,19},{19,3},{4,20},{20... | collective-permute-start | bytes 786440 | tf_op jit(solution)/shard_map/ppermute | solution.py:31
  90.1 6.4 %copy.38.x_ref = bf16[256,8192]{1,0:T(8,128)(2,1)} copy(bf16[256,8192]{0,1:T(8,128)(2,1)} %fusion.2) | data formatting | bytes 8388608 | tf_op jit(solution)/shard_map/convert_element_type | solution.py:295
  106.4 4.6 %collective-permute-done.5.refs_6_ = bf16[32,32,128]{2,1,0:T(8,128)(2,1)S(1)} collective-permute-done((bf16[32,32,128]{2,1,0:T(8,128)(2,1)}, bf16[32,32,128]{2,1,0:T(8,128)(2,1)S(1)}, u32[]{:S(2)}, u32[]{:S(2)}) %collective-permute-start.5) | collective-permute-done | bytes 262176 | tf_op jit(solution)/shard_map/ppermute | solution.py:31
  112.6 8.8 %up_product.1 = (f32[256,256]{1,0:T(8,128)S(1)}, bf16[256,256]{1,0:T(8,128)(2,1)S(1)}) custom-call(s32[6]{0:T(128)S(1)} %pad_add_fusion.1.meta, f32[64,2]{1,0:T(8,128)S(1)} %copy-done.17, bf16[256,8192]{1,0:T(8,128)(2,1)} %copy.38.x_ref, bf16[64,16,256]{2,1,0:T(8,128)(2,1)S(1)} %copy-done.2, bf16[32,16,256]{2,1,0:T(8,128)(2,1)S(1)} %copy-done.7, ...), custom_call_target="tpu_custom_call" | custom-call | flops 1073741824 | bytes 8388608 | tf_op jit(solution)/shard_map/up_product/pallas_call | solution.py:145
  121.5 8.4 %gate_product.1 = (f32[256,256]{1,0:T(8,128)S(1)}, bf16[256,256]{1,0:T(8,128)(2,1)S(1)}) custom-call(s32[6]{0:T(128)S(1)} %pad_add_fusion.1.meta, f32[64,2]{1,0:T(8,128)S(1)} %copy-done.16, bf16[256,8192]{1,0:T(8,128)(2,1)} %copy.38.x_ref, bf16[64,16,256]{2,1,0:T(8,128)(2,1)S(1)} %copy-done.3, bf16[32,16,256]{2,1,0:T(8,128)(2,1)S(1)} %copy-done.5, ...), custom_call_target="tpu_custom_call" | custom-call | flops 1073741824 | bytes 8388608 | tf_op jit(solution)/shard_map/gate_product/pallas_call | solution.py:145
  132.1 10.6 %hidden_gradient.1 = (f32[256,256]{1,0:T(8,128)S(1)}, bf16[256,256]{1,0:T(8,128)(2,1)S(1)}) custom-call(s32[6]{0:T(128)S(1)} %pad_add_fusion.1.meta, f32[2,64]{1,0:T(2,128)S(1)} %convert_element_type.224.scale, bf16[256,8192]{1,0:T(8,128)(2,1)} %copy-done.18, bf16[64,32,128]{2,1,0:T(8,128)(2,1)S(1)} %bitcast.24, ...), custom_call_target="tpu_custom_call" | custom-call | flops 1073741824 | bytes 8388608 | tf_op jit(solution)/shard_map/hidden_gradient/pallas_call | solution.py:145
  144.8 4.3 %hidden_units.1 = (f32[256,256]{1,0:T(8,128)S(1)}, bf16[128,4096]{1,0:T(8,128)(2,1)S(1)}, bf16[128,4096]{1,0:T(8,128)(2,1)}, bf16[128,128]{1,0:T(8,128)(2,1)S(1)}) custom-call(s32[2]{0:T(128)S(1)} %pad_add_fusion.refs_0_, f32[256,256]{1,0:T(8,128)S(1)} %get-tuple-element.18.refs_1_, f32[256,256]{1,0:T(8,128)S(1)} %get-tuple-element.19.refs_2_, ...), custom_call_target="tpu_custom_call" | custom-call | flops 1073741824 | bytes 6291456 | tf_op jit(solution)/shard_map/hidden_units/pallas_call | solution.py:225
  159.6 10.1 %collective-permute-done.65 = bf16[2,128,128]{2,1,0:T(8,128)(2,1)S(1)} collective-permute-done((bf16[2,128,128]{2,1,0:T(8,128)(2,1)S(1)}, bf16[2,128,128]{2,1,0:T(8,128)(2,1)S(1)}, u32[]{:S(2)}, u32[]{:S(2)}) %collective-permute-start.65) | collective-permute-done | bytes 65568 | tf_op jit(solution)/shard_map/ppermute | solution.py:74
  180.2 4.4 %collective-permute-start.50 = (bf16[1024,128]{1,0:T(8,128)(2,1)S(1)}, bf16[1024,128]{1,0:T(8,128)(2,1)S(1)}, u32[]{:S(2)}, u32[]{:S(2)}) collective-permute-start(bf16[1024,128]{1,0:T(8,128)(2,1)S(1)} %get-tuple-element.44), channel_id=1, source_target_pairs={{0,4},{12,8},{1,5},{13,9},{2,6},{14,10},{3,7},{15,11},{16,20},{28,... | collective-permute-start | bytes 786440 | tf_op jit(solution)/shard_map/ppermute | solution.py:71
  185.9 4.4 %collective-permute-start.54 = (bf16[1024,128]{1,0:T(8,128)(2,1)S(1)}, bf16[1024,128]{1,0:T(8,128)(2,1)S(1)}, u32[]{:S(2)}, u32[]{:S(2)}) collective-permute-start(bf16[1024,128]{1,0:T(8,128)(2,1)S(1)} %get-tuple-element.43), channel_id=1, source_target_pairs={{0,4},{12,8},{1,5},{13,9},{2,6},{14,10},{3,7},{15,11},{16,20},{28,... | collective-permute-start | bytes 786440 | tf_op jit(solution)/shard_map/ppermute | solution.py:71
  191.5 4.4 %collective-permute-start.58 = (bf16[1024,128]{1,0:T(8,128)(2,1)S(1)}, bf16[1024,128]{1,0:T(8,128)(2,1)S(1)}, u32[]{:S(2)}, u32[]{:S(2)}) collective-permute-start(bf16[1024,128]{1,0:T(8,128)(2,1)S(1)} %get-tuple-element.42), channel_id=1, source_target_pairs={{0,4},{12,8},{1,5},{13,9},{2,6},{14,10},{3,7},{15,11},{16,20},{28,... | collective-permute-start | bytes 786440 | tf_op jit(solution)/shard_map/ppermute | solution.py:71
  198.2 4.5 %collective-permute-done.46 = bf16[1024,128]{1,0:T(8,128)(2,1)S(1)} collective-permute-done((bf16[1024,128]{1,0:T(8,128)(2,1)S(1)}, bf16[1024,128]{1,0:T(8,128)(2,1)S(1)}, u32[]{:S(2)}, u32[]{:S(2)}) %collective-permute-start.46) | collective-permute-done | bytes 262176 | tf_op jit(solution)/shard_map/ppermute | solution.py:71
  203.4 4.9 %collective-permute-done.50 = bf16[1024,128]{1,0:T(8,128)(2,1)S(1)} collective-permute-done((bf16[1024,128]{1,0:T(8,128)(2,1)S(1)}, bf16[1024,128]{1,0:T(8,128)(2,1)S(1)}, u32[]{:S(2)}, u32[]{:S(2)}) %collective-permute-start.50) | collective-permute-done | bytes 262176 | tf_op jit(solution)/shard_map/ppermute | solution.py:71
  209.0 4.9 %collective-permute-done.54 = bf16[1024,128]{1,0:T(8,128)(2,1)S(1)} collective-permute-done((bf16[1024,128]{1,0:T(8,128)(2,1)S(1)}, bf16[1024,128]{1,0:T(8,128)(2,1)S(1)}, u32[]{:S(2)}, u32[]{:S(2)}) %collective-permute-start.54) | collective-permute-done | bytes 262176 | tf_op jit(solution)/shard_map/ppermute | solution.py:71
  227.5 13.0 %collective-permute-done.81 = bf16[128,1024]{1,0:T(8,128)(2,1)S(1)} collective-permute-done((bf16[128,1024]{1,0:T(8,128)(2,1)S(1)}, bf16[128,1024]{1,0:T(8,128)(2,1)S(1)}, u32[]{:S(2)}, u32[]{:S(2)}) %collective-permute-start.81) | collective-permute-done | bytes 262176 | tf_op jit(solution)/shard_map/ppermute | solution.py:74
  257.4 5.6 %collective-permute-done.60 = bf16[1024,128]{1,0:T(8,128)(2,1)S(1)} collective-permute-done((bf16[1024,128]{1,0:T(8,128)(2,1)S(1)}, bf16[1024,128]{1,0:T(8,128)(2,1)S(1)}, u32[]{:S(2)}, u32[]{:S(2)}) %collective-permute-start.60) | collective-permute-done | bytes 262176 | tf_op jit(solution)/shard_map/ppermute | solution.py:74
  263.0 5.6 %collective-permute-done.56 = bf16[1024,128]{1,0:T(8,128)(2,1)S(1)} collective-permute-done((bf16[1024,128]{1,0:T(8,128)(2,1)S(1)}, bf16[1024,128]{1,0:T(8,128)(2,1)S(1)}, u32[]{:S(2)}, u32[]{:S(2)}) %collective-permute-start.56) | collective-permute-done | bytes 262176 | tf_op jit(solution)/shard_map/ppermute | solution.py:74
  268.6 4.3 %collective-permute-done.52 = bf16[1024,128]{1,0:T(8,128)(2,1)S(1)} collective-permute-done((bf16[1024,128]{1,0:T(8,128)(2,1)S(1)}, bf16[1024,128]{1,0:T(8,128)(2,1)S(1)}, u32[]{:S(2)}, u32[]{:S(2)}) %collective-permute-start.52) | collective-permute-done | bytes 262176 | tf_op jit(solution)/shard_map/ppermute | solution.py:74
  (274 shorter events, 134.3 us)
Async XLA Ops:
  1.8 28.4 %collective-permute-start.27 = (bf16[32,16,256]{2,1,0:T(8,128)(2,1)S(1)}, bf16[32,16,256]{2,1,0:T(8,128)(2,1)S(1)}, u32[]{:S(2)}, u32[]{:S(2)}) collective-permute-start(bf16[32,16,256]{2,1,0:T(8,128)(2,1)S(1)} %constant_dynamic-slice_fusion), channel_id=1, source_target_pairs={{0,4},{4,12},{12,8},{8,0},{1,5},{5,13},{13,9},{9,1},{2,6},{6,14},{... | collective-permute-start | bytes 786440 | tf_op jit(solution)/shard_map/ppermute | solution.py:51
  5.8 26.3 %collective-permute-start.14 = (bf16[32,16,256]{2,1,0:T(8,128)(2,1)S(1)}, bf16[32,16,256]{2,1,0:T(8,128)(2,1)S(1)}, u32[]{:S(2)}, u32[]{:S(2)}) collective-permute-start(bf16[32,16,256]{2,1,0:T(8,128)(2,1)S(1)} %constant_dynamic-slice_fusion.1), channel_id=1, source_target_pairs={{0,4},{4,12},{12,8},{8,0},{1,5},{5,13},{13,9},{9,1},{2,6},{6,14},{... | collective-permute-start | bytes 786440 | tf_op jit(solution)/shard_map/ppermute | solution.py:51
  53.3 19.2 %collective-permute-start.6 = (bf16[64,32,128]{2,1,0:T(8,128)(2,1)S(1)}, bf16[64,32,128]{2,1,0:T(8,128)(2,1)S(1)}, u32[]{:S(2)}, u32[]{:S(2)}) collective-permute-start(bf16[64,32,128]{2,1,0:T(8,128)(2,1)S(1)} %bitcast.23), channel_id=1, source_target_pairs={{0,1},{1,0},{2,3},{3,2},{4,5},{5,4},{6,7},{7,6},{8,9},{9,8},{10,11... | collective-permute-start | bytes 1572872 | tf_op jit(solution)/shard_map/ppermute | solution.py:31
  54.9 20.4 %collective-permute-start.30 = (bf16[32,16,256]{2,1,0:T(8,128)(2,1)}, bf16[32,16,256]{2,1,0:T(8,128)(2,1)}, u32[]{:S(2)}, u32[]{:S(2)}) collective-permute-start(bf16[32,16,256]{2,1,0:T(8,128)(2,1)} %collective-permute-done.29.refs_3_), channel_id=1, source_target_pairs={{0,16},{16,0},{1,17},{17,1},{2,18},{18,2},{3,19},{19,3},{4,20},{20... | collective-permute-start | bytes 786440 | tf_op jit(solution)/shard_map/ppermute | solution.py:31
  105.8 24.1 %collective-permute-start.8 = (bf16[32,32,128]{2,1,0:T(8,128)(2,1)}, bf16[32,32,128]{2,1,0:T(8,128)(2,1)S(1)}, u32[]{:S(2)}, u32[]{:S(2)}) collective-permute-start(bf16[32,32,128]{2,1,0:T(8,128)(2,1)} %collective-permute-done.1.refs_2_), channel_id=1, source_target_pairs={{0,1},{1,0},{2,3},{3,2},{4,5},{5,4},{6,7},{7,6},{8,9},{9,8},{10,11... | collective-permute-start | bytes 786440 | tf_op jit(solution)/shard_map/ppermute | solution.py:31
  105.8 26.2 %collective-permute-start.11 = (bf16[32,32,128]{2,1,0:T(8,128)(2,1)}, bf16[32,32,128]{2,1,0:T(8,128)(2,1)S(1)}, u32[]{:S(2)}, u32[]{:S(2)}) collective-permute-start(bf16[32,32,128]{2,1,0:T(8,128)(2,1)} %collective-permute-done.4.refs_5_), channel_id=1, source_target_pairs={{0,1},{1,0},{2,3},{3,2},{4,5},{5,4},{6,7},{7,6},{8,9},{9,8},{10,11... | collective-permute-start | bytes 786440 | tf_op jit(solution)/shard_map/ppermute | solution.py:31
  106.4 25.8 %collective-permute-start.10 = (bf16[32,32,128]{2,1,0:T(8,128)(2,1)}, bf16[32,32,128]{2,1,0:T(8,128)(2,1)S(1)}, u32[]{:S(2)}, u32[]{:S(2)}) collective-permute-start(bf16[32,32,128]{2,1,0:T(8,128)(2,1)} %collective-permute-done.3.refs_4_), channel_id=1, source_target_pairs={{0,1},{1,0},{2,3},{3,2},{4,5},{5,4},{6,7},{7,6},{8,9},{9,8},{10,11... | collective-permute-start | bytes 786440 | tf_op jit(solution)/shard_map/ppermute | solution.py:31
  111.1 21.1 %collective-permute-start.12 = (bf16[32,32,128]{2,1,0:T(8,128)(2,1)S(1)}, bf16[32,32,128]{2,1,0:T(8,128)(2,1)S(1)}, u32[]{:S(2)}, u32[]{:S(2)}) collective-permute-start(bf16[32,32,128]{2,1,0:T(8,128)(2,1)S(1)} %collective-permute-done.5.refs_6_), channel_id=1, source_target_pairs={{0,1},{1,0},{2,3},{3,2},{4,5},{5,4},{6,7},{7,6},{8,9},{9,8},{10,11... | collective-permute-start | bytes 786440 | tf_op jit(solution)/shard_map/ppermute | solution.py:31
  121.4 23.3 %collective-permute-start.40 = (f32[256,128]{1,0:T(8,128)S(1)}, f32[256,128]{1,0:T(8,128)S(1)}, u32[]{:S(2)}, u32[]{:S(2)}) collective-permute-start(f32[256,128]{1,0:T(8,128)S(1)} %fusion.8), channel_id=1, source_target_pairs={{0,2},{2,0},{1,3},{3,1},{4,6},{6,4},{5,7},{7,5},{8,10},{10,8},{9,1... | collective-permute-start | bytes 393224 | tf_op jit(solution)/shard_map/ppermute | solution.py:36
  176.1 21.0 %collective-permute-start.79 = (bf16[128,1024]{1,0:T(8,128)(2,1)S(1)}, bf16[128,1024]{1,0:T(8,128)(2,1)S(1)}, u32[]{:S(2)}, u32[]{:S(2)}) collective-permute-start(bf16[128,1024]{1,0:T(8,128)(2,1)S(1)} %get-tuple-element.34), channel_id=1, source_target_pairs={{0,4},{12,8},{1,5},{13,9},{2,6},{14,10},{3,7},{15,11},{16,20},{28,... | collective-permute-start | bytes 786440 | tf_op jit(solution)/shard_map/ppermute | solution.py:71
  177.8 24.9 %collective-permute-start.46 = (bf16[1024,128]{1,0:T(8,128)(2,1)S(1)}, bf16[1024,128]{1,0:T(8,128)(2,1)S(1)}, u32[]{:S(2)}, u32[]{:S(2)}) collective-permute-start(bf16[1024,128]{1,0:T(8,128)(2,1)S(1)} %get-tuple-element.45), channel_id=1, source_target_pairs={{0,4},{12,8},{1,5},{13,9},{2,6},{14,10},{3,7},{15,11},{16,20},{28,... | collective-permute-start | bytes 786440 | tf_op jit(solution)/shard_map/ppermute | solution.py:71
  180.2 28.1 %collective-permute-start.50 = (bf16[1024,128]{1,0:T(8,128)(2,1)S(1)}, bf16[1024,128]{1,0:T(8,128)(2,1)S(1)}, u32[]{:S(2)}, u32[]{:S(2)}) collective-permute-start(bf16[1024,128]{1,0:T(8,128)(2,1)S(1)} %get-tuple-element.44), channel_id=1, source_target_pairs={{0,4},{12,8},{1,5},{13,9},{2,6},{14,10},{3,7},{15,11},{16,20},{28,... | collective-permute-start | bytes 786440 | tf_op jit(solution)/shard_map/ppermute | solution.py:71
  185.9 28.1 %collective-permute-start.54 = (bf16[1024,128]{1,0:T(8,128)(2,1)S(1)}, bf16[1024,128]{1,0:T(8,128)(2,1)S(1)}, u32[]{:S(2)}, u32[]{:S(2)}) collective-permute-start(bf16[1024,128]{1,0:T(8,128)(2,1)S(1)} %get-tuple-element.43), channel_id=1, source_target_pairs={{0,4},{12,8},{1,5},{13,9},{2,6},{14,10},{3,7},{15,11},{16,20},{28,... | collective-permute-start | bytes 786440 | tf_op jit(solution)/shard_map/ppermute | solution.py:71
  191.5 25.8 %collective-permute-start.58 = (bf16[1024,128]{1,0:T(8,128)(2,1)S(1)}, bf16[1024,128]{1,0:T(8,128)(2,1)S(1)}, u32[]{:S(2)}, u32[]{:S(2)}) collective-permute-start(bf16[1024,128]{1,0:T(8,128)(2,1)S(1)} %get-tuple-element.42), channel_id=1, source_target_pairs={{0,4},{12,8},{1,5},{13,9},{2,6},{14,10},{3,7},{15,11},{16,20},{28,... | collective-permute-start | bytes 786440 | tf_op jit(solution)/shard_map/ppermute | solution.py:71
  197.5 20.7 %collective-permute-start.80 = (bf16[128,1024]{1,0:T(8,128)(2,1)S(1)}, bf16[128,1024]{1,0:T(8,128)(2,1)S(1)}, u32[]{:S(2)}, u32[]{:S(2)}) collective-permute-start(bf16[128,1024]{1,0:T(8,128)(2,1)S(1)} %get-tuple-element.30), channel_id=1, source_target_pairs={{4,8},{8,4},{5,9},{9,5},{6,10},{10,6},{7,11},{11,7},{20,24},{24,20... | collective-permute-start | bytes 786440 | tf_op jit(solution)/shard_map/ppermute | solution.py:72
  220.5 20.0 %collective-permute-start.81 = (bf16[128,1024]{1,0:T(8,128)(2,1)S(1)}, bf16[128,1024]{1,0:T(8,128)(2,1)S(1)}, u32[]{:S(2)}, u32[]{:S(2)}) collective-permute-start(bf16[128,1024]{1,0:T(8,128)(2,1)S(1)} %add_convert_fusion.2), channel_id=1, source_target_pairs={{4,0},{8,12},{5,1},{9,13},{6,2},{10,14},{7,3},{11,15},{20,16},{24,... | collective-permute-start | bytes 786440 | tf_op jit(solution)/shard_map/ppermute | solution.py:74
  221.9 24.2 %collective-permute-start.77 = (bf16[128,1024]{1,0:T(8,128)(2,1)S(1)}, bf16[128,1024]{1,0:T(8,128)(2,1)S(1)}, u32[]{:S(2)}, u32[]{:S(2)}) collective-permute-start(bf16[128,1024]{1,0:T(8,128)(2,1)S(1)} %add_convert_fusion.4), channel_id=1, source_target_pairs={{4,0},{8,12},{5,1},{9,13},{6,2},{10,14},{7,3},{11,15},{20,16},{24,... | collective-permute-start | bytes 786440 | tf_op jit(solution)/shard_map/ppermute | solution.py:74
  223.3 28.4 %collective-permute-start.73 = (bf16[128,1024]{1,0:T(8,128)(2,1)S(1)}, bf16[128,1024]{1,0:T(8,128)(2,1)S(1)}, u32[]{:S(2)}, u32[]{:S(2)}) collective-permute-start(bf16[128,1024]{1,0:T(8,128)(2,1)S(1)} %add_convert_fusion.6), channel_id=1, source_target_pairs={{4,0},{8,12},{5,1},{9,13},{6,2},{10,14},{7,3},{11,15},{20,16},{24,... | collective-permute-start | bytes 786440 | tf_op jit(solution)/shard_map/ppermute | solution.py:74
  224.7 32.6 %collective-permute-start.69 = (bf16[128,1024]{1,0:T(8,128)(2,1)S(1)}, bf16[128,1024]{1,0:T(8,128)(2,1)S(1)}, u32[]{:S(2)}, u32[]{:S(2)}) collective-permute-start(bf16[128,1024]{1,0:T(8,128)(2,1)S(1)} %add_convert_fusion.8), channel_id=1, source_target_pairs={{4,0},{8,12},{5,1},{9,13},{6,2},{10,14},{7,3},{11,15},{20,16},{24,... | collective-permute-start | bytes 786440 | tf_op jit(solution)/shard_map/ppermute | solution.py:74
  226.1 36.9 %collective-permute-start.60 = (bf16[1024,128]{1,0:T(8,128)(2,1)S(1)}, bf16[1024,128]{1,0:T(8,128)(2,1)S(1)}, u32[]{:S(2)}, u32[]{:S(2)}) collective-permute-start(bf16[1024,128]{1,0:T(8,128)(2,1)S(1)} %add_convert_fusion.10), channel_id=1, source_target_pairs={{4,0},{8,12},{5,1},{9,13},{6,2},{10,14},{7,3},{11,15},{20,16},{24,... | collective-permute-start | bytes 786440 | tf_op jit(solution)/shard_map/ppermute | solution.py:74
  240.5 28.1 %collective-permute-start.56 = (bf16[1024,128]{1,0:T(8,128)(2,1)S(1)}, bf16[1024,128]{1,0:T(8,128)(2,1)S(1)}, u32[]{:S(2)}, u32[]{:S(2)}) collective-permute-start(bf16[1024,128]{1,0:T(8,128)(2,1)S(1)} %add_convert_fusion.12), channel_id=1, source_target_pairs={{4,0},{8,12},{5,1},{9,13},{6,2},{10,14},{7,3},{11,15},{20,16},{24,... | collective-permute-start | bytes 786440 | tf_op jit(solution)/shard_map/ppermute | solution.py:74
  246.1 26.8 %collective-permute-start.52 = (bf16[1024,128]{1,0:T(8,128)(2,1)S(1)}, bf16[1024,128]{1,0:T(8,128)(2,1)S(1)}, u32[]{:S(2)}, u32[]{:S(2)}) collective-permute-start(bf16[1024,128]{1,0:T(8,128)(2,1)S(1)} %add_convert_fusion.14), channel_id=1, source_target_pairs={{4,0},{8,12},{5,1},{9,13},{6,2},{10,14},{7,3},{11,15},{20,16},{24,... | collective-permute-start | bytes 786440 | tf_op jit(solution)/shard_map/ppermute | solution.py:74
  251.7 24.0 %collective-permute-start.48 = (bf16[1024,128]{1,0:T(8,128)(2,1)S(1)}, bf16[1024,128]{1,0:T(8,128)(2,1)S(1)}, u32[]{:S(2)}, u32[]{:S(2)}) collective-permute-start(bf16[1024,128]{1,0:T(8,128)(2,1)S(1)} %add_convert_fusion.16), channel_id=1, source_target_pairs={{4,0},{8,12},{5,1},{9,13},{6,2},{10,14},{7,3},{11,15},{20,16},{24,... | collective-permute-start | bytes 786440 | tf_op jit(solution)/shard_map/ppermute | solution.py:74
  257.3 19.9 %collective-permute-start.82 = (bf16[128,1024]{1,0:T(8,128)(2,1)S(1)}, bf16[128,1024]{1,0:T(8,128)(2,1)S(1)}, u32[]{:S(2)}, u32[]{:S(2)}) collective-permute-start(bf16[128,1024]{1,0:T(8,128)(2,1)S(1)} %broadcast_select_fusion), channel_id=1, source_target_pairs={{0,1},{1,0},{2,3},{3,2},{4,5},{5,4},{6,7},{7,6},{8,9},{9,8},{10,11... | collective-permute-start | bytes 786440 | tf_op jit(solution)/shard_map/ppermute | solution.py:31
  (87 other events, 842.1 us)

commit v2 on v0

--- a/solution.py
+++ b/solution.py
@@ -3,19 +3,568 @@
 import jax
 import jax.numpy as jnp
 from jax import lax
+from jax.experimental import pallas as pl
+from jax.experimental.pallas import tpu as pltpu
 from jax.sharding import PartitionSpec as P
 
 ADAPTER_SCALE = 2.0
 EPS = 1e-05
+ROW_TILE = 16
+LANES = 128
+MIB = 1024 * 1024
+
+F32 = jnp.float32
+BF16 = jnp.bfloat16
 
 
 def contract_dims(left, right, left_dim, right_dim):
     return lax.dot_general(
-        left, right, (((left_dim,), (right_dim,)), ((), ())), preferred_element_type=jnp.float32
-    )
-
-
-def body(
+        left, right, (((left_dim,), (right_dim,)), ((), ())), preferred_element_type=F32
+    )
+
+
+def dot(left, right):
+    return jnp.dot(left, right, preferred_element_type=F32)
+
+
+def ring_at(pos, n):
+    if isinstance(pos, int):
+        return 0 if pos == 0 else (2 * pos - 1 if 2 * pos <= n else 2 * (n - pos))
+    return jnp.where(pos == 0, 0, jnp.where(2 * pos <= n, 2 * pos - 1, 2 * (n - pos)))
+
+
+def ring_position():
+    n = lax.axis_size("dp")
+    place = lax.axis_index("dp")
+    odd = lax.rem(place, 2) == 1
+    return jnp.where(place == 0, 0, jnp.where(odd, (place + 1) // 2, n - place // 2))
+
+
+def ring_step(x):
+    n = lax.axis_size("dp")
+    return lax.ppermute(x, "dp", [(ring_at(i, n), ring_at((i + 1) % n, n)) for i in range(n)])
+
+
+def swap(x, axis):
+    return lax.ppermute(x, axis, [(0, 1), (1, 0)])
+
+
+def others(x, axis):
+    n = lax.axis_size(axis)
+    return [lax.ppermute(x, axis, [(i, (i + k) % n) for i in range(n)]) for k in range(1, n)]
+
+
+def after(x, *done):
+    return lax.optimization_barrier((x, *done))[0]
+
+
+def add(*terms):
+    return sum(t.astype(F32) for t in terms).astype(BF16)
+
+
+def ring_sum(parts):
+    total = parts[0]
+    for part in parts[1:]:
+        total = add(ring_step(total), part)
+    return total
+
+
+def ring_gather(block):
+    blocks = [block]
+    for _ in range(lax.axis_size("dp") - 1):
+        blocks.append(ring_step(blocks[-1]))
+    return blocks, [swap(b, "sub") for b in blocks]
+
+
+def call(kernel, name, args, out_shape, scratch=(), specs=None, limit=24, flops=0, out_specs=None):
+    vmem = pl.BlockSpec(memory_space=pltpu.VMEM)
+    moved = sum(a.size * a.dtype.itemsize for a in args) + sum(
+        math.prod(s.shape) * s.dtype.itemsize for s in out_shape
+    )
+    return pl.pallas_call(
+        kernel,
+        out_shape=tuple(out_shape),
+        in_specs=specs or [vmem] * len(args),
+        out_specs=out_specs or tuple([vmem] * len(out_shape)),
+        scratch_shapes=list(scratch),
+        compiler_params=pltpu.CompilerParams(vmem_limit_bytes=limit * MIB),
+        cost_estimate=pl.CostEstimate(flops=flops, bytes_accessed=moved, transcendentals=0),
+        name=name,
+    )(*args)
+
+
+def shape(dims, dtype=BF16):
+    return jax.ShapeDtypeStruct(tuple(dims), dtype)
+
+
+def halves_call(kernel, name, place, wide, narrow, adapter, adapter_rows):
+    rows, width = wide.shape
+    step = width // 8
+    per = width // 2 // step
+    rank = adapter.shape[1] if adapter_rows else adapter.shape[0]
+
+    def at(j, place):
+        return jnp.where(j < per, (1 - place[0]) * per + j, place[0] * per + j - per)
+
+    adapter_spec = (
+        pl.BlockSpec((step, rank), lambda j, place: (at(j, place), 0))
+        if adapter_rows
+        else pl.BlockSpec((rank, step), lambda j, place: (0, at(j, place)))
+    )
+    narrow_specs = [
+        pl.BlockSpec((rows, 1), lambda j, place: (0, 0))
+        if n.shape[0] == rows
+        else pl.BlockSpec((1, step), lambda j, place: (0, at(j, place)))
+        for n in narrow
+    ]
+    return pl.pallas_call(
+        kernel,
+        out_shape=(shape((rows, width // 2)), shape((rows, width // 2)), shape((rows, rank), F32)),
+        grid_spec=pltpu.PrefetchScalarGridSpec(
+            num_scalar_prefetch=1,
+            grid=(2 * per,),
+            in_specs=[pl.BlockSpec((rows, step), lambda j, place: (0, at(j, place)))]
+            + narrow_specs
+            + [adapter_spec],
+            out_specs=(
+                pl.BlockSpec((rows, step), lambda j, place: (0, jnp.minimum(j, per - 1))),
+                pl.BlockSpec((rows, step), lambda j, place: (0, jnp.maximum(j - per, 0))),
+                pl.BlockSpec((rows, rank), lambda j, place: (0, 0)),
+            ),
+        ),
+        compiler_params=pltpu.CompilerParams(vmem_limit_bytes=16 * MIB),
+        cost_estimate=pl.CostEstimate(
+            flops=2 * rows * width * rank, bytes_accessed=4 * wide.size, transcendentals=0
+        ),
+        name=name,
+    )(place, wide, *narrow, adapter)
+
+
+def store_half(value, send_ref, own_ref):
+    j = pl.program_id(0)
+    first = j < pl.num_programs(0) // 2
+
+    @pl.when(first)
+    def _():
+        send_ref[...] = value
+
+    @pl.when(jnp.logical_not(first))
+    def _():
+        own_ref[...] = value
+
+
+def accumulate(ref, term):
+    j = pl.program_id(0)
+
+    @pl.when(j == 0)
+    def _():
+        ref[...] = term
+
+    @pl.when(j > 0)
+    def _():
+        ref[...] += term
+
+
+def token_kernel(place, tokens, inv_rms, gain, adapter, send_ref, own_ref, low_ref):
+    value = tokens[...].astype(F32) * inv_rms[...] * gain[...].astype(F32)
+    value = value.astype(BF16)
+    store_half(value, send_ref, own_ref)
+    accumulate(low_ref, dot(value, adapter[...]))
+
+
+def cotangent_kernel(place, cotangent, weight, adapter, send_ref, own_ref, low_ref):
+    value = (cotangent[...].astype(F32) * weight[...]).astype(BF16)
+    store_half(value, send_ref, own_ref)
+    accumulate(low_ref, contract_dims(value, adapter[...], 1, 1))
+
+
+def transpose_kernel(own, got, out_ref):
+    rows, step = own.shape[0], out_ref.shape[0]
+    for i, ref in enumerate((own, got)):
+        out_ref[:, i * rows : (i + 1) * rows] = ref[...].astype(F32).T.astype(BF16)
+
+
+def widen(scale, wide):
+    table = scale[...].astype(F32)
+    for g in range(scale.shape[1]):
+        wide[g] = jnp.broadcast_to(table[:, g : g + 1], wide.shape[1:])
+
+
+def place_shards(codes, got, moved, store):
+    n = lax.axis_size("dp")
+    sub, grp, place = (lax.axis_index(a) for a in ("sub", "grp", "dp"))
+    pos = ring_position()
+    blocks = got.shape[0]
+    quarter = blocks // 2
+
+    @pl.loop(0, blocks, unroll=4)
+    def _(b):
+        store(b, place * 2 + sub, codes[sub * blocks + b])
+        store(b, place * 2 + 1 - sub, got[b])
+
+    for k in range(n - 1):
+        there = ring_at(lax.rem(pos - k - 1 + n, n), n)
+        for which in range(2):
+            piece = moved[2 * k + which]
+            start = (grp if which == 0 else 1 - grp) * quarter
+
+            @pl.loop(0, quarter, unroll=4)
+            def _(b, piece=piece, start=start, there=there):
+                store(start + b, there * 2 + sub, piece[b])
+                store(start + b, there * 2 + 1 - sub, piece[quarter + b])
+
+
+def front_kernel(own, got, scale, codes, codes_got, *refs):
+    moved, (mine_ref, theirs_ref, wide, weight) = refs[:-4], refs[-4:]
+    blocks, rows, units = codes_got.shape
+    first = lax.axis_index("sub") * blocks
+    widen(scale, wide)
+
+    def store(b, shard, piece):
+        at = pl.ds(pl.multiple_of(shard * rows, ROW_TILE), rows)
+        for g in range(units // LANES):
+            cols = slice(g * LANES, (g + 1) * LANES)
+            factor = wide[g * wide.shape[0] * LANES // units, pl.ds(first + b, 1), :]
+            weight[b, at, cols] = (piece[:, cols].astype(F32) * factor).astype(BF16)
+
+    place_shards(codes, codes_got, moved, store)
+    matrix = weight[...].reshape(-1, units)
+    mine_ref[...] = dot(own[...], matrix)
+    theirs_ref[...] = dot(got[...], matrix).astype(BF16)
+
+
+def back_kernel(own, got, scale, codes, codes_got, *refs):
+    moved, (mine_ref, theirs_ref, wide, weight) = refs[:-4], refs[-4:]
+    blocks, rows, block = codes_got.shape
+    first = lax.axis_index("sub") * blocks
+    per_group = weight.shape[0] // wide.shape[0]
+    widen(scale, wide)
+
+    def store(b, shard, piece):
+        at = pl.multiple_of(shard * rows, ROW_TILE)
+        factor = wide[at // per_group, pl.ds(first + b, 1), :]
+        cols = pl.ds(pl.multiple_of(b * block, block), block)
+        weight[pl.ds(at, rows), cols] = (piece.astype(F32) * factor).astype(BF16)
+
+    place_shards(codes, codes_got, moved, store)
+    matrix = weight[...]
+    mine_ref[...] = contract_dims(own[...], matrix, 1, 1)
+    theirs_ref[...] = contract_dims(got[...], matrix, 1, 1).astype(BF16)
+
+
+def place_own(scratch, own, more, axis):
+    n = len(more) + 1
+    size = own.shape[axis]
+    for k, ref in enumerate((own, *more)):
+        at = pl.ds(pl.multiple_of(lax.rem(lax.axis_index("mp") + n - k, n) * size, size), size)
+        if axis == 0:
+            scratch[at, :] = ref[...]
+        else:
+            scratch[:, at] = ref[...]
+
+
+def own_units(full, ref, axis):
+    size = ref.shape[axis]
+    for i in range(full.shape[axis] // size):
+
+        @pl.when(lax.axis_index("mp") == i)
+        def _(i=i):
+            ref[...] = lax.slice_in_dim(full, i * size, (i + 1) * size, axis=axis).astype(BF16)
+
+
+def hidden_kernel(more, gate, up, low_up, low_out, up_out, down_in, *refs):
+    gate_more, up_more = refs[:more], refs[more : 2 * more]
+    up_out_more, down_in_more = refs[2 * more : 3 * more], refs[3 * more : 4 * more]
+    silu_ref, low_ref, down_in_term, up_out_all, down_in_all = refs[4 * more :]
+    place_own(up_out_all, up_out, up_out_more, 1)
+    place_own(down_in_all, down_in, down_in_more, 0)
+    gate_sum, up_sum = gate[...], up[...]
+    for ref in gate_more:
+        gate_sum = gate_sum + ref[...].astype(F32)
+    for ref in up_more:
+        up_sum = up_sum + ref[...].astype(F32)
+    up_sum = up_sum + ADAPTER_SCALE * dot(low_up[...], up_out_all[...])
+    silu = gate_sum * jax.nn.sigmoid(gate_sum)
+    silu_ref[...] = silu
+    hidden = (silu * up_sum).astype(BF16)
+    low_ref[...] = (ADAPTER_SCALE * dot(hidden, down_in_all[...])).astype(BF16)
+    hidden_t = hidden.astype(F32).T.astype(BF16)
+    own_units(ADAPTER_SCALE * dot(hidden_t, low_out[...]), down_in_term, 0)
+
+
+def up_grad_kernel(more, back, silu, low_up, low_out, up_out, down_in, *refs):
+    back_more, up_out_more, down_in_more = (refs[i * more : (i + 1) * more] for i in range(3))
+    low_ref, up_out_term, up_out_all, down_in_all = refs[3 * more :]
+    place_own(up_out_all, up_out, up_out_more, 1)
+    place_own(down_in_all, down_in, down_in_more, 0)
+    total = back[...]
+    for ref in back_more:
+        total = total + ref[...].astype(F32)
+    total = total + ADAPTER_SCALE * contract_dims(low_out[...], down_in_all[...], 1, 1)
+    up_grad = (total * silu[...]).astype(BF16)
+    low_ref[...] = (ADAPTER_SCALE * contract_dims(up_grad, up_out_all[...], 1, 1)).astype(BF16)
+    low_up_t = low_up[...].astype(F32).T.astype(BF16)
+    own_units(ADAPTER_SCALE * dot(low_up_t, up_grad), up_out_term, 1)
+
+
+def down_out_kernel(low, low_got, grad, grad_got, *out_refs):
+    n = len(out_refs)
+    pos = ring_position()
+    low_t = jnp.concatenate([low[...], low_got[...]], axis=0).astype(F32).T.astype(BF16)
+    rows = low.shape[0]
+    for k, ref in enumerate(out_refs):
+        size = ref.shape[1]
+        at = pl.ds(pl.multiple_of(lax.rem(pos - 1 - k + 2 * n, n) * size, size), size)
+        ref[...] = (
+            dot(low_t[:, :rows], grad[:, at]) + dot(low_t[:, rows:], grad_got[:, at])
+        ).astype(BF16)
+
+
+def up_in_kernel(low, low_got, normed_t, up_out_term, down_in_term, *out_refs):
+    n = len(out_refs)
+    pos = ring_position()
+    size = normed_t.shape[0] // n
+    extra = out_refs[0].shape[0] - size
+    both = jnp.concatenate([low[...], low_got[...]], axis=0)
+    for k, ref in enumerate(out_refs):
+        block = lax.rem(pos - 1 - k + 2 * n, n)
+        at = pl.ds(pl.multiple_of(block * size, size), size)
+        ref[pl.ds(0, size), :] = dot(normed_t[at, :], both).astype(BF16)
+        per = up_out_term.shape[0] // extra
+        index = pl.ds(pl.multiple_of(lax.rem(block, per) * extra, extra), extra)
+
+        @pl.when(block < per)
+        def _(ref=ref, index=index):
+            ref[pl.ds(size, extra), :] = up_out_term[index, :]
+
+        @pl.when(block >= per)
+        def _(ref=ref, index=index):
+            ref[pl.ds(size, extra), :] = down_in_term[index, :]
+
+
+def copy_all(copies):
+    for c in copies:
+        c.start()
+    for c in copies:
+        c.wait()
+
+
+def down_out_place_kernel(n, *refs):
+    pieces, out_ref, sems = refs[: 2 * n], refs[2 * n], refs[2 * n + 1]
+    pos, sub = ring_position(), lax.axis_index("sub")
+    copies = []
+    for i, piece in enumerate(pieces):
+        half = sub if i < n else 1 - sub
+        block = lax.rem(pos - i % n + n, n)
+        size = piece.shape[1]
+        at = pl.ds(pl.multiple_of((half * n + block) * size, size), size)
+        copies.append(pltpu.make_async_copy(piece, out_ref.at[:, at], sems.at[i]))
+    copy_all(copies)
+
+
+def up_in_place_kernel(n, *refs):
+    pieces = refs[: 2 * n]
+    out_ref, up_out_ref, down_in_ref, small, sems = refs[2 * n :]
+    pos, sub = ring_position(), lax.axis_index("sub")
+    size = out_ref.shape[0] // (2 * n)
+    extra = pieces[0].shape[0] - size
+    copies = []
+    for i, piece in enumerate(pieces):
+        half = sub if i < n else 1 - sub
+        block = lax.rem(pos - i % n + n, n)
+        at = pl.ds(pl.multiple_of((half * n + block) * size, size), size)
+        copies.append(
+            pltpu.make_async_copy(piece.at[pl.ds(0, size), :], out_ref.at[at, :], sems.at[2 * i])
+        )
+        at = pl.ds(pl.multiple_of(block * extra, extra), extra)
+        copies.append(
+            pltpu.make_async_copy(
+                piece.at[pl.ds(size, extra), :], small.at[i // n, at, :], sems.at[2 * i + 1]
+            )
+        )
+    copy_all(copies)
+    total = (small[0].astype(F32) + small[1].astype(F32)).astype(BF16)
+    rows = up_out_ref.shape[0]
+    up_out_ref[...] = total[:rows]
+    down_in_ref[...] = total[rows:]
+
+
+def token_weights(sequence_length_list, slot_sequence_index, rows):
+    seq_count = sequence_length_list.shape[1]
+    longest = rows // seq_count
+    total = rows * lax.axis_size("dp") * lax.axis_size("sub")
+    ratios = longest / sequence_length_list[0].astype(F32)
+    match = slot_sequence_index[:, None] == jnp.arange(seq_count, dtype=jnp.int32)[None, :]
+    weight = jnp.sum(jnp.where(match, ratios[None, :], F32(0.0)), axis=-1)
+    return weight * F32(1.0 / math.sqrt(total))
+
+
+class Shards:
+    def __init__(self, codes):
+        sub, grp = lax.axis_index("sub"), lax.axis_index("grp")
+        half = codes.shape[0] // 2
+        quarter = half // 2
+        self.codes = codes
+        self.got = swap(lax.dynamic_slice_in_dim(codes, (1 - sub) * half, half, 0), "sub")
+        own = lax.dynamic_slice_in_dim(codes, sub * half + grp * quarter, quarter, 0)
+        got = lax.dynamic_slice_in_dim(self.got, grp * quarter, quarter, 0)
+        self.moving = jnp.concatenate([own, got], axis=0)
+        self.moved = []
+
+    def step(self, *done):
+        self.moving = ring_step(after(self.moving, *done) if done else self.moving)
+        self.moved += [self.moving, swap(self.moving, "grp")]
+        return self.moving
+
+    def args(self):
+        return [self.codes, self.got, *self.moved]
+
+
+def fast_body(
+    tokens,
+    cotangent,
+    rms_norm_gain,
+    gate_codes,
+    gate_block_scale,
+    up_codes,
+    up_block_scale,
+    down_codes,
+    down_block_scale,
+    up_adapter_in,
+    up_adapter_out,
+    down_adapter_in,
+    down_adapter_out,
+    sequence_length_list,
+    slot_sequence_index,
+):
+    rows, local_width = tokens.shape
+    blocks, _, units = gate_codes.shape
+    block = local_width // blocks
+    half = local_width // 2
+    rank = up_adapter_in.shape[1]
+    total_width = local_width * lax.axis_size("mp")
+    n = lax.axis_size("dp")
+    more = lax.axis_size("mp") - 1
+    place = lax.axis_index("sub").astype(jnp.int32).reshape(1)
+
+    gate_shards = Shards(gate_codes)
+    up_shards = Shards(up_codes)
+    down_shards = Shards(jnp.swapaxes(down_codes, 0, 1))
+    order = [gate_shards, up_shards] * 2 + [down_shards, gate_shards, up_shards]
+    if n != 4:
+        order = [gate_shards, up_shards] * (n - 1)
+    order += [down_shards] * (n - 1 - order.count(down_shards))
+    arrived = []
+    for shards in order:
+        arrived.append(shards.step(*arrived[-2:-1]))
+
+    weight = token_weights(sequence_length_list, slot_sequence_index, rows)
+    grad_send, grad, low_out = halves_call(
+        cotangent_kernel, "cotangent", place, cotangent, [weight[:, None]], down_adapter_out, False
+    )
+    grad_got = swap(grad_send, "sub")
+    own_squares = jnp.sum(jnp.square(tokens.astype(F32)), axis=-1)
+    squares = sum(others(own_squares, "mp"), own_squares) / total_width
+    inv_rms = lax.rsqrt(squares + EPS)[:, None]
+    normed_send, normed, low_up = halves_call(
+        token_kernel, "tokens", place, tokens, [inv_rms, rms_norm_gain[None, :]], up_adapter_in, True
+    )
+    normed_got = swap(normed_send, "sub")
+    low_up = sum(others(low_up, "mp"), low_up).astype(BF16)
+    low_out = sum(others(low_out, "mp"), low_out).astype(BF16)
+    up_out_more = others(up_adapter_out, "mp")
+    down_in_more = others(down_adapter_in, "mp")
+    (normed_t,) = call(
+        transpose_kernel, "transpose", [normed, normed_got], [shape((half, 2 * rows))], limit=32
+    )
+
+    def product(kernel, name, own, got, scale, shards, weight_shape):
+        groups = scale.shape[1]
+        mine, theirs = call(
+            kernel,
+            name,
+            [own, got, scale, *shards.args()],
+            [shape((rows, units), F32), shape((rows, units))],
+            scratch=[pltpu.VMEM((groups, blocks, LANES), F32), pltpu.VMEM(weight_shape, BF16)],
+            flops=4 * rows * half * units,
+        )
+        mine = mine + swap(theirs, "sub").astype(F32)
+        return mine, others(mine.astype(BF16), "mp")
+
+    front = (blocks // 2, block, units)
+    gate, gate_more = product(
+        front_kernel, "gate", normed, normed_got, gate_block_scale, gate_shards, front
+    )
+    up, up_more = product(front_kernel, "up", normed, normed_got, up_block_scale, up_shards, front)
+    small_scratch = [
+        pltpu.VMEM((rank, units), BF16),
+        pltpu.VMEM((units, rank), BF16),
+    ]
+    adapters = [low_up, low_out, up_adapter_out, down_adapter_in]
+    silu, low_hidden, down_in_term = call(
+        lambda *refs: hidden_kernel(more, *refs),
+        "hidden",
+        [gate, up, *adapters, *gate_more, *up_more, *up_out_more, *down_in_more],
+        [shape((rows, units), F32), shape((rows, rank)), shape(down_adapter_in.shape)],
+        scratch=small_scratch,
+        limit=8,
+    )
+    down_out_parts = call(
+        down_out_kernel,
+        "down_out",
+        [low_hidden, swap(low_hidden, "sub"), grad, grad_got],
+        [shape((rank, half // n))] * n,
+        flops=4 * rows * half * rank,
+    )
+    down_out_blocks = ring_gather(ring_sum(down_out_parts))
+
+    back, back_more = product(
+        back_kernel, "back", grad, grad_got, down_block_scale.T, down_shards, (units, half)
+    )
+    low_grad, up_out_term = call(
+        lambda *refs: up_grad_kernel(more, *refs),
+        "up_grad",
+        [back, silu, *adapters, *back_more, *up_out_more, *down_in_more],
+        [shape((rows, rank)), shape(up_adapter_out.shape)],
+        scratch=small_scratch,
+        limit=8,
+    )
+    extra = 2 * rank // n
+    up_in_parts = call(
+        up_in_kernel,
+        "up_in",
+        [low_grad, swap(low_grad, "sub"), normed_t, up_out_term, down_in_term],
+        [shape((half // n + extra, rank))] * n,
+        flops=4 * rows * half * rank,
+    )
+    up_in_blocks = ring_gather(ring_sum(up_in_parts))
+
+    anywhere = pl.BlockSpec(memory_space=pl.ANY)
+    vmem = pl.BlockSpec(memory_space=pltpu.VMEM)
+    (down_out_gradient,) = call(
+        lambda *refs: down_out_place_kernel(n, *refs),
+        "down_out_place",
+        [*down_out_blocks[0], *down_out_blocks[1]],
+        [shape((rank, local_width))],
+        scratch=[pltpu.SemaphoreType.DMA((2 * n,))],
+        specs=[anywhere] * (2 * n),
+        out_specs=(anywhere,),
+        limit=4,
+    )
+    up_in_gradient, up_out_gradient, down_in_gradient = call(
+        lambda *refs: up_in_place_kernel(n, *refs),
+        "up_in_place",
+        [*up_in_blocks[0], *up_in_blocks[1]],
+        [shape((local_width, rank)), shape(up_adapter_out.shape), shape(down_adapter_in.shape)],
+        scratch=[pltpu.VMEM((2, 2 * rank, rank), BF16), pltpu.SemaphoreType.DMA((4 * n,))],
+        specs=[anywhere] * (2 * n),
+        out_specs=(anywhere, vmem, vmem),
+        limit=4,
+    )
+    return up_in_gradient, up_out_gradient, down_in_gradient, down_out_gradient
+
+
+def general_body(
     tokens,
     cotangent,
     rms_norm_gain,
@@ -111,6 +660,12 @@
     )
 
 
+def body(tokens, cotangent, rms_norm_gain, gate_codes, *rest):
+    whole_tiles = gate_codes.shape[1] % ROW_TILE == 0
+    form = fast_body if whole_tiles else general_body
+    return form(tokens, cotangent, rms_norm_gain, gate_codes, *rest)
+
+
 def solution(mesh):
     placed = (
         P(("grp", "dp", "sub"), "mp"),

time: 396 us -> 241 us (0.61)
  blocking collectives: 201 us -> 0 us
  starting transfers between devices: 0.42 us -> 52.5 us
  Pallas kernels: 0 us -> 35.8 us
  matrix products: 32.5 us -> 0 us
  local copies, waits for them, and re-layouts: 2.07 us -> 23.7 us
  waiting for transfers between devices: 136 us -> 121 us
  between operations: 14.3 us -> 1.41 us
    psum x4 -> x0, blocking collectives: 201 us -> none  [the longest x1 172 us: body(): lax.psum((up_in_term, up_out_term, down_in_term, down_out_term), ('dp', '...]
    ppermute x0 -> x56, waiting for transfers between devices: none -> 121 us  [the longest x21 90.7 us: ring_step(): lax.ppermute(x, 'dp', [(ring_at(i, n), ring_at((i + 1) % n, n)) for i in...]
    all_gather x3 -> x0, waiting for transfers between devices: 103 us -> none  [the longest x1 41.5 us: body(): quant_u = lax.all_gather(up_codes, ('dp', 'sub'), axis=1, tiled=True)]
    ppermute x0 -> x56, starting transfers between devices: none -> 52.5 us  [the longest x21 26.8 us: ring_step(): lax.ppermute(x, 'dp', [(ring_at(i, n), ring_at((i + 1) % n, n)) for i in...]
    pallas_call x0 -> x12, Pallas kernels: none -> 35.8 us  [the longest x10 23.8 us: call(): pl.pallas_call(kernel, out_shape=tuple(out_shape), in_specs=specs or [vme...]
    dot_general x13 -> x0, matrix products: 32.5 us -> none  [the longest x7 12.1 us: contract_dims(): lax.dot_general(left, right, (((left_dim,), (right_dim,)), ((), ())), pre...]
    reduce_scatter x3 -> x0, waiting for transfers between devices: 30.9 us -> none  [the longest x1 13.9 us: body(): lax.psum_scatter(up_next, 'mp', scatter_dimension=1, tiled=True)]
    unnamed x22 -> x92, local copies, waits for them, and re-layouts: 0.32 us -> 19 us
  transfers between devices with their start and end apart: 6 -> 56, of which waited for: 6 -> 30; matrix products, arithmetic and copies ran while one was open for 8% -> 5% of each run, Pallas kernels for 0% -> 10%
where the time goes in v2:
time: 241 us; the launch traced here: 240 us
  waiting for transfers between devices  121 us (50%)
  starting transfers between devices  52.5 us (22%)
  Pallas kernels  35.8 us (15%)
  local copies, waits for them, and re-layouts  23.7 us (10%)
  other arithmetic  6.08 us (3%)
    ppermute x21, waiting for transfers between devices, ring_step(): lax.ppermute(x, 'dp', [(ring_at(i, n), ring_at((i + 1) % n, n)) for i in...  90.7 us
    ppermute x21, starting transfers between devices, ring_step(): lax.ppermute(x, 'dp', [(ring_at(i, n), ring_at((i + 1) % n, n)) for i in...  26.8 us
    pallas_call x10, Pallas kernels, call(): pl.pallas_call(kernel, out_shape=tuple(out_shape), in_specs=specs or [vme...  23.8 us
    ppermute x27, waiting for transfers between devices, swap(): return lax.ppermute(x, axis, [(0, 1), (1, 0)])  22.1 us
    unnamed x92, local copies, waits for them, and re-layouts  19 us
    ppermute x27, starting transfers between devices, swap(): return lax.ppermute(x, axis, [(0, 1), (1, 0)])  15.5 us
    pallas_call x2, Pallas kernels, halves_call(): pl.pallas_call(kernel, out_shape=(shape((rows, width // 2)), shape((rows,...  12 us
    ppermute x8, starting transfers between devices, others(): lax.ppermute(x, axis, [(i, (i + k) % n) for i in range(n)])  10.2 us
  transfers between devices with their start and end apart: 56, of which 30 were waited for; matrix products, arithmetic and copies ran while one was open for 5% of the time, Pallas kernels for 10%

profile of v2, /device:TPU:0, one launch (start us, length us, event | category | flops | bytes accessed | tf_op | source)
XLA Modules:
  0.0 240.3 jit_solution(11393771099694239430)
XLA Ops:
  6.0 5.9 %cotangent.2 = (bf16[256,4096]{1,0:T(8,128)(2,1)}, bf16[256,4096]{1,0:T(8,128)(2,1)S(1)}, f32[256,128]{1,0:T(8,128)S(1)}) custom-call(s32[1]{0:T(128)} %bitcast.place, bf16[256,8192]{1,0:T(8,128)(2,1)S(1)} %copy-done.4, f32[256,1]{1,0:T(8,128)S(1)} %copy.33.weight, bf16[128,8192]{1,0:T(8,128)(2,1)S(1)} %copy-done.5), custom_call_target="tpu_custom_call" | custom-call | flops 536870912 | bytes 8388608 | tf_op jit(solution)/shard_map/cotangent/pallas_call | solution.py:120
  28.5 6.1 %tokens.2 = (bf16[256,4096]{1,0:T(8,128)(2,1)}, bf16[256,4096]{1,0:T(8,128)(2,1)S(1)}, f32[256,128]{1,0:T(8,128)S(1)}) custom-call(s32[1]{0:T(128)} %bitcast.place, bf16[256,8192]{1,0:T(8,128)(2,1)S(1)} %copy-done, f32[256,1]{1,0:T(8,128)S(1)} %copy.38.inv_rms, bf16[1,8192]{1,0:T(2,128)(2,1)S(1)} %copy-done.28, bf16[8192,128]{1,0:T(8,128)(2,1)S(1)} %copy-done.6), custom_call_target="tpu_custom_call" | custom-call | flops 536870912 | bytes 8388608 | tf_op jit(solution)/shard_map/tokens/pallas_call | solution.py:120
  40.2 5.6 %collective-permute-done.3.refs_0_ = bf16[32,16,256]{2,1,0:T(8,128)(2,1)S(1)} collective-permute-done((bf16[32,16,256]{2,1,0:T(8,128)(2,1)S(1)}, bf16[32,16,256]{2,1,0:T(8,128)(2,1)S(1)}, u32[]{:S(2)}, u32[]{:S(2)}) %collective-permute-start.3) | collective-permute-done | bytes 262176 | tf_op jit(solution)/shard_map/ppermute | solution.py:45
  46.7 4.8 %collective-permute-done.8.refs_0_ = bf16[32,16,256]{2,1,0:T(8,128)(2,1)S(1)} collective-permute-done((bf16[32,16,256]{2,1,0:T(8,128)(2,1)S(1)}, bf16[32,16,256]{2,1,0:T(8,128)(2,1)S(1)}, u32[]{:S(2)}, u32[]{:S(2)}) %collective-permute-start.8) | collective-permute-done | bytes 262176 | tf_op jit(solution)/shard_map/ppermute | solution.py:45
  53.1 4.0 %collective-permute-done.4.refs_2_ = bf16[32,16,256]{2,1,0:T(8,128)(2,1)S(1)} collective-permute-done((bf16[32,16,256]{2,1,0:T(8,128)(2,1)S(1)}, bf16[32,16,256]{2,1,0:T(8,128)(2,1)S(1)}, u32[]{:S(2)}, u32[]{:S(2)}) %collective-permute-start.4) | collective-permute-done | bytes 262176 | tf_op jit(solution)/shard_map/ppermute | solution.py:45
  57.9 4.8 %collective-permute-done.9.refs_2_ = bf16[32,16,256]{2,1,0:T(8,128)(2,1)S(1)} collective-permute-done((bf16[32,16,256]{2,1,0:T(8,128)(2,1)S(1)}, bf16[32,16,256]{2,1,0:T(8,128)(2,1)S(1)}, u32[]{:S(2)}, u32[]{:S(2)}) %collective-permute-start.9) | collective-permute-done | bytes 262176 | tf_op jit(solution)/shard_map/ppermute | solution.py:45
  63.5 4.9 %collective-permute-done.5.refs_0_ = bf16[32,32,128]{2,1,0:T(8,128)(2,1)} collective-permute-done((bf16[32,32,128]{2,1,0:T(8,128)(2,1)S(1)}, bf16[32,32,128]{2,1,0:T(8,128)(2,1)}, u32[]{:S(2)}, u32[]{:S(2)}) %collective-permute-start.5) | collective-permute-done | bytes 262176 | tf_op jit(solution)/shard_map/ppermute | solution.py:45
  68.5 4.9 %collective-permute-done.10.refs_4_ = bf16[32,16,256]{2,1,0:T(8,128)(2,1)S(1)} collective-permute-done((bf16[32,16,256]{2,1,0:T(8,128)(2,1)S(1)}, bf16[32,16,256]{2,1,0:T(8,128)(2,1)S(1)}, u32[]{:S(2)}, u32[]{:S(2)}) %collective-permute-start.10) | collective-permute-done | bytes 262176 | tf_op jit(solution)/shard_map/ppermute | solution.py:45
  79.5 5.0 %collective-permute-done.11.refs_2_ = bf16[32,32,128]{2,1,0:T(8,128)(2,1)} collective-permute-done((bf16[32,32,128]{2,1,0:T(8,128)(2,1)}, bf16[32,32,128]{2,1,0:T(8,128)(2,1)}, u32[]{:S(2)}, u32[]{:S(2)}) %collective-permute-start.11) | collective-permute-done | bytes 262176 | tf_op jit(solution)/shard_map/ppermute | solution.py:45
  105.1 4.1 %collective-permute-done.12.refs_3_ = bf16[32,32,128]{2,1,0:T(8,128)(2,1)} collective-permute-done((bf16[32,32,128]{2,1,0:T(8,128)(2,1)}, bf16[32,32,128]{2,1,0:T(8,128)(2,1)}, u32[]{:S(2)}, u32[]{:S(2)}) %collective-permute-start.12) | collective-permute-done | bytes 262176 | tf_op jit(solution)/shard_map/ppermute | solution.py:49
  110.7 4.1 %collective-permute-done.15.refs_5_ = bf16[32,32,128]{2,1,0:T(8,128)(2,1)} collective-permute-done((bf16[32,32,128]{2,1,0:T(8,128)(2,1)}, bf16[32,32,128]{2,1,0:T(8,128)(2,1)}, u32[]{:S(2)}, u32[]{:S(2)}) %collective-permute-start.15) | collective-permute-done | bytes 262176 | tf_op jit(solution)/shard_map/ppermute | solution.py:49
  121.1 4.3 %back.1 = (f32[256,256]{1,0:T(8,128)S(1)}, bf16[256,256]{1,0:T(8,128)(2,1)S(1)}) custom-call(bf16[256,4096]{1,0:T(8,128)(2,1)S(1)} %copy-done.2, bf16[256,4096]{1,0:T(8,128)(2,1)} %collective-permute-done.got.grad_got, bf16[64,2]{1,0:T(8,128)(2,1)S(1)} %bitcast.13, bf16[64,32,128]{2,1,0:T(8,128)(2,1)S(1)} %bitcast.12, bf16[32,32,128]{2,1,0:T(8,128)(2,1)S(1)} %copy-done.11, ...), custom_call_target="tpu_custom_call" | custom-call | flops 1073741824 | bytes 6947072 | tf_op jit(solution)/shard_map/back/pallas_call | solution.py:84
  125.4 6.2 %collective-permute-done.21.refs_5_ = bf16[32,16,256]{2,1,0:T(8,128)(2,1)S(1)} collective-permute-done((bf16[32,16,256]{2,1,0:T(8,128)(2,1)}, bf16[32,16,256]{2,1,0:T(8,128)(2,1)S(1)}, u32[]{:S(2)}, u32[]{:S(2)}) %collective-permute-start.21) | collective-permute-done | bytes 262176 | tf_op jit(solution)/shard_map/ppermute | solution.py:49
  146.1 6.1 %collective-permute-done.29.refs_6_ = bf16[256,256]{1,0:T(8,128)(2,1)S(1)} collective-permute-done((bf16[256,256]{1,0:T(8,128)(2,1)S(1)}, bf16[256,256]{1,0:T(8,128)(2,1)S(1)}, u32[]{:S(2)}, u32[]{:S(2)}) %collective-permute-start.29) | collective-permute-done | bytes 131104 | tf_op jit(solution)/shard_map/ppermute | solution.py:54
  172.1 4.7 %collective-permute-done.46 = bf16[128,1024]{1,0:T(8,128)(2,1)S(1)} collective-permute-done((bf16[128,1024]{1,0:T(8,128)(2,1)S(1)}, bf16[128,1024]{1,0:T(8,128)(2,1)S(1)}, u32[]{:S(2)}, u32[]{:S(2)}) %collective-permute-start.46) | collective-permute-done | bytes 262176 | tf_op jit(solution)/shard_map/ppermute | solution.py:45
  177.9 4.8 %collective-permute-done.36 = bf16[1088,128]{1,0:T(8,128)(2,1)S(1)} collective-permute-done((bf16[1088,128]{1,0:T(8,128)(2,1)S(1)}, bf16[1088,128]{1,0:T(8,128)(2,1)S(1)}, u32[]{:S(2)}, u32[]{:S(2)}) %collective-permute-start.36) | collective-permute-done | bytes 278560 | tf_op jit(solution)/shard_map/ppermute | solution.py:45
  183.9 4.5 %collective-permute-done.47 = bf16[128,1024]{1,0:T(8,128)(2,1)S(1)} collective-permute-done((bf16[128,1024]{1,0:T(8,128)(2,1)S(1)}, bf16[128,1024]{1,0:T(8,128)(2,1)S(1)}, u32[]{:S(2)}, u32[]{:S(2)}) %collective-permute-start.47) | collective-permute-done | bytes 262176 | tf_op jit(solution)/shard_map/ppermute | solution.py:45
  189.5 4.8 %collective-permute-done.37 = bf16[1088,128]{1,0:T(8,128)(2,1)S(1)} collective-permute-done((bf16[1088,128]{1,0:T(8,128)(2,1)S(1)}, bf16[1088,128]{1,0:T(8,128)(2,1)S(1)}, u32[]{:S(2)}, u32[]{:S(2)}) %collective-permute-start.37) | collective-permute-done | bytes 278560 | tf_op jit(solution)/shard_map/ppermute | solution.py:45
  195.5 4.5 %collective-permute-done.48 = bf16[128,1024]{1,0:T(8,128)(2,1)S(1)} collective-permute-done((bf16[128,1024]{1,0:T(8,128)(2,1)S(1)}, bf16[128,1024]{1,0:T(8,128)(2,1)S(1)}, u32[]{:S(2)}, u32[]{:S(2)}) %collective-permute-start.48) | collective-permute-done | bytes 262176 | tf_op jit(solution)/shard_map/ppermute | solution.py:45
  201.1 4.8 %collective-permute-done.38.refs_1_ = bf16[1088,128]{1,0:T(8,128)(2,1)S(1)} collective-permute-done((bf16[1088,128]{1,0:T(8,128)(2,1)S(1)}, bf16[1088,128]{1,0:T(8,128)(2,1)S(1)}, u32[]{:S(2)}, u32[]{:S(2)}) %collective-permute-start.38) | collective-permute-done | bytes 278560 | tf_op jit(solution)/shard_map/ppermute | solution.py:45
  206.9 4.6 %collective-permute-done.49.refs_1_ = bf16[128,1024]{1,0:T(8,128)(2,1)S(1)} collective-permute-done((bf16[128,1024]{1,0:T(8,128)(2,1)S(1)}, bf16[128,1024]{1,0:T(8,128)(2,1)S(1)}, u32[]{:S(2)}, u32[]{:S(2)}) %collective-permute-start.49) | collective-permute-done | bytes 262176 | tf_op jit(solution)/shard_map/ppermute | solution.py:45
  212.5 5.0 %collective-permute-done.39.refs_2_ = bf16[1088,128]{1,0:T(8,128)(2,1)S(1)} collective-permute-done((bf16[1088,128]{1,0:T(8,128)(2,1)S(1)}, bf16[1088,128]{1,0:T(8,128)(2,1)S(1)}, u32[]{:S(2)}, u32[]{:S(2)}) %collective-permute-start.39) | collective-permute-done | bytes 278560 | tf_op jit(solution)/shard_map/ppermute | solution.py:45
  219.0 4.1 %collective-permute-done.50.refs_2_ = bf16[128,1024]{1,0:T(8,128)(2,1)S(1)} collective-permute-done((bf16[128,1024]{1,0:T(8,128)(2,1)S(1)}, bf16[128,1024]{1,0:T(8,128)(2,1)S(1)}, u32[]{:S(2)}, u32[]{:S(2)}) %collective-permute-start.50) | collective-permute-done | bytes 262176 | tf_op jit(solution)/shard_map/ppermute | solution.py:45
  224.7 9.6 %collective-permute-done.51.refs_3_ = bf16[128,1024]{1,0:T(8,128)(2,1)S(1)} collective-permute-done((bf16[128,1024]{1,0:T(8,128)(2,1)S(1)}, bf16[128,1024]{1,0:T(8,128)(2,1)S(1)}, u32[]{:S(2)}, u32[]{:S(2)}) %collective-permute-start.51) | collective-permute-done | bytes 262176 | tf_op jit(solution)/shard_map/ppermute | solution.py:45
  (223 shorter events, 116.4 us)
Async XLA Ops:
  13.3 103.1 %collective-permute-start = (bf16[256,4096]{1,0:T(8,128)(2,1)}, bf16[256,4096]{1,0:T(8,128)(2,1)}, u32[]{:S(2)}, u32[]{:S(2)}) collective-permute-start(bf16[256,4096]{1,0:T(8,128)(2,1)} %get-tuple-element.40), channel_id=1, source_target_pairs={{0,1},{1,0},{2,3},{3,2},{4,5},{5,4},{6,7},{7,6},{8,9},{9,8},{10,11... | collective-permute-start | bytes 6291464 | tf_op jit(solution)/shard_map/ppermute | solution.py:49
  14.5 20.4 %collective-permute-start.2 = (bf16[32,16,256]{2,1,0:T(8,128)(2,1)}, bf16[32,16,256]{2,1,0:T(8,128)(2,1)}, u32[]{:S(2)}, u32[]{:S(2)}) collective-permute-start(bf16[32,16,256]{2,1,0:T(8,128)(2,1)} %constant_dynamic-slice_fusion.4), channel_id=1, source_target_pairs={{0,1},{1,0},{2,3},{3,2},{4,5},{5,4},{6,7},{7,6},{8,9},{9,8},{10,11... | collective-permute-start | bytes 786440 | tf_op jit(solution)/shard_map/ppermute | solution.py:49
  15.3 22.1 %collective-permute-start.7 = (bf16[32,16,256]{2,1,0:T(8,128)(2,1)}, bf16[32,16,256]{2,1,0:T(8,128)(2,1)S(1)}, u32[]{:S(2)}, u32[]{:S(2)}) collective-permute-start(bf16[32,16,256]{2,1,0:T(8,128)(2,1)} %constant_dynamic-slice_fusion.1), channel_id=1, source_target_pairs={{0,1},{1,0},{2,3},{3,2},{4,5},{5,4},{6,7},{7,6},{8,9},{9,8},{10,11... | collective-permute-start | bytes 786440 | tf_op jit(solution)/shard_map/ppermute | solution.py:49
  34.6 98.3 %collective-permute-start.18 = (bf16[256,4096]{1,0:T(8,128)(2,1)}, bf16[256,4096]{1,0:T(8,128)(2,1)}, u32[]{:S(2)}, u32[]{:S(2)}) collective-permute-start(bf16[256,4096]{1,0:T(8,128)(2,1)} %get-tuple-element.51), channel_id=1, source_target_pairs={{0,1},{1,0},{2,3},{3,2},{4,5},{5,4},{6,7},{7,6},{8,9},{9,8},{10,11... | collective-permute-start | bytes 6291464 | tf_op jit(solution)/shard_map/ppermute | solution.py:49
  37.5 14.0 %collective-permute-start.8 = (bf16[32,16,256]{2,1,0:T(8,128)(2,1)S(1)}, bf16[32,16,256]{2,1,0:T(8,128)(2,1)S(1)}, u32[]{:S(2)}, u32[]{:S(2)}) collective-permute-start(bf16[32,16,256]{2,1,0:T(8,128)(2,1)S(1)} %pad_maximum_fusion.2), channel_id=1, source_target_pairs={{0,4},{4,12},{12,8},{8,0},{1,5},{5,13},{13,9},{9,1},{2,6},{6,14},{... | collective-permute-start | bytes 786440 | tf_op jit(solution)/shard_map/ppermute | solution.py:45
  40.2 12.1 %collective-permute-start.1 = (bf16[32,32,128]{2,1,0:T(8,128)(2,1)S(1)}, bf16[32,32,128]{2,1,0:T(8,128)(2,1)S(1)}, u32[]{:S(2)}, u32[]{:S(2)}) collective-permute-start(bf16[32,32,128]{2,1,0:T(8,128)(2,1)S(1)} %dynamic-slice_bitcast_fusion), channel_id=1, source_target_pairs={{0,1},{1,0},{2,3},{3,2},{4,5},{5,4},{6,7},{7,6},{8,9},{9,8},{10,11... | collective-permute-start | bytes 786440 | tf_op jit(solution)/shard_map/ppermute | solution.py:49
  74.9 13.7 %collective-permute-start.13 = (bf16[32,16,256]{2,1,0:T(8,128)(2,1)S(1)}, bf16[32,16,256]{2,1,0:T(8,128)(2,1)S(1)}, u32[]{:S(2)}, u32[]{:S(2)}) collective-permute-start(bf16[32,16,256]{2,1,0:T(8,128)(2,1)S(1)} %collective-permute-done.9.refs_2_), channel_id=1, source_target_pairs={{0,4},{4,12},{12,8},{8,0},{1,5},{5,13},{13,9},{9,1},{2,6},{6,14},{... | collective-permute-start | bytes 786440 | tf_op jit(solution)/shard_map/ppermute | solution.py:45
  78.3 12.5 %collective-permute-start.28 = (f32[256,128]{1,0:T(8,128)S(1)}, f32[256,128]{1,0:T(8,128)S(1)}, u32[]{:S(2)}, u32[]{:S(2)}) collective-permute-start(f32[256,128]{1,0:T(8,128)S(1)} %copy-done.34), channel_id=1, source_target_pairs={{0,2},{2,0},{1,3},{3,1},{4,6},{6,4},{5,7},{7,5},{8,10},{10,8},{9,1... | collective-permute-start | bytes 393224 | tf_op jit(solution)/shard_map/ppermute | solution.py:54
  100.1 14.7 %collective-permute-start.15 = (bf16[32,32,128]{2,1,0:T(8,128)(2,1)}, bf16[32,32,128]{2,1,0:T(8,128)(2,1)}, u32[]{:S(2)}, u32[]{:S(2)}) collective-permute-start(bf16[32,32,128]{2,1,0:T(8,128)(2,1)} %collective-permute-done.14.refs_4_), channel_id=1, source_target_pairs={{0,16},{16,0},{1,17},{17,1},{2,18},{18,2},{3,19},{19,3},{4,20},{20... | collective-permute-start | bytes 786440 | tf_op jit(solution)/shard_map/ppermute | solution.py:49
  103.6 33.1 %collective-permute-start.23 = (bf16[32,16,256]{2,1,0:T(8,128)(2,1)}, bf16[32,16,256]{2,1,0:T(8,128)(2,1)S(1)}, u32[]{:S(2)}, u32[]{:S(2)}) collective-permute-start(bf16[32,16,256]{2,1,0:T(8,128)(2,1)} %copy-done.12), channel_id=1, source_target_pairs={{0,16},{16,0},{1,17},{17,1},{2,18},{18,2},{3,19},{19,3},{4,20},{20... | collective-permute-start | bytes 786440 | tf_op jit(solution)/shard_map/ppermute | solution.py:49
  109.2 28.2 %collective-permute-start.24 = (bf16[32,16,256]{2,1,0:T(8,128)(2,1)}, bf16[32,16,256]{2,1,0:T(8,128)(2,1)S(1)}, u32[]{:S(2)}, u32[]{:S(2)}) collective-permute-start(bf16[32,16,256]{2,1,0:T(8,128)(2,1)} %copy-done.16), channel_id=1, source_target_pairs={{0,16},{16,0},{1,17},{17,1},{2,18},{18,2},{3,19},{19,3},{4,20},{20... | collective-permute-start | bytes 786440 | tf_op jit(solution)/shard_map/ppermute | solution.py:49
  114.8 16.7 %collective-permute-start.21 = (bf16[32,16,256]{2,1,0:T(8,128)(2,1)}, bf16[32,16,256]{2,1,0:T(8,128)(2,1)S(1)}, u32[]{:S(2)}, u32[]{:S(2)}) collective-permute-start(bf16[32,16,256]{2,1,0:T(8,128)(2,1)} %copy-done.22), channel_id=1, source_target_pairs={{0,16},{16,0},{1,17},{17,1},{2,18},{18,2},{3,19},{19,3},{4,20},{20... | collective-permute-start | bytes 786440 | tf_op jit(solution)/shard_map/ppermute | solution.py:49
  116.3 22.5 %collective-permute-start.25 = (bf16[32,16,256]{2,1,0:T(8,128)(2,1)}, bf16[32,16,256]{2,1,0:T(8,128)(2,1)S(1)}, u32[]{:S(2)}, u32[]{:S(2)}) collective-permute-start(bf16[32,16,256]{2,1,0:T(8,128)(2,1)} %copy-done.20), channel_id=1, source_target_pairs={{0,16},{16,0},{1,17},{17,1},{2,18},{18,2},{3,19},{19,3},{4,20},{20... | collective-permute-start | bytes 786440 | tf_op jit(solution)/shard_map/ppermute | solution.py:49
  131.5 14.5 %collective-permute-start.31 = (bf16[128,128]{1,0:T(8,128)(2,1)S(1)}, bf16[128,128]{1,0:T(8,128)(2,1)S(1)}, u32[]{:S(2)}, u32[]{:S(2)}) collective-permute-start(bf16[128,128]{1,0:T(8,128)(2,1)S(1)} %copy-done.29), channel_id=1, source_target_pairs={{0,2},{2,0},{1,3},{3,1},{4,6},{6,4},{5,7},{7,5},{8,10},{10,8},{9,1... | collective-permute-start | bytes 98312 | tf_op jit(solution)/shard_map/ppermute | solution.py:54
  143.0 11.6 %collective-permute-start.33 = (bf16[256,256]{1,0:T(8,128)(2,1)S(1)}, bf16[256,256]{1,0:T(8,128)(2,1)S(1)}, u32[]{:S(2)}, u32[]{:S(2)}) collective-permute-start(bf16[256,256]{1,0:T(8,128)(2,1)S(1)} %get-tuple-element.74), channel_id=1, source_target_pairs={{0,2},{2,0},{1,3},{3,1},{4,6},{6,4},{5,7},{7,5},{8,10},{10,8},{9,1... | collective-permute-start | bytes 393224 | tf_op jit(solution)/shard_map/ppermute | solution.py:54
  176.8 11.5 %collective-permute-start.47 = (bf16[128,1024]{1,0:T(8,128)(2,1)S(1)}, bf16[128,1024]{1,0:T(8,128)(2,1)S(1)}, u32[]{:S(2)}, u32[]{:S(2)}) collective-permute-start(bf16[128,1024]{1,0:T(8,128)(2,1)S(1)} %add_convert_fusion.5), channel_id=1, source_target_pairs={{0,4},{4,12},{12,8},{8,0},{1,5},{5,13},{13,9},{9,1},{2,6},{6,14},{... | collective-permute-start | bytes 786440 | tf_op jit(solution)/shard_map/ppermute | solution.py:45
  188.4 11.5 %collective-permute-start.48 = (bf16[128,1024]{1,0:T(8,128)(2,1)S(1)}, bf16[128,1024]{1,0:T(8,128)(2,1)S(1)}, u32[]{:S(2)}, u32[]{:S(2)}) collective-permute-start(bf16[128,1024]{1,0:T(8,128)(2,1)S(1)} %add_convert_fusion.4), channel_id=1, source_target_pairs={{0,4},{4,12},{12,8},{8,0},{1,5},{5,13},{13,9},{9,1},{2,6},{6,14},{... | collective-permute-start | bytes 786440 | tf_op jit(solution)/shard_map/ppermute | solution.py:45
  194.4 11.5 %collective-permute-start.38 = (bf16[1088,128]{1,0:T(8,128)(2,1)S(1)}, bf16[1088,128]{1,0:T(8,128)(2,1)S(1)}, u32[]{:S(2)}, u32[]{:S(2)}) collective-permute-start(bf16[1088,128]{1,0:T(8,128)(2,1)S(1)} %add_convert_fusion.refs_0_), channel_id=1, source_target_pairs={{0,4},{4,12},{12,8},{8,0},{1,5},{5,13},{13,9},{9,1},{2,6},{6,14},{... | collective-permute-start | bytes 835592 | tf_op jit(solution)/shard_map/ppermute | solution.py:45
  200.0 11.5 %collective-permute-start.49 = (bf16[128,1024]{1,0:T(8,128)(2,1)S(1)}, bf16[128,1024]{1,0:T(8,128)(2,1)S(1)}, u32[]{:S(2)}, u32[]{:S(2)}) collective-permute-start(bf16[128,1024]{1,0:T(8,128)(2,1)S(1)} %add_convert_fusion.3.refs_0_), channel_id=1, source_target_pairs={{0,4},{4,12},{12,8},{8,0},{1,5},{5,13},{13,9},{9,1},{2,6},{6,14},{... | collective-permute-start | bytes 786440 | tf_op jit(solution)/shard_map/ppermute | solution.py:45
  205.9 11.6 %collective-permute-start.39 = (bf16[1088,128]{1,0:T(8,128)(2,1)S(1)}, bf16[1088,128]{1,0:T(8,128)(2,1)S(1)}, u32[]{:S(2)}, u32[]{:S(2)}) collective-permute-start(bf16[1088,128]{1,0:T(8,128)(2,1)S(1)} %collective-permute-done.38.refs_1_), channel_id=1, source_target_pairs={{0,4},{4,12},{12,8},{8,0},{1,5},{5,13},{13,9},{9,1},{2,6},{6,14},{... | collective-permute-start | bytes 835592 | tf_op jit(solution)/shard_map/ppermute | solution.py:45
  211.5 11.6 %collective-permute-start.50 = (bf16[128,1024]{1,0:T(8,128)(2,1)S(1)}, bf16[128,1024]{1,0:T(8,128)(2,1)S(1)}, u32[]{:S(2)}, u32[]{:S(2)}) collective-permute-start(bf16[128,1024]{1,0:T(8,128)(2,1)S(1)} %collective-permute-done.49.refs_1_), channel_id=1, source_target_pairs={{0,4},{4,12},{12,8},{8,0},{1,5},{5,13},{13,9},{9,1},{2,6},{6,14},{... | collective-permute-start | bytes 786440 | tf_op jit(solution)/shard_map/ppermute | solution.py:45
  217.5 16.8 %collective-permute-start.40 = (bf16[1088,128]{1,0:T(8,128)(2,1)S(1)}, bf16[1088,128]{1,0:T(8,128)(2,1)S(1)}, u32[]{:S(2)}, u32[]{:S(2)}) collective-permute-start(bf16[1088,128]{1,0:T(8,128)(2,1)S(1)} %collective-permute-done.39.refs_2_), channel_id=1, source_target_pairs={{0,4},{4,12},{12,8},{8,0},{1,5},{5,13},{13,9},{9,1},{2,6},{6,14},{... | collective-permute-start | bytes 835592 | tf_op jit(solution)/shard_map/ppermute | solution.py:45
  224.1 13.9 %collective-permute-start.41 = (bf16[1088,128]{1,0:T(8,128)(2,1)S(1)}, bf16[1088,128]{1,0:T(8,128)(2,1)S(1)}, u32[]{:S(2)}, u32[]{:S(2)}) collective-permute-start(bf16[1088,128]{1,0:T(8,128)(2,1)S(1)} %add_convert_fusion.refs_0_), channel_id=1, source_target_pairs={{0,1},{1,0},{2,3},{3,2},{4,5},{5,4},{6,7},{7,6},{8,9},{9,8},{10,11... | collective-permute-start | bytes 835592 | tf_op jit(solution)/shard_map/ppermute | solution.py:49
  224.6 13.4 %collective-permute-start.42 = (bf16[1088,128]{1,0:T(8,128)(2,1)S(1)}, bf16[1088,128]{1,0:T(8,128)(2,1)S(1)}, u32[]{:S(2)}, u32[]{:S(2)}) collective-permute-start(bf16[1088,128]{1,0:T(8,128)(2,1)S(1)} %collective-permute-done.38.refs_1_), channel_id=1, source_target_pairs={{0,1},{1,0},{2,3},{3,2},{4,5},{5,4},{6,7},{7,6},{8,9},{9,8},{10,11... | collective-permute-start | bytes 835592 | tf_op jit(solution)/shard_map/ppermute | solution.py:49
  (76 other events, 776.3 us)

commit v3 on v2

--- a/solution.py
+++ b/solution.py
@@ -11,6 +11,7 @@
 EPS = 1e-05
 ROW_TILE = 16
 LANES = 128
+PIECES = 4
 MIB = 1024 * 1024
 
 F32 = jnp.float32
@@ -62,18 +63,24 @@
     return sum(t.astype(F32) for t in terms).astype(BF16)
 
 
-def ring_sum(parts):
-    total = parts[0]
-    for part in parts[1:]:
-        total = add(ring_step(total), part)
-    return total
-
-
-def ring_gather(block):
-    blocks = [block]
-    for _ in range(lax.axis_size("dp") - 1):
-        blocks.append(ring_step(blocks[-1]))
-    return blocks, [swap(b, "sub") for b in blocks]
+def line_sums(parts):
+    n = lax.axis_size("dp")
+    place = lax.axis_index("dp")
+    middle = n // 2
+    entered, sums = [], []
+    for x in parts:
+        if len(entered) > 1:
+            x = after(x, entered[-2])
+        for s in range(middle - 1):
+            x = add(x, lax.ppermute(x, "dp", [(s, s + 1), (n - 1 - s, n - 2 - s)]))
+            if s == 0:
+                entered.append(x)
+        x = add(x, lax.ppermute(x, "dp", [(middle - 1, middle), (middle, middle - 1)]))
+        for s in reversed(range(middle - 1)):
+            got = lax.ppermute(x, "dp", [(s + 1, s), (n - 2 - s, n - 1 - s)])
+            x = jnp.where((place == s) | (place == n - 1 - s), got, x)
+        sums.append(x)
+    return sums, [swap(x, "sub") for x in sums]
 
 
 def call(kernel, name, args, out_shape, scratch=(), specs=None, limit=24, flops=0, out_specs=None):
@@ -97,10 +104,10 @@
     return jax.ShapeDtypeStruct(tuple(dims), dtype)
 
 
-def halves_call(kernel, name, place, wide, narrow, adapter, adapter_rows):
-    rows, width = wide.shape
-    step = width // 8
-    per = width // 2 // step
+def halves_call(kernel, name, place, wide, adapter, adapter_rows, rest, rest_specs, outs):
+    rows, width = wide[0].shape
+    per = 2
+    step = width // (2 * per)
     rank = adapter.shape[1] if adapter_rows else adapter.shape[0]
 
     def at(j, place):
@@ -111,33 +118,34 @@
         if adapter_rows
         else pl.BlockSpec((rank, step), lambda j, place: (0, at(j, place)))
     )
-    narrow_specs = [
-        pl.BlockSpec((rows, 1), lambda j, place: (0, 0))
-        if n.shape[0] == rows
-        else pl.BlockSpec((1, step), lambda j, place: (0, at(j, place)))
-        for n in narrow
-    ]
+    specs = [pl.BlockSpec((rows, step), lambda j, place: (0, at(j, place)))] * len(wide)
+    whole = pl.BlockSpec(memory_space=pltpu.VMEM)
+    for kind in rest_specs:
+        specs.append(
+            pl.BlockSpec((1, step), lambda j, place: (0, at(j, place)))
+            if kind == "features"
+            else (pl.BlockSpec(memory_space=pltpu.SMEM) if kind == "scalars" else whole)
+        )
     return pl.pallas_call(
         kernel,
-        out_shape=(shape((rows, width // 2)), shape((rows, width // 2)), shape((rows, rank), F32)),
+        out_shape=(shape((rows, width // 2)),) * 2 + tuple(shape((rows, c), F32) for c in outs),
         grid_spec=pltpu.PrefetchScalarGridSpec(
             num_scalar_prefetch=1,
             grid=(2 * per,),
-            in_specs=[pl.BlockSpec((rows, step), lambda j, place: (0, at(j, place)))]
-            + narrow_specs
-            + [adapter_spec],
+            in_specs=specs + [adapter_spec],
             out_specs=(
                 pl.BlockSpec((rows, step), lambda j, place: (0, jnp.minimum(j, per - 1))),
                 pl.BlockSpec((rows, step), lambda j, place: (0, jnp.maximum(j - per, 0))),
-                pl.BlockSpec((rows, rank), lambda j, place: (0, 0)),
-            ),
+            )
+            + tuple(pl.BlockSpec((rows, c), lambda j, place: (0, 0)) for c in outs),
+            scratch_shapes=[pltpu.VMEM((rows, LANES), F32)],
         ),
-        compiler_params=pltpu.CompilerParams(vmem_limit_bytes=16 * MIB),
+        compiler_params=pltpu.CompilerParams(vmem_limit_bytes=60 * MIB),
         cost_estimate=pl.CostEstimate(
-            flops=2 * rows * width * rank, bytes_accessed=4 * wide.size, transcendentals=0
+            flops=2 * rows * width * rank, bytes_accessed=8 * rows * width, transcendentals=0
         ),
         name=name,
-    )(place, wide, *narrow, adapter)
+    )(place, *wide, *rest, adapter)
 
 
 def store_half(value, send_ref, own_ref):
@@ -153,29 +161,59 @@
         own_ref[...] = value
 
 
-def accumulate(ref, term):
+def accumulate(ref, term, cols=slice(None)):
     j = pl.program_id(0)
 
     @pl.when(j == 0)
     def _():
-        ref[...] = term
+        ref[:, cols] = term
 
     @pl.when(j > 0)
     def _():
-        ref[...] += term
-
-
-def token_kernel(place, tokens, inv_rms, gain, adapter, send_ref, own_ref, low_ref):
-    value = tokens[...].astype(F32) * inv_rms[...] * gain[...].astype(F32)
+        ref[:, cols] += term
+
+
+def cotangent_kernel(
+    total, place, cotangent, tokens, lengths, slots, adapter, send_ref, own_ref, low_ref, square_ref, row
+):
+    rows = cotangent.shape[0]
+    count = lengths.shape[1]
+
+    @pl.when(pl.program_id(0) == 0)
+    def _():
+        index = jnp.broadcast_to(slots[...], (LANES, rows))
+        weight = jnp.zeros((LANES, rows), F32)
+        for s in range(count):
+            length = jnp.full((LANES, rows), lengths[0, s], jnp.int32).astype(F32)
+            weight = weight + jnp.where(index == s, (rows // count) / length, 0.0)
+        row[...] = (weight * F32(1.0 / math.sqrt(total))).T
+
+    value = (cotangent[...].astype(F32) * row[:, :1]).astype(BF16)
+    store_half(value, send_ref, own_ref)
+    accumulate(low_ref, contract_dims(value, adapter[...], 1, 1))
+    squares = jnp.zeros((rows, LANES), F32)
+    for i in range(tokens.shape[1] // LANES):
+        squares = squares + jnp.square(tokens[:, i * LANES : (i + 1) * LANES].astype(F32))
+    squares = jnp.broadcast_to(jnp.sum(squares, axis=1, keepdims=True), (rows, LANES))
+    accumulate(square_ref, squares)
+
+
+def token_kernel(total_width, place, tokens, gain, low_out, squares, *refs):
+    squares_more, (adapter, send_ref, own_ref, low_ref, row) = refs[:-5], refs[-5:]
+    rank = adapter.shape[1]
+
+    @pl.when(pl.program_id(0) == 0)
+    def _():
+        total = squares[...]
+        for ref in squares_more:
+            total = total + ref[...]
+        row[...] = lax.rsqrt(total / total_width + EPS)
+        low_ref[:, rank:] = low_out[...]
+
+    value = tokens[...].astype(F32) * row[:, :1] * gain[...].astype(F32)
     value = value.astype(BF16)
     store_half(value, send_ref, own_ref)
-    accumulate(low_ref, dot(value, adapter[...]))
-
-
-def cotangent_kernel(place, cotangent, weight, adapter, send_ref, own_ref, low_ref):
-    value = (cotangent[...].astype(F32) * weight[...]).astype(BF16)
-    store_half(value, send_ref, own_ref)
-    accumulate(low_ref, contract_dims(value, adapter[...], 1, 1))
+    accumulate(low_ref, dot(value, adapter[...]), slice(0, rank))
 
 
 def transpose_kernel(own, got, out_ref):
@@ -185,9 +223,9 @@
 
 
 def widen(scale, wide):
-    table = scale[...].astype(F32)
-    for g in range(scale.shape[1]):
-        wide[g] = jnp.broadcast_to(table[:, g : g + 1], wide.shape[1:])
+    for g in range(scale.shape[0]):
+        row = scale[g : g + 1, :].astype(F32)
+        wide[g] = jnp.broadcast_to(row, (LANES, row.shape[1])).T
 
 
 def place_shards(codes, got, moved, store):
@@ -272,49 +310,60 @@
             ref[...] = lax.slice_in_dim(full, i * size, (i + 1) * size, axis=axis).astype(BF16)
 
 
-def hidden_kernel(more, gate, up, low_up, low_out, up_out, down_in, *refs):
-    gate_more, up_more = refs[:more], refs[more : 2 * more]
-    up_out_more, down_in_more = refs[2 * more : 3 * more], refs[3 * more : 4 * more]
+def low_sums(low, low_more):
+    total = low[...]
+    for ref in low_more:
+        total = total + ref[...]
+    half = total.shape[1] // 2
+    return total[:, :half].astype(BF16), total[:, half:].astype(BF16)
+
+
+def gather_adapters(adapters, adapters_more, up_out_all, down_in_all):
+    rank = up_out_all.shape[0]
+    place_own(up_out_all, adapters.at[:rank], [r.at[:rank] for r in adapters_more], 1)
+    place_own(down_in_all, adapters.at[rank:], [r.at[rank:] for r in adapters_more], 0)
+
+
+def hidden_kernel(more, gate, up, low, adapters, *refs):
+    gate_more, up_more, low_more, adapters_more = (refs[i * more : (i + 1) * more] for i in range(4))
     silu_ref, low_ref, down_in_term, up_out_all, down_in_all = refs[4 * more :]
-    place_own(up_out_all, up_out, up_out_more, 1)
-    place_own(down_in_all, down_in, down_in_more, 0)
+    gather_adapters(adapters, adapters_more, up_out_all, down_in_all)
+    low_up, low_out = low_sums(low, low_more)
     gate_sum, up_sum = gate[...], up[...]
     for ref in gate_more:
         gate_sum = gate_sum + ref[...].astype(F32)
     for ref in up_more:
         up_sum = up_sum + ref[...].astype(F32)
-    up_sum = up_sum + ADAPTER_SCALE * dot(low_up[...], up_out_all[...])
+    up_sum = up_sum + ADAPTER_SCALE * dot(low_up, up_out_all[...])
     silu = gate_sum * jax.nn.sigmoid(gate_sum)
     silu_ref[...] = silu
     hidden = (silu * up_sum).astype(BF16)
     low_ref[...] = (ADAPTER_SCALE * dot(hidden, down_in_all[...])).astype(BF16)
     hidden_t = hidden.astype(F32).T.astype(BF16)
-    own_units(ADAPTER_SCALE * dot(hidden_t, low_out[...]), down_in_term, 0)
-
-
-def up_grad_kernel(more, back, silu, low_up, low_out, up_out, down_in, *refs):
-    back_more, up_out_more, down_in_more = (refs[i * more : (i + 1) * more] for i in range(3))
+    own_units(ADAPTER_SCALE * dot(hidden_t, low_out), down_in_term, 0)
+
+
+def up_grad_kernel(more, back, silu, low, adapters, *refs):
+    back_more, low_more, adapters_more = (refs[i * more : (i + 1) * more] for i in range(3))
     low_ref, up_out_term, up_out_all, down_in_all = refs[3 * more :]
-    place_own(up_out_all, up_out, up_out_more, 1)
-    place_own(down_in_all, down_in, down_in_more, 0)
+    gather_adapters(adapters, adapters_more, up_out_all, down_in_all)
+    low_up, low_out = low_sums(low, low_more)
     total = back[...]
     for ref in back_more:
         total = total + ref[...].astype(F32)
-    total = total + ADAPTER_SCALE * contract_dims(low_out[...], down_in_all[...], 1, 1)
+    total = total + ADAPTER_SCALE * contract_dims(low_out, down_in_all[...], 1, 1)
     up_grad = (total * silu[...]).astype(BF16)
     low_ref[...] = (ADAPTER_SCALE * contract_dims(up_grad, up_out_all[...], 1, 1)).astype(BF16)
-    low_up_t = low_up[...].astype(F32).T.astype(BF16)
+    low_up_t = low_up.astype(F32).T.astype(BF16)
     own_units(ADAPTER_SCALE * dot(low_up_t, up_grad), up_out_term, 1)
 
 
 def down_out_kernel(low, low_got, grad, grad_got, *out_refs):
-    n = len(out_refs)
-    pos = ring_position()
     low_t = jnp.concatenate([low[...], low_got[...]], axis=0).astype(F32).T.astype(BF16)
     rows = low.shape[0]
     for k, ref in enumerate(out_refs):
         size = ref.shape[1]
-        at = pl.ds(pl.multiple_of(lax.rem(pos - 1 - k + 2 * n, n) * size, size), size)
+        at = slice(k * size, (k + 1) * size)
         ref[...] = (
             dot(low_t[:, :rows], grad[:, at]) + dot(low_t[:, rows:], grad_got[:, at])
         ).astype(BF16)
@@ -322,24 +371,13 @@
 
 def up_in_kernel(low, low_got, normed_t, up_out_term, down_in_term, *out_refs):
     n = len(out_refs)
-    pos = ring_position()
     size = normed_t.shape[0] // n
     extra = out_refs[0].shape[0] - size
     both = jnp.concatenate([low[...], low_got[...]], axis=0)
+    small = jnp.concatenate([up_out_term[...], down_in_term[...]], axis=0)
     for k, ref in enumerate(out_refs):
-        block = lax.rem(pos - 1 - k + 2 * n, n)
-        at = pl.ds(pl.multiple_of(block * size, size), size)
-        ref[pl.ds(0, size), :] = dot(normed_t[at, :], both).astype(BF16)
-        per = up_out_term.shape[0] // extra
-        index = pl.ds(pl.multiple_of(lax.rem(block, per) * extra, extra), extra)
-
-        @pl.when(block < per)
-        def _(ref=ref, index=index):
-            ref[pl.ds(size, extra), :] = up_out_term[index, :]
-
-        @pl.when(block >= per)
-        def _(ref=ref, index=index):
-            ref[pl.ds(size, extra), :] = down_in_term[index, :]
+        ref[:size, :] = dot(normed_t[k * size : (k + 1) * size, :], both).astype(BF16)
+        ref[size:, :] = small[k * extra : (k + 1) * extra, :]
 
 
 def copy_all(copies):
@@ -351,13 +389,12 @@
 
 def down_out_place_kernel(n, *refs):
     pieces, out_ref, sems = refs[: 2 * n], refs[2 * n], refs[2 * n + 1]
-    pos, sub = ring_position(), lax.axis_index("sub")
+    sub = lax.axis_index("sub")
     copies = []
     for i, piece in enumerate(pieces):
         half = sub if i < n else 1 - sub
-        block = lax.rem(pos - i % n + n, n)
         size = piece.shape[1]
-        at = pl.ds(pl.multiple_of((half * n + block) * size, size), size)
+        at = pl.ds(pl.multiple_of((half * n + i % n) * size, size), size)
         copies.append(pltpu.make_async_copy(piece, out_ref.at[:, at], sems.at[i]))
     copy_all(copies)
 
@@ -365,21 +402,22 @@
 def up_in_place_kernel(n, *refs):
     pieces = refs[: 2 * n]
     out_ref, up_out_ref, down_in_ref, small, sems = refs[2 * n :]
-    pos, sub = ring_position(), lax.axis_index("sub")
+    sub = lax.axis_index("sub")
     size = out_ref.shape[0] // (2 * n)
     extra = pieces[0].shape[0] - size
     copies = []
     for i, piece in enumerate(pieces):
         half = sub if i < n else 1 - sub
-        block = lax.rem(pos - i % n + n, n)
-        at = pl.ds(pl.multiple_of((half * n + block) * size, size), size)
+        k = i % n
+        at = pl.ds(pl.multiple_of((half * n + k) * size, size), size)
         copies.append(
             pltpu.make_async_copy(piece.at[pl.ds(0, size), :], out_ref.at[at, :], sems.at[2 * i])
         )
-        at = pl.ds(pl.multiple_of(block * extra, extra), extra)
         copies.append(
             pltpu.make_async_copy(
-                piece.at[pl.ds(size, extra), :], small.at[i // n, at, :], sems.at[2 * i + 1]
+                piece.at[pl.ds(size, extra), :],
+                small.at[i // n, pl.ds(k * extra, extra), :],
+                sems.at[2 * i + 1],
             )
         )
     copy_all(copies)
@@ -387,16 +425,6 @@
     rows = up_out_ref.shape[0]
     up_out_ref[...] = total[:rows]
     down_in_ref[...] = total[rows:]
-
-
-def token_weights(sequence_length_list, slot_sequence_index, rows):
-    seq_count = sequence_length_list.shape[1]
-    longest = rows // seq_count
-    total = rows * lax.axis_size("dp") * lax.axis_size("sub")
-    ratios = longest / sequence_length_list[0].astype(F32)
-    match = slot_sequence_index[:, None] == jnp.arange(seq_count, dtype=jnp.int32)[None, :]
-    weight = jnp.sum(jnp.where(match, ratios[None, :], F32(0.0)), axis=-1)
-    return weight * F32(1.0 / math.sqrt(total))
 
 
 class Shards:
@@ -414,7 +442,7 @@
     def step(self, *done):
         self.moving = ring_step(after(self.moving, *done) if done else self.moving)
         self.moved += [self.moving, swap(self.moving, "grp")]
-        return self.moving
+        return self.moved[-2:]
 
     def args(self):
         return [self.codes, self.got, *self.moved]
@@ -449,37 +477,45 @@
 
     gate_shards = Shards(gate_codes)
     up_shards = Shards(up_codes)
-    down_shards = Shards(jnp.swapaxes(down_codes, 0, 1))
-    order = [gate_shards, up_shards] * 2 + [down_shards, gate_shards, up_shards]
-    if n != 4:
-        order = [gate_shards, up_shards] * (n - 1)
-    order += [down_shards] * (n - 1 - order.count(down_shards))
+    down_shards = Shards(jnp.swapaxes(after(down_codes, up_shards.moving), 0, 1))
     arrived = []
-    for shards in order:
-        arrived.append(shards.step(*arrived[-2:-1]))
-
-    weight = token_weights(sequence_length_list, slot_sequence_index, rows)
-    grad_send, grad, low_out = halves_call(
-        cotangent_kernel, "cotangent", place, cotangent, [weight[:, None]], down_adapter_out, False
+    for shards in [gate_shards, up_shards] * (n - 1) + [down_shards] * (n - 1):
+        done = [ring for ring, _ in arrived[-2:-1]] + [crossed for _, crossed in arrived[-4:-3]]
+        arrived.append(shards.step(*done))
+
+    adapters = jnp.concatenate([up_adapter_out, down_adapter_in], axis=0)
+    adapters_more = others(after(adapters, arrived[0][0]), "mp")
+    tokens_then, cotangent_then, _ = lax.optimization_barrier((tokens, cotangent, arrived[0][0]))
+    grad_send, grad, low_out, squares = halves_call(
+        lambda *refs: cotangent_kernel(rows * n * lax.axis_size("sub"), *refs),
+        "cotangent",
+        place,
+        [cotangent_then, tokens_then],
+        down_adapter_out,
+        False,
+        [sequence_length_list, slot_sequence_index[None, :]],
+        ["scalars", "whole"],
+        [rank, LANES],
     )
     grad_got = swap(grad_send, "sub")
-    own_squares = jnp.sum(jnp.square(tokens.astype(F32)), axis=-1)
-    squares = sum(others(own_squares, "mp"), own_squares) / total_width
-    inv_rms = lax.rsqrt(squares + EPS)[:, None]
-    normed_send, normed, low_up = halves_call(
-        token_kernel, "tokens", place, tokens, [inv_rms, rms_norm_gain[None, :]], up_adapter_in, True
+    squares_more = others(squares, "mp")
+    tokens_then = after(tokens, arrived[2][0])
+    normed_send, normed, low = halves_call(
+        lambda *refs: token_kernel(total_width, *refs),
+        "tokens",
+        place,
+        [tokens_then],
+        up_adapter_in,
+        True,
+        [rms_norm_gain[None, :], low_out, squares, *squares_more],
+        ["features"] + ["whole"] * (2 + more),
+        [2 * rank],
     )
     normed_got = swap(normed_send, "sub")
-    low_up = sum(others(low_up, "mp"), low_up).astype(BF16)
-    low_out = sum(others(low_out, "mp"), low_out).astype(BF16)
-    up_out_more = others(up_adapter_out, "mp")
-    down_in_more = others(down_adapter_in, "mp")
-    (normed_t,) = call(
-        transpose_kernel, "transpose", [normed, normed_got], [shape((half, 2 * rows))], limit=32
-    )
+    low_more = others(low, "mp")
 
     def product(kernel, name, own, got, scale, shards, weight_shape):
-        groups = scale.shape[1]
+        groups = scale.shape[0]
         mine, theirs = call(
             kernel,
             name,
@@ -493,18 +529,17 @@
 
     front = (blocks // 2, block, units)
     gate, gate_more = product(
-        front_kernel, "gate", normed, normed_got, gate_block_scale, gate_shards, front
-    )
-    up, up_more = product(front_kernel, "up", normed, normed_got, up_block_scale, up_shards, front)
+        front_kernel, "gate", normed, normed_got, gate_block_scale.T, gate_shards, front
+    )
+    up, up_more = product(front_kernel, "up", normed, normed_got, up_block_scale.T, up_shards, front)
     small_scratch = [
         pltpu.VMEM((rank, units), BF16),
         pltpu.VMEM((units, rank), BF16),
     ]
-    adapters = [low_up, low_out, up_adapter_out, down_adapter_in]
     silu, low_hidden, down_in_term = call(
         lambda *refs: hidden_kernel(more, *refs),
         "hidden",
-        [gate, up, *adapters, *gate_more, *up_more, *up_out_more, *down_in_more],
+        [gate, up, low, adapters, *gate_more, *up_more, *low_more, *adapters_more],
         [shape((rows, units), F32), shape((rows, rank)), shape(down_adapter_in.shape)],
         scratch=small_scratch,
         limit=8,
@@ -513,51 +548,57 @@
         down_out_kernel,
         "down_out",
         [low_hidden, swap(low_hidden, "sub"), grad, grad_got],
-        [shape((rank, half // n))] * n,
+        [shape((rank, half // PIECES))] * PIECES,
         flops=4 * rows * half * rank,
     )
-    down_out_blocks = ring_gather(ring_sum(down_out_parts))
+    (normed_t,) = call(
+        transpose_kernel,
+        "transpose",
+        [normed, after(normed_got, low_hidden)],
+        [shape((half, 2 * rows))],
+        limit=32,
+    )
 
     back, back_more = product(
-        back_kernel, "back", grad, grad_got, down_block_scale.T, down_shards, (units, half)
+        back_kernel, "back", grad, grad_got, down_block_scale, down_shards, (units, half)
     )
     low_grad, up_out_term = call(
         lambda *refs: up_grad_kernel(more, *refs),
         "up_grad",
-        [back, silu, *adapters, *back_more, *up_out_more, *down_in_more],
+        [back, silu, low, adapters, *back_more, *low_more, *adapters_more],
         [shape((rows, rank)), shape(up_adapter_out.shape)],
         scratch=small_scratch,
         limit=8,
     )
-    extra = 2 * rank // n
+    extra = 2 * rank // PIECES
     up_in_parts = call(
         up_in_kernel,
         "up_in",
         [low_grad, swap(low_grad, "sub"), normed_t, up_out_term, down_in_term],
-        [shape((half // n + extra, rank))] * n,
+        [shape((half // PIECES + extra, rank))] * PIECES,
         flops=4 * rows * half * rank,
     )
-    up_in_blocks = ring_gather(ring_sum(up_in_parts))
+    sums, sums_got = line_sums([*down_out_parts, *up_in_parts])
 
     anywhere = pl.BlockSpec(memory_space=pl.ANY)
     vmem = pl.BlockSpec(memory_space=pltpu.VMEM)
     (down_out_gradient,) = call(
-        lambda *refs: down_out_place_kernel(n, *refs),
+        lambda *refs: down_out_place_kernel(PIECES, *refs),
         "down_out_place",
-        [*down_out_blocks[0], *down_out_blocks[1]],
+        [*sums[:PIECES], *sums_got[:PIECES]],
         [shape((rank, local_width))],
-        scratch=[pltpu.SemaphoreType.DMA((2 * n,))],
-        specs=[anywhere] * (2 * n),
+        scratch=[pltpu.SemaphoreType.DMA((2 * PIECES,))],
+        specs=[anywhere] * (2 * PIECES),
         out_specs=(anywhere,),
         limit=4,
     )
     up_in_gradient, up_out_gradient, down_in_gradient = call(
-        lambda *refs: up_in_place_kernel(n, *refs),
+        lambda *refs: up_in_place_kernel(PIECES, *refs),
         "up_in_place",
-        [*up_in_blocks[0], *up_in_blocks[1]],
+        [*sums[PIECES:], *sums_got[PIECES:]],
         [shape((local_width, rank)), shape(up_adapter_out.shape), shape(down_adapter_in.shape)],
-        scratch=[pltpu.VMEM((2, 2 * rank, rank), BF16), pltpu.SemaphoreType.DMA((4 * n,))],
-        specs=[anywhere] * (2 * n),
+        scratch=[pltpu.VMEM((2, 2 * rank, rank), BF16), pltpu.SemaphoreType.DMA((4 * PIECES,))],
+        specs=[anywhere] * (2 * PIECES),
         out_specs=(anywhere, vmem, vmem),
         limit=4,
     )

time: 241 us -> 251 us (1.041)
  starting transfers between devices: 52.5 us -> 86.8 us
  local copies, waits for them, and re-layouts: 23.7 us -> 7.53 us
  Pallas kernels: 35.8 us -> 31.1 us
    ppermute x0 -> x24, waiting for transfers between devices: none -> 64.8 us  [the longest x8 58.4 us: line_sums(): got = lax.ppermute(x, 'dp', [(s + 1, s), (n - 2 - s, n - 1 - s)])]
    ppermute x21 -> x9, waiting for transfers between devices: 90.7 us -> 30.2 us  [ring_step(): lax.ppermute(x, 'dp', [(ring_at(i, n), ring_at((i + 1) % n, n)) for i in...]
    ppermute x0 -> x24, starting transfers between devices: none -> 47.9 us  [the longest x8 32.2 us: line_sums(): x = add(x, lax.ppermute(x, 'dp', [(s, s + 1), (n - 1 - s, n - 2 - s)]))]
    unnamed x92 -> x39, local copies, waits for them, and re-layouts: 19 us -> 4.57 us
    ppermute x21 -> x9, starting transfers between devices: 26.8 us -> 14.8 us  [ring_step(): lax.ppermute(x, 'dp', [(ring_at(i, n), ring_at((i + 1) % n, n)) for i in...]
    pallas_call x10, Pallas kernels: 23.8 us -> 15.2 us  [call(): pl.pallas_call(kernel, out_shape=tuple(out_shape), in_specs=specs or [vme...]
    ppermute x27, waiting for transfers between devices: 22.1 us -> 16.7 us  [swap(): return lax.ppermute(x, axis, [(0, 1), (1, 0)])]
    pallas_call x2, Pallas kernels: 12 us -> 15.9 us  [halves_call(): pl.pallas_call(kernel, out_shape=(shape((rows, width // 2)),) * 2 + tuple...]
  transfers between devices with their start and end apart: 56 -> 66, of which waited for: 30 -> 26; matrix products, arithmetic and copies ran while one was open for 5% -> 3% of each run, Pallas kernels for 10% -> 9%
where the time goes in v3:
time: 251 us; the launch traced here: 250 us
  waiting for transfers between devices  119 us (47%)
  starting transfers between devices  86.8 us (35%)
  Pallas kernels  31.1 us (12%)
  local copies, waits for them, and re-layouts  7.53 us (3%)
  other arithmetic  4.3 us (2%)
    ppermute x8, waiting for transfers between devices, line_sums(): got = lax.ppermute(x, 'dp', [(s + 1, s), (n - 2 - s, n - 1 - s)])  58.4 us
    ppermute x8, starting transfers between devices, line_sums(): x = add(x, lax.ppermute(x, 'dp', [(s, s + 1), (n - 1 - s, n - 2 - s)]))  32.2 us
    ppermute x9, waiting for transfers between devices, ring_step(): lax.ppermute(x, 'dp', [(ring_at(i, n), ring_at((i + 1) % n, n)) for i in...  30.2 us
    ppermute x27, waiting for transfers between devices, swap(): return lax.ppermute(x, axis, [(0, 1), (1, 0)])  16.7 us
    pallas_call x2, Pallas kernels, halves_call(): pl.pallas_call(kernel, out_shape=(shape((rows, width // 2)),) * 2 + tuple...  15.9 us
    ppermute x27, starting transfers between devices, swap(): return lax.ppermute(x, axis, [(0, 1), (1, 0)])  15.9 us
    pallas_call x10, Pallas kernels, call(): pl.pallas_call(kernel, out_shape=tuple(out_shape), in_specs=specs or [vme...  15.2 us
    ppermute x9, starting transfers between devices, ring_step(): lax.ppermute(x, 'dp', [(ring_at(i, n), ring_at((i + 1) % n, n)) for i in...  14.8 us
  transfers between devices with their start and end apart: 66, of which 26 were waited for; matrix products, arithmetic and copies ran while one was open for 3% of the time, Pallas kernels for 9%

profile of v3, /device:TPU:0, one launch (start us, length us, event | category | flops | bytes accessed | tf_op | source)
XLA Modules:
  0.0 250.1 jit_solution(11849166601497967505)
XLA Ops:
  6.3 7.6 %collective-permute-done.1.refs_0_ = bf16[32,16,256]{2,1,0:T(8,128)(2,1)S(1)} collective-permute-done((bf16[32,16,256]{2,1,0:T(8,128)(2,1)S(1)}, bf16[32,16,256]{2,1,0:T(8,128)(2,1)S(1)}, u32[]{:S(2)}, u32[]{:S(2)}) %collective-permute-start.1) | collective-permute-done | bytes 262176 | tf_op jit(solution)/shard_map/ppermute | solution.py:46
  14.8 8.6 %cotangent.1 = (bf16[256,4096]{1,0:T(8,128)(2,1)}, bf16[256,4096]{1,0:T(8,128)(2,1)}, f32[256,128]{1,0:T(8,128)}, f32[256,128]{1,0:T(8,128)}) custom-call(s32[1]{0:T(128)} %bitcast.refs_0_, bf16[256,8192]{1,0:T(8,128)(2,1)} %refs_1_, bf16[256,8192]{1,0:T(8,128)(2,1)} %refs_1_.1, s32[1,2]{1,0:T(1,128)} %refs_3_.1, s32[1,256]{1,0:T(1,128)} %bitcast.13, ...), custom_call_target="tpu_custom_call" | custom-call | flops 536870912 | bytes 16777216 | tf_op jit(solution)/shard_map/cotangent/pallas_call | solution.py:129
  29.3 7.3 %tokens.1 = (bf16[256,4096]{1,0:T(8,128)(2,1)}, bf16[256,4096]{1,0:T(8,128)(2,1)}, f32[256,256]{1,0:T(8,128)}) custom-call(s32[1]{0:T(128)} %bitcast.refs_0_, bf16[256,8192]{1,0:T(8,128)(2,1)} %refs_1_.1, bf16[1,8192]{1,0:T(2,128)(2,1)} %broadcast_in_dim.7.refs_2_, f32[256,128]{1,0:T(8,128)} %get-tuple-element.67.refs_3_, ...), custom_call_target="tpu_custom_call" | custom-call | flops 536870912 | bytes 16777216 | tf_op jit(solution)/shard_map/tokens/pallas_call | solution.py:129
  37.3 3.6 %collective-permute-done.3.codes_got = bf16[32,16,256]{2,1,0:T(8,128)(2,1)S(1)} collective-permute-done((bf16[32,16,256]{2,1,0:T(8,128)(2,1)S(1)}, bf16[32,16,256]{2,1,0:T(8,128)(2,1)S(1)}, u32[]{:S(2)}, u32[]{:S(2)}) %collective-permute-start.3) | collective-permute-done | bytes 262176 | tf_op jit(solution)/shard_map/ppermute | solution.py:50
  40.9 3.4 %collective-permute-start.11 = (bf16[32,16,256]{2,1,0:T(8,128)(2,1)S(1)}, bf16[32,16,256]{2,1,0:T(8,128)(2,1)S(1)}, u32[]{:S(2)}, u32[]{:S(2)}) collective-permute-start(bf16[32,16,256]{2,1,0:T(8,128)(2,1)S(1)} %pad_maximum_fusion.1), channel_id=1, source_target_pairs={{0,4},{4,12},{12,8},{8,0},{1,5},{5,13},{13,9},{9,1},{2,6},{6,14},{... | collective-permute-start | bytes 786440 | tf_op jit(solution)/shard_map/ppermute | solution.py:46
  46.3 4.2 %collective-permute-done.11.refs_0_ = bf16[32,16,256]{2,1,0:T(8,128)(2,1)S(1)} collective-permute-done((bf16[32,16,256]{2,1,0:T(8,128)(2,1)S(1)}, bf16[32,16,256]{2,1,0:T(8,128)(2,1)S(1)}, u32[]{:S(2)}, u32[]{:S(2)}) %collective-permute-start.11) | collective-permute-done | bytes 262176 | tf_op jit(solution)/shard_map/ppermute | solution.py:46
  54.6 4.6 %collective-permute-done.12.refs_2_ = bf16[32,16,256]{2,1,0:T(8,128)(2,1)S(1)} collective-permute-done((bf16[32,16,256]{2,1,0:T(8,128)(2,1)S(1)}, bf16[32,16,256]{2,1,0:T(8,128)(2,1)S(1)}, u32[]{:S(2)}, u32[]{:S(2)}) %collective-permute-start.12) | collective-permute-done | bytes 262176 | tf_op jit(solution)/shard_map/ppermute | solution.py:46
  64.7 4.6 %collective-permute-done.7.refs_4_ = bf16[32,16,256]{2,1,0:T(8,128)(2,1)S(1)} collective-permute-done((bf16[32,16,256]{2,1,0:T(8,128)(2,1)S(1)}, bf16[32,16,256]{2,1,0:T(8,128)(2,1)S(1)}, u32[]{:S(2)}, u32[]{:S(2)}) %collective-permute-start.7) | collective-permute-done | bytes 262176 | tf_op jit(solution)/shard_map/ppermute | solution.py:46
  71.5 3.4 %collective-permute-done.14.refs_4_ = bf16[32,16,256]{2,1,0:T(8,128)(2,1)S(1)} collective-permute-done((bf16[32,16,256]{2,1,0:T(8,128)(2,1)S(1)}, bf16[32,16,256]{2,1,0:T(8,128)(2,1)S(1)}, u32[]{:S(2)}, u32[]{:S(2)}) %collective-permute-start.14) | collective-permute-done | bytes 262176 | tf_op jit(solution)/shard_map/ppermute | solution.py:46
  90.5 5.9 %collective-permute-done.19.refs_4_ = bf16[32,32,128]{2,1,0:T(8,128)(2,1)S(1)} collective-permute-done((bf16[32,32,128]{2,1,0:T(8,128)(2,1)S(1)}, bf16[32,32,128]{2,1,0:T(8,128)(2,1)S(1)}, u32[]{:S(2)}, u32[]{:S(2)}) %collective-permute-start.19) | collective-permute-done | bytes 262176 | tf_op jit(solution)/shard_map/ppermute | solution.py:46
  101.7 3.7 %collective-permute-done.20.refs_5_ = bf16[32,32,128]{2,1,0:T(8,128)(2,1)S(1)} collective-permute-done((bf16[32,32,128]{2,1,0:T(8,128)(2,1)S(1)}, bf16[32,32,128]{2,1,0:T(8,128)(2,1)S(1)}, u32[]{:S(2)}, u32[]{:S(2)}) %collective-permute-start.20) | collective-permute-done | bytes 262176 | tf_op jit(solution)/shard_map/ppermute | solution.py:50
  115.3 3.3 %collective-permute-start.34 = (bf16[128,1024]{1,0:T(8,128)(2,1)}, bf16[128,1024]{1,0:T(8,128)(2,1)}, u32[]{:S(2)}, u32[]{:S(2)}) collective-permute-start(bf16[128,1024]{1,0:T(8,128)(2,1)} %get-tuple-element.85), channel_id=1, source_target_pairs={{0,4},{12,8},{1,5},{13,9},{2,6},{14,10},{3,7},{15,11},{16,20},{28,... | collective-permute-start | bytes 786440 | tf_op jit(solution)/shard_map/ppermute | solution.py:75
  140.0 7.3 %collective-permute-start.36 = (bf16[1088,128]{1,0:T(8,128)(2,1)S(1)}, bf16[1088,128]{1,0:T(8,128)(2,1)S(1)}, u32[]{:S(2)}, u32[]{:S(2)}) collective-permute-start(bf16[1088,128]{1,0:T(8,128)(2,1)S(1)} %get-tuple-element.87), channel_id=1, source_target_pairs={{0,4},{12,8},{1,5},{13,9},{2,6},{14,10},{3,7},{15,11},{16,20},{28,... | collective-permute-start | bytes 835592 | tf_op jit(solution)/shard_map/ppermute | solution.py:75
  148.1 4.6 %collective-permute-start.41 = (bf16[1088,128]{1,0:T(8,128)(2,1)S(1)}, bf16[1088,128]{1,0:T(8,128)(2,1)S(1)}, u32[]{:S(2)}, u32[]{:S(2)}) collective-permute-start(bf16[1088,128]{1,0:T(8,128)(2,1)S(1)} %get-tuple-element.92), channel_id=1, source_target_pairs={{0,4},{12,8},{1,5},{13,9},{2,6},{14,10},{3,7},{15,11},{16,20},{28,... | collective-permute-start | bytes 835592 | tf_op jit(solution)/shard_map/ppermute | solution.py:75
  157.0 7.0 %collective-permute-done.55 = bf16[128,1024]{1,0:T(8,128)(2,1)S(1)} collective-permute-done((bf16[128,1024]{1,0:T(8,128)(2,1)S(1)}, bf16[128,1024]{1,0:T(8,128)(2,1)S(1)}, u32[]{:S(2)}, u32[]{:S(2)}) %collective-permute-start.55) | collective-permute-done | bytes 262176 | tf_op jit(solution)/shard_map/ppermute | solution.py:80
  165.3 4.3 %collective-permute-done.57 = bf16[128,1024]{1,0:T(8,128)(2,1)S(1)} collective-permute-done((bf16[128,1024]{1,0:T(8,128)(2,1)S(1)}, bf16[128,1024]{1,0:T(8,128)(2,1)S(1)}, u32[]{:S(2)}, u32[]{:S(2)}) %collective-permute-start.57) | collective-permute-done | bytes 262176 | tf_op jit(solution)/shard_map/ppermute | solution.py:80
  171.1 4.1 %collective-permute-done.59 = bf16[128,1024]{1,0:T(8,128)(2,1)S(1)} collective-permute-done((bf16[128,1024]{1,0:T(8,128)(2,1)S(1)}, bf16[128,1024]{1,0:T(8,128)(2,1)S(1)}, u32[]{:S(2)}, u32[]{:S(2)}) %collective-permute-start.59) | collective-permute-done | bytes 262176 | tf_op jit(solution)/shard_map/ppermute | solution.py:80
  175.9 7.2 %collective-permute-start.44 = (bf16[1088,128]{1,0:T(8,128)(2,1)S(1)}, bf16[1088,128]{1,0:T(8,128)(2,1)S(1)}, u32[]{:S(2)}, u32[]{:S(2)}) collective-permute-start(bf16[1088,128]{1,0:T(8,128)(2,1)S(1)} %get-tuple-element.94), channel_id=1, source_target_pairs={{0,4},{12,8},{1,5},{13,9},{2,6},{14,10},{3,7},{15,11},{16,20},{28,... | collective-permute-start | bytes 835592 | tf_op jit(solution)/shard_map/ppermute | solution.py:75
  183.3 4.9 %collective-permute-start.47 = (bf16[1088,128]{1,0:T(8,128)(2,1)S(1)}, bf16[1088,128]{1,0:T(8,128)(2,1)S(1)}, u32[]{:S(2)}, u32[]{:S(2)}) collective-permute-start(bf16[1088,128]{1,0:T(8,128)(2,1)S(1)} %get-tuple-element.96), channel_id=1, source_target_pairs={{0,4},{12,8},{1,5},{13,9},{2,6},{14,10},{3,7},{15,11},{16,20},{28,... | collective-permute-start | bytes 835592 | tf_op jit(solution)/shard_map/ppermute | solution.py:75
  188.4 5.0 %collective-permute-done.47 = bf16[1088,128]{1,0:T(8,128)(2,1)S(1)} collective-permute-done((bf16[1088,128]{1,0:T(8,128)(2,1)S(1)}, bf16[1088,128]{1,0:T(8,128)(2,1)S(1)}, u32[]{:S(2)}, u32[]{:S(2)}) %collective-permute-start.47) | collective-permute-done | bytes 278560 | tf_op jit(solution)/shard_map/ppermute | solution.py:75
  194.8 7.4 %collective-permute-done.38 = bf16[1088,128]{1,0:T(8,128)(2,1)S(1)} collective-permute-done((bf16[1088,128]{1,0:T(8,128)(2,1)S(1)}, bf16[1088,128]{1,0:T(8,128)(2,1)S(1)}, u32[]{:S(2)}, u32[]{:S(2)}) %collective-permute-start.38) | collective-permute-done | bytes 278560 | tf_op jit(solution)/shard_map/ppermute | solution.py:80
  203.5 7.1 %collective-permute-done.43 = bf16[1088,128]{1,0:T(8,128)(2,1)S(1)} collective-permute-done((bf16[1088,128]{1,0:T(8,128)(2,1)S(1)}, bf16[1088,128]{1,0:T(8,128)(2,1)S(1)}, u32[]{:S(2)}, u32[]{:S(2)}) %collective-permute-start.43) | collective-permute-done | bytes 278560 | tf_op jit(solution)/shard_map/ppermute | solution.py:80
  213.5 21.4 %collective-permute-done.46 = bf16[1088,128]{1,0:T(8,128)(2,1)S(1)} collective-permute-done((bf16[1088,128]{1,0:T(8,128)(2,1)S(1)}, bf16[1088,128]{1,0:T(8,128)(2,1)S(1)}, u32[]{:S(2)}, u32[]{:S(2)}) %collective-permute-start.46) | collective-permute-done | bytes 278560 | tf_op jit(solution)/shard_map/ppermute | solution.py:80
  236.2 7.1 %collective-permute-done.49 = bf16[1088,128]{1,0:T(8,128)(2,1)S(1)} collective-permute-done((bf16[1088,128]{1,0:T(8,128)(2,1)S(1)}, bf16[1088,128]{1,0:T(8,128)(2,1)S(1)}, u32[]{:S(2)}, u32[]{:S(2)}) %collective-permute-start.49) | collective-permute-done | bytes 278560 | tf_op jit(solution)/shard_map/ppermute | solution.py:80
  (201 shorter events, 100.8 us)
Async XLA Ops:
  14.0 11.6 %collective-permute-start.5 = (bf16[32,16,256]{2,1,0:T(8,128)(2,1)S(1)}, bf16[32,16,256]{2,1,0:T(8,128)(2,1)S(1)}, u32[]{:S(2)}, u32[]{:S(2)}) collective-permute-start(bf16[32,16,256]{2,1,0:T(8,128)(2,1)S(1)} %collective-permute-done.1.refs_0_), channel_id=1, source_target_pairs={{0,4},{4,12},{12,8},{8,0},{1,5},{5,13},{13,9},{9,1},{2,6},{6,14},{... | collective-permute-start | bytes 786440 | tf_op jit(solution)/shard_map/ppermute | solution.py:46
  36.7 46.7 %collective-permute-start.23 = (bf16[256,4096]{1,0:T(8,128)(2,1)}, bf16[256,4096]{1,0:T(8,128)(2,1)S(1)}, u32[]{:S(2)}, u32[]{:S(2)}) collective-permute-start(bf16[256,4096]{1,0:T(8,128)(2,1)} %get-tuple-element.70), channel_id=1, source_target_pairs={{0,1},{1,0},{2,3},{3,2},{4,5},{5,4},{6,7},{7,6},{8,9},{9,8},{10,11... | collective-permute-start | bytes 6291464 | tf_op jit(solution)/shard_map/ppermute | solution.py:50
  44.4 62.4 %collective-permute-start.2 = (bf16[256,4096]{1,0:T(8,128)(2,1)}, bf16[256,4096]{1,0:T(8,128)(2,1)S(1)}, u32[]{:S(2)}, u32[]{:S(2)}) collective-permute-start(bf16[256,4096]{1,0:T(8,128)(2,1)} %get-tuple-element.55), channel_id=1, source_target_pairs={{0,1},{1,0},{2,3},{3,2},{4,5},{5,4},{6,7},{7,6},{8,9},{9,8},{10,11... | collective-permute-start | bytes 6291464 | tf_op jit(solution)/shard_map/ppermute | solution.py:50
  62.3 12.6 %collective-permute-start.14 = (bf16[32,16,256]{2,1,0:T(8,128)(2,1)S(1)}, bf16[32,16,256]{2,1,0:T(8,128)(2,1)S(1)}, u32[]{:S(2)}, u32[]{:S(2)}) collective-permute-start(bf16[32,16,256]{2,1,0:T(8,128)(2,1)S(1)} %collective-permute-done.12.refs_2_), channel_id=1, source_target_pairs={{0,4},{4,12},{12,8},{8,0},{1,5},{5,13},{13,9},{9,1},{2,6},{6,14},{... | collective-permute-start | bytes 786440 | tf_op jit(solution)/shard_map/ppermute | solution.py:46
  85.4 12.8 %collective-permute-start.10 = (bf16[32,32,128]{2,1,0:T(8,128)(2,1)S(1)}, bf16[32,32,128]{2,1,0:T(8,128)(2,1)S(1)}, u32[]{:S(2)}, u32[]{:S(2)}) collective-permute-start(bf16[32,32,128]{2,1,0:T(8,128)(2,1)S(1)} %collective-permute-done.9.refs_0_), channel_id=1, source_target_pairs={{0,16},{16,0},{1,17},{17,1},{2,18},{18,2},{3,19},{19,3},{4,20},{20... | collective-permute-start | bytes 786440 | tf_op jit(solution)/shard_map/ppermute | solution.py:50
  87.1 12.9 %collective-permute-start.17 = (bf16[32,32,128]{2,1,0:T(8,128)(2,1)S(1)}, bf16[32,32,128]{2,1,0:T(8,128)(2,1)S(1)}, u32[]{:S(2)}, u32[]{:S(2)}) collective-permute-start(bf16[32,32,128]{2,1,0:T(8,128)(2,1)S(1)} %collective-permute-done.16.refs_2_), channel_id=1, source_target_pairs={{0,16},{16,0},{1,17},{17,1},{2,18},{18,2},{3,19},{19,3},{4,20},{20... | collective-permute-start | bytes 786440 | tf_op jit(solution)/shard_map/ppermute | solution.py:50
  96.4 14.6 %collective-permute-start.29 = (f32[256,256]{1,0:T(8,128)S(1)}, f32[256,256]{1,0:T(8,128)S(1)}, u32[]{:S(2)}, u32[]{:S(2)}) collective-permute-start(f32[256,256]{1,0:T(8,128)S(1)} %copy-done.6), channel_id=1, source_target_pairs={{0,2},{2,0},{1,3},{3,1},{4,6},{6,4},{5,7},{7,5},{8,10},{10,8},{9,1... | collective-permute-start | bytes 786440 | tf_op jit(solution)/shard_map/ppermute | solution.py:55
  98.3 12.7 %collective-permute-start.27 = (bf16[256,256]{1,0:T(8,128)(2,1)S(1)}, bf16[256,256]{1,0:T(8,128)(2,1)S(1)}, u32[]{:S(2)}, u32[]{:S(2)}) collective-permute-start(bf16[256,256]{1,0:T(8,128)(2,1)S(1)} %get-tuple-element.104), channel_id=1, source_target_pairs={{0,2},{2,0},{1,3},{3,1},{4,6},{6,4},{5,7},{7,5},{8,10},{10,8},{9,1... | collective-permute-start | bytes 393224 | tf_op jit(solution)/shard_map/ppermute | solution.py:55
  115.3 14.9 %collective-permute-start.34 = (bf16[128,1024]{1,0:T(8,128)(2,1)}, bf16[128,1024]{1,0:T(8,128)(2,1)}, u32[]{:S(2)}, u32[]{:S(2)}) collective-permute-start(bf16[128,1024]{1,0:T(8,128)(2,1)} %get-tuple-element.85), channel_id=1, source_target_pairs={{0,4},{12,8},{1,5},{13,9},{2,6},{14,10},{3,7},{15,11},{16,20},{28,... | collective-permute-start | bytes 786440 | tf_op jit(solution)/shard_map/ppermute | solution.py:75
  120.8 11.8 %collective-permute-start.39 = (bf16[128,1024]{1,0:T(8,128)(2,1)}, bf16[128,1024]{1,0:T(8,128)(2,1)}, u32[]{:S(2)}, u32[]{:S(2)}) collective-permute-start(bf16[128,1024]{1,0:T(8,128)(2,1)} %get-tuple-element.90), channel_id=1, source_target_pairs={{0,4},{12,8},{1,5},{13,9},{2,6},{14,10},{3,7},{15,11},{16,20},{28,... | collective-permute-start | bytes 786440 | tf_op jit(solution)/shard_map/ppermute | solution.py:75
  133.7 13.6 %collective-permute-start.40 = (bf16[128,1024]{1,0:T(8,128)(2,1)S(1)}, bf16[128,1024]{1,0:T(8,128)(2,1)S(1)}, u32[]{:S(2)}, u32[]{:S(2)}) collective-permute-start(bf16[128,1024]{1,0:T(8,128)(2,1)S(1)} %get-tuple-element.91), channel_id=1, source_target_pairs={{0,4},{12,8},{1,5},{13,9},{2,6},{14,10},{3,7},{15,11},{16,20},{28,... | collective-permute-start | bytes 786440 | tf_op jit(solution)/shard_map/ppermute | solution.py:75
  136.5 11.6 %collective-permute-start.54 = (bf16[128,1024]{1,0:T(8,128)(2,1)S(1)}, bf16[128,1024]{1,0:T(8,128)(2,1)S(1)}, u32[]{:S(2)}, u32[]{:S(2)}) collective-permute-start(bf16[128,1024]{1,0:T(8,128)(2,1)S(1)} %add_convert_fusion.15), channel_id=1, source_target_pairs={{4,8},{8,4},{5,9},{9,5},{6,10},{10,6},{7,11},{11,7},{20,24},{24,20... | collective-permute-start | bytes 786440 | tf_op jit(solution)/shard_map/ppermute | solution.py:78
  137.2 15.6 %collective-permute-start.56 = (bf16[128,1024]{1,0:T(8,128)(2,1)S(1)}, bf16[128,1024]{1,0:T(8,128)(2,1)S(1)}, u32[]{:S(2)}, u32[]{:S(2)}) collective-permute-start(bf16[128,1024]{1,0:T(8,128)(2,1)S(1)} %add_convert_fusion.13), channel_id=1, source_target_pairs={{4,8},{8,4},{5,9},{9,5},{6,10},{10,6},{7,11},{11,7},{20,24},{24,20... | collective-permute-start | bytes 786440 | tf_op jit(solution)/shard_map/ppermute | solution.py:78
  139.3 14.8 %collective-permute-start.58 = (bf16[128,1024]{1,0:T(8,128)(2,1)S(1)}, bf16[128,1024]{1,0:T(8,128)(2,1)S(1)}, u32[]{:S(2)}, u32[]{:S(2)}) collective-permute-start(bf16[128,1024]{1,0:T(8,128)(2,1)S(1)} %add_convert_fusion.14), channel_id=1, source_target_pairs={{4,8},{8,4},{5,9},{9,5},{6,10},{10,6},{7,11},{11,7},{20,24},{24,20... | collective-permute-start | bytes 786440 | tf_op jit(solution)/shard_map/ppermute | solution.py:78
  140.0 29.6 %collective-permute-start.36 = (bf16[1088,128]{1,0:T(8,128)(2,1)S(1)}, bf16[1088,128]{1,0:T(8,128)(2,1)S(1)}, u32[]{:S(2)}, u32[]{:S(2)}) collective-permute-start(bf16[1088,128]{1,0:T(8,128)(2,1)S(1)} %get-tuple-element.87), channel_id=1, source_target_pairs={{0,4},{12,8},{1,5},{13,9},{2,6},{14,10},{3,7},{15,11},{16,20},{28,... | collective-permute-start | bytes 835592 | tf_op jit(solution)/shard_map/ppermute | solution.py:75
  148.1 22.2 %collective-permute-start.41 = (bf16[1088,128]{1,0:T(8,128)(2,1)S(1)}, bf16[1088,128]{1,0:T(8,128)(2,1)S(1)}, u32[]{:S(2)}, u32[]{:S(2)}) collective-permute-start(bf16[1088,128]{1,0:T(8,128)(2,1)S(1)} %get-tuple-element.92), channel_id=1, source_target_pairs={{0,4},{12,8},{1,5},{13,9},{2,6},{14,10},{3,7},{15,11},{16,20},{28,... | collective-permute-start | bytes 835592 | tf_op jit(solution)/shard_map/ppermute | solution.py:75
  154.2 15.4 %collective-permute-start.57 = (bf16[128,1024]{1,0:T(8,128)(2,1)S(1)}, bf16[128,1024]{1,0:T(8,128)(2,1)S(1)}, u32[]{:S(2)}, u32[]{:S(2)}) collective-permute-start(bf16[128,1024]{1,0:T(8,128)(2,1)S(1)} %add_convert_fusion.10), channel_id=1, source_target_pairs={{4,0},{8,12},{5,1},{9,13},{6,2},{10,14},{7,3},{11,15},{20,16},{24,... | collective-permute-start | bytes 786440 | tf_op jit(solution)/shard_map/ppermute | solution.py:80
  155.6 19.6 %collective-permute-start.59 = (bf16[128,1024]{1,0:T(8,128)(2,1)S(1)}, bf16[128,1024]{1,0:T(8,128)(2,1)S(1)}, u32[]{:S(2)}, u32[]{:S(2)}) collective-permute-start(bf16[128,1024]{1,0:T(8,128)(2,1)S(1)} %add_convert_fusion.9), channel_id=1, source_target_pairs={{4,0},{8,12},{5,1},{9,13},{6,2},{10,14},{7,3},{11,15},{20,16},{24,... | collective-permute-start | bytes 786440 | tf_op jit(solution)/shard_map/ppermute | solution.py:80
  164.0 79.4 %collective-permute-start.61 = (bf16[128,1024]{1,0:T(8,128)(2,1)S(1)}, bf16[128,1024]{1,0:T(8,128)(2,1)S(1)}, u32[]{:S(2)}, u32[]{:S(2)}) collective-permute-start(bf16[128,1024]{1,0:T(8,128)(2,1)S(1)} %add_convert_fusion.8), channel_id=1, source_target_pairs={{4,0},{8,12},{5,1},{9,13},{6,2},{10,14},{7,3},{11,15},{20,16},{24,... | collective-permute-start | bytes 786440 | tf_op jit(solution)/shard_map/ppermute | solution.py:80
  169.6 74.4 %collective-permute-start.62 = (bf16[128,1024]{1,0:T(8,128)(2,1)S(1)}, bf16[128,1024]{1,0:T(8,128)(2,1)S(1)}, u32[]{:S(2)}, u32[]{:S(2)}) collective-permute-start(bf16[128,1024]{1,0:T(8,128)(2,1)S(1)} %broadcast_select_fusion.7.refs_0_), channel_id=1, source_target_pairs={{0,1},{1,0},{2,3},{3,2},{4,5},{5,4},{6,7},{7,6},{8,9},{9,8},{10,11... | collective-permute-start | bytes 786440 | tf_op jit(solution)/shard_map/ppermute | solution.py:50
  169.6 74.4 %collective-permute-start.63 = (bf16[128,1024]{1,0:T(8,128)(2,1)S(1)}, bf16[128,1024]{1,0:T(8,128)(2,1)S(1)}, u32[]{:S(2)}, u32[]{:S(2)}) collective-permute-start(bf16[128,1024]{1,0:T(8,128)(2,1)S(1)} %broadcast_select_fusion.6.refs_1_), channel_id=1, source_target_pairs={{0,1},{1,0},{2,3},{3,2},{4,5},{5,4},{6,7},{7,6},{8,9},{9,8},{10,11... | collective-permute-start | bytes 786440 | tf_op jit(solution)/shard_map/ppermute | solution.py:50
  175.9 12.4 %collective-permute-start.44 = (bf16[1088,128]{1,0:T(8,128)(2,1)S(1)}, bf16[1088,128]{1,0:T(8,128)(2,1)S(1)}, u32[]{:S(2)}, u32[]{:S(2)}) collective-permute-start(bf16[1088,128]{1,0:T(8,128)(2,1)S(1)} %get-tuple-element.94), channel_id=1, source_target_pairs={{0,4},{12,8},{1,5},{13,9},{2,6},{14,10},{3,7},{15,11},{16,20},{28,... | collective-permute-start | bytes 835592 | tf_op jit(solution)/shard_map/ppermute | solution.py:75
  188.3 56.2 %collective-permute-start.64 = (bf16[128,1024]{1,0:T(8,128)(2,1)S(1)}, bf16[128,1024]{1,0:T(8,128)(2,1)S(1)}, u32[]{:S(2)}, u32[]{:S(2)}) collective-permute-start(bf16[128,1024]{1,0:T(8,128)(2,1)S(1)} %broadcast_select_fusion.5.refs_2_), channel_id=1, source_target_pairs={{0,1},{1,0},{2,3},{3,2},{4,5},{5,4},{6,7},{7,6},{8,9},{9,8},{10,11... | collective-permute-start | bytes 786440 | tf_op jit(solution)/shard_map/ppermute | solution.py:50
  212.2 22.7 %collective-permute-start.46 = (bf16[1088,128]{1,0:T(8,128)(2,1)S(1)}, bf16[1088,128]{1,0:T(8,128)(2,1)S(1)}, u32[]{:S(2)}, u32[]{:S(2)}) collective-permute-start(bf16[1088,128]{1,0:T(8,128)(2,1)S(1)} %add_convert_fusion.2), channel_id=1, source_target_pairs={{4,0},{8,12},{5,1},{9,13},{6,2},{10,14},{7,3},{11,15},{20,16},{24,... | collective-permute-start | bytes 835592 | tf_op jit(solution)/shard_map/ppermute | solution.py:80
  (61 other events, 550.2 us)

commit v4 on v2

--- a/solution.py
+++ b/solution.py
@@ -62,10 +62,13 @@
     return sum(t.astype(F32) for t in terms).astype(BF16)
 
 
-def ring_sum(parts):
+def ring_sum(parts, seen=None):
     total = parts[0]
     for part in parts[1:]:
-        total = add(ring_step(total), part)
+        total = ring_step(total)
+        if seen is not None:
+            seen.append(total)
+        total = add(total, part)
     return total
 
 
@@ -97,85 +100,77 @@
     return jax.ShapeDtypeStruct(tuple(dims), dtype)
 
 
-def halves_call(kernel, name, place, wide, narrow, adapter, adapter_rows):
-    rows, width = wide.shape
-    step = width // 8
-    per = width // 2 // step
-    rank = adapter.shape[1] if adapter_rows else adapter.shape[0]
-
-    def at(j, place):
-        return jnp.where(j < per, (1 - place[0]) * per + j, place[0] * per + j - per)
-
-    adapter_spec = (
-        pl.BlockSpec((step, rank), lambda j, place: (at(j, place), 0))
-        if adapter_rows
-        else pl.BlockSpec((rank, step), lambda j, place: (0, at(j, place)))
-    )
-    narrow_specs = [
-        pl.BlockSpec((rows, 1), lambda j, place: (0, 0))
-        if n.shape[0] == rows
-        else pl.BlockSpec((1, step), lambda j, place: (0, at(j, place)))
-        for n in narrow
-    ]
-    return pl.pallas_call(
-        kernel,
-        out_shape=(shape((rows, width // 2)), shape((rows, width // 2)), shape((rows, rank), F32)),
-        grid_spec=pltpu.PrefetchScalarGridSpec(
-            num_scalar_prefetch=1,
-            grid=(2 * per,),
-            in_specs=[pl.BlockSpec((rows, step), lambda j, place: (0, at(j, place)))]
-            + narrow_specs
-            + [adapter_spec],
-            out_specs=(
-                pl.BlockSpec((rows, step), lambda j, place: (0, jnp.minimum(j, per - 1))),
-                pl.BlockSpec((rows, step), lambda j, place: (0, jnp.maximum(j - per, 0))),
-                pl.BlockSpec((rows, rank), lambda j, place: (0, 0)),
-            ),
-        ),
-        compiler_params=pltpu.CompilerParams(vmem_limit_bytes=16 * MIB),
-        cost_estimate=pl.CostEstimate(
-            flops=2 * rows * width * rank, bytes_accessed=4 * wide.size, transcendentals=0
-        ),
-        name=name,
-    )(place, wide, *narrow, adapter)
-
-
-def store_half(value, send_ref, own_ref):
-    j = pl.program_id(0)
-    first = j < pl.num_programs(0) // 2
-
-    @pl.when(first)
-    def _():
-        send_ref[...] = value
-
-    @pl.when(jnp.logical_not(first))
-    def _():
-        own_ref[...] = value
-
-
-def accumulate(ref, term):
-    j = pl.program_id(0)
-
-    @pl.when(j == 0)
-    def _():
-        ref[...] = term
-
-    @pl.when(j > 0)
-    def _():
-        ref[...] += term
-
-
-def token_kernel(place, tokens, inv_rms, gain, adapter, send_ref, own_ref, low_ref):
-    value = tokens[...].astype(F32) * inv_rms[...] * gain[...].astype(F32)
-    value = value.astype(BF16)
-    store_half(value, send_ref, own_ref)
-    accumulate(low_ref, dot(value, adapter[...]))
-
-
-def cotangent_kernel(place, cotangent, weight, adapter, send_ref, own_ref, low_ref):
-    value = (cotangent[...].astype(F32) * weight[...]).astype(BF16)
-    store_half(value, send_ref, own_ref)
-    accumulate(low_ref, contract_dims(value, adapter[...], 1, 1))
+def scaled_halves(wide, low_ref, cols, scaled, product, send_ref, own_ref):
+    half = send_ref.shape[1]
+    step = half // 4
+    sub = lax.axis_index("sub")
+    low_ref[:, cols] = jnp.zeros((wide.shape[0], LANES), F32)
+    for which, out_ref in ((1 - sub, send_ref), (sub, own_ref)):
+
+        @pl.loop(0, half // step)
+        def _(j, which=which, out_ref=out_ref):
+            first = pl.multiple_of(which * half + j * step, step)
+            parts = []
+            for i in range(step // LANES):
+                tile = pl.ds(pl.multiple_of(first + i * LANES, LANES), LANES)
+                parts.append(scaled(wide[:, tile].astype(F32), tile).astype(BF16))
+            value = jnp.concatenate(parts, axis=1)
+            out_ref[:, pl.ds(pl.multiple_of(j * step, step), step)] = value
+            low_ref[:, cols] += product(value, pl.ds(first, step))
+
+
+def cotangent_kernel(
+    total, cotangent, tokens, lengths, slots, adapter, send_ref, own_ref, low_ref, square_ref
+):
+    rows, width = cotangent.shape
+    index = jnp.broadcast_to(slots[...], (LANES, rows))
+    weight = jnp.zeros((LANES, rows), F32)
+    for s in range(lengths.shape[1]):
+        length = jnp.full((LANES, rows), lengths[0, s], jnp.int32).astype(F32)
+        weight = weight + jnp.where(index == s, (rows // lengths.shape[1]) / length, 0.0)
+    row = (weight * F32(1.0 / math.sqrt(total))).T
+
+    square_ref[...] = jnp.zeros_like(square_ref)
+
+    @pl.loop(0, width // (8 * LANES))
+    def _(j):
+        squares = square_ref[...]
+        for i in range(8):
+            tile = pl.ds(pl.multiple_of((j * 8 + i) * LANES, LANES), LANES)
+            squares = squares + jnp.square(tokens[:, tile].astype(F32))
+        square_ref[...] = squares
+
+    square_ref[...] = jnp.broadcast_to(
+        jnp.sum(square_ref[...], axis=1, keepdims=True), square_ref.shape
+    )
+    scaled_halves(
+        cotangent,
+        low_ref,
+        slice(None),
+        lambda tile, cols: tile * row,
+        lambda value, cols: contract_dims(value, adapter[:, cols], 1, 1),
+        send_ref,
+        own_ref,
+    )
+
+
+def token_kernel(total_width, tokens, gain, adapter, low_out, squares, *refs):
+    squares_more, (send_ref, own_ref, low_ref) = refs[:-3], refs[-3:]
+    rank = adapter.shape[1]
+    total = squares[...]
+    for ref in squares_more:
+        total = total + ref[...]
+    row = lax.rsqrt(total / total_width + EPS)
+    low_ref[:, rank:] = low_out[...]
+    scaled_halves(
+        tokens,
+        low_ref,
+        slice(0, rank),
+        lambda tile, cols: tile * row * gain[:, cols].astype(F32),
+        lambda value, cols: dot(value, adapter[cols, :]),
+        send_ref,
+        own_ref,
+    )
 
 
 def transpose_kernel(own, got, out_ref):
@@ -185,22 +180,22 @@
 
 
 def widen(scale, wide):
-    table = scale[...].astype(F32)
-    for g in range(scale.shape[1]):
-        wide[g] = jnp.broadcast_to(table[:, g : g + 1], wide.shape[1:])
-
-
-def place_shards(codes, got, moved, store):
+    for g in range(scale.shape[0]):
+        row = scale[g : g + 1, :].astype(F32)
+        wide[g] = jnp.broadcast_to(row, (LANES, row.shape[1])).T
+
+
+def place_shards(codes, got, first_got, moved, store):
     n = lax.axis_size("dp")
     sub, grp, place = (lax.axis_index(a) for a in ("sub", "grp", "dp"))
     pos = ring_position()
-    blocks = got.shape[0]
+    blocks = codes.shape[0] // 2
     quarter = blocks // 2
 
     @pl.loop(0, blocks, unroll=4)
     def _(b):
         store(b, place * 2 + sub, codes[sub * blocks + b])
-        store(b, place * 2 + 1 - sub, got[b])
+        store(b, place * 2 + 1 - sub, got[first_got + b])
 
     for k in range(n - 1):
         there = ring_at(lax.rem(pos - k - 1 + n, n), n)
@@ -214,10 +209,10 @@
                 store(start + b, there * 2 + 1 - sub, piece[quarter + b])
 
 
-def front_kernel(own, got, scale, codes, codes_got, *refs):
+def front_kernel(first_got, own, got, scale, codes, codes_got, *refs):
     moved, (mine_ref, theirs_ref, wide, weight) = refs[:-4], refs[-4:]
-    blocks, rows, units = codes_got.shape
-    first = lax.axis_index("sub") * blocks
+    blocks, rows, units = codes.shape
+    first = lax.axis_index("sub") * (blocks // 2)
     widen(scale, wide)
 
     def store(b, shard, piece):
@@ -227,16 +222,16 @@
             factor = wide[g * wide.shape[0] * LANES // units, pl.ds(first + b, 1), :]
             weight[b, at, cols] = (piece[:, cols].astype(F32) * factor).astype(BF16)
 
-    place_shards(codes, codes_got, moved, store)
+    place_shards(codes, codes_got, first_got, moved, store)
     matrix = weight[...].reshape(-1, units)
     mine_ref[...] = dot(own[...], matrix)
     theirs_ref[...] = dot(got[...], matrix).astype(BF16)
 
 
-def back_kernel(own, got, scale, codes, codes_got, *refs):
+def back_kernel(first_got, own, got, scale, codes, codes_got, *refs):
     moved, (mine_ref, theirs_ref, wide, weight) = refs[:-4], refs[-4:]
-    blocks, rows, block = codes_got.shape
-    first = lax.axis_index("sub") * blocks
+    blocks, rows, block = codes.shape
+    first = lax.axis_index("sub") * (blocks // 2)
     per_group = weight.shape[0] // wide.shape[0]
     widen(scale, wide)
 
@@ -246,7 +241,7 @@
         cols = pl.ds(pl.multiple_of(b * block, block), block)
         weight[pl.ds(at, rows), cols] = (piece.astype(F32) * factor).astype(BF16)
 
-    place_shards(codes, codes_got, moved, store)
+    place_shards(codes, codes_got, first_got, moved, store)
     matrix = weight[...]
     mine_ref[...] = contract_dims(own[...], matrix, 1, 1)
     theirs_ref[...] = contract_dims(got[...], matrix, 1, 1).astype(BF16)
@@ -272,38 +267,51 @@
             ref[...] = lax.slice_in_dim(full, i * size, (i + 1) * size, axis=axis).astype(BF16)
 
 
-def hidden_kernel(more, gate, up, low_up, low_out, up_out, down_in, *refs):
-    gate_more, up_more = refs[:more], refs[more : 2 * more]
-    up_out_more, down_in_more = refs[2 * more : 3 * more], refs[3 * more : 4 * more]
+def low_sums(low, low_more):
+    total = low[...]
+    for ref in low_more:
+        total = total + ref[...]
+    half = total.shape[1] // 2
+    return total[:, :half].astype(BF16), total[:, half:].astype(BF16)
+
+
+def gather_adapters(adapters, adapters_more, up_out_all, down_in_all):
+    rank = up_out_all.shape[0]
+    place_own(up_out_all, adapters.at[:rank], [r.at[:rank] for r in adapters_more], 1)
+    place_own(down_in_all, adapters.at[rank:], [r.at[rank:] for r in adapters_more], 0)
+
+
+def hidden_kernel(more, gate, up, low, adapters, *refs):
+    gate_more, up_more, low_more, adapters_more = (refs[i * more : (i + 1) * more] for i in range(4))
     silu_ref, low_ref, down_in_term, up_out_all, down_in_all = refs[4 * more :]
-    place_own(up_out_all, up_out, up_out_more, 1)
-    place_own(down_in_all, down_in, down_in_more, 0)
+    gather_adapters(adapters, adapters_more, up_out_all, down_in_all)
+    low_up, low_out = low_sums(low, low_more)
     gate_sum, up_sum = gate[...], up[...]
     for ref in gate_more:
         gate_sum = gate_sum + ref[...].astype(F32)
     for ref in up_more:
         up_sum = up_sum + ref[...].astype(F32)
-    up_sum = up_sum + ADAPTER_SCALE * dot(low_up[...], up_out_all[...])
+    up_sum = up_sum + ADAPTER_SCALE * dot(low_up, up_out_all[...])
     silu = gate_sum * jax.nn.sigmoid(gate_sum)
     silu_ref[...] = silu
     hidden = (silu * up_sum).astype(BF16)
     low_ref[...] = (ADAPTER_SCALE * dot(hidden, down_in_all[...])).astype(BF16)
     hidden_t = hidden.astype(F32).T.astype(BF16)
-    own_units(ADAPTER_SCALE * dot(hidden_t, low_out[...]), down_in_term, 0)
-
-
-def up_grad_kernel(more, back, silu, low_up, low_out, up_out, down_in, *refs):
-    back_more, up_out_more, down_in_more = (refs[i * more : (i + 1) * more] for i in range(3))
+    own_units(ADAPTER_SCALE * dot(hidden_t, low_out), down_in_term, 0)
+
+
+def up_grad_kernel(more, back, silu, low, adapters, *refs):
+    back_more, low_more, adapters_more = (refs[i * more : (i + 1) * more] for i in range(3))
     low_ref, up_out_term, up_out_all, down_in_all = refs[3 * more :]
-    place_own(up_out_all, up_out, up_out_more, 1)
-    place_own(down_in_all, down_in, down_in_more, 0)
+    gather_adapters(adapters, adapters_more, up_out_all, down_in_all)
+    low_up, low_out = low_sums(low, low_more)
     total = back[...]
     for ref in back_more:
         total = total + ref[...].astype(F32)
-    total = total + ADAPTER_SCALE * contract_dims(low_out[...], down_in_all[...], 1, 1)
+    total = total + ADAPTER_SCALE * contract_dims(low_out, down_in_all[...], 1, 1)
     up_grad = (total * silu[...]).astype(BF16)
     low_ref[...] = (ADAPTER_SCALE * contract_dims(up_grad, up_out_all[...], 1, 1)).astype(BF16)
-    low_up_t = low_up[...].astype(F32).T.astype(BF16)
+    low_up_t = low_up.astype(F32).T.astype(BF16)
     own_units(ADAPTER_SCALE * dot(low_up_t, up_grad), up_out_term, 1)
 
 
@@ -389,35 +397,65 @@
     down_in_ref[...] = total[rows:]
 
 
-def token_weights(sequence_length_list, slot_sequence_index, rows):
-    seq_count = sequence_length_list.shape[1]
-    longest = rows // seq_count
-    total = rows * lax.axis_size("dp") * lax.axis_size("sub")
-    ratios = longest / sequence_length_list[0].astype(F32)
-    match = slot_sequence_index[:, None] == jnp.arange(seq_count, dtype=jnp.int32)[None, :]
-    weight = jnp.sum(jnp.where(match, ratios[None, :], F32(0.0)), axis=-1)
-    return weight * F32(1.0 / math.sqrt(total))
-
-
-class Shards:
-    def __init__(self, codes):
-        sub, grp = lax.axis_index("sub"), lax.axis_index("grp")
-        half = codes.shape[0] // 2
-        quarter = half // 2
-        self.codes = codes
-        self.got = swap(lax.dynamic_slice_in_dim(codes, (1 - sub) * half, half, 0), "sub")
-        own = lax.dynamic_slice_in_dim(codes, sub * half + grp * quarter, quarter, 0)
-        got = lax.dynamic_slice_in_dim(self.got, grp * quarter, quarter, 0)
-        self.moving = jnp.concatenate([own, got], axis=0)
-        self.moved = []
-
-    def step(self, *done):
-        self.moving = ring_step(after(self.moving, *done) if done else self.moving)
-        self.moved += [self.moving, swap(self.moving, "grp")]
-        return self.moving
-
-    def args(self):
-        return [self.codes, self.got, *self.moved]
+def half_kernel(*refs):
+    sources, out_ref, sems = refs[:-2], refs[-2], refs[-1]
+    other = 1 - lax.axis_index("sub")
+    half = sources[0].shape[0] // 2
+    copy_all(
+        [
+            pltpu.make_async_copy(
+                ref.at[pl.ds(other * half, half)], out_ref.at[pl.ds(i * half, half)], sems.at[i]
+            )
+            for i, ref in enumerate(sources)
+        ]
+    )
+
+
+def quarter_kernel(*refs):
+    count = (len(refs) - 2) // 2
+    sources, got, out_refs, sems = refs[:count], refs[count], refs[count + 1 : -1], refs[-1]
+    sub, grp = lax.axis_index("sub"), lax.axis_index("grp")
+    half = sources[0].shape[0] // 2
+    quarter = half // 2
+    copies = []
+    for i, (ref, out_ref) in enumerate(zip(sources, out_refs)):
+        own = ref.at[pl.ds(sub * half + grp * quarter, quarter)]
+        theirs = got.at[pl.ds(i * half + grp * quarter, quarter)]
+        for k, source in enumerate((own, theirs)):
+            copies.append(
+                pltpu.make_async_copy(
+                    source, out_ref.at[pl.ds(k * quarter, quarter)], sems.at[2 * i + k]
+                )
+            )
+    copy_all(copies)
+
+
+def start_shards(codes):
+    blocks, rows, units = codes[0].shape
+    count = len(codes)
+    anywhere = pl.BlockSpec(memory_space=pl.ANY)
+    (send,) = call(
+        half_kernel,
+        "halves",
+        codes,
+        [shape((count * blocks // 2, rows, units))],
+        scratch=[pltpu.SemaphoreType.DMA((count,))],
+        specs=[anywhere] * count,
+        out_specs=(anywhere,),
+        limit=4,
+    )
+    got = swap(send, "sub")
+    moving = call(
+        quarter_kernel,
+        "quarters",
+        [*codes, got],
+        [shape((blocks // 2, rows, units))] * count,
+        scratch=[pltpu.SemaphoreType.DMA((2 * count,))],
+        specs=[anywhere] * (count + 1),
+        out_specs=(anywhere,) * count,
+        limit=4,
+    )
+    return list(moving), got
 
 
 def fast_body(
@@ -445,66 +483,89 @@
     total_width = local_width * lax.axis_size("mp")
     n = lax.axis_size("dp")
     more = lax.axis_size("mp") - 1
-    place = lax.axis_index("sub").astype(jnp.int32).reshape(1)
-
-    gate_shards = Shards(gate_codes)
-    up_shards = Shards(up_codes)
-    down_shards = Shards(jnp.swapaxes(down_codes, 0, 1))
-    order = [gate_shards, up_shards] * 2 + [down_shards, gate_shards, up_shards]
-    if n != 4:
-        order = [gate_shards, up_shards] * (n - 1)
-    order += [down_shards] * (n - 1 - order.count(down_shards))
-    arrived = []
-    for shards in order:
-        arrived.append(shards.step(*arrived[-2:-1]))
-
-    weight = token_weights(sequence_length_list, slot_sequence_index, rows)
-    grad_send, grad, low_out = halves_call(
-        cotangent_kernel, "cotangent", place, cotangent, [weight[:, None]], down_adapter_out, False
-    )
+
+    (gate_moving, up_moving), front_got = start_shards([gate_codes, up_codes])
+    ring, crossed = [], []
+
+    def step(moving, *done):
+        k = len(ring)
+        waits = ring[k - 2 : k - 1] if k > 1 else []
+        waits += ring[k - 3 : k - 2] if k > 2 else []
+        waits += crossed[k - 4 : k - 3] if k > 3 else []
+        ring.append(ring_step(after(moving, *waits, *done) if waits else moving))
+        crossed.append(swap(ring[-1], "grp"))
+        return ring[-1]
+
+    step(gate_moving)
+    step(up_moving)
+
+    adapters = jnp.concatenate([up_adapter_out, down_adapter_in], axis=0)
+    adapters_more = others(after(adapters, ring[1]), "mp")
+    tokens_then, cotangent_then, down_then, _ = lax.optimization_barrier(
+        (tokens, cotangent, down_codes, ring[1])
+    )
+    vmem = pl.BlockSpec(memory_space=pltpu.VMEM)
+    smem = pl.BlockSpec(memory_space=pltpu.SMEM)
+    grad_send, grad, low_out, squares = call(
+        lambda *refs: cotangent_kernel(rows * n * lax.axis_size("sub"), *refs),
+        "cotangent",
+        [cotangent_then, tokens_then, sequence_length_list, slot_sequence_index[None, :], down_adapter_out],
+        [shape((rows, half))] * 2 + [shape((rows, rank), F32), shape((rows, LANES), F32)],
+        specs=[vmem, vmem, smem, vmem, vmem],
+        flops=2 * rows * local_width * rank,
+    )
+    step(ring[0])
+    squares_more = others(squares, "mp")
+    down_turned = jnp.swapaxes(down_then, 0, 1)
+    (down_moving,), down_got = start_shards([down_turned])
+    step(ring[1])
     grad_got = swap(grad_send, "sub")
-    own_squares = jnp.sum(jnp.square(tokens.astype(F32)), axis=-1)
-    squares = sum(others(own_squares, "mp"), own_squares) / total_width
-    inv_rms = lax.rsqrt(squares + EPS)[:, None]
-    normed_send, normed, low_up = halves_call(
-        token_kernel, "tokens", place, tokens, [inv_rms, rms_norm_gain[None, :]], up_adapter_in, True
+    step(ring[2], grad, down_moving)
+    step(ring[3])
+    normed_send, normed, low = call(
+        lambda *refs: token_kernel(total_width, *refs),
+        "tokens",
+        [after(tokens, ring[3]), rms_norm_gain[None, :], up_adapter_in, low_out, squares, *squares_more],
+        [shape((rows, half))] * 2 + [shape((rows, 2 * rank), F32)],
+        flops=2 * rows * local_width * rank,
     )
     normed_got = swap(normed_send, "sub")
-    low_up = sum(others(low_up, "mp"), low_up).astype(BF16)
-    low_out = sum(others(low_out, "mp"), low_out).astype(BF16)
-    up_out_more = others(up_adapter_out, "mp")
-    down_in_more = others(down_adapter_in, "mp")
-    (normed_t,) = call(
-        transpose_kernel, "transpose", [normed, normed_got], [shape((half, 2 * rows))], limit=32
-    )
-
-    def product(kernel, name, own, got, scale, shards, weight_shape):
-        groups = scale.shape[1]
+    low_more = others(low, "mp")
+    step(down_moving, normed)
+    step(ring[6], grad_got, *adapters_more)
+
+    def product(kernel, name, own, got, scale, codes, codes_got, first_got, steps, weight_shape):
+        groups = scale.shape[0]
         mine, theirs = call(
-            kernel,
+            lambda *refs: kernel(first_got, *refs),
             name,
-            [own, got, scale, *shards.args()],
+            [own, got, scale, codes, codes_got, *[x for k in steps for x in (ring[k], crossed[k])]],
             [shape((rows, units), F32), shape((rows, units))],
             scratch=[pltpu.VMEM((groups, blocks, LANES), F32), pltpu.VMEM(weight_shape, BF16)],
             flops=4 * rows * half * units,
         )
-        mine = mine + swap(theirs, "sub").astype(F32)
-        return mine, others(mine.astype(BF16), "mp")
+        total = mine + swap(theirs, "sub").astype(F32)
+        return total, others(total.astype(BF16), "mp"), mine
 
     front = (blocks // 2, block, units)
-    gate, gate_more = product(
-        front_kernel, "gate", normed, normed_got, gate_block_scale, gate_shards, front
-    )
-    up, up_more = product(front_kernel, "up", normed, normed_got, up_block_scale, up_shards, front)
+    half_blocks = blocks // 2
+    gate, gate_more, gate_mine = product(
+        front_kernel, "gate", normed, normed_got, gate_block_scale.T, gate_codes, front_got, 0,
+        range(0, 2 * (n - 1), 2), front,
+    )
+    up, up_more, up_mine = product(
+        front_kernel, "up", normed, normed_got, up_block_scale.T, up_codes, front_got, half_blocks,
+        range(1, 2 * (n - 1), 2), front,
+    )
+    step(ring[7], gate_mine, up_mine)
     small_scratch = [
         pltpu.VMEM((rank, units), BF16),
         pltpu.VMEM((units, rank), BF16),
     ]
-    adapters = [low_up, low_out, up_adapter_out, down_adapter_in]
     silu, low_hidden, down_in_term = call(
         lambda *refs: hidden_kernel(more, *refs),
         "hidden",
-        [gate, up, *adapters, *gate_more, *up_more, *up_out_more, *down_in_more],
+        [gate, up, low, adapters, *gate_more, *up_more, *low_more, *adapters_more],
         [shape((rows, units), F32), shape((rows, rank)), shape(down_adapter_in.shape)],
         scratch=small_scratch,
         limit=8,
@@ -516,15 +577,24 @@
         [shape((rank, half // n))] * n,
         flops=4 * rows * half * rank,
     )
-    down_out_blocks = ring_gather(ring_sum(down_out_parts))
-
-    back, back_more = product(
-        back_kernel, "back", grad, grad_got, down_block_scale.T, down_shards, (units, half)
+    seen = []
+    down_out_blocks = ring_gather(ring_sum(down_out_parts, seen))
+    (normed_t,) = call(
+        transpose_kernel,
+        "transpose",
+        [normed, after(normed_got, low_hidden)],
+        [shape((half, 2 * rows))],
+        limit=32,
+    )
+
+    back, back_more, _ = product(
+        back_kernel, "back", after(grad, down_out_parts[0]), grad_got, down_block_scale, down_turned, down_got, 0,
+        range(2 * (n - 1), 3 * (n - 1)), (units, half),
     )
     low_grad, up_out_term = call(
         lambda *refs: up_grad_kernel(more, *refs),
         "up_grad",
-        [back, silu, *adapters, *back_more, *up_out_more, *down_in_more],
+        [after(back, seen[0]), silu, low, adapters, *back_more, *low_more, *adapters_more],
         [shape((rows, rank)), shape(up_adapter_out.shape)],
         scratch=small_scratch,
         limit=8,
@@ -540,7 +610,6 @@
     up_in_blocks = ring_gather(ring_sum(up_in_parts))
 
     anywhere = pl.BlockSpec(memory_space=pl.ANY)
-    vmem = pl.BlockSpec(memory_space=pltpu.VMEM)
     (down_out_gradient,) = call(
         lambda *refs: down_out_place_kernel(n, *refs),
         "down_out_place",

time: 241 us -> 200 us (0.83)
  local copies, waits for them, and re-layouts: 23.7 us -> 6.89 us
  Pallas kernels: 35.8 us -> 23.7 us
  starting transfers between devices: 52.5 us -> 42.2 us
  other arithmetic: 6.08 us -> 0.53 us
  waiting for transfers between devices: 121 us -> 125 us
    unnamed x92 -> x37, local copies, waits for them, and re-layouts: 19 us -> 6.52 us
    pallas_call x2 -> x0, Pallas kernels: 12 us -> none  [halves_call(): pl.pallas_call(kernel, out_shape=(shape((rows, width // 2)), shape((rows,...]
    ppermute x21, starting transfers between devices: 26.8 us -> 20.6 us  [ring_step(): lax.ppermute(x, 'dp', [(ring_at(i, n), ring_at((i + 1) % n, n)) for i in...]
    ppermute x21, waiting for transfers between devices: 90.7 us -> 95.1 us  [ring_step(): lax.ppermute(x, 'dp', [(ring_at(i, n), ring_at((i + 1) % n, n)) for i in...]
    reduce_sum x2 -> x0, other arithmetic: 3.87 us -> none  [the longest x1 3.1 us: fast_body(): own_squares = jnp.sum(jnp.square(tokens.astype(F32)), axis=-1)]
    dynamic_slice x9 -> x0, local copies, waits for them, and re-layouts: 3.78 us -> none  [the longest x3 1.52 us: __init__(): lax.dynamic_slice_in_dim(codes, (1 - sub) * half, half, 0)]
    ppermute x8 -> x6, starting transfers between devices: 10.2 us -> 7.28 us  [others(): lax.ppermute(x, axis, [(i, (i + k) % n) for i in range(n)])]
    ppermute x27 -> x26, waiting for transfers between devices: 22.1 us -> 19.9 us  [swap(): return lax.ppermute(x, axis, [(0, 1), (1, 0)])]
  transfers between devices with their start and end apart: 56 -> 53, of which waited for: 30 -> 31; matrix products, arithmetic and copies ran while one was open for 5% -> 0% of each run, Pallas kernels for 10% -> 8%
where the time goes in v4:
time: 200 us; the launch traced here: 199 us
  waiting for transfers between devices  125 us (62%)
  starting transfers between devices  42.2 us (21%)
  Pallas kernels  23.7 us (12%)
  local copies, waits for them, and re-layouts  6.89 us (3%)
    ppermute x21, waiting for transfers between devices, ring_step(): lax.ppermute(x, 'dp', [(ring_at(i, n), ring_at((i + 1) % n, n)) for i in...  95.1 us
    pallas_call x16, Pallas kernels, call(): pl.pallas_call(kernel, out_shape=tuple(out_shape), in_specs=specs or [vme...  23.7 us
    ppermute x21, starting transfers between devices, ring_step(): lax.ppermute(x, 'dp', [(ring_at(i, n), ring_at((i + 1) % n, n)) for i in...  20.6 us
    ppermute x26, waiting for transfers between devices, swap(): return lax.ppermute(x, axis, [(0, 1), (1, 0)])  19.9 us
    ppermute x26, starting transfers between devices, swap(): return lax.ppermute(x, axis, [(0, 1), (1, 0)])  14.4 us
    ppermute x6, waiting for transfers between devices, others(): lax.ppermute(x, axis, [(i, (i + k) % n) for i in range(n)])  9.64 us
    ppermute x6, starting transfers between devices, others(): lax.ppermute(x, axis, [(i, (i + k) % n) for i in range(n)])  7.28 us
    unnamed x37, local copies, waits for them, and re-layouts  6.52 us
  transfers between devices with their start and end apart: 53, of which 31 were waited for; matrix products, arithmetic and copies ran while one was open for 0% of the time, Pallas kernels for 8%

profile of v4, /device:TPU:0, one launch (start us, length us, event | category | flops | bytes accessed | tf_op | source)
XLA Modules:
  0.0 199.3 jit_solution(11677721267046147304)
XLA Ops:
  5.5 3.0 %collective-permute-start.1 = (bf16[32,16,256]{2,1,0:T(8,128)(2,1)S(1)}, bf16[32,16,256]{2,1,0:T(8,128)(2,1)S(1)}, u32[]{:S(2)}, u32[]{:S(2)}) collective-permute-start(bf16[32,16,256]{2,1,0:T(8,128)(2,1)S(1)} %get-tuple-element.50), channel_id=1, source_target_pairs={{0,4},{4,12},{12,8},{8,0},{1,5},{5,13},{13,9},{9,1},{2,6},{6,14},{... | collective-permute-start | bytes 786440 | tf_op jit(solution)/shard_map/ppermute | solution.py:45
  11.1 5.5 %collective-permute-done.1.refs_5_ = bf16[32,16,256]{2,1,0:T(8,128)(2,1)S(1)} collective-permute-done((bf16[32,16,256]{2,1,0:T(8,128)(2,1)S(1)}, bf16[32,16,256]{2,1,0:T(8,128)(2,1)S(1)}, u32[]{:S(2)}, u32[]{:S(2)}) %collective-permute-start.1) | collective-permute-done | bytes 262176 | tf_op jit(solution)/shard_map/ppermute | solution.py:45
  16.6 5.1 %collective-permute-done.2.refs_5_ = bf16[32,16,256]{2,1,0:T(8,128)(2,1)S(1)} collective-permute-done((bf16[32,16,256]{2,1,0:T(8,128)(2,1)S(1)}, bf16[32,16,256]{2,1,0:T(8,128)(2,1)S(1)}, u32[]{:S(2)}, u32[]{:S(2)}) %collective-permute-start.2) | collective-permute-done | bytes 262176 | tf_op jit(solution)/shard_map/ppermute | solution.py:45
  27.0 4.9 %cotangent.1 = (bf16[256,4096]{1,0:T(8,128)(2,1)S(1)}, bf16[256,4096]{1,0:T(8,128)(2,1)S(1)}, f32[256,128]{1,0:T(8,128)S(1)}, f32[256,128]{1,0:T(8,128)S(1)}) custom-call(bf16[256,8192]{1,0:T(8,128)(2,1)S(1)} %copy-done.6, bf16[256,8192]{1,0:T(8,128)(2,1)S(1)} %copy-done, s32[1,2]{1,0:T(1,128)S(1)} %copy-done.10, s32[1,256]{1,0:T(1,128)S(1)} %bitcast.9, ...), custom_call_target="tpu_custom_call" | custom-call | flops 536870912 | bytes 14943240 | tf_op jit(solution)/shard_map/cotangent/pallas_call | solution.py:87
  33.6 3.4 %collective-permute-done.4.refs_5_ = f32[256,128]{1,0:T(8,128)S(1)} collective-permute-done((f32[256,128]{1,0:T(8,128)S(1)}, f32[256,128]{1,0:T(8,128)S(1)}, u32[]{:S(2)}, u32[]{:S(2)}) %collective-permute-start.4) | collective-permute-done | bytes 131104 | tf_op jit(solution)/shard_map/ppermute | solution.py:54
  39.6 3.4 %collective-permute-start.7 = (bf16[32,16,256]{2,1,0:T(8,128)(2,1)S(1)}, bf16[32,16,256]{2,1,0:T(8,128)(2,1)S(1)}, u32[]{:S(2)}, u32[]{:S(2)}) collective-permute-start(bf16[32,16,256]{2,1,0:T(8,128)(2,1)S(1)} %collective-permute-done.2.refs_5_), channel_id=1, source_target_pairs={{0,4},{4,12},{12,8},{8,0},{1,5},{5,13},{13,9},{9,1},{2,6},{6,14},{... | collective-permute-start | bytes 786440 | tf_op jit(solution)/shard_map/ppermute | solution.py:45
  45.1 4.0 %collective-permute-done.7.refs_7_ = bf16[32,16,256]{2,1,0:T(8,128)(2,1)S(1)} collective-permute-done((bf16[32,16,256]{2,1,0:T(8,128)(2,1)S(1)}, bf16[32,16,256]{2,1,0:T(8,128)(2,1)S(1)}, u32[]{:S(2)}, u32[]{:S(2)}) %collective-permute-start.7) | collective-permute-done | bytes 262176 | tf_op jit(solution)/shard_map/ppermute | solution.py:45
  54.1 4.3 %collective-permute-done.13.refs_6_ = bf16[32,16,256]{2,1,0:T(8,128)(2,1)S(1)} collective-permute-done((bf16[32,16,256]{2,1,0:T(8,128)(2,1)S(1)}, bf16[32,16,256]{2,1,0:T(8,128)(2,1)S(1)}, u32[]{:S(2)}, u32[]{:S(2)}) %collective-permute-start.13) | collective-permute-done | bytes 262176 | tf_op jit(solution)/shard_map/ppermute | solution.py:49
  59.9 4.1 %collective-permute-done.8.refs_8_ = bf16[32,16,256]{2,1,0:T(8,128)(2,1)S(1)} collective-permute-done((bf16[32,16,256]{2,1,0:T(8,128)(2,1)S(1)}, bf16[32,16,256]{2,1,0:T(8,128)(2,1)S(1)}, u32[]{:S(2)}, u32[]{:S(2)}) %collective-permute-start.8) | collective-permute-done | bytes 262176 | tf_op jit(solution)/shard_map/ppermute | solution.py:49
  75.0 3.1 %collective-permute-done.24.refs_5_ = bf16[32,32,128]{2,1,0:T(8,128)(2,1)S(1)} collective-permute-done((bf16[32,32,128]{2,1,0:T(8,128)(2,1)S(1)}, bf16[32,32,128]{2,1,0:T(8,128)(2,1)S(1)}, u32[]{:S(2)}, u32[]{:S(2)}) %collective-permute-start.24) | collective-permute-done | bytes 262176 | tf_op jit(solution)/shard_map/ppermute | solution.py:45
  90.3 3.0 %collective-permute-done.28.refs_9_ = bf16[32,32,128]{2,1,0:T(8,128)(2,1)S(1)} collective-permute-done((bf16[32,32,128]{2,1,0:T(8,128)(2,1)S(1)}, bf16[32,32,128]{2,1,0:T(8,128)(2,1)S(1)}, u32[]{:S(2)}, u32[]{:S(2)}) %collective-permute-start.28) | collective-permute-done | bytes 262176 | tf_op jit(solution)/shard_map/ppermute | solution.py:45
  96.4 3.5 %collective-permute-done.19.refs_5_ = bf16[256,256]{1,0:T(8,128)(2,1)S(1)} collective-permute-done((bf16[256,256]{1,0:T(8,128)(2,1)S(1)}, bf16[256,256]{1,0:T(8,128)(2,1)S(1)}, u32[]{:S(2)}, u32[]{:S(2)}) %collective-permute-start.19) | collective-permute-done | bytes 131104 | tf_op jit(solution)/shard_map/ppermute | solution.py:54
  102.4 3.1 %collective-permute-done.29.refs_10_ = bf16[32,32,128]{2,1,0:T(8,128)(2,1)S(1)} collective-permute-done((bf16[32,32,128]{2,1,0:T(8,128)(2,1)S(1)}, bf16[32,32,128]{2,1,0:T(8,128)(2,1)S(1)}, u32[]{:S(2)}, u32[]{:S(2)}) %collective-permute-start.29) | collective-permute-done | bytes 262176 | tf_op jit(solution)/shard_map/ppermute | solution.py:49
  110.1 7.3 %collective-permute-done.31 = bf16[128,1024]{1,0:T(8,128)(2,1)S(1)} collective-permute-done((bf16[128,1024]{1,0:T(8,128)(2,1)S(1)}, bf16[128,1024]{1,0:T(8,128)(2,1)S(1)}, u32[]{:S(2)}, u32[]{:S(2)}) %collective-permute-start.31) | collective-permute-done | bytes 262176 | tf_op jit(solution)/shard_map/ppermute | solution.py:45
  122.8 9.2 %collective-permute-done.34 = bf16[1088,128]{1,0:T(8,128)(2,1)S(1)} collective-permute-done((bf16[1088,128]{1,0:T(8,128)(2,1)S(1)}, bf16[1088,128]{1,0:T(8,128)(2,1)S(1)}, u32[]{:S(2)}, u32[]{:S(2)}) %collective-permute-start.34) | collective-permute-done | bytes 278560 | tf_op jit(solution)/shard_map/ppermute | solution.py:45
  134.8 7.8 %collective-permute-done.35 = bf16[1088,128]{1,0:T(8,128)(2,1)S(1)} collective-permute-done((bf16[1088,128]{1,0:T(8,128)(2,1)S(1)}, bf16[1088,128]{1,0:T(8,128)(2,1)S(1)}, u32[]{:S(2)}, u32[]{:S(2)}) %collective-permute-start.35) | collective-permute-done | bytes 278560 | tf_op jit(solution)/shard_map/ppermute | solution.py:45
  142.8 5.5 %collective-permute-done.44 = bf16[128,1024]{1,0:T(8,128)(2,1)S(1)} collective-permute-done((bf16[128,1024]{1,0:T(8,128)(2,1)S(1)}, bf16[128,1024]{1,0:T(8,128)(2,1)S(1)}, u32[]{:S(2)}, u32[]{:S(2)}) %collective-permute-start.44) | collective-permute-done | bytes 262176 | tf_op jit(solution)/shard_map/ppermute | solution.py:45
  148.4 5.8 %collective-permute-done.36 = bf16[1088,128]{1,0:T(8,128)(2,1)S(1)} collective-permute-done((bf16[1088,128]{1,0:T(8,128)(2,1)S(1)}, bf16[1088,128]{1,0:T(8,128)(2,1)S(1)}, u32[]{:S(2)}, u32[]{:S(2)}) %collective-permute-start.36) | collective-permute-done | bytes 278560 | tf_op jit(solution)/shard_map/ppermute | solution.py:45
  154.4 5.5 %collective-permute-done.45 = bf16[128,1024]{1,0:T(8,128)(2,1)S(1)} collective-permute-done((bf16[128,1024]{1,0:T(8,128)(2,1)S(1)}, bf16[128,1024]{1,0:T(8,128)(2,1)S(1)}, u32[]{:S(2)}, u32[]{:S(2)}) %collective-permute-start.45) | collective-permute-done | bytes 262176 | tf_op jit(solution)/shard_map/ppermute | solution.py:45
  160.0 5.8 %collective-permute-done.37.refs_1_ = bf16[1088,128]{1,0:T(8,128)(2,1)S(1)} collective-permute-done((bf16[1088,128]{1,0:T(8,128)(2,1)S(1)}, bf16[1088,128]{1,0:T(8,128)(2,1)S(1)}, u32[]{:S(2)}, u32[]{:S(2)}) %collective-permute-start.37) | collective-permute-done | bytes 278560 | tf_op jit(solution)/shard_map/ppermute | solution.py:45
  165.8 5.6 %collective-permute-done.46.refs_1_ = bf16[128,1024]{1,0:T(8,128)(2,1)S(1)} collective-permute-done((bf16[128,1024]{1,0:T(8,128)(2,1)S(1)}, bf16[128,1024]{1,0:T(8,128)(2,1)S(1)}, u32[]{:S(2)}, u32[]{:S(2)}) %collective-permute-start.46) | collective-permute-done | bytes 262176 | tf_op jit(solution)/shard_map/ppermute | solution.py:45
  171.4 6.0 %collective-permute-done.38.refs_2_ = bf16[1088,128]{1,0:T(8,128)(2,1)S(1)} collective-permute-done((bf16[1088,128]{1,0:T(8,128)(2,1)S(1)}, bf16[1088,128]{1,0:T(8,128)(2,1)S(1)}, u32[]{:S(2)}, u32[]{:S(2)}) %collective-permute-start.38) | collective-permute-done | bytes 278560 | tf_op jit(solution)/shard_map/ppermute | solution.py:45
  177.9 5.1 %collective-permute-done.47.refs_2_ = bf16[128,1024]{1,0:T(8,128)(2,1)S(1)} collective-permute-done((bf16[128,1024]{1,0:T(8,128)(2,1)S(1)}, bf16[128,1024]{1,0:T(8,128)(2,1)S(1)}, u32[]{:S(2)}, u32[]{:S(2)}) %collective-permute-start.47) | collective-permute-done | bytes 262176 | tf_op jit(solution)/shard_map/ppermute | solution.py:45
  183.6 9.6 %collective-permute-done.48.refs_3_ = bf16[128,1024]{1,0:T(8,128)(2,1)S(1)} collective-permute-done((bf16[128,1024]{1,0:T(8,128)(2,1)S(1)}, bf16[128,1024]{1,0:T(8,128)(2,1)S(1)}, u32[]{:S(2)}, u32[]{:S(2)}) %collective-permute-start.48) | collective-permute-done | bytes 262176 | tf_op jit(solution)/shard_map/ppermute | solution.py:45
  (147 shorter events, 74.4 us)
Async XLA Ops:
  5.5 11.1 %collective-permute-start.1 = (bf16[32,16,256]{2,1,0:T(8,128)(2,1)S(1)}, bf16[32,16,256]{2,1,0:T(8,128)(2,1)S(1)}, u32[]{:S(2)}, u32[]{:S(2)}) collective-permute-start(bf16[32,16,256]{2,1,0:T(8,128)(2,1)S(1)} %get-tuple-element.50), channel_id=1, source_target_pairs={{0,4},{4,12},{12,8},{8,0},{1,5},{5,13},{13,9},{9,1},{2,6},{6,14},{... | collective-permute-start | bytes 786440 | tf_op jit(solution)/shard_map/ppermute | solution.py:45
  8.5 13.2 %collective-permute-start.2 = (bf16[32,16,256]{2,1,0:T(8,128)(2,1)S(1)}, bf16[32,16,256]{2,1,0:T(8,128)(2,1)S(1)}, u32[]{:S(2)}, u32[]{:S(2)}) collective-permute-start(bf16[32,16,256]{2,1,0:T(8,128)(2,1)S(1)} %get-tuple-element.54), channel_id=1, source_target_pairs={{0,4},{4,12},{12,8},{8,0},{1,5},{5,13},{13,9},{9,1},{2,6},{6,14},{... | collective-permute-start | bytes 786440 | tf_op jit(solution)/shard_map/ppermute | solution.py:45
  21.8 11.8 %collective-permute-start.3 = (bf16[32,16,256]{2,1,0:T(8,128)(2,1)S(1)}, bf16[32,16,256]{2,1,0:T(8,128)(2,1)S(1)}, u32[]{:S(2)}, u32[]{:S(2)}) collective-permute-start(bf16[32,16,256]{2,1,0:T(8,128)(2,1)S(1)} %collective-permute-done.1.refs_5_), channel_id=1, source_target_pairs={{0,4},{4,12},{12,8},{8,0},{1,5},{5,13},{13,9},{9,1},{2,6},{6,14},{... | collective-permute-start | bytes 786440 | tf_op jit(solution)/shard_map/ppermute | solution.py:45
  33.5 44.6 %collective-permute-start.23 = (bf16[256,4096]{1,0:T(8,128)(2,1)S(1)}, bf16[256,4096]{1,0:T(8,128)(2,1)S(1)}, u32[]{:S(2)}, u32[]{:S(2)}) collective-permute-start(bf16[256,4096]{1,0:T(8,128)(2,1)S(1)} %get-tuple-element.72), channel_id=1, source_target_pairs={{0,1},{1,0},{2,3},{3,2},{4,5},{5,4},{6,7},{7,6},{8,9},{9,8},{10,11... | collective-permute-start | bytes 6291464 | tf_op jit(solution)/shard_map/ppermute | solution.py:49
  39.5 40.1 %collective-permute-start.5 = (bf16[256,4096]{1,0:T(8,128)(2,1)S(1)}, bf16[256,4096]{1,0:T(8,128)(2,1)S(1)}, u32[]{:S(2)}, u32[]{:S(2)}) collective-permute-start(bf16[256,4096]{1,0:T(8,128)(2,1)S(1)} %get-tuple-element.60), channel_id=1, source_target_pairs={{0,1},{1,0},{2,3},{3,2},{4,5},{5,4},{6,7},{7,6},{8,9},{9,8},{10,11... | collective-permute-start | bytes 6291464 | tf_op jit(solution)/shard_map/ppermute | solution.py:49
  50.7 13.3 %collective-permute-start.8 = (bf16[32,16,256]{2,1,0:T(8,128)(2,1)S(1)}, bf16[32,16,256]{2,1,0:T(8,128)(2,1)S(1)}, u32[]{:S(2)}, u32[]{:S(2)}) collective-permute-start(bf16[32,16,256]{2,1,0:T(8,128)(2,1)S(1)} %collective-permute-done.7.refs_7_), channel_id=1, source_target_pairs={{0,16},{16,0},{1,17},{17,1},{2,18},{18,2},{3,19},{19,3},{4,20},{20... | collective-permute-start | bytes 786440 | tf_op jit(solution)/shard_map/ppermute | solution.py:49
  52.8 13.8 %collective-permute-start.10 = (bf16[32,16,256]{2,1,0:T(8,128)(2,1)S(1)}, bf16[32,16,256]{2,1,0:T(8,128)(2,1)S(1)}, u32[]{:S(2)}, u32[]{:S(2)}) collective-permute-start(bf16[32,16,256]{2,1,0:T(8,128)(2,1)S(1)} %collective-permute-done.7.refs_7_), channel_id=1, source_target_pairs={{0,4},{4,12},{12,8},{8,0},{1,5},{5,13},{13,9},{9,1},{2,6},{6,14},{... | collective-permute-start | bytes 786440 | tf_op jit(solution)/shard_map/ppermute | solution.py:45
  58.4 13.6 %collective-permute-start.14 = (bf16[32,16,256]{2,1,0:T(8,128)(2,1)S(1)}, bf16[32,16,256]{2,1,0:T(8,128)(2,1)S(1)}, u32[]{:S(2)}, u32[]{:S(2)}) collective-permute-start(bf16[32,16,256]{2,1,0:T(8,128)(2,1)S(1)} %collective-permute-done.3.refs_7_), channel_id=1, source_target_pairs={{0,16},{16,0},{1,17},{17,1},{2,18},{18,2},{3,19},{19,3},{4,20},{20... | collective-permute-start | bytes 786440 | tf_op jit(solution)/shard_map/ppermute | solution.py:49
  86.9 15.5 %collective-permute-start.25 = (bf16[32,32,128]{2,1,0:T(8,128)(2,1)S(1)}, bf16[32,32,128]{2,1,0:T(8,128)(2,1)S(1)}, u32[]{:S(2)}, u32[]{:S(2)}) collective-permute-start(bf16[32,32,128]{2,1,0:T(8,128)(2,1)S(1)} %collective-permute-done.24.refs_5_), channel_id=1, source_target_pairs={{0,16},{16,0},{1,17},{17,1},{2,18},{18,2},{3,19},{19,3},{4,20},{20... | collective-permute-start | bytes 786440 | tf_op jit(solution)/shard_map/ppermute | solution.py:49
  88.4 14.0 %collective-permute-start.27 = (bf16[32,32,128]{2,1,0:T(8,128)(2,1)S(1)}, bf16[32,32,128]{2,1,0:T(8,128)(2,1)S(1)}, u32[]{:S(2)}, u32[]{:S(2)}) collective-permute-start(bf16[32,32,128]{2,1,0:T(8,128)(2,1)S(1)} %collective-permute-done.26.refs_7_), channel_id=1, source_target_pairs={{0,16},{16,0},{1,17},{17,1},{2,18},{18,2},{3,19},{19,3},{4,20},{20... | collective-permute-start | bytes 786440 | tf_op jit(solution)/shard_map/ppermute | solution.py:49
  93.3 12.2 %collective-permute-start.29 = (bf16[32,32,128]{2,1,0:T(8,128)(2,1)S(1)}, bf16[32,32,128]{2,1,0:T(8,128)(2,1)S(1)}, u32[]{:S(2)}, u32[]{:S(2)}) collective-permute-start(bf16[32,32,128]{2,1,0:T(8,128)(2,1)S(1)} %collective-permute-done.28.refs_9_), channel_id=1, source_target_pairs={{0,16},{16,0},{1,17},{17,1},{2,18},{18,2},{3,19},{19,3},{4,20},{20... | collective-permute-start | bytes 786440 | tf_op jit(solution)/shard_map/ppermute | solution.py:49
  132.1 10.5 %collective-permute-start.35 = (bf16[1088,128]{1,0:T(8,128)(2,1)S(1)}, bf16[1088,128]{1,0:T(8,128)(2,1)S(1)}, u32[]{:S(2)}, u32[]{:S(2)}) collective-permute-start(bf16[1088,128]{1,0:T(8,128)(2,1)S(1)} %add_convert_fusion.2), channel_id=1, source_target_pairs={{0,4},{4,12},{12,8},{8,0},{1,5},{5,13},{13,9},{9,1},{2,6},{6,14},{... | collective-permute-start | bytes 835592 | tf_op jit(solution)/shard_map/ppermute | solution.py:45
  132.2 16.0 %collective-permute-start.44 = (bf16[128,1024]{1,0:T(8,128)(2,1)S(1)}, bf16[128,1024]{1,0:T(8,128)(2,1)S(1)}, u32[]{:S(2)}, u32[]{:S(2)}) collective-permute-start(bf16[128,1024]{1,0:T(8,128)(2,1)S(1)} %add_convert_fusion.5), channel_id=1, source_target_pairs={{0,4},{4,12},{12,8},{8,0},{1,5},{5,13},{13,9},{9,1},{2,6},{6,14},{... | collective-permute-start | bytes 786440 | tf_op jit(solution)/shard_map/ppermute | solution.py:45
  142.7 11.5 %collective-permute-start.36 = (bf16[1088,128]{1,0:T(8,128)(2,1)S(1)}, bf16[1088,128]{1,0:T(8,128)(2,1)S(1)}, u32[]{:S(2)}, u32[]{:S(2)}) collective-permute-start(bf16[1088,128]{1,0:T(8,128)(2,1)S(1)} %add_convert_fusion.1), channel_id=1, source_target_pairs={{0,4},{4,12},{12,8},{8,0},{1,5},{5,13},{13,9},{9,1},{2,6},{6,14},{... | collective-permute-start | bytes 835592 | tf_op jit(solution)/shard_map/ppermute | solution.py:45
  148.3 11.5 %collective-permute-start.45 = (bf16[128,1024]{1,0:T(8,128)(2,1)S(1)}, bf16[128,1024]{1,0:T(8,128)(2,1)S(1)}, u32[]{:S(2)}, u32[]{:S(2)}) collective-permute-start(bf16[128,1024]{1,0:T(8,128)(2,1)S(1)} %add_convert_fusion.4), channel_id=1, source_target_pairs={{0,4},{4,12},{12,8},{8,0},{1,5},{5,13},{13,9},{9,1},{2,6},{6,14},{... | collective-permute-start | bytes 786440 | tf_op jit(solution)/shard_map/ppermute | solution.py:45
  154.3 11.5 %collective-permute-start.37 = (bf16[1088,128]{1,0:T(8,128)(2,1)S(1)}, bf16[1088,128]{1,0:T(8,128)(2,1)S(1)}, u32[]{:S(2)}, u32[]{:S(2)}) collective-permute-start(bf16[1088,128]{1,0:T(8,128)(2,1)S(1)} %add_convert_fusion.refs_0_), channel_id=1, source_target_pairs={{0,4},{4,12},{12,8},{8,0},{1,5},{5,13},{13,9},{9,1},{2,6},{6,14},{... | collective-permute-start | bytes 835592 | tf_op jit(solution)/shard_map/ppermute | solution.py:45
  159.9 11.5 %collective-permute-start.46 = (bf16[128,1024]{1,0:T(8,128)(2,1)S(1)}, bf16[128,1024]{1,0:T(8,128)(2,1)S(1)}, u32[]{:S(2)}, u32[]{:S(2)}) collective-permute-start(bf16[128,1024]{1,0:T(8,128)(2,1)S(1)} %add_convert_fusion.3.refs_0_), channel_id=1, source_target_pairs={{0,4},{4,12},{12,8},{8,0},{1,5},{5,13},{13,9},{9,1},{2,6},{6,14},{... | collective-permute-start | bytes 786440 | tf_op jit(solution)/shard_map/ppermute | solution.py:45
  165.8 11.6 %collective-permute-start.38 = (bf16[1088,128]{1,0:T(8,128)(2,1)S(1)}, bf16[1088,128]{1,0:T(8,128)(2,1)S(1)}, u32[]{:S(2)}, u32[]{:S(2)}) collective-permute-start(bf16[1088,128]{1,0:T(8,128)(2,1)S(1)} %collective-permute-done.37.refs_1_), channel_id=1, source_target_pairs={{0,4},{4,12},{12,8},{8,0},{1,5},{5,13},{13,9},{9,1},{2,6},{6,14},{... | collective-permute-start | bytes 835592 | tf_op jit(solution)/shard_map/ppermute | solution.py:45
  171.4 11.6 %collective-permute-start.47 = (bf16[128,1024]{1,0:T(8,128)(2,1)S(1)}, bf16[128,1024]{1,0:T(8,128)(2,1)S(1)}, u32[]{:S(2)}, u32[]{:S(2)}) collective-permute-start(bf16[128,1024]{1,0:T(8,128)(2,1)S(1)} %collective-permute-done.46.refs_1_), channel_id=1, source_target_pairs={{0,4},{4,12},{12,8},{8,0},{1,5},{5,13},{13,9},{9,1},{2,6},{6,14},{... | collective-permute-start | bytes 786440 | tf_op jit(solution)/shard_map/ppermute | solution.py:45
  177.4 15.9 %collective-permute-start.39 = (bf16[1088,128]{1,0:T(8,128)(2,1)S(1)}, bf16[1088,128]{1,0:T(8,128)(2,1)S(1)}, u32[]{:S(2)}, u32[]{:S(2)}) collective-permute-start(bf16[1088,128]{1,0:T(8,128)(2,1)S(1)} %collective-permute-done.38.refs_2_), channel_id=1, source_target_pairs={{0,4},{4,12},{12,8},{8,0},{1,5},{5,13},{13,9},{9,1},{2,6},{6,14},{... | collective-permute-start | bytes 835592 | tf_op jit(solution)/shard_map/ppermute | solution.py:45
  183.0 10.2 %collective-permute-start.48 = (bf16[128,1024]{1,0:T(8,128)(2,1)S(1)}, bf16[128,1024]{1,0:T(8,128)(2,1)S(1)}, u32[]{:S(2)}, u32[]{:S(2)}) collective-permute-start(bf16[128,1024]{1,0:T(8,128)(2,1)S(1)} %collective-permute-done.47.refs_2_), channel_id=1, source_target_pairs={{0,4},{4,12},{12,8},{8,0},{1,5},{5,13},{13,9},{9,1},{2,6},{6,14},{... | collective-permute-start | bytes 786440 | tf_op jit(solution)/shard_map/ppermute | solution.py:45
  183.0 10.8 %collective-permute-start.51 = (bf16[128,1024]{1,0:T(8,128)(2,1)S(1)}, bf16[128,1024]{1,0:T(8,128)(2,1)S(1)}, u32[]{:S(2)}, u32[]{:S(2)}) collective-permute-start(bf16[128,1024]{1,0:T(8,128)(2,1)S(1)} %collective-permute-done.47.refs_2_), channel_id=1, source_target_pairs={{0,1},{1,0},{2,3},{3,2},{4,5},{5,4},{6,7},{7,6},{8,9},{9,8},{10,11... | collective-permute-start | bytes 786440 | tf_op jit(solution)/shard_map/ppermute | solution.py:49
  183.0 13.9 %collective-permute-start.40 = (bf16[1088,128]{1,0:T(8,128)(2,1)S(1)}, bf16[1088,128]{1,0:T(8,128)(2,1)S(1)}, u32[]{:S(2)}, u32[]{:S(2)}) collective-permute-start(bf16[1088,128]{1,0:T(8,128)(2,1)S(1)} %add_convert_fusion.refs_0_), channel_id=1, source_target_pairs={{0,1},{1,0},{2,3},{3,2},{4,5},{5,4},{6,7},{7,6},{8,9},{9,8},{10,11... | collective-permute-start | bytes 835592 | tf_op jit(solution)/shard_map/ppermute | solution.py:49
  183.5 13.4 %collective-permute-start.41 = (bf16[1088,128]{1,0:T(8,128)(2,1)S(1)}, bf16[1088,128]{1,0:T(8,128)(2,1)S(1)}, u32[]{:S(2)}, u32[]{:S(2)}) collective-permute-start(bf16[1088,128]{1,0:T(8,128)(2,1)S(1)} %collective-permute-done.37.refs_1_), channel_id=1, source_target_pairs={{0,1},{1,0},{2,3},{3,2},{4,5},{5,4},{6,7},{7,6},{8,9},{9,8},{10,11... | collective-permute-start | bytes 835592 | tf_op jit(solution)/shard_map/ppermute | solution.py:49
  (47 other events, 414.4 us)

commit v5 on v4

--- a/solution.py
+++ b/solution.py
@@ -62,20 +62,20 @@
     return sum(t.astype(F32) for t in terms).astype(BF16)
 
 
-def ring_sum(parts, seen=None):
+def ring_all(parts, seen, gates=()):
+    n = lax.axis_size("dp")
+
+    def step(x):
+        k = len(seen)
+        seen.append(ring_step(after(x, gates[k]) if k < len(gates) else x))
+        return seen[-1]
+
     total = parts[0]
     for part in parts[1:]:
-        total = ring_step(total)
-        if seen is not None:
-            seen.append(total)
-        total = add(total, part)
-    return total
-
-
-def ring_gather(block):
-    blocks = [block]
-    for _ in range(lax.axis_size("dp") - 1):
-        blocks.append(ring_step(blocks[-1]))
+        total = add(step(total), part)
+    blocks = [total]
+    for _ in range(n - 1):
+        blocks.append(step(blocks[-1]))
     return blocks, [swap(b, "sub") for b in blocks]
 
 
@@ -442,7 +442,7 @@
         scratch=[pltpu.SemaphoreType.DMA((count,))],
         specs=[anywhere] * count,
         out_specs=(anywhere,),
-        limit=4,
+        limit=60,
     )
     got = swap(send, "sub")
     moving = call(
@@ -453,7 +453,7 @@
         scratch=[pltpu.SemaphoreType.DMA((2 * count,))],
         specs=[anywhere] * (count + 1),
         out_specs=(anywhere,) * count,
-        limit=4,
+        limit=60,
     )
     return list(moving), got
 
@@ -488,51 +488,44 @@
     ring, crossed = [], []
 
     def step(moving, *done):
-        k = len(ring)
-        waits = ring[k - 2 : k - 1] if k > 1 else []
-        waits += ring[k - 3 : k - 2] if k > 2 else []
-        waits += crossed[k - 4 : k - 3] if k > 3 else []
-        ring.append(ring_step(after(moving, *waits, *done) if waits else moving))
+        ring.append(ring_step(after(moving, *done) if done else moving))
         crossed.append(swap(ring[-1], "grp"))
-        return ring[-1]
 
     step(gate_moving)
     step(up_moving)
 
-    adapters = jnp.concatenate([up_adapter_out, down_adapter_in], axis=0)
-    adapters_more = others(after(adapters, ring[1]), "mp")
-    tokens_then, cotangent_then, down_then, _ = lax.optimization_barrier(
-        (tokens, cotangent, down_codes, ring[1])
-    )
     vmem = pl.BlockSpec(memory_space=pltpu.VMEM)
     smem = pl.BlockSpec(memory_space=pltpu.SMEM)
+    lengths = after(sequence_length_list, gate_moving, up_moving)
     grad_send, grad, low_out, squares = call(
         lambda *refs: cotangent_kernel(rows * n * lax.axis_size("sub"), *refs),
         "cotangent",
-        [cotangent_then, tokens_then, sequence_length_list, slot_sequence_index[None, :], down_adapter_out],
+        [cotangent, tokens, lengths, slot_sequence_index[None, :], down_adapter_out],
         [shape((rows, half))] * 2 + [shape((rows, rank), F32), shape((rows, LANES), F32)],
         specs=[vmem, vmem, smem, vmem, vmem],
         flops=2 * rows * local_width * rank,
     )
-    step(ring[0])
     squares_more = others(squares, "mp")
-    down_turned = jnp.swapaxes(down_then, 0, 1)
-    (down_moving,), down_got = start_shards([down_turned])
-    step(ring[1])
-    grad_got = swap(grad_send, "sub")
-    step(ring[2], grad, down_moving)
-    step(ring[3])
+    step(ring[0], ring[1], grad)
+    step(ring[1], ring[0], grad)
     normed_send, normed, low = call(
         lambda *refs: token_kernel(total_width, *refs),
         "tokens",
-        [after(tokens, ring[3]), rms_norm_gain[None, :], up_adapter_in, low_out, squares, *squares_more],
+        [tokens, rms_norm_gain[None, :], up_adapter_in, low_out, after(squares, *ring[:2]), *squares_more],
         [shape((rows, half))] * 2 + [shape((rows, 2 * rank), F32)],
         flops=2 * rows * local_width * rank,
     )
+    grad_got = swap(grad_send, "sub")
     normed_got = swap(normed_send, "sub")
     low_more = others(low, "mp")
-    step(down_moving, normed)
-    step(ring[6], grad_got, *adapters_more)
+    step(ring[2], ring[3], normed, *crossed[:2])
+    step(ring[3], ring[2], normed, *crossed[:2])
+    down_turned = jnp.swapaxes(after(down_codes, *ring[2:4]), 0, 1)
+    (down_moving,), down_got = start_shards([down_turned])
+    adapters = jnp.concatenate([up_adapter_out, down_adapter_in], axis=0)
+    adapters_more = others(after(adapters, *ring[2:4]), "mp")
+    step(down_moving, *ring[4:6], *crossed[2:4], grad_got, normed_got, *low_more, *adapters_more)
+    step(ring[6])
 
     def product(kernel, name, own, got, scale, codes, codes_got, first_got, steps, weight_shape):
         groups = scale.shape[0]
@@ -557,7 +550,7 @@
         front_kernel, "up", normed, normed_got, up_block_scale.T, up_codes, front_got, half_blocks,
         range(1, 2 * (n - 1), 2), front,
     )
-    step(ring[7], gate_mine, up_mine)
+    step(ring[7], gate_mine, up_mine, crossed[6])
     small_scratch = [
         pltpu.VMEM((rank, units), BF16),
         pltpu.VMEM((units, rank), BF16),
@@ -578,7 +571,7 @@
         flops=4 * rows * half * rank,
     )
     seen = []
-    down_out_blocks = ring_gather(ring_sum(down_out_parts, seen))
+    down_out_blocks = ring_all(down_out_parts, seen)
     (normed_t,) = call(
         transpose_kernel,
         "transpose",
@@ -588,13 +581,13 @@
     )
 
     back, back_more, _ = product(
-        back_kernel, "back", after(grad, down_out_parts[0]), grad_got, down_block_scale, down_turned, down_got, 0,
+        back_kernel, "back", after(grad, seen[0]), grad_got, down_block_scale, down_turned, down_got, 0,
         range(2 * (n - 1), 3 * (n - 1)), (units, half),
     )
     low_grad, up_out_term = call(
         lambda *refs: up_grad_kernel(more, *refs),
         "up_grad",
-        [after(back, seen[0]), silu, low, adapters, *back_more, *low_more, *adapters_more],
+        [back, silu, low, adapters, *back_more, *low_more, *adapters_more],
         [shape((rows, rank)), shape(up_adapter_out.shape)],
         scratch=small_scratch,
         limit=8,
@@ -603,11 +596,11 @@
     up_in_parts = call(
         up_in_kernel,
         "up_in",
-        [low_grad, swap(low_grad, "sub"), normed_t, up_out_term, down_in_term],
+        [after(low_grad, seen[1]), swap(low_grad, "sub"), normed_t, up_out_term, down_in_term],
         [shape((half // n + extra, rank))] * n,
         flops=4 * rows * half * rank,
     )
-    up_in_blocks = ring_gather(ring_sum(up_in_parts))
+    up_in_blocks = ring_all(up_in_parts, [], seen[1:])
 
     anywhere = pl.BlockSpec(memory_space=pl.ANY)
     (down_out_gradient,) = call(

time: 200 us -> 247 us (1.24)
  Pallas kernels: 23.7 us -> 85.4 us
  waiting for transfers between devices: 125 us -> 107 us
  local copies, waits for them, and re-layouts: 6.89 us -> 9.84 us
    pallas_call x16, Pallas kernels: 23.7 us -> 85.4 us  [call(): pl.pallas_call(kernel, out_shape=tuple(out_shape), in_specs=specs or [vme...]
    ppermute x21, waiting for transfers between devices: 95.1 us -> 72.1 us  [ring_step(): lax.ppermute(x, 'dp', [(ring_at(i, n), ring_at((i + 1) % n, n)) for i in...]
    ppermute x21, starting transfers between devices: 20.6 us -> 23.9 us  [ring_step(): lax.ppermute(x, 'dp', [(ring_at(i, n), ring_at((i + 1) % n, n)) for i in...]
    ppermute x6, waiting for transfers between devices: 9.64 us -> 12.8 us  [others(): lax.ppermute(x, axis, [(i, (i + k) % n) for i in range(n)])]
    unnamed x37 -> x67, local copies, waits for them, and re-layouts: 6.52 us -> 8.64 us
  transfers between devices with their start and end apart: 53 -> 53, of which waited for: 31 -> 31; matrix products, arithmetic and copies ran while one was open for 0% -> 1% of each run, Pallas kernels for 8% -> 17%
where the time goes in v5:
time: 247 us
  waiting for transfers between devices  107 us (43%)
  Pallas kernels  85.4 us (35%)
  starting transfers between devices  42.9 us (17%)
  local copies, waits for them, and re-layouts  9.84 us (4%)
    pallas_call x16, Pallas kernels, call(): pl.pallas_call(kernel, out_shape=tuple(out_shape), in_specs=specs or [vme...  85.4 us
    ppermute x21, waiting for transfers between devices, ring_step(): lax.ppermute(x, 'dp', [(ring_at(i, n), ring_at((i + 1) % n, n)) for i in...  72.1 us
    ppermute x21, starting transfers between devices, ring_step(): lax.ppermute(x, 'dp', [(ring_at(i, n), ring_at((i + 1) % n, n)) for i in...  23.9 us
    ppermute x26, waiting for transfers between devices, swap(): return lax.ppermute(x, axis, [(0, 1), (1, 0)])  21.6 us
    ppermute x6, waiting for transfers between devices, others(): lax.ppermute(x, axis, [(i, (i + k) % n) for i in range(n)])  12.8 us
    ppermute x26, starting transfers between devices, swap(): return lax.ppermute(x, axis, [(0, 1), (1, 0)])  12.6 us
    unnamed x67, local copies, waits for them, and re-layouts  8.64 us
    ppermute x6, starting transfers between devices, others(): lax.ppermute(x, axis, [(i, (i + k) % n) for i in range(n)])  6.34 us
  transfers between devices with their start and end apart: 53, of which 31 were waited for; matrix products, arithmetic and copies ran while one was open for 1% of the time, Pallas kernels for 17%

profile of v5, /device:TPU:0, one launch (start us, length us, event | category | flops | bytes accessed | tf_op | source)
XLA Modules:
  0.0 246.6 jit_solution(16325787759834529179)
XLA Ops:
  0.7 17.0 %halves.2 = bf16[64,16,256]{2,1,0:T(8,128)(2,1)} custom-call(bf16[64,16,256]{2,1,0:T(8,128)(2,1)} %refs_3_.2, bf16[64,16,256]{2,1,0:T(8,128)(2,1)} %refs_3_.3), custom_call_target="tpu_custom_call" | custom-call | bytes 1572864 | tf_op jit(solution)/shard_map/halves/pallas_call | solution.py:87
  20.8 17.0 %quarters.2 = (bf16[32,16,256]{2,1,0:T(8,128)(2,1)}, bf16[32,16,256]{2,1,0:T(8,128)(2,1)}) custom-call(bf16[64,16,256]{2,1,0:T(8,128)(2,1)} %refs_3_.2, bf16[64,16,256]{2,1,0:T(8,128)(2,1)} %refs_3_.3, bf16[64,16,256]{2,1,0:T(8,128)(2,1)} %copy-done.7), custom_call_target="tpu_custom_call" | custom-call | bytes 2097152 | tf_op jit(solution)/shard_map/quarters/pallas_call | solution.py:87
  47.8 6.0 %cotangent.1 = (bf16[256,4096]{1,0:T(8,128)(2,1)}, bf16[256,4096]{1,0:T(8,128)(2,1)S(1)}, f32[256,128]{1,0:T(8,128)S(1)}, f32[256,128]{1,0:T(8,128)S(1)}) custom-call(bf16[256,8192]{1,0:T(8,128)(2,1)S(1)} %copy-done.9, bf16[256,8192]{1,0:T(8,128)(2,1)S(1)} %copy-done, s32[1,2]{1,0:T(1,128)S(1)} %copy-done.25, s32[1,256]{1,0:T(1,128)S(1)} %bitcast.9, ...), custom_call_target="tpu_custom_call" | custom-call | flops 536870912 | bytes 14943240 | tf_op jit(solution)/shard_map/cotangent/pallas_call | solution.py:87
  55.4 3.3 %collective-permute-done.3.refs_5_ = f32[256,128]{1,0:T(8,128)S(1)} collective-permute-done((f32[256,128]{1,0:T(8,128)S(1)}, f32[256,128]{1,0:T(8,128)S(1)}, u32[]{:S(2)}, u32[]{:S(2)}) %collective-permute-start.3) | collective-permute-done | bytes 131104 | tf_op jit(solution)/shard_map/ppermute | solution.py:54
  58.8 3.7 %tokens.1 = (bf16[256,4096]{1,0:T(8,128)(2,1)}, bf16[256,4096]{1,0:T(8,128)(2,1)S(1)}, f32[256,256]{1,0:T(8,128)S(1)}) custom-call(bf16[256,8192]{1,0:T(8,128)(2,1)S(1)} %copy-done.1, bf16[1,8192]{1,0:T(2,128)(2,1)S(1)} %broadcast_in_dim.7.refs_1_, bf16[8192,128]{1,0:T(8,128)(2,1)S(1)} %copy-done.10, f32[256,128]{1,0:T(8,128)S(1)} %get-tuple-element.57.refs_3_, ...), custom_call_target="tpu_custom_call" | custom-call | flops 536870912 | bytes 11157504 | tf_op jit(solution)/shard_map/tokens/pallas_call | solution.py:87
  64.9 6.3 %collective-permute-done.5.refs_6_ = bf16[32,16,256]{2,1,0:T(8,128)(2,1)S(1)} collective-permute-done((bf16[32,16,256]{2,1,0:T(8,128)(2,1)S(1)}, bf16[32,16,256]{2,1,0:T(8,128)(2,1)S(1)}, u32[]{:S(2)}, u32[]{:S(2)}) %collective-permute-start.5) | collective-permute-done | bytes 262176 | tf_op jit(solution)/shard_map/ppermute | solution.py:49
  85.4 9.0 %halves.3 = bf16[32,32,128]{2,1,0:T(8,128)(2,1)} custom-call(bf16[64,32,128]{2,1,0:T(8,128)(2,1)} %bitcast.6), custom_call_target="tpu_custom_call" | custom-call | bytes 786432 | tf_op jit(solution)/shard_map/halves/pallas_call | solution.py:87
  97.0 9.1 %quarters.3 = bf16[32,32,128]{2,1,0:T(8,128)(2,1)} custom-call(bf16[64,32,128]{2,1,0:T(8,128)(2,1)} %bitcast.7, bf16[32,32,128]{2,1,0:T(8,128)(2,1)} %copy-done.12), custom_call_target="tpu_custom_call" | custom-call | bytes 1048576 | tf_op jit(solution)/shard_map/quarters/pallas_call | solution.py:87
  111.1 3.9 %gate.1 = (f32[256,256]{1,0:T(8,128)S(1)}, bf16[256,256]{1,0:T(8,128)(2,1)S(1)}) custom-call(bf16[256,4096]{1,0:T(8,128)(2,1)S(1)} %get-tuple-element.60.refs_0_.own, bf16[256,4096]{1,0:T(8,128)(2,1)} %collective-permute-done.4.refs_1_.got, bf16[2,64]{1,0:T(2,128)(2,1)S(1)} %bitcast.10, bf16[64,16,256]{2,1,0:T(8,128)(2,1)S(1)} %copy-done.5, ...), custom_call_target="tpu_custom_call" | custom-call | flops 1073741824 | bytes 7209216 | tf_op jit(solution)/shard_map/gate/pallas_call | solution.py:87
  118.3 3.6 %up.1 = (f32[256,256]{1,0:T(8,128)S(1)}, bf16[256,256]{1,0:T(8,128)(2,1)S(1)}) custom-call(bf16[256,4096]{1,0:T(8,128)(2,1)S(1)} %get-tuple-element.60.refs_0_.own, bf16[256,4096]{1,0:T(8,128)(2,1)} %collective-permute-done.4.refs_1_.got, bf16[2,64]{1,0:T(2,128)(2,1)S(1)} %bitcast.11, bf16[64,16,256]{2,1,0:T(8,128)(2,1)S(1)} %copy-done.6, ...), custom_call_target="tpu_custom_call" | custom-call | flops 1073741824 | bytes 7209216 | tf_op jit(solution)/shard_map/up/pallas_call | solution.py:87
  128.1 3.7 %collective-permute-done.18.refs_5_ = bf16[256,256]{1,0:T(8,128)(2,1)S(1)} collective-permute-done((bf16[256,256]{1,0:T(8,128)(2,1)S(1)}, bf16[256,256]{1,0:T(8,128)(2,1)S(1)}, u32[]{:S(2)}, u32[]{:S(2)}) %collective-permute-start.18) | collective-permute-done | bytes 131104 | tf_op jit(solution)/shard_map/ppermute | solution.py:54
  139.4 5.9 %collective-permute-done.23 = bf16[128,1024]{1,0:T(8,128)(2,1)S(1)} collective-permute-done((bf16[128,1024]{1,0:T(8,128)(2,1)S(1)}, bf16[128,1024]{1,0:T(8,128)(2,1)S(1)}, u32[]{:S(2)}, u32[]{:S(2)}) %collective-permute-start.23) | collective-permute-done | bytes 262176 | tf_op jit(solution)/shard_map/ppermute | solution.py:45
  146.5 4.5 %collective-permute-done.30.refs_10_ = bf16[32,32,128]{2,1,0:T(8,128)(2,1)S(1)} collective-permute-done((bf16[32,32,128]{2,1,0:T(8,128)(2,1)S(1)}, bf16[32,32,128]{2,1,0:T(8,128)(2,1)S(1)}, u32[]{:S(2)}, u32[]{:S(2)}) %collective-permute-start.30) | collective-permute-done | bytes 262176 | tf_op jit(solution)/shard_map/ppermute | solution.py:49
  151.1 3.8 %back.1 = (f32[256,256]{1,0:T(8,128)S(1)}, bf16[256,256]{1,0:T(8,128)(2,1)S(1)}) custom-call(bf16[256,4096]{1,0:T(8,128)(2,1)S(1)} %copy-done.3, bf16[256,4096]{1,0:T(8,128)(2,1)} %collective-permute-done.22.grad_got.refs_1_, bf16[2,64]{1,0:T(2,128)(2,1)S(1)} %copy-done.28, bf16[64,32,128]{2,1,0:T(8,128)(2,1)S(1)} %bitcast.8, ...), custom_call_target="tpu_custom_call" | custom-call | flops 1073741824 | bytes 6947072 | tf_op jit(solution)/shard_map/back/pallas_call | solution.py:87
  156.9 5.0 %collective-permute-done.32.refs_4_ = bf16[256,256]{1,0:T(8,128)(2,1)S(1)} collective-permute-done((bf16[256,256]{1,0:T(8,128)(2,1)S(1)}, bf16[256,256]{1,0:T(8,128)(2,1)S(1)}, u32[]{:S(2)}, u32[]{:S(2)}) %collective-permute-start.32) | collective-permute-done | bytes 131104 | tf_op jit(solution)/shard_map/ppermute | solution.py:54
  170.7 7.8 %collective-permute-done.35 = bf16[1088,128]{1,0:T(8,128)(2,1)S(1)} collective-permute-done((bf16[1088,128]{1,0:T(8,128)(2,1)S(1)}, bf16[1088,128]{1,0:T(8,128)(2,1)S(1)}, u32[]{:S(2)}, u32[]{:S(2)}) %collective-permute-start.35) | collective-permute-done | bytes 278560 | tf_op jit(solution)/shard_map/ppermute | solution.py:45
  178.6 5.1 %collective-permute-done.36 = bf16[128,1024]{1,0:T(8,128)(2,1)S(1)} collective-permute-done((bf16[128,1024]{1,0:T(8,128)(2,1)S(1)}, bf16[128,1024]{1,0:T(8,128)(2,1)S(1)}, u32[]{:S(2)}, u32[]{:S(2)}) %collective-permute-start.36) | collective-permute-done | bytes 262176 | tf_op jit(solution)/shard_map/ppermute | solution.py:45
  186.3 7.9 %collective-permute-done.37 = bf16[1088,128]{1,0:T(8,128)(2,1)S(1)} collective-permute-done((bf16[1088,128]{1,0:T(8,128)(2,1)S(1)}, bf16[1088,128]{1,0:T(8,128)(2,1)S(1)}, u32[]{:S(2)}, u32[]{:S(2)}) %collective-permute-start.37) | collective-permute-done | bytes 278560 | tf_op jit(solution)/shard_map/ppermute | solution.py:45
  194.3 4.3 %collective-permute-done.38.refs_1_ = bf16[128,1024]{1,0:T(8,128)(2,1)S(1)} collective-permute-done((bf16[128,1024]{1,0:T(8,128)(2,1)S(1)}, bf16[128,1024]{1,0:T(8,128)(2,1)S(1)}, u32[]{:S(2)}, u32[]{:S(2)}) %collective-permute-start.38) | collective-permute-done | bytes 262176 | tf_op jit(solution)/shard_map/ppermute | solution.py:45
  201.0 8.1 %collective-permute-done.39 = bf16[1088,128]{1,0:T(8,128)(2,1)S(1)} collective-permute-done((bf16[1088,128]{1,0:T(8,128)(2,1)S(1)}, bf16[1088,128]{1,0:T(8,128)(2,1)S(1)}, u32[]{:S(2)}, u32[]{:S(2)}) %collective-permute-start.39) | collective-permute-done | bytes 278560 | tf_op jit(solution)/shard_map/ppermute | solution.py:45
  209.1 3.3 %collective-permute-done.40.refs_2_ = bf16[128,1024]{1,0:T(8,128)(2,1)S(1)} collective-permute-done((bf16[128,1024]{1,0:T(8,128)(2,1)S(1)}, bf16[128,1024]{1,0:T(8,128)(2,1)S(1)}, u32[]{:S(2)}, u32[]{:S(2)}) %collective-permute-start.40) | collective-permute-done | bytes 262176 | tf_op jit(solution)/shard_map/ppermute | solution.py:45
  214.9 10.6 %collective-permute-done.42.refs_3_ = bf16[128,1024]{1,0:T(8,128)(2,1)S(1)} collective-permute-done((bf16[128,1024]{1,0:T(8,128)(2,1)S(1)}, bf16[128,1024]{1,0:T(8,128)(2,1)S(1)}, u32[]{:S(2)}, u32[]{:S(2)}) %collective-permute-start.42) | collective-permute-done | bytes 262176 | tf_op jit(solution)/shard_map/ppermute | solution.py:45
  225.5 8.0 %collective-permute-done.43.refs_2_ = bf16[1088,128]{1,0:T(8,128)(2,1)S(1)} collective-permute-done((bf16[1088,128]{1,0:T(8,128)(2,1)S(1)}, bf16[1088,128]{1,0:T(8,128)(2,1)S(1)}, u32[]{:S(2)}, u32[]{:S(2)}) %collective-permute-start.43) | collective-permute-done | bytes 278560 | tf_op jit(solution)/shard_map/ppermute | solution.py:45
  235.6 5.4 %collective-permute-done.44.refs_3_ = bf16[1088,128]{1,0:T(8,128)(2,1)S(1)} collective-permute-done((bf16[1088,128]{1,0:T(8,128)(2,1)S(1)}, bf16[1088,128]{1,0:T(8,128)(2,1)S(1)}, u32[]{:S(2)}, u32[]{:S(2)}) %collective-permute-start.44) | collective-permute-done | bytes 278560 | tf_op jit(solution)/shard_map/ppermute | solution.py:45
  (177 shorter events, 82.9 us)
Async XLA Ops:
  37.8 17.5 %collective-permute-start.1 = (bf16[32,16,256]{2,1,0:T(8,128)(2,1)}, bf16[32,16,256]{2,1,0:T(8,128)(2,1)S(1)}, u32[]{:S(2)}, u32[]{:S(2)}) collective-permute-start(bf16[32,16,256]{2,1,0:T(8,128)(2,1)} %get-tuple-element.53), channel_id=1, source_target_pairs={{0,4},{4,12},{12,8},{8,0},{1,5},{5,13},{13,9},{9,1},{2,6},{6,14},{... | collective-permute-start | bytes 786440 | tf_op jit(solution)/shard_map/ppermute | solution.py:45
  40.8 14.6 %collective-permute-start.2 = (bf16[32,16,256]{2,1,0:T(8,128)(2,1)}, bf16[32,16,256]{2,1,0:T(8,128)(2,1)S(1)}, u32[]{:S(2)}, u32[]{:S(2)}) collective-permute-start(bf16[32,16,256]{2,1,0:T(8,128)(2,1)} %get-tuple-element.54), channel_id=1, source_target_pairs={{0,4},{4,12},{12,8},{8,0},{1,5},{5,13},{13,9},{9,1},{2,6},{6,14},{... | collective-permute-start | bytes 786440 | tf_op jit(solution)/shard_map/ppermute | solution.py:45
  55.3 50.8 %collective-permute-start.22 = (bf16[256,4096]{1,0:T(8,128)(2,1)}, bf16[256,4096]{1,0:T(8,128)(2,1)}, u32[]{:S(2)}, u32[]{:S(2)}) collective-permute-start(bf16[256,4096]{1,0:T(8,128)(2,1)} %get-tuple-element.73), channel_id=1, source_target_pairs={{0,1},{1,0},{2,3},{3,2},{4,5},{5,4},{6,7},{7,6},{8,9},{9,8},{10,11... | collective-permute-start | bytes 6291464 | tf_op jit(solution)/shard_map/ppermute | solution.py:49
  62.4 43.7 %collective-permute-start.4 = (bf16[256,4096]{1,0:T(8,128)(2,1)}, bf16[256,4096]{1,0:T(8,128)(2,1)}, u32[]{:S(2)}, u32[]{:S(2)}) collective-permute-start(bf16[256,4096]{1,0:T(8,128)(2,1)} %get-tuple-element.61), channel_id=1, source_target_pairs={{0,1},{1,0},{2,3},{3,2},{4,5},{5,4},{6,7},{7,6},{8,9},{9,8},{10,11... | collective-permute-start | bytes 6291464 | tf_op jit(solution)/shard_map/ppermute | solution.py:49
  64.1 10.2 %collective-permute-start.6 = (bf16[32,16,256]{2,1,0:T(8,128)(2,1)S(1)}, bf16[32,16,256]{2,1,0:T(8,128)(2,1)}, u32[]{:S(2)}, u32[]{:S(2)}) collective-permute-start(bf16[32,16,256]{2,1,0:T(8,128)(2,1)S(1)} %collective-permute-done.1.refs_5_), channel_id=1, source_target_pairs={{0,4},{4,12},{12,8},{8,0},{1,5},{5,13},{13,9},{9,1},{2,6},{6,14},{... | collective-permute-start | bytes 786440 | tf_op jit(solution)/shard_map/ppermute | solution.py:45
  64.6 14.4 %collective-permute-start.8 = (bf16[32,16,256]{2,1,0:T(8,128)(2,1)S(1)}, bf16[32,16,256]{2,1,0:T(8,128)(2,1)S(1)}, u32[]{:S(2)}, u32[]{:S(2)}) collective-permute-start(bf16[32,16,256]{2,1,0:T(8,128)(2,1)S(1)} %collective-permute-done.2.refs_5_), channel_id=1, source_target_pairs={{0,4},{4,12},{12,8},{8,0},{1,5},{5,13},{13,9},{9,1},{2,6},{6,14},{... | collective-permute-start | bytes 786440 | tf_op jit(solution)/shard_map/ppermute | solution.py:45
  80.7 14.5 %collective-permute-start.10 = (bf16[32,16,256]{2,1,0:T(8,128)(2,1)}, bf16[32,16,256]{2,1,0:T(8,128)(2,1)}, u32[]{:S(2)}, u32[]{:S(2)}) collective-permute-start(bf16[32,16,256]{2,1,0:T(8,128)(2,1)} %collective-permute-done.6.refs_7_), channel_id=1, source_target_pairs={{0,4},{4,12},{12,8},{8,0},{1,5},{5,13},{13,9},{9,1},{2,6},{6,14},{... | collective-permute-start | bytes 786440 | tf_op jit(solution)/shard_map/ppermute | solution.py:45
  81.1 13.4 %collective-permute-start.7 = (bf16[32,16,256]{2,1,0:T(8,128)(2,1)}, bf16[32,16,256]{2,1,0:T(8,128)(2,1)}, u32[]{:S(2)}, u32[]{:S(2)}) collective-permute-start(bf16[32,16,256]{2,1,0:T(8,128)(2,1)} %collective-permute-done.6.refs_7_), channel_id=1, source_target_pairs={{0,16},{16,0},{1,17},{17,1},{2,18},{18,2},{3,19},{19,3},{4,20},{20... | collective-permute-start | bytes 786440 | tf_op jit(solution)/shard_map/ppermute | solution.py:49
  82.7 11.8 %collective-permute-start.20 = (bf16[256,128]{1,0:T(8,128)(2,1)S(1)}, bf16[256,128]{1,0:T(8,128)(2,1)S(1)}, u32[]{:S(2)}, u32[]{:S(2)}) collective-permute-start(bf16[256,128]{1,0:T(8,128)(2,1)S(1)} %constant_dynamic-update-slice_fusion.refs_3_), channel_id=1, source_target_pairs={{0,2},{2,0},{1,3},{3,1},{4,6},{6,4},{5,7},{7,5},{8,10},{10,8},{9,1... | collective-permute-start | bytes 196616 | tf_op jit(solution)/shard_map/ppermute | solution.py:54
  94.6 11.5 %collective-permute-start.13 = (bf16[32,16,256]{2,1,0:T(8,128)(2,1)}, bf16[32,16,256]{2,1,0:T(8,128)(2,1)}, u32[]{:S(2)}, u32[]{:S(2)}) collective-permute-start(bf16[32,16,256]{2,1,0:T(8,128)(2,1)} %copy-done.18), channel_id=1, source_target_pairs={{0,16},{16,0},{1,17},{17,1},{2,18},{18,2},{3,19},{19,3},{4,20},{20... | collective-permute-start | bytes 786440 | tf_op jit(solution)/shard_map/ppermute | solution.py:49
  95.1 10.9 %collective-permute-start.14 = (bf16[32,16,256]{2,1,0:T(8,128)(2,1)}, bf16[32,16,256]{2,1,0:T(8,128)(2,1)}, u32[]{:S(2)}, u32[]{:S(2)}) collective-permute-start(bf16[32,16,256]{2,1,0:T(8,128)(2,1)} %copy-done.18), channel_id=1, source_target_pairs={{0,4},{4,12},{12,8},{8,0},{1,5},{5,13},{13,9},{9,1},{2,6},{6,14},{... | collective-permute-start | bytes 786440 | tf_op jit(solution)/shard_map/ppermute | solution.py:45
  96.3 12.9 %collective-permute-start.11 = (bf16[32,16,256]{2,1,0:T(8,128)(2,1)}, bf16[32,16,256]{2,1,0:T(8,128)(2,1)}, u32[]{:S(2)}, u32[]{:S(2)}) collective-permute-start(bf16[32,16,256]{2,1,0:T(8,128)(2,1)} %collective-permute-done.10.refs_9_), channel_id=1, source_target_pairs={{0,16},{16,0},{1,17},{17,1},{2,18},{18,2},{3,19},{19,3},{4,20},{20... | collective-permute-start | bytes 786440 | tf_op jit(solution)/shard_map/ppermute | solution.py:49
  107.7 10.6 %collective-permute-start.15 = (bf16[32,16,256]{2,1,0:T(8,128)(2,1)}, bf16[32,16,256]{2,1,0:T(8,128)(2,1)S(1)}, u32[]{:S(2)}, u32[]{:S(2)}) collective-permute-start(bf16[32,16,256]{2,1,0:T(8,128)(2,1)} %collective-permute-done.14.refs_9_), channel_id=1, source_target_pairs={{0,16},{16,0},{1,17},{17,1},{2,18},{18,2},{3,19},{19,3},{4,20},{20... | collective-permute-start | bytes 786440 | tf_op jit(solution)/shard_map/ppermute | solution.py:49
  125.0 13.5 %collective-permute-start.29 = (bf16[32,32,128]{2,1,0:T(8,128)(2,1)S(1)}, bf16[32,32,128]{2,1,0:T(8,128)(2,1)S(1)}, u32[]{:S(2)}, u32[]{:S(2)}) collective-permute-start(bf16[32,32,128]{2,1,0:T(8,128)(2,1)S(1)} %collective-permute-done.27.refs_7_), channel_id=1, source_target_pairs={{0,4},{4,12},{12,8},{8,0},{1,5},{5,13},{13,9},{9,1},{2,6},{6,14},{... | collective-permute-start | bytes 786440 | tf_op jit(solution)/shard_map/ppermute | solution.py:45
  138.5 12.6 %collective-permute-start.30 = (bf16[32,32,128]{2,1,0:T(8,128)(2,1)S(1)}, bf16[32,32,128]{2,1,0:T(8,128)(2,1)S(1)}, u32[]{:S(2)}, u32[]{:S(2)}) collective-permute-start(bf16[32,32,128]{2,1,0:T(8,128)(2,1)S(1)} %collective-permute-done.29.refs_9_), channel_id=1, source_target_pairs={{0,16},{16,0},{1,17},{17,1},{2,18},{18,2},{3,19},{19,3},{4,20},{20... | collective-permute-start | bytes 786440 | tf_op jit(solution)/shard_map/ppermute | solution.py:49
  168.1 10.4 %collective-permute-start.35 = (bf16[1088,128]{1,0:T(8,128)(2,1)S(1)}, bf16[1088,128]{1,0:T(8,128)(2,1)S(1)}, u32[]{:S(2)}, u32[]{:S(2)}) collective-permute-start(bf16[1088,128]{1,0:T(8,128)(2,1)S(1)} %get-tuple-element.89), channel_id=1, source_target_pairs={{0,4},{4,12},{12,8},{8,0},{1,5},{5,13},{13,9},{9,1},{2,6},{6,14},{... | collective-permute-start | bytes 835592 | tf_op jit(solution)/shard_map/ppermute | solution.py:45
  169.0 14.8 %collective-permute-start.36 = (bf16[128,1024]{1,0:T(8,128)(2,1)S(1)}, bf16[128,1024]{1,0:T(8,128)(2,1)S(1)}, u32[]{:S(2)}, u32[]{:S(2)}) collective-permute-start(bf16[128,1024]{1,0:T(8,128)(2,1)S(1)} %add_convert_fusion.4), channel_id=1, source_target_pairs={{0,4},{4,12},{12,8},{8,0},{1,5},{5,13},{13,9},{9,1},{2,6},{6,14},{... | collective-permute-start | bytes 786440 | tf_op jit(solution)/shard_map/ppermute | solution.py:45
  183.8 10.5 %collective-permute-start.37 = (bf16[1088,128]{1,0:T(8,128)(2,1)S(1)}, bf16[1088,128]{1,0:T(8,128)(2,1)S(1)}, u32[]{:S(2)}, u32[]{:S(2)}) collective-permute-start(bf16[1088,128]{1,0:T(8,128)(2,1)S(1)} %add_convert_fusion.2), channel_id=1, source_target_pairs={{0,4},{4,12},{12,8},{8,0},{1,5},{5,13},{13,9},{9,1},{2,6},{6,14},{... | collective-permute-start | bytes 835592 | tf_op jit(solution)/shard_map/ppermute | solution.py:45
  183.8 14.7 %collective-permute-start.38 = (bf16[128,1024]{1,0:T(8,128)(2,1)S(1)}, bf16[128,1024]{1,0:T(8,128)(2,1)S(1)}, u32[]{:S(2)}, u32[]{:S(2)}) collective-permute-start(bf16[128,1024]{1,0:T(8,128)(2,1)S(1)} %add_convert_fusion.3.refs_0_), channel_id=1, source_target_pairs={{0,4},{4,12},{12,8},{8,0},{1,5},{5,13},{13,9},{9,1},{2,6},{6,14},{... | collective-permute-start | bytes 786440 | tf_op jit(solution)/shard_map/ppermute | solution.py:45
  198.6 10.5 %collective-permute-start.39 = (bf16[1088,128]{1,0:T(8,128)(2,1)S(1)}, bf16[1088,128]{1,0:T(8,128)(2,1)S(1)}, u32[]{:S(2)}, u32[]{:S(2)}) collective-permute-start(bf16[1088,128]{1,0:T(8,128)(2,1)S(1)} %add_convert_fusion.1), channel_id=1, source_target_pairs={{0,4},{4,12},{12,8},{8,0},{1,5},{5,13},{13,9},{9,1},{2,6},{6,14},{... | collective-permute-start | bytes 835592 | tf_op jit(solution)/shard_map/ppermute | solution.py:45
  198.6 13.9 %collective-permute-start.40 = (bf16[128,1024]{1,0:T(8,128)(2,1)S(1)}, bf16[128,1024]{1,0:T(8,128)(2,1)S(1)}, u32[]{:S(2)}, u32[]{:S(2)}) collective-permute-start(bf16[128,1024]{1,0:T(8,128)(2,1)S(1)} %collective-permute-done.38.refs_1_), channel_id=1, source_target_pairs={{0,4},{4,12},{12,8},{8,0},{1,5},{5,13},{13,9},{9,1},{2,6},{6,14},{... | collective-permute-start | bytes 786440 | tf_op jit(solution)/shard_map/ppermute | solution.py:45
  212.5 13.0 %collective-permute-start.41 = (bf16[1088,128]{1,0:T(8,128)(2,1)S(1)}, bf16[1088,128]{1,0:T(8,128)(2,1)S(1)}, u32[]{:S(2)}, u32[]{:S(2)}) collective-permute-start(bf16[1088,128]{1,0:T(8,128)(2,1)S(1)} %add_convert_fusion.refs_0_), channel_id=1, source_target_pairs={{0,4},{4,12},{12,8},{8,0},{1,5},{5,13},{13,9},{9,1},{2,6},{6,14},{... | collective-permute-start | bytes 835592 | tf_op jit(solution)/shard_map/ppermute | solution.py:45
  212.5 13.0 %collective-permute-start.42 = (bf16[128,1024]{1,0:T(8,128)(2,1)S(1)}, bf16[128,1024]{1,0:T(8,128)(2,1)S(1)}, u32[]{:S(2)}, u32[]{:S(2)}) collective-permute-start(bf16[128,1024]{1,0:T(8,128)(2,1)S(1)} %collective-permute-done.40.refs_2_), channel_id=1, source_target_pairs={{0,4},{4,12},{12,8},{8,0},{1,5},{5,13},{13,9},{9,1},{2,6},{6,14},{... | collective-permute-start | bytes 786440 | tf_op jit(solution)/shard_map/ppermute | solution.py:45
  234.0 10.2 %collective-permute-start.45 = (bf16[1088,128]{1,0:T(8,128)(2,1)S(1)}, bf16[1088,128]{1,0:T(8,128)(2,1)S(1)}, u32[]{:S(2)}, u32[]{:S(2)}) collective-permute-start(bf16[1088,128]{1,0:T(8,128)(2,1)S(1)} %add_convert_fusion.refs_0_), channel_id=1, source_target_pairs={{0,1},{1,0},{2,3},{3,2},{4,5},{5,4},{6,7},{7,6},{8,9},{9,8},{10,11... | collective-permute-start | bytes 835592 | tf_op jit(solution)/shard_map/ppermute | solution.py:49
  (62 other events, 686.7 us)

commit v6 on v5

--- a/solution.py
+++ b/solution.py
@@ -442,7 +442,7 @@
         scratch=[pltpu.SemaphoreType.DMA((count,))],
         specs=[anywhere] * count,
         out_specs=(anywhere,),
-        limit=60,
+        limit=4,
     )
     got = swap(send, "sub")
     moving = call(
@@ -453,7 +453,7 @@
         scratch=[pltpu.SemaphoreType.DMA((2 * count,))],
         specs=[anywhere] * (count + 1),
         out_specs=(anywhere,) * count,
-        limit=60,
+        limit=4,
     )
     return list(moving), got
 
@@ -596,11 +596,11 @@
     up_in_parts = call(
         up_in_kernel,
         "up_in",
-        [after(low_grad, seen[1]), swap(low_grad, "sub"), normed_t, up_out_term, down_in_term],
+        [after(low_grad, seen[2]), swap(low_grad, "sub"), normed_t, up_out_term, down_in_term],
         [shape((half // n + extra, rank))] * n,
         flops=4 * rows * half * rank,
     )
-    up_in_blocks = ring_all(up_in_parts, [], seen[1:])
+    up_in_blocks = ring_all(up_in_parts, [])
 
     anywhere = pl.BlockSpec(memory_space=pl.ANY)
     (down_out_gradient,) = call(

time: 247 us -> 189 us (0.77)
  Pallas kernels: 85.4 us -> 23.8 us
  waiting for transfers between devices: 107 us -> 120 us
  starting transfers between devices: 42.9 us -> 36.1 us
  local copies, waits for them, and re-layouts: 9.84 us -> 6.89 us
    pallas_call x16, Pallas kernels: 85.4 us -> 23.8 us  [call(): pl.pallas_call(kernel, out_shape=tuple(out_shape), in_specs=specs or [vme...]
    ppermute x21, waiting for transfers between devices: 72.1 us -> 87.9 us  [ring_step(): lax.ppermute(x, 'dp', [(ring_at(i, n), ring_at((i + 1) % n, n)) for i in...]
    ppermute x21, starting transfers between devices: 23.9 us -> 13.2 us  [ring_step(): lax.ppermute(x, 'dp', [(ring_at(i, n), ring_at((i + 1) % n, n)) for i in...]
    unnamed x67 -> x37, local copies, waits for them, and re-layouts: 8.64 us -> 6.51 us
  transfers between devices with their start and end apart: 53 -> 53, of which waited for: 31 -> 31; matrix products, arithmetic and copies ran while one was open for 1% -> 0% of each run, Pallas kernels for 17% -> 8%
where the time goes in v6:
time: 189 us; the launch traced here: 188 us
  waiting for transfers between devices  120 us (63%)
  starting transfers between devices  36.1 us (19%)
  Pallas kernels  23.8 us (13%)
  local copies, waits for them, and re-layouts  6.89 us (4%)
    ppermute x21, waiting for transfers between devices, ring_step(): lax.ppermute(x, 'dp', [(ring_at(i, n), ring_at((i + 1) % n, n)) for i in...  87.9 us
    pallas_call x16, Pallas kernels, call(): pl.pallas_call(kernel, out_shape=tuple(out_shape), in_specs=specs or [vme...  23.8 us
    ppermute x26, waiting for transfers between devices, swap(): return lax.ppermute(x, axis, [(0, 1), (1, 0)])  19.6 us
    ppermute x26, starting transfers between devices, swap(): return lax.ppermute(x, axis, [(0, 1), (1, 0)])  15 us
    ppermute x21, starting transfers between devices, ring_step(): lax.ppermute(x, 'dp', [(ring_at(i, n), ring_at((i + 1) % n, n)) for i in...  13.2 us
    ppermute x6, waiting for transfers between devices, others(): lax.ppermute(x, axis, [(i, (i + k) % n) for i in range(n)])  12.4 us
    ppermute x6, starting transfers between devices, others(): lax.ppermute(x, axis, [(i, (i + k) % n) for i in range(n)])  7.93 us
    unnamed x37, local copies, waits for them, and re-layouts  6.51 us
  transfers between devices with their start and end apart: 53, of which 31 were waited for; matrix products, arithmetic and copies ran while one was open for 0% of the time, Pallas kernels for 8%

profile of v6, /device:TPU:0, one launch (start us, length us, event | category | flops | bytes accessed | tf_op | source)
XLA Modules:
  0.0 188.5 jit_solution(15268877322153883076)
XLA Ops:
  5.5 3.0 %collective-permute-start.1 = (bf16[32,16,256]{2,1,0:T(8,128)(2,1)S(1)}, bf16[32,16,256]{2,1,0:T(8,128)(2,1)S(1)}, u32[]{:S(2)}, u32[]{:S(2)}) collective-permute-start(bf16[32,16,256]{2,1,0:T(8,128)(2,1)S(1)} %get-tuple-element.48), channel_id=1, source_target_pairs={{0,4},{4,12},{12,8},{8,0},{1,5},{5,13},{13,9},{9,1},{2,6},{6,14},{... | collective-permute-start | bytes 786440 | tf_op jit(solution)/shard_map/ppermute | solution.py:45
  8.5 2.6 %collective-permute-start.2 = (bf16[32,16,256]{2,1,0:T(8,128)(2,1)S(1)}, bf16[32,16,256]{2,1,0:T(8,128)(2,1)S(1)}, u32[]{:S(2)}, u32[]{:S(2)}) collective-permute-start(bf16[32,16,256]{2,1,0:T(8,128)(2,1)S(1)} %get-tuple-element.49), channel_id=1, source_target_pairs={{0,4},{4,12},{12,8},{8,0},{1,5},{5,13},{13,9},{9,1},{2,6},{6,14},{... | collective-permute-start | bytes 786440 | tf_op jit(solution)/shard_map/ppermute | solution.py:45
  15.5 4.9 %cotangent.1 = (bf16[256,4096]{1,0:T(8,128)(2,1)S(1)}, bf16[256,4096]{1,0:T(8,128)(2,1)S(1)}, f32[256,128]{1,0:T(8,128)S(1)}, f32[256,128]{1,0:T(8,128)S(1)}) custom-call(bf16[256,8192]{1,0:T(8,128)(2,1)S(1)} %copy-done.6, bf16[256,8192]{1,0:T(8,128)(2,1)S(1)} %copy-done, s32[1,2]{1,0:T(1,128)S(1)} %copy-done.10, s32[1,256]{1,0:T(1,128)S(1)} %bitcast.9, ...), custom_call_target="tpu_custom_call" | custom-call | flops 536870912 | bytes 14943240 | tf_op jit(solution)/shard_map/cotangent/pallas_call | solution.py:87
  22.0 3.4 %collective-permute-done.3.refs_5_ = f32[256,128]{1,0:T(8,128)S(1)} collective-permute-done((f32[256,128]{1,0:T(8,128)S(1)}, f32[256,128]{1,0:T(8,128)S(1)}, u32[]{:S(2)}, u32[]{:S(2)}) %collective-permute-start.3) | collective-permute-done | bytes 131104 | tf_op jit(solution)/shard_map/ppermute | solution.py:54
  30.9 6.0 %collective-permute-done.5.refs_6_ = bf16[32,16,256]{2,1,0:T(8,128)(2,1)S(1)} collective-permute-done((bf16[32,16,256]{2,1,0:T(8,128)(2,1)S(1)}, bf16[32,16,256]{2,1,0:T(8,128)(2,1)S(1)}, u32[]{:S(2)}, u32[]{:S(2)}) %collective-permute-start.5) | collective-permute-done | bytes 262176 | tf_op jit(solution)/shard_map/ppermute | solution.py:49
  41.7 2.9 %collective-permute-done.8.refs_7_ = bf16[32,16,256]{2,1,0:T(8,128)(2,1)S(1)} collective-permute-done((bf16[32,16,256]{2,1,0:T(8,128)(2,1)S(1)}, bf16[32,16,256]{2,1,0:T(8,128)(2,1)S(1)}, u32[]{:S(2)}, u32[]{:S(2)}) %collective-permute-start.8) | collective-permute-done | bytes 262176 | tf_op jit(solution)/shard_map/ppermute | solution.py:45
  46.6 8.1 %collective-permute-done.10.refs_9_ = bf16[32,16,256]{2,1,0:T(8,128)(2,1)S(1)} collective-permute-done((bf16[32,16,256]{2,1,0:T(8,128)(2,1)S(1)}, bf16[32,16,256]{2,1,0:T(8,128)(2,1)S(1)}, u32[]{:S(2)}, u32[]{:S(2)}) %collective-permute-start.10) | collective-permute-done | bytes 262176 | tf_op jit(solution)/shard_map/ppermute | solution.py:45
  58.9 3.8 %collective-permute-done.11.refs_10_ = bf16[32,16,256]{2,1,0:T(8,128)(2,1)S(1)} collective-permute-done((bf16[32,16,256]{2,1,0:T(8,128)(2,1)S(1)}, bf16[32,16,256]{2,1,0:T(8,128)(2,1)S(1)}, u32[]{:S(2)}, u32[]{:S(2)}) %collective-permute-start.11) | collective-permute-done | bytes 262176 | tf_op jit(solution)/shard_map/ppermute | solution.py:49
  68.7 3.6 %collective-permute-done.15.refs_10_ = bf16[32,16,256]{2,1,0:T(8,128)(2,1)S(1)} collective-permute-done((bf16[32,16,256]{2,1,0:T(8,128)(2,1)S(1)}, bf16[32,16,256]{2,1,0:T(8,128)(2,1)S(1)}, u32[]{:S(2)}, u32[]{:S(2)}) %collective-permute-start.15) | collective-permute-done | bytes 262176 | tf_op jit(solution)/shard_map/ppermute | solution.py:49
  80.7 2.8 %collective-permute-done.18.refs_5_ = bf16[256,256]{1,0:T(8,128)(2,1)S(1)} collective-permute-done((bf16[256,256]{1,0:T(8,128)(2,1)S(1)}, bf16[256,256]{1,0:T(8,128)(2,1)S(1)}, u32[]{:S(2)}, u32[]{:S(2)}) %collective-permute-start.18) | collective-permute-done | bytes 131104 | tf_op jit(solution)/shard_map/ppermute | solution.py:54
  89.3 7.3 %collective-permute-done.29.refs_9_ = bf16[32,32,128]{2,1,0:T(8,128)(2,1)S(1)} collective-permute-done((bf16[32,32,128]{2,1,0:T(8,128)(2,1)S(1)}, bf16[32,32,128]{2,1,0:T(8,128)(2,1)S(1)}, u32[]{:S(2)}, u32[]{:S(2)}) %collective-permute-start.29) | collective-permute-done | bytes 262176 | tf_op jit(solution)/shard_map/ppermute | solution.py:45
  98.3 2.9 %collective-permute-done.23 = bf16[128,1024]{1,0:T(8,128)(2,1)S(1)} collective-permute-done((bf16[128,1024]{1,0:T(8,128)(2,1)S(1)}, bf16[128,1024]{1,0:T(8,128)(2,1)S(1)}, u32[]{:S(2)}, u32[]{:S(2)}) %collective-permute-start.23) | collective-permute-done | bytes 262176 | tf_op jit(solution)/shard_map/ppermute | solution.py:45
  105.4 4.3 %collective-permute-done.33 = bf16[128,1024]{1,0:T(8,128)(2,1)S(1)} collective-permute-done((bf16[128,1024]{1,0:T(8,128)(2,1)S(1)}, bf16[128,1024]{1,0:T(8,128)(2,1)S(1)}, u32[]{:S(2)}, u32[]{:S(2)}) %collective-permute-start.33) | collective-permute-done | bytes 262176 | tf_op jit(solution)/shard_map/ppermute | solution.py:45
  111.0 3.9 %collective-permute-done.32.refs_4_ = bf16[256,256]{1,0:T(8,128)(2,1)S(1)} collective-permute-done((bf16[256,256]{1,0:T(8,128)(2,1)S(1)}, bf16[256,256]{1,0:T(8,128)(2,1)S(1)}, u32[]{:S(2)}, u32[]{:S(2)}) %collective-permute-start.32) | collective-permute-done | bytes 131104 | tf_op jit(solution)/shard_map/ppermute | solution.py:54
  117.2 2.9 %up_in.1 = (bf16[1088,128]{1,0:T(8,128)(2,1)S(1)}, bf16[1088,128]{1,0:T(8,128)(2,1)S(1)}, bf16[1088,128]{1,0:T(8,128)(2,1)S(1)}, bf16[1088,128]{1,0:T(8,128)(2,1)S(1)}) custom-call(bf16[256,128]{1,0:T(8,128)(2,1)S(1)} %get-tuple-element.80.low, bf16[256,128]{1,0:T(8,128)(2,1)S(1)} %collective-permute-done.35.low_got, ...), custom_call_target="tpu_custom_call" | custom-call | flops 536870912 | bytes 5505024 | tf_op jit(solution)/shard_map/up_in/pallas_call | solution.py:87
  121.0 8.8 %collective-permute-done.36 = bf16[1088,128]{1,0:T(8,128)(2,1)S(1)} collective-permute-done((bf16[1088,128]{1,0:T(8,128)(2,1)S(1)}, bf16[1088,128]{1,0:T(8,128)(2,1)S(1)}, u32[]{:S(2)}, u32[]{:S(2)}) %collective-permute-start.36) | collective-permute-done | bytes 278560 | tf_op jit(solution)/shard_map/ppermute | solution.py:45
  130.2 8.5 %collective-permute-done.37 = bf16[1088,128]{1,0:T(8,128)(2,1)S(1)} collective-permute-done((bf16[1088,128]{1,0:T(8,128)(2,1)S(1)}, bf16[1088,128]{1,0:T(8,128)(2,1)S(1)}, u32[]{:S(2)}, u32[]{:S(2)}) %collective-permute-start.37) | collective-permute-done | bytes 278560 | tf_op jit(solution)/shard_map/ppermute | solution.py:45
  138.8 7.8 %collective-permute-done.38 = bf16[1088,128]{1,0:T(8,128)(2,1)S(1)} collective-permute-done((bf16[1088,128]{1,0:T(8,128)(2,1)S(1)}, bf16[1088,128]{1,0:T(8,128)(2,1)S(1)}, u32[]{:S(2)}, u32[]{:S(2)}) %collective-permute-start.38) | collective-permute-done | bytes 278560 | tf_op jit(solution)/shard_map/ppermute | solution.py:45
  146.9 3.4 %collective-permute-start.46 = (bf16[128,1024]{1,0:T(8,128)(2,1)S(1)}, bf16[128,1024]{1,0:T(8,128)(2,1)S(1)}, u32[]{:S(2)}, u32[]{:S(2)}) collective-permute-start(bf16[128,1024]{1,0:T(8,128)(2,1)S(1)} %add_convert_fusion.3.refs_0_), channel_id=1, source_target_pairs={{0,4},{4,12},{12,8},{8,0},{1,5},{5,13},{13,9},{9,1},{2,6},{6,14},{... | collective-permute-start | bytes 786440 | tf_op jit(solution)/shard_map/ppermute | solution.py:45
  150.4 6.9 %collective-permute-done.39.refs_1_ = bf16[1088,128]{1,0:T(8,128)(2,1)S(1)} collective-permute-done((bf16[1088,128]{1,0:T(8,128)(2,1)S(1)}, bf16[1088,128]{1,0:T(8,128)(2,1)S(1)}, u32[]{:S(2)}, u32[]{:S(2)}) %collective-permute-start.39) | collective-permute-done | bytes 278560 | tf_op jit(solution)/shard_map/ppermute | solution.py:45
  157.4 5.5 %collective-permute-done.46.refs_1_ = bf16[128,1024]{1,0:T(8,128)(2,1)S(1)} collective-permute-done((bf16[128,1024]{1,0:T(8,128)(2,1)S(1)}, bf16[128,1024]{1,0:T(8,128)(2,1)S(1)}, u32[]{:S(2)}, u32[]{:S(2)}) %collective-permute-start.46) | collective-permute-done | bytes 262176 | tf_op jit(solution)/shard_map/ppermute | solution.py:45
  163.0 5.8 %collective-permute-done.40.refs_2_ = bf16[1088,128]{1,0:T(8,128)(2,1)S(1)} collective-permute-done((bf16[1088,128]{1,0:T(8,128)(2,1)S(1)}, bf16[1088,128]{1,0:T(8,128)(2,1)S(1)}, u32[]{:S(2)}, u32[]{:S(2)}) %collective-permute-start.40) | collective-permute-done | bytes 278560 | tf_op jit(solution)/shard_map/ppermute | solution.py:45
  169.5 5.0 %collective-permute-done.47.refs_2_ = bf16[128,1024]{1,0:T(8,128)(2,1)S(1)} collective-permute-done((bf16[128,1024]{1,0:T(8,128)(2,1)S(1)}, bf16[128,1024]{1,0:T(8,128)(2,1)S(1)}, u32[]{:S(2)}, u32[]{:S(2)}) %collective-permute-start.47) | collective-permute-done | bytes 262176 | tf_op jit(solution)/shard_map/ppermute | solution.py:45
  175.2 7.3 %collective-permute-done.48.refs_3_ = bf16[128,1024]{1,0:T(8,128)(2,1)S(1)} collective-permute-done((bf16[128,1024]{1,0:T(8,128)(2,1)S(1)}, bf16[128,1024]{1,0:T(8,128)(2,1)S(1)}, u32[]{:S(2)}, u32[]{:S(2)}) %collective-permute-start.48) | collective-permute-done | bytes 262176 | tf_op jit(solution)/shard_map/ppermute | solution.py:45
  (147 shorter events, 65.7 us)
Async XLA Ops:
  5.5 16.5 %collective-permute-start.1 = (bf16[32,16,256]{2,1,0:T(8,128)(2,1)S(1)}, bf16[32,16,256]{2,1,0:T(8,128)(2,1)S(1)}, u32[]{:S(2)}, u32[]{:S(2)}) collective-permute-start(bf16[32,16,256]{2,1,0:T(8,128)(2,1)S(1)} %get-tuple-element.48), channel_id=1, source_target_pairs={{0,4},{4,12},{12,8},{8,0},{1,5},{5,13},{13,9},{9,1},{2,6},{6,14},{... | collective-permute-start | bytes 786440 | tf_op jit(solution)/shard_map/ppermute | solution.py:45
  8.5 13.5 %collective-permute-start.2 = (bf16[32,16,256]{2,1,0:T(8,128)(2,1)S(1)}, bf16[32,16,256]{2,1,0:T(8,128)(2,1)S(1)}, u32[]{:S(2)}, u32[]{:S(2)}) collective-permute-start(bf16[32,16,256]{2,1,0:T(8,128)(2,1)S(1)} %get-tuple-element.49), channel_id=1, source_target_pairs={{0,4},{4,12},{12,8},{8,0},{1,5},{5,13},{13,9},{9,1},{2,6},{6,14},{... | collective-permute-start | bytes 786440 | tf_op jit(solution)/shard_map/ppermute | solution.py:45
  28.0 36.4 %collective-permute-start.4 = (bf16[256,4096]{1,0:T(8,128)(2,1)S(1)}, bf16[256,4096]{1,0:T(8,128)(2,1)S(1)}, u32[]{:S(2)}, u32[]{:S(2)}) collective-permute-start(bf16[256,4096]{1,0:T(8,128)(2,1)S(1)} %get-tuple-element.56), channel_id=1, source_target_pairs={{0,1},{1,0},{2,3},{3,2},{4,5},{5,4},{6,7},{7,6},{8,9},{9,8},{10,11... | collective-permute-start | bytes 6291464 | tf_op jit(solution)/shard_map/ppermute | solution.py:49
  28.1 40.6 %collective-permute-start.22 = (bf16[256,4096]{1,0:T(8,128)(2,1)S(1)}, bf16[256,4096]{1,0:T(8,128)(2,1)S(1)}, u32[]{:S(2)}, u32[]{:S(2)}) collective-permute-start(bf16[256,4096]{1,0:T(8,128)(2,1)S(1)} %get-tuple-element.68), channel_id=1, source_target_pairs={{0,1},{1,0},{2,3},{3,2},{4,5},{5,4},{6,7},{7,6},{8,9},{9,8},{10,11... | collective-permute-start | bytes 6291464 | tf_op jit(solution)/shard_map/ppermute | solution.py:49
  30.1 10.1 %collective-permute-start.6 = (bf16[32,16,256]{2,1,0:T(8,128)(2,1)S(1)}, bf16[32,16,256]{2,1,0:T(8,128)(2,1)S(1)}, u32[]{:S(2)}, u32[]{:S(2)}) collective-permute-start(bf16[32,16,256]{2,1,0:T(8,128)(2,1)S(1)} %collective-permute-done.1.refs_5_), channel_id=1, source_target_pairs={{0,4},{4,12},{12,8},{8,0},{1,5},{5,13},{13,9},{9,1},{2,6},{6,14},{... | collective-permute-start | bytes 786440 | tf_op jit(solution)/shard_map/ppermute | solution.py:45
  30.6 14.1 %collective-permute-start.8 = (bf16[32,16,256]{2,1,0:T(8,128)(2,1)S(1)}, bf16[32,16,256]{2,1,0:T(8,128)(2,1)S(1)}, u32[]{:S(2)}, u32[]{:S(2)}) collective-permute-start(bf16[32,16,256]{2,1,0:T(8,128)(2,1)S(1)} %collective-permute-done.2.refs_5_), channel_id=1, source_target_pairs={{0,4},{4,12},{12,8},{8,0},{1,5},{5,13},{13,9},{9,1},{2,6},{6,14},{... | collective-permute-start | bytes 786440 | tf_op jit(solution)/shard_map/ppermute | solution.py:45
  44.6 10.1 %collective-permute-start.10 = (bf16[32,16,256]{2,1,0:T(8,128)(2,1)S(1)}, bf16[32,16,256]{2,1,0:T(8,128)(2,1)S(1)}, u32[]{:S(2)}, u32[]{:S(2)}) collective-permute-start(bf16[32,16,256]{2,1,0:T(8,128)(2,1)S(1)} %collective-permute-done.6.refs_7_), channel_id=1, source_target_pairs={{0,4},{4,12},{12,8},{8,0},{1,5},{5,13},{13,9},{9,1},{2,6},{6,14},{... | collective-permute-start | bytes 786440 | tf_op jit(solution)/shard_map/ppermute | solution.py:45
  44.8 11.6 %collective-permute-start.7 = (bf16[32,16,256]{2,1,0:T(8,128)(2,1)S(1)}, bf16[32,16,256]{2,1,0:T(8,128)(2,1)S(1)}, u32[]{:S(2)}, u32[]{:S(2)}) collective-permute-start(bf16[32,16,256]{2,1,0:T(8,128)(2,1)S(1)} %collective-permute-done.6.refs_7_), channel_id=1, source_target_pairs={{0,16},{16,0},{1,17},{17,1},{2,18},{18,2},{3,19},{19,3},{4,20},{20... | collective-permute-start | bytes 786440 | tf_op jit(solution)/shard_map/ppermute | solution.py:49
  46.6 11.7 %collective-permute-start.14 = (bf16[32,16,256]{2,1,0:T(8,128)(2,1)S(1)}, bf16[32,16,256]{2,1,0:T(8,128)(2,1)S(1)}, u32[]{:S(2)}, u32[]{:S(2)}) collective-permute-start(bf16[32,16,256]{2,1,0:T(8,128)(2,1)S(1)} %collective-permute-done.8.refs_7_), channel_id=1, source_target_pairs={{0,4},{4,12},{12,8},{8,0},{1,5},{5,13},{13,9},{9,1},{2,6},{6,14},{... | collective-permute-start | bytes 786440 | tf_op jit(solution)/shard_map/ppermute | solution.py:45
  56.4 11.5 %collective-permute-start.24 = (bf16[32,32,128]{2,1,0:T(8,128)(2,1)S(1)}, bf16[32,32,128]{2,1,0:T(8,128)(2,1)S(1)}, u32[]{:S(2)}, u32[]{:S(2)}) collective-permute-start(bf16[32,32,128]{2,1,0:T(8,128)(2,1)S(1)} %halves.3), channel_id=1, source_target_pairs={{0,1},{1,0},{2,3},{3,2},{4,5},{5,4},{6,7},{7,6},{8,9},{9,8},{10,11... | collective-permute-start | bytes 786440 | tf_op jit(solution)/shard_map/ppermute | solution.py:49
  58.3 10.4 %collective-permute-start.13 = (bf16[32,16,256]{2,1,0:T(8,128)(2,1)S(1)}, bf16[32,16,256]{2,1,0:T(8,128)(2,1)S(1)}, u32[]{:S(2)}, u32[]{:S(2)}) collective-permute-start(bf16[32,16,256]{2,1,0:T(8,128)(2,1)S(1)} %collective-permute-done.8.refs_7_), channel_id=1, source_target_pairs={{0,16},{16,0},{1,17},{17,1},{2,18},{18,2},{3,19},{19,3},{4,20},{20... | collective-permute-start | bytes 786440 | tf_op jit(solution)/shard_map/ppermute | solution.py:49
  62.7 9.7 %collective-permute-start.15 = (bf16[32,16,256]{2,1,0:T(8,128)(2,1)S(1)}, bf16[32,16,256]{2,1,0:T(8,128)(2,1)S(1)}, u32[]{:S(2)}, u32[]{:S(2)}) collective-permute-start(bf16[32,16,256]{2,1,0:T(8,128)(2,1)S(1)} %collective-permute-done.14.refs_9_), channel_id=1, source_target_pairs={{0,16},{16,0},{1,17},{17,1},{2,18},{18,2},{3,19},{19,3},{4,20},{20... | collective-permute-start | bytes 786440 | tf_op jit(solution)/shard_map/ppermute | solution.py:49
  68.7 9.3 %collective-permute-start.25 = (bf16[32,32,128]{2,1,0:T(8,128)(2,1)S(1)}, bf16[32,32,128]{2,1,0:T(8,128)(2,1)S(1)}, u32[]{:S(2)}, u32[]{:S(2)}) collective-permute-start(bf16[32,32,128]{2,1,0:T(8,128)(2,1)S(1)} %quarters.3), channel_id=1, source_target_pairs={{0,4},{4,12},{12,8},{8,0},{1,5},{5,13},{13,9},{9,1},{2,6},{6,14},{... | collective-permute-start | bytes 786440 | tf_op jit(solution)/shard_map/ppermute | solution.py:45
  86.5 10.1 %collective-permute-start.29 = (bf16[32,32,128]{2,1,0:T(8,128)(2,1)S(1)}, bf16[32,32,128]{2,1,0:T(8,128)(2,1)S(1)}, u32[]{:S(2)}, u32[]{:S(2)}) collective-permute-start(bf16[32,32,128]{2,1,0:T(8,128)(2,1)S(1)} %collective-permute-done.27.refs_7_), channel_id=1, source_target_pairs={{0,4},{4,12},{12,8},{8,0},{1,5},{5,13},{13,9},{9,1},{2,6},{6,14},{... | collective-permute-start | bytes 786440 | tf_op jit(solution)/shard_map/ppermute | solution.py:45
  86.9 14.4 %collective-permute-start.23 = (bf16[128,1024]{1,0:T(8,128)(2,1)S(1)}, bf16[128,1024]{1,0:T(8,128)(2,1)S(1)}, u32[]{:S(2)}, u32[]{:S(2)}) collective-permute-start(bf16[128,1024]{1,0:T(8,128)(2,1)S(1)} %get-tuple-element.69), channel_id=1, source_target_pairs={{0,4},{4,12},{12,8},{8,0},{1,5},{5,13},{13,9},{9,1},{2,6},{6,14},{... | collective-permute-start | bytes 786440 | tf_op jit(solution)/shard_map/ppermute | solution.py:45
  87.7 13.7 %collective-permute-start.28 = (bf16[32,32,128]{2,1,0:T(8,128)(2,1)S(1)}, bf16[32,32,128]{2,1,0:T(8,128)(2,1)S(1)}, u32[]{:S(2)}, u32[]{:S(2)}) collective-permute-start(bf16[32,32,128]{2,1,0:T(8,128)(2,1)S(1)} %collective-permute-done.27.refs_7_), channel_id=1, source_target_pairs={{0,16},{16,0},{1,17},{17,1},{2,18},{18,2},{3,19},{19,3},{4,20},{20... | collective-permute-start | bytes 786440 | tf_op jit(solution)/shard_map/ppermute | solution.py:49
  120.1 9.6 %collective-permute-start.36 = (bf16[1088,128]{1,0:T(8,128)(2,1)S(1)}, bf16[1088,128]{1,0:T(8,128)(2,1)S(1)}, u32[]{:S(2)}, u32[]{:S(2)}) collective-permute-start(bf16[1088,128]{1,0:T(8,128)(2,1)S(1)} %get-tuple-element.84), channel_id=1, source_target_pairs={{0,4},{4,12},{12,8},{8,0},{1,5},{5,13},{13,9},{9,1},{2,6},{6,14},{... | collective-permute-start | bytes 835592 | tf_op jit(solution)/shard_map/ppermute | solution.py:45
  146.7 10.5 %collective-permute-start.39 = (bf16[1088,128]{1,0:T(8,128)(2,1)S(1)}, bf16[1088,128]{1,0:T(8,128)(2,1)S(1)}, u32[]{:S(2)}, u32[]{:S(2)}) collective-permute-start(bf16[1088,128]{1,0:T(8,128)(2,1)S(1)} %add_convert_fusion.refs_0_), channel_id=1, source_target_pairs={{0,4},{4,12},{12,8},{8,0},{1,5},{5,13},{13,9},{9,1},{2,6},{6,14},{... | collective-permute-start | bytes 835592 | tf_op jit(solution)/shard_map/ppermute | solution.py:45
  146.9 15.9 %collective-permute-start.46 = (bf16[128,1024]{1,0:T(8,128)(2,1)S(1)}, bf16[128,1024]{1,0:T(8,128)(2,1)S(1)}, u32[]{:S(2)}, u32[]{:S(2)}) collective-permute-start(bf16[128,1024]{1,0:T(8,128)(2,1)S(1)} %add_convert_fusion.3.refs_0_), channel_id=1, source_target_pairs={{0,4},{4,12},{12,8},{8,0},{1,5},{5,13},{13,9},{9,1},{2,6},{6,14},{... | collective-permute-start | bytes 786440 | tf_op jit(solution)/shard_map/ppermute | solution.py:45
  157.3 11.6 %collective-permute-start.40 = (bf16[1088,128]{1,0:T(8,128)(2,1)S(1)}, bf16[1088,128]{1,0:T(8,128)(2,1)S(1)}, u32[]{:S(2)}, u32[]{:S(2)}) collective-permute-start(bf16[1088,128]{1,0:T(8,128)(2,1)S(1)} %collective-permute-done.39.refs_1_), channel_id=1, source_target_pairs={{0,4},{4,12},{12,8},{8,0},{1,5},{5,13},{13,9},{9,1},{2,6},{6,14},{... | collective-permute-start | bytes 835592 | tf_op jit(solution)/shard_map/ppermute | solution.py:45
  162.9 11.6 %collective-permute-start.47 = (bf16[128,1024]{1,0:T(8,128)(2,1)S(1)}, bf16[128,1024]{1,0:T(8,128)(2,1)S(1)}, u32[]{:S(2)}, u32[]{:S(2)}) collective-permute-start(bf16[128,1024]{1,0:T(8,128)(2,1)S(1)} %collective-permute-done.46.refs_1_), channel_id=1, source_target_pairs={{0,4},{4,12},{12,8},{8,0},{1,5},{5,13},{13,9},{9,1},{2,6},{6,14},{... | collective-permute-start | bytes 786440 | tf_op jit(solution)/shard_map/ppermute | solution.py:45
  168.8 13.6 %collective-permute-start.41 = (bf16[1088,128]{1,0:T(8,128)(2,1)S(1)}, bf16[1088,128]{1,0:T(8,128)(2,1)S(1)}, u32[]{:S(2)}, u32[]{:S(2)}) collective-permute-start(bf16[1088,128]{1,0:T(8,128)(2,1)S(1)} %collective-permute-done.40.refs_2_), channel_id=1, source_target_pairs={{0,4},{4,12},{12,8},{8,0},{1,5},{5,13},{13,9},{9,1},{2,6},{6,14},{... | collective-permute-start | bytes 835592 | tf_op jit(solution)/shard_map/ppermute | solution.py:45
  174.6 11.6 %collective-permute-start.42 = (bf16[1088,128]{1,0:T(8,128)(2,1)S(1)}, bf16[1088,128]{1,0:T(8,128)(2,1)S(1)}, u32[]{:S(2)}, u32[]{:S(2)}) collective-permute-start(bf16[1088,128]{1,0:T(8,128)(2,1)S(1)} %add_convert_fusion.refs_0_), channel_id=1, source_target_pairs={{0,1},{1,0},{2,3},{3,2},{4,5},{5,4},{6,7},{7,6},{8,9},{9,8},{10,11... | collective-permute-start | bytes 835592 | tf_op jit(solution)/shard_map/ppermute | solution.py:49
  175.1 11.1 %collective-permute-start.43 = (bf16[1088,128]{1,0:T(8,128)(2,1)S(1)}, bf16[1088,128]{1,0:T(8,128)(2,1)S(1)}, u32[]{:S(2)}, u32[]{:S(2)}) collective-permute-start(bf16[1088,128]{1,0:T(8,128)(2,1)S(1)} %collective-permute-done.39.refs_1_), channel_id=1, source_target_pairs={{0,1},{1,0},{2,3},{3,2},{4,5},{5,4},{6,7},{7,6},{8,9},{9,8},{10,11... | collective-permute-start | bytes 835592 | tf_op jit(solution)/shard_map/ppermute | solution.py:49
  (47 other events, 445.6 us)

commit v7 on v6

--- a/solution.py
+++ b/solution.py
@@ -11,6 +11,7 @@
 EPS = 1e-05
 ROW_TILE = 16
 LANES = 128
+STREAMS = 2
 MIB = 1024 * 1024
 
 F32 = jnp.float32
@@ -62,21 +63,19 @@
     return sum(t.astype(F32) for t in terms).astype(BF16)
 
 
-def ring_all(parts, seen, gates=()):
+def ring_all(parts, streams):
     n = lax.axis_size("dp")
-
-    def step(x):
-        k = len(seen)
-        seen.append(ring_step(after(x, gates[k]) if k < len(gates) else x))
-        return seen[-1]
-
-    total = parts[0]
-    for part in parts[1:]:
-        total = add(step(total), part)
-    blocks = [total]
+    seen = []
+    totals = list(parts[:streams])
+    for k in range(1, n):
+        seen.append([ring_step(t) for t in totals])
+        totals = [add(t, p) for t, p in zip(seen[-1], parts[k * streams : (k + 1) * streams])]
+    blocks = list(totals)
     for _ in range(n - 1):
-        blocks.append(step(blocks[-1]))
-    return blocks, [swap(b, "sub") for b in blocks]
+        totals = [ring_step(t) for t in totals]
+        seen.append(totals)
+        blocks += totals
+    return blocks + [swap(b, "sub") for b in blocks], seen
 
 
 def call(kernel, name, args, out_shape, scratch=(), specs=None, limit=24, flops=0, out_specs=None):
@@ -91,7 +90,7 @@
         out_specs=out_specs or tuple([vmem] * len(out_shape)),
         scratch_shapes=list(scratch),
         compiler_params=pltpu.CompilerParams(vmem_limit_bytes=limit * MIB),
-        cost_estimate=pl.CostEstimate(flops=flops, bytes_accessed=moved, transcendentals=0),
+        cost_estimate=pl.CostEstimate(flops=0, bytes_accessed=0, transcendentals=0),
         name=name,
     )(*args)
 
@@ -100,16 +99,18 @@
     return jax.ShapeDtypeStruct(tuple(dims), dtype)
 
 
-def scaled_halves(wide, low_ref, cols, scaled, product, send_ref, own_ref):
+def scaled_halves(wide, low_ref, cols, scaled, product, send_ref, own_ref, arrive=None):
     half = send_ref.shape[1]
     step = half // 4
     sub = lax.axis_index("sub")
     low_ref[:, cols] = jnp.zeros((wide.shape[0], LANES), F32)
-    for which, out_ref in ((1 - sub, send_ref), (sub, own_ref)):
+    for n, (which, out_ref) in enumerate(((1 - sub, send_ref), (sub, own_ref))):
 
         @pl.loop(0, half // step)
-        def _(j, which=which, out_ref=out_ref):
+        def _(j, n=n, which=which, out_ref=out_ref):
             first = pl.multiple_of(which * half + j * step, step)
+            if arrive is not None:
+                arrive(n * (half // step) + j, first, step)
             parts = []
             for i in range(step // LANES):
                 tile = pl.ds(pl.multiple_of(first + i * LANES, LANES), LANES)
@@ -119,38 +120,55 @@
             low_ref[:, cols] += product(value, pl.ds(first, step))
 
 
+def column_copy(source, buffer, sems):
+    def copy(k, first, step):
+        at = pl.ds(first, step)
+        return pltpu.make_async_copy(source.at[:, at], buffer.at[:, at], sems.at[k])
+
+    return copy
+
+
+def square_kernel(tokens, square_ref, buffer, sems):
+    width = tokens.shape[1]
+    step = width // sems.shape[0]
+    copy = column_copy(tokens, buffer, sems)
+    for k in range(width // step):
+        copy(k, k * step, step).start()
+    squares = jnp.zeros(square_ref.shape, F32)
+    for k in range(width // step):
+        copy(k, k * step, step).wait()
+        for i in range(step // LANES):
+            at = k * step + i * LANES
+            squares = squares + jnp.square(buffer[:, at : at + LANES].astype(F32))
+    square_ref[...] = jnp.broadcast_to(jnp.sum(squares, axis=1, keepdims=True), square_ref.shape)
+
+
 def cotangent_kernel(
-    total, cotangent, tokens, lengths, slots, adapter, send_ref, own_ref, low_ref, square_ref
+    total, cotangent, lengths, slots, adapter, send_ref, own_ref, low_ref, buffer, sems
 ):
     rows, width = cotangent.shape
+    half = width // 2
+    step = half // 4
+    copy = column_copy(cotangent, buffer, sems)
+    sub = lax.axis_index("sub")
+    for k in range(8):
+        which = 1 - sub if k < 4 else sub
+        copy(k, pl.multiple_of(which * half + k % 4 * step, step), step).start()
     index = jnp.broadcast_to(slots[...], (LANES, rows))
     weight = jnp.zeros((LANES, rows), F32)
     for s in range(lengths.shape[1]):
         length = jnp.full((LANES, rows), lengths[0, s], jnp.int32).astype(F32)
         weight = weight + jnp.where(index == s, (rows // lengths.shape[1]) / length, 0.0)
     row = (weight * F32(1.0 / math.sqrt(total))).T
-
-    square_ref[...] = jnp.zeros_like(square_ref)
-
-    @pl.loop(0, width // (8 * LANES))
-    def _(j):
-        squares = square_ref[...]
-        for i in range(8):
-            tile = pl.ds(pl.multiple_of((j * 8 + i) * LANES, LANES), LANES)
-            squares = squares + jnp.square(tokens[:, tile].astype(F32))
-        square_ref[...] = squares
-
-    square_ref[...] = jnp.broadcast_to(
-        jnp.sum(square_ref[...], axis=1, keepdims=True), square_ref.shape
-    )
     scaled_halves(
-        cotangent,
+        buffer,
         low_ref,
         slice(None),
         lambda tile, cols: tile * row,
         lambda value, cols: contract_dims(value, adapter[:, cols], 1, 1),
         send_ref,
         own_ref,
+        lambda k, first, step: copy(k, first, step).wait(),
     )
 
 
@@ -197,16 +215,18 @@
         store(b, place * 2 + sub, codes[sub * blocks + b])
         store(b, place * 2 + 1 - sub, got[first_got + b])
 
+    streams = len(moved) // (2 * (n - 1))
+    size = quarter // streams
     for k in range(n - 1):
         there = ring_at(lax.rem(pos - k - 1 + n, n), n)
-        for which in range(2):
-            piece = moved[2 * k + which]
-            start = (grp if which == 0 else 1 - grp) * quarter
-
-            @pl.loop(0, quarter, unroll=4)
+        for i in range(2 * streams):
+            piece = moved[2 * streams * k + i]
+            start = (grp if i % 2 == 0 else 1 - grp) * quarter + i // 2 * size
+
+            @pl.loop(0, size, unroll=4)
             def _(b, piece=piece, start=start, there=there):
                 store(start + b, there * 2 + sub, piece[b])
-                store(start + b, there * 2 + 1 - sub, piece[quarter + b])
+                store(start + b, there * 2 + 1 - sub, piece[size + b])
 
 
 def front_kernel(first_got, own, got, scale, codes, codes_got, *refs):
@@ -315,27 +335,28 @@
     own_units(ADAPTER_SCALE * dot(low_up_t, up_grad), up_out_term, 1)
 
 
-def down_out_kernel(low, low_got, grad, grad_got, *out_refs):
-    n = len(out_refs)
+def down_out_kernel(n, low, low_got, grad, grad_got, *out_refs):
     pos = ring_position()
+    streams = len(out_refs) // n
     low_t = jnp.concatenate([low[...], low_got[...]], axis=0).astype(F32).T.astype(BF16)
     rows = low.shape[0]
     for k, ref in enumerate(out_refs):
         size = ref.shape[1]
-        at = pl.ds(pl.multiple_of(lax.rem(pos - 1 - k + 2 * n, n) * size, size), size)
+        block = lax.rem(pos - 1 - k // streams + 2 * n, n) * streams + k % streams
+        at = pl.ds(pl.multiple_of(block * size, size), size)
         ref[...] = (
             dot(low_t[:, :rows], grad[:, at]) + dot(low_t[:, rows:], grad_got[:, at])
         ).astype(BF16)
 
 
-def up_in_kernel(low, low_got, normed_t, up_out_term, down_in_term, *out_refs):
-    n = len(out_refs)
+def up_in_kernel(n, low, low_got, normed_t, up_out_term, down_in_term, *out_refs):
     pos = ring_position()
-    size = normed_t.shape[0] // n
+    streams = len(out_refs) // n
+    size = normed_t.shape[0] // len(out_refs)
     extra = out_refs[0].shape[0] - size
     both = jnp.concatenate([low[...], low_got[...]], axis=0)
     for k, ref in enumerate(out_refs):
-        block = lax.rem(pos - 1 - k + 2 * n, n)
+        block = lax.rem(pos - 1 - k // streams + 2 * n, n) * streams + k % streams
         at = pl.ds(pl.multiple_of(block * size, size), size)
         ref[pl.ds(0, size), :] = dot(normed_t[at, :], both).astype(BF16)
         per = up_out_term.shape[0] // extra
@@ -358,36 +379,39 @@
 
 
 def down_out_place_kernel(n, *refs):
-    pieces, out_ref, sems = refs[: 2 * n], refs[2 * n], refs[2 * n + 1]
+    pieces, (out_ref, sems) = refs[:-2], refs[-2:]
     pos, sub = ring_position(), lax.axis_index("sub")
+    per_core = len(pieces) // 2
+    streams = per_core // n
     copies = []
     for i, piece in enumerate(pieces):
-        half = sub if i < n else 1 - sub
-        block = lax.rem(pos - i % n + n, n)
+        half = sub if i < per_core else 1 - sub
+        block = lax.rem(pos - i % per_core // streams + n, n) * streams + i % streams
         size = piece.shape[1]
-        at = pl.ds(pl.multiple_of((half * n + block) * size, size), size)
+        at = pl.ds(pl.multiple_of((half * per_core + block) * size, size), size)
         copies.append(pltpu.make_async_copy(piece, out_ref.at[:, at], sems.at[i]))
     copy_all(copies)
 
 
 def up_in_place_kernel(n, *refs):
-    pieces = refs[: 2 * n]
-    out_ref, up_out_ref, down_in_ref, small, sems = refs[2 * n :]
+    pieces, (out_ref, up_out_ref, down_in_ref, small, sems) = refs[:-5], refs[-5:]
     pos, sub = ring_position(), lax.axis_index("sub")
-    size = out_ref.shape[0] // (2 * n)
+    per_core = len(pieces) // 2
+    streams = per_core // n
+    size = out_ref.shape[0] // len(pieces)
     extra = pieces[0].shape[0] - size
     copies = []
     for i, piece in enumerate(pieces):
-        half = sub if i < n else 1 - sub
-        block = lax.rem(pos - i % n + n, n)
-        at = pl.ds(pl.multiple_of((half * n + block) * size, size), size)
+        half = sub if i < per_core else 1 - sub
+        block = lax.rem(pos - i % per_core // streams + n, n) * streams + i % streams
+        at = pl.ds(pl.multiple_of((half * per_core + block) * size, size), size)
         copies.append(
             pltpu.make_async_copy(piece.at[pl.ds(0, size), :], out_ref.at[at, :], sems.at[2 * i])
         )
         at = pl.ds(pl.multiple_of(block * extra, extra), extra)
         copies.append(
             pltpu.make_async_copy(
-                piece.at[pl.ds(size, extra), :], small.at[i // n, at, :], sems.at[2 * i + 1]
+                piece.at[pl.ds(size, extra), :], small.at[i // per_core, at, :], sems.at[2 * i + 1]
             )
         )
     copy_all(copies)
@@ -411,26 +435,26 @@
     )
 
 
-def quarter_kernel(*refs):
-    count = (len(refs) - 2) // 2
+def quarter_kernel(count, *refs):
     sources, got, out_refs, sems = refs[:count], refs[count], refs[count + 1 : -1], refs[-1]
+    streams = len(out_refs) // count
     sub, grp = lax.axis_index("sub"), lax.axis_index("grp")
     half = sources[0].shape[0] // 2
     quarter = half // 2
     copies = []
-    for i, (ref, out_ref) in enumerate(zip(sources, out_refs)):
-        own = ref.at[pl.ds(sub * half + grp * quarter, quarter)]
-        theirs = got.at[pl.ds(i * half + grp * quarter, quarter)]
+    size = quarter // streams
+    for i, out_ref in enumerate(out_refs):
+        first = grp * quarter + i % streams * size
+        own = sources[i // streams].at[pl.ds(sub * half + first, size)]
+        theirs = got.at[pl.ds(i // streams * half + first, size)]
         for k, source in enumerate((own, theirs)):
             copies.append(
-                pltpu.make_async_copy(
-                    source, out_ref.at[pl.ds(k * quarter, quarter)], sems.at[2 * i + k]
-                )
+                pltpu.make_async_copy(source, out_ref.at[pl.ds(k * size, size)], sems.at[2 * i + k])
             )
     copy_all(copies)
 
 
-def start_shards(codes):
+def start_shards(codes, streams):
     blocks, rows, units = codes[0].shape
     count = len(codes)
     anywhere = pl.BlockSpec(memory_space=pl.ANY)
@@ -446,13 +470,13 @@
     )
     got = swap(send, "sub")
     moving = call(
-        quarter_kernel,
+        lambda *refs: quarter_kernel(count, *refs),
         "quarters",
         [*codes, got],
-        [shape((blocks // 2, rows, units))] * count,
-        scratch=[pltpu.SemaphoreType.DMA((2 * count,))],
+        [shape((blocks // 2 // streams, rows, units))] * (count * streams),
+        scratch=[pltpu.SemaphoreType.DMA((2 * count * streams,))],
         specs=[anywhere] * (count + 1),
-        out_specs=(anywhere,) * count,
+        out_specs=(anywhere,) * (count * streams),
         limit=4,
     )
     return list(moving), got
@@ -484,7 +508,7 @@
     n = lax.axis_size("dp")
     more = lax.axis_size("mp") - 1
 
-    (gate_moving, up_moving), front_got = start_shards([gate_codes, up_codes])
+    (gate_moving, up_moving), front_got = start_shards([gate_codes, up_codes], 1)
     ring, crossed = [], []
 
     def step(moving, *done):
@@ -496,36 +520,44 @@
 
     vmem = pl.BlockSpec(memory_space=pltpu.VMEM)
     smem = pl.BlockSpec(memory_space=pltpu.SMEM)
-    lengths = after(sequence_length_list, gate_moving, up_moving)
-    grad_send, grad, low_out, squares = call(
+    hbm = pl.BlockSpec(memory_space=pltpu.HBM)
+    buffers = [pltpu.VMEM((rows, local_width), BF16), pltpu.SemaphoreType.DMA((8,))]
+    (squares,) = call(
+        square_kernel, "squares", [tokens], [shape((rows, LANES), F32)],
+        scratch=buffers, specs=[hbm], limit=16,
+    )
+    squares_more = others(squares, "mp")
+    lengths = after(sequence_length_list, gate_moving, up_moving, squares)
+    grad_send, grad, low_out = call(
         lambda *refs: cotangent_kernel(rows * n * lax.axis_size("sub"), *refs),
         "cotangent",
-        [cotangent, tokens, lengths, slot_sequence_index[None, :], down_adapter_out],
-        [shape((rows, half))] * 2 + [shape((rows, rank), F32), shape((rows, LANES), F32)],
-        specs=[vmem, vmem, smem, vmem, vmem],
-        flops=2 * rows * local_width * rank,
-    )
-    squares_more = others(squares, "mp")
+        [cotangent, lengths, slot_sequence_index[None, :], down_adapter_out],
+        [shape((rows, half))] * 2 + [shape((rows, rank), F32)],
+        scratch=buffers,
+        specs=[hbm, smem, vmem, vmem],
+    )
     step(ring[0], ring[1], grad)
     step(ring[1], ring[0], grad)
     normed_send, normed, low = call(
         lambda *refs: token_kernel(total_width, *refs),
         "tokens",
-        [tokens, rms_norm_gain[None, :], up_adapter_in, low_out, after(squares, *ring[:2]), *squares_more],
+        [tokens, rms_norm_gain[None, :], up_adapter_in, low_out, squares, *squares_more],
         [shape((rows, half))] * 2 + [shape((rows, 2 * rank), F32)],
-        flops=2 * rows * local_width * rank,
     )
     grad_got = swap(grad_send, "sub")
     normed_got = swap(normed_send, "sub")
     low_more = others(low, "mp")
-    step(ring[2], ring[3], normed, *crossed[:2])
-    step(ring[3], ring[2], normed, *crossed[:2])
-    down_turned = jnp.swapaxes(after(down_codes, *ring[2:4]), 0, 1)
-    (down_moving,), down_got = start_shards([down_turned])
+    down_turned = jnp.swapaxes(after(down_codes, *ring[:2]), 0, 1)
+    down_moving, down_got = start_shards([down_turned], STREAMS)
+    step(ring[2], ring[3], normed, *down_moving, *crossed[:2])
+    step(ring[3], ring[2], normed, *down_moving, *crossed[:2])
     adapters = jnp.concatenate([up_adapter_out, down_adapter_in], axis=0)
     adapters_more = others(after(adapters, *ring[2:4]), "mp")
-    step(down_moving, *ring[4:6], *crossed[2:4], grad_got, normed_got, *low_more, *adapters_more)
-    step(ring[6])
+    pinned = [*ring[4:6], *crossed[2:4], grad_got, normed_got, *low_more, *adapters_more]
+    for moving in down_moving:
+        step(moving, *pinned)
+    for moving in ring[-STREAMS:]:
+        step(moving)
 
     def product(kernel, name, own, got, scale, codes, codes_got, first_got, steps, weight_shape):
         groups = scale.shape[0]
@@ -550,7 +582,9 @@
         front_kernel, "up", normed, normed_got, up_block_scale.T, up_codes, front_got, half_blocks,
         range(1, 2 * (n - 1), 2), front,
     )
-    step(ring[7], gate_mine, up_mine, crossed[6])
+    for _ in range(n - 3):
+        for moving, other in zip(ring[-STREAMS:], crossed[-2 * STREAMS : -STREAMS]):
+            step(moving, gate_mine, up_mine, other)
     small_scratch = [
         pltpu.VMEM((rank, units), BF16),
         pltpu.VMEM((units, rank), BF16),
@@ -563,15 +597,15 @@
         scratch=small_scratch,
         limit=8,
     )
+    pieces = STREAMS * n
     down_out_parts = call(
-        down_out_kernel,
+        lambda *refs: down_out_kernel(n, *refs),
         "down_out",
         [low_hidden, swap(low_hidden, "sub"), grad, grad_got],
-        [shape((rank, half // n))] * n,
+        [shape((rank, half // pieces))] * pieces,
         flops=4 * rows * half * rank,
     )
-    seen = []
-    down_out_blocks = ring_all(down_out_parts, seen)
+    down_out_blocks, seen = ring_all(down_out_parts, STREAMS)
     (normed_t,) = call(
         transpose_kernel,
         "transpose",
@@ -581,8 +615,8 @@
     )
 
     back, back_more, _ = product(
-        back_kernel, "back", after(grad, seen[0]), grad_got, down_block_scale, down_turned, down_got, 0,
-        range(2 * (n - 1), 3 * (n - 1)), (units, half),
+        back_kernel, "back", after(grad, *seen[0]), grad_got, down_block_scale, down_turned, down_got, 0,
+        range(2 * (n - 1), (2 + STREAMS) * (n - 1)), (units, half),
     )
     low_grad, up_out_term = call(
         lambda *refs: up_grad_kernel(more, *refs),
@@ -592,34 +626,34 @@
         scratch=small_scratch,
         limit=8,
     )
-    extra = 2 * rank // n
+    extra = 2 * rank // pieces
     up_in_parts = call(
-        up_in_kernel,
+        lambda *refs: up_in_kernel(n, *refs),
         "up_in",
-        [after(low_grad, seen[2]), swap(low_grad, "sub"), normed_t, up_out_term, down_in_term],
-        [shape((half // n + extra, rank))] * n,
+        [after(low_grad, *seen[3]), swap(low_grad, "sub"), normed_t, up_out_term, down_in_term],
+        [shape((half // pieces + extra, rank))] * pieces,
         flops=4 * rows * half * rank,
     )
-    up_in_blocks = ring_all(up_in_parts, [])
+    up_in_blocks, _ = ring_all(up_in_parts, STREAMS)
 
     anywhere = pl.BlockSpec(memory_space=pl.ANY)
     (down_out_gradient,) = call(
         lambda *refs: down_out_place_kernel(n, *refs),
         "down_out_place",
-        [*down_out_blocks[0], *down_out_blocks[1]],
+        down_out_blocks,
         [shape((rank, local_width))],
-        scratch=[pltpu.SemaphoreType.DMA((2 * n,))],
-        specs=[anywhere] * (2 * n),
+        scratch=[pltpu.SemaphoreType.DMA((2 * pieces,))],
+        specs=[anywhere] * (2 * pieces),
         out_specs=(anywhere,),
         limit=4,
     )
     up_in_gradient, up_out_gradient, down_in_gradient = call(
         lambda *refs: up_in_place_kernel(n, *refs),
         "up_in_place",
-        [*up_in_blocks[0], *up_in_blocks[1]],
+        up_in_blocks,
         [shape((local_width, rank)), shape(up_adapter_out.shape), shape(down_adapter_in.shape)],
-        scratch=[pltpu.VMEM((2, 2 * rank, rank), BF16), pltpu.SemaphoreType.DMA((4 * n,))],
-        specs=[anywhere] * (2 * n),
+        scratch=[pltpu.VMEM((2, 2 * rank, rank), BF16), pltpu.SemaphoreType.DMA((4 * pieces,))],
+        specs=[anywhere] * (2 * pieces),
         out_specs=(anywhere, vmem, vmem),
         limit=4,
     )

time: 189 us -> 204 us (1.079)
  starting transfers between devices: 36.1 us -> 57.7 us
  waiting for transfers between devices: 120 us -> 112 us
    ppermute x21 -> x36, starting transfers between devices: 13.2 us -> 35.2 us  [ring_step(): lax.ppermute(x, 'dp', [(ring_at(i, n), ring_at((i + 1) % n, n)) for i in...]
    ppermute x6, waiting for transfers between devices: 12.4 us -> 0.26 us  [others(): lax.ppermute(x, axis, [(i, (i + k) % n) for i in range(n)])]
    ppermute x21 -> x36, waiting for transfers between devices: 87.9 us -> 95.1 us  [ring_step(): lax.ppermute(x, 'dp', [(ring_at(i, n), ring_at((i + 1) % n, n)) for i in...]
    ppermute x26 -> x37, waiting for transfers between devices: 19.6 us -> 16.7 us  [swap(): return lax.ppermute(x, axis, [(0, 1), (1, 0)])]
    ppermute x6, starting transfers between devices: 7.93 us -> 5.63 us  [others(): lax.ppermute(x, axis, [(i, (i + k) % n) for i in range(n)])]
    ppermute x26 -> x37, starting transfers between devices: 15 us -> 16.9 us  [swap(): return lax.ppermute(x, axis, [(0, 1), (1, 0)])]
    pallas_call x16 -> x17, Pallas kernels: 23.8 us -> 25.5 us  [call(): pl.pallas_call(kernel, out_shape=tuple(out_shape), in_specs=specs or [vme...]
  transfers between devices with their start and end apart: 53 -> 79, of which waited for: 31 -> 38; matrix products, arithmetic and copies ran while one was open for 0% -> 0% of each run, Pallas kernels for 8% -> 9%
where the time goes in v7:
time: 204 us
  waiting for transfers between devices  112 us (55%)
  starting transfers between devices  57.7 us (28%)
  Pallas kernels  25.5 us (12%)
  local copies, waits for them, and re-layouts  6.3 us (3%)
    ppermute x36, waiting for transfers between devices, ring_step(): lax.ppermute(x, 'dp', [(ring_at(i, n), ring_at((i + 1) % n, n)) for i in...  95.1 us
    ppermute x36, starting transfers between devices, ring_step(): lax.ppermute(x, 'dp', [(ring_at(i, n), ring_at((i + 1) % n, n)) for i in...  35.2 us
    pallas_call x17, Pallas kernels, call(): pl.pallas_call(kernel, out_shape=tuple(out_shape), in_specs=specs or [vme...  25.5 us
    ppermute x37, starting transfers between devices, swap(): return lax.ppermute(x, axis, [(0, 1), (1, 0)])  16.9 us
    ppermute x37, waiting for transfers between devices, swap(): return lax.ppermute(x, axis, [(0, 1), (1, 0)])  16.7 us
    unnamed x37, local copies, waits for them, and re-layouts  5.92 us
    ppermute x6, starting transfers between devices, others(): lax.ppermute(x, axis, [(i, (i + k) % n) for i in range(n)])  5.63 us
  transfers between devices with their start and end apart: 79, of which 38 were waited for; matrix products, arithmetic and copies ran while one was open for 0% of the time, Pallas kernels for 9%

profile of v7, /device:TPU:0, one launch (start us, length us, event | category | flops | bytes accessed | tf_op | source)
XLA Modules:
  0.0 203.6 jit_solution(16455207498923110145)
XLA Ops:
  12.4 4.2 %cotangent.1 = (bf16[256,4096]{1,0:T(8,128)(2,1)S(1)}, bf16[256,4096]{1,0:T(8,128)(2,1)S(1)}, f32[256,128]{1,0:T(8,128)S(1)}) custom-call(bf16[256,8192]{1,0:T(8,128)(2,1)S(1)} %copy-done.6, s32[1,2]{1,0:T(1,128)S(1)} %copy-done.10, s32[1,256]{1,0:T(1,128)S(1)} %bitcast.9, bf16[128,8192]{1,0:T(8,128)(2,1)S(1)} %copy-done.8), custom_call_target="tpu_custom_call" | custom-call | tf_op jit(solution)/shard_map/cotangent/pallas_call | solution.py:86
  23.8 5.8 %collective-permute-done.3.refs_5_ = bf16[32,16,256]{2,1,0:T(8,128)(2,1)S(1)} collective-permute-done((bf16[32,16,256]{2,1,0:T(8,128)(2,1)S(1)}, bf16[32,16,256]{2,1,0:T(8,128)(2,1)S(1)}, u32[]{:S(2)}, u32[]{:S(2)}) %collective-permute-start.3) | collective-permute-done | bytes 262176 | tf_op jit(solution)/shard_map/ppermute | solution.py:46
  29.7 4.9 %collective-permute-done.5.refs_5_ = bf16[32,16,256]{2,1,0:T(8,128)(2,1)S(1)} collective-permute-done((bf16[32,16,256]{2,1,0:T(8,128)(2,1)S(1)}, bf16[32,16,256]{2,1,0:T(8,128)(2,1)S(1)}, u32[]{:S(2)}, u32[]{:S(2)}) %collective-permute-start.5) | collective-permute-done | bytes 262176 | tf_op jit(solution)/shard_map/ppermute | solution.py:46
  37.5 5.1 %collective-permute-done.4.refs_6_ = bf16[32,16,256]{2,1,0:T(8,128)(2,1)S(1)} collective-permute-done((bf16[32,16,256]{2,1,0:T(8,128)(2,1)S(1)}, bf16[32,16,256]{2,1,0:T(8,128)(2,1)S(1)}, u32[]{:S(2)}, u32[]{:S(2)}) %collective-permute-start.4) | collective-permute-done | bytes 262176 | tf_op jit(solution)/shard_map/ppermute | solution.py:50
  46.7 5.2 %collective-permute-done.8.refs_7_ = bf16[32,16,256]{2,1,0:T(8,128)(2,1)S(1)} collective-permute-done((bf16[32,16,256]{2,1,0:T(8,128)(2,1)S(1)}, bf16[32,16,256]{2,1,0:T(8,128)(2,1)S(1)}, u32[]{:S(2)}, u32[]{:S(2)}) %collective-permute-start.8) | collective-permute-done | bytes 262176 | tf_op jit(solution)/shard_map/ppermute | solution.py:46
  56.5 5.5 %collective-permute-done.11.refs_9_ = bf16[32,16,256]{2,1,0:T(8,128)(2,1)S(1)} collective-permute-done((bf16[32,16,256]{2,1,0:T(8,128)(2,1)S(1)}, bf16[32,16,256]{2,1,0:T(8,128)(2,1)S(1)}, u32[]{:S(2)}, u32[]{:S(2)}) %collective-permute-start.11) | collective-permute-done | bytes 262176 | tf_op jit(solution)/shard_map/ppermute | solution.py:46
  66.1 5.2 %collective-permute-done.12.refs_10_ = bf16[32,16,256]{2,1,0:T(8,128)(2,1)S(1)} collective-permute-done((bf16[32,16,256]{2,1,0:T(8,128)(2,1)S(1)}, bf16[32,16,256]{2,1,0:T(8,128)(2,1)S(1)}, u32[]{:S(2)}, u32[]{:S(2)}) %collective-permute-start.12) | collective-permute-done | bytes 262176 | tf_op jit(solution)/shard_map/ppermute | solution.py:50
  75.1 2.8 %collective-permute-done.16.refs_10_ = bf16[32,16,256]{2,1,0:T(8,128)(2,1)S(1)} collective-permute-done((bf16[32,16,256]{2,1,0:T(8,128)(2,1)S(1)}, bf16[32,16,256]{2,1,0:T(8,128)(2,1)S(1)}, u32[]{:S(2)}, u32[]{:S(2)}) %collective-permute-start.16) | collective-permute-done | bytes 262176 | tf_op jit(solution)/shard_map/ppermute | solution.py:50
  90.7 2.7 %collective-permute-start.32 = (bf16[16,32,128]{2,1,0:T(8,128)(2,1)S(1)}, bf16[16,32,128]{2,1,0:T(8,128)(2,1)S(1)}, u32[]{:S(2)}, u32[]{:S(2)}) collective-permute-start(bf16[16,32,128]{2,1,0:T(8,128)(2,1)S(1)} %collective-permute-done.28.refs_7_), channel_id=1, source_target_pairs={{0,4},{4,12},{12,8},{8,0},{1,5},{5,13},{13,9},{9,1},{2,6},{6,14},{... | collective-permute-start | bytes 393224 | tf_op jit(solution)/shard_map/ppermute | solution.py:46
  109.8 3.3 %collective-permute-start.43 = (bf16[128,512]{1,0:T(8,128)(2,1)S(1)}, bf16[128,512]{1,0:T(8,128)(2,1)S(1)}, u32[]{:S(2)}, u32[]{:S(2)}) collective-permute-start(bf16[128,512]{1,0:T(8,128)(2,1)S(1)} %add_convert_fusion.8), channel_id=1, source_target_pairs={{0,4},{4,12},{12,8},{8,0},{1,5},{5,13},{13,9},{9,1},{2,6},{6,14},{... | collective-permute-start | bytes 393224 | tf_op jit(solution)/shard_map/ppermute | solution.py:46
  119.6 4.3 %collective-permute-done.41 = bf16[128,512]{1,0:T(8,128)(2,1)S(1)} collective-permute-done((bf16[128,512]{1,0:T(8,128)(2,1)S(1)}, bf16[128,512]{1,0:T(8,128)(2,1)S(1)}, u32[]{:S(2)}, u32[]{:S(2)}) %collective-permute-start.41) | collective-permute-done | bytes 131104 | tf_op jit(solution)/shard_map/ppermute | solution.py:46
  132.7 3.4 %up_in.1 = (bf16[544,128]{1,0:T(8,128)(2,1)S(1)}, bf16[544,128]{1,0:T(8,128)(2,1)S(1)}, bf16[544,128]{1,0:T(8,128)(2,1)S(1)}, bf16[544,128]{1,0:T(8,128)(2,1)S(1...) custom-call(bf16[256,128]{1,0:T(8,128)(2,1)S(1)} %get-tuple-element., ...), custom_call_target="tpu_custom_call" | custom-call | tf_op jit(solution)/shard_map/up_in/pallas_call | solution.py:86
  138.9 4.6 %collective-permute-done.47 = bf16[544,128]{1,0:T(8,128)(2,1)S(1)} collective-permute-done((bf16[544,128]{1,0:T(8,128)(2,1)S(1)}, bf16[544,128]{1,0:T(8,128)(2,1)S(1)}, u32[]{:S(2)}, u32[]{:S(2)}) %collective-permute-start.47) | collective-permute-done | bytes 139296 | tf_op jit(solution)/shard_map/ppermute | solution.py:46
  143.6 2.9 %collective-permute-done.50 = bf16[544,128]{1,0:T(8,128)(2,1)S(1)} collective-permute-done((bf16[544,128]{1,0:T(8,128)(2,1)S(1)}, bf16[544,128]{1,0:T(8,128)(2,1)S(1)}, u32[]{:S(2)}, u32[]{:S(2)}) %collective-permute-start.50) | collective-permute-done | bytes 139296 | tf_op jit(solution)/shard_map/ppermute | solution.py:46
  146.6 6.9 %collective-permute-done.48 = bf16[544,128]{1,0:T(8,128)(2,1)S(1)} collective-permute-done((bf16[544,128]{1,0:T(8,128)(2,1)S(1)}, bf16[544,128]{1,0:T(8,128)(2,1)S(1)}, u32[]{:S(2)}, u32[]{:S(2)}) %collective-permute-start.48) | collective-permute-done | bytes 139296 | tf_op jit(solution)/shard_map/ppermute | solution.py:46
  153.5 5.9 %collective-permute-done.51 = bf16[544,128]{1,0:T(8,128)(2,1)S(1)} collective-permute-done((bf16[544,128]{1,0:T(8,128)(2,1)S(1)}, bf16[544,128]{1,0:T(8,128)(2,1)S(1)}, u32[]{:S(2)}, u32[]{:S(2)}) %collective-permute-start.51) | collective-permute-done | bytes 139296 | tf_op jit(solution)/shard_map/ppermute | solution.py:46
  159.5 6.2 %collective-permute-done.49 = bf16[544,128]{1,0:T(8,128)(2,1)S(1)} collective-permute-done((bf16[544,128]{1,0:T(8,128)(2,1)S(1)}, bf16[544,128]{1,0:T(8,128)(2,1)S(1)}, u32[]{:S(2)}, u32[]{:S(2)}) %collective-permute-start.49) | collective-permute-done | bytes 139296 | tf_op jit(solution)/shard_map/ppermute | solution.py:46
  165.9 5.8 %collective-permute-done.52 = bf16[544,128]{1,0:T(8,128)(2,1)S(1)} collective-permute-done((bf16[544,128]{1,0:T(8,128)(2,1)S(1)}, bf16[544,128]{1,0:T(8,128)(2,1)S(1)}, u32[]{:S(2)}, u32[]{:S(2)}) %collective-permute-start.52) | collective-permute-done | bytes 139296 | tf_op jit(solution)/shard_map/ppermute | solution.py:46
  174.0 2.7 %collective-permute-start.70 = (bf16[128,512]{1,0:T(8,128)(2,1)S(1)}, bf16[128,512]{1,0:T(8,128)(2,1)S(1)}, u32[]{:S(2)}, u32[]{:S(2)}) collective-permute-start(bf16[128,512]{1,0:T(8,128)(2,1)S(1)} %collective-permute-done.68.refs_5_), channel_id=1, source_target_pairs={{0,4},{4,12},{12,8},{8,0},{1,5},{5,13},{13,9},{9,1},{2,6},{6,14},{... | collective-permute-start | bytes 393224 | tf_op jit(solution)/shard_map/ppermute | solution.py:46
  179.2 3.0 %collective-permute-done.54.refs_3_ = bf16[544,128]{1,0:T(8,128)(2,1)S(1)} collective-permute-done((bf16[544,128]{1,0:T(8,128)(2,1)S(1)}, bf16[544,128]{1,0:T(8,128)(2,1)S(1)}, u32[]{:S(2)}, u32[]{:S(2)}) %collective-permute-start.54) | collective-permute-done | bytes 139296 | tf_op jit(solution)/shard_map/ppermute | solution.py:46
  182.1 2.8 %collective-permute-done.69.refs_6_ = bf16[128,512]{1,0:T(8,128)(2,1)S(1)} collective-permute-done((bf16[128,512]{1,0:T(8,128)(2,1)S(1)}, bf16[128,512]{1,0:T(8,128)(2,1)S(1)}, u32[]{:S(2)}, u32[]{:S(2)}) %collective-permute-start.69) | collective-permute-done | bytes 131104 | tf_op jit(solution)/shard_map/ppermute | solution.py:46
  184.9 2.8 %collective-permute-done.70.refs_7_ = bf16[128,512]{1,0:T(8,128)(2,1)S(1)} collective-permute-done((bf16[128,512]{1,0:T(8,128)(2,1)S(1)}, bf16[128,512]{1,0:T(8,128)(2,1)S(1)}, u32[]{:S(2)}, u32[]{:S(2)}) %collective-permute-start.70) | collective-permute-done | bytes 131104 | tf_op jit(solution)/shard_map/ppermute | solution.py:46
  194.0 2.8 %collective-permute-done.57.refs_6_ = bf16[544,128]{1,0:T(8,128)(2,1)S(1)} collective-permute-done((bf16[544,128]{1,0:T(8,128)(2,1)S(1)}, bf16[544,128]{1,0:T(8,128)(2,1)S(1)}, u32[]{:S(2)}, u32[]{:S(2)}) %collective-permute-start.57) | collective-permute-done | bytes 139296 | tf_op jit(solution)/shard_map/ppermute | solution.py:46
  196.7 2.9 %collective-permute-done.58.refs_7_ = bf16[544,128]{1,0:T(8,128)(2,1)S(1)} collective-permute-done((bf16[544,128]{1,0:T(8,128)(2,1)S(1)}, bf16[544,128]{1,0:T(8,128)(2,1)S(1)}, u32[]{:S(2)}, u32[]{:S(2)}) %collective-permute-start.58) | collective-permute-done | bytes 139296 | tf_op jit(solution)/shard_map/ppermute | solution.py:46
  (206 shorter events, 100.3 us)
Async XLA Ops:
  19.1 52.7 %collective-permute-start.2 = (bf16[256,4096]{1,0:T(8,128)(2,1)S(1)}, bf16[256,4096]{1,0:T(8,128)(2,1)S(1)}, u32[]{:S(2)}, u32[]{:S(2)}) collective-permute-start(bf16[256,4096]{1,0:T(8,128)(2,1)S(1)} %get-tuple-element.64), channel_id=1, source_target_pairs={{0,1},{1,0},{2,3},{3,2},{4,5},{5,4},{6,7},{7,6},{8,9},{9,8},{10,11... | collective-permute-start | bytes 6291464 | tf_op jit(solution)/shard_map/ppermute | solution.py:50
  19.4 60.6 %collective-permute-start.23 = (bf16[256,4096]{1,0:T(8,128)(2,1)S(1)}, bf16[256,4096]{1,0:T(8,128)(2,1)S(1)}, u32[]{:S(2)}, u32[]{:S(2)}) collective-permute-start(bf16[256,4096]{1,0:T(8,128)(2,1)S(1)} %get-tuple-element.79), channel_id=1, source_target_pairs={{0,1},{1,0},{2,3},{3,2},{4,5},{5,4},{6,7},{7,6},{8,9},{9,8},{10,11... | collective-permute-start | bytes 6291464 | tf_op jit(solution)/shard_map/ppermute | solution.py:50
  19.6 10.0 %collective-permute-start.3 = (bf16[32,16,256]{2,1,0:T(8,128)(2,1)S(1)}, bf16[32,16,256]{2,1,0:T(8,128)(2,1)S(1)}, u32[]{:S(2)}, u32[]{:S(2)}) collective-permute-start(bf16[32,16,256]{2,1,0:T(8,128)(2,1)S(1)} %get-tuple-element.58), channel_id=1, source_target_pairs={{0,4},{4,12},{12,8},{8,0},{1,5},{5,13},{13,9},{9,1},{2,6},{6,14},{... | collective-permute-start | bytes 786440 | tf_op jit(solution)/shard_map/ppermute | solution.py:46
  21.2 13.4 %collective-permute-start.5 = (bf16[32,16,256]{2,1,0:T(8,128)(2,1)S(1)}, bf16[32,16,256]{2,1,0:T(8,128)(2,1)S(1)}, u32[]{:S(2)}, u32[]{:S(2)}) collective-permute-start(bf16[32,16,256]{2,1,0:T(8,128)(2,1)S(1)} %get-tuple-element.59), channel_id=1, source_target_pairs={{0,4},{4,12},{12,8},{8,0},{1,5},{5,13},{13,9},{9,1},{2,6},{6,14},{... | collective-permute-start | bytes 786440 | tf_op jit(solution)/shard_map/ppermute | solution.py:46
  36.6 10.1 %collective-permute-start.6 = (bf16[32,16,256]{2,1,0:T(8,128)(2,1)S(1)}, bf16[32,16,256]{2,1,0:T(8,128)(2,1)S(1)}, u32[]{:S(2)}, u32[]{:S(2)}) collective-permute-start(bf16[32,16,256]{2,1,0:T(8,128)(2,1)S(1)} %collective-permute-done.3.refs_5_), channel_id=1, source_target_pairs={{0,4},{4,12},{12,8},{8,0},{1,5},{5,13},{13,9},{9,1},{2,6},{6,14},{... | collective-permute-start | bytes 786440 | tf_op jit(solution)/shard_map/ppermute | solution.py:46
  42.6 9.3 %collective-permute-start.8 = (bf16[32,16,256]{2,1,0:T(8,128)(2,1)S(1)}, bf16[32,16,256]{2,1,0:T(8,128)(2,1)S(1)}, u32[]{:S(2)}, u32[]{:S(2)}) collective-permute-start(bf16[32,16,256]{2,1,0:T(8,128)(2,1)S(1)} %collective-permute-done.5.refs_5_), channel_id=1, source_target_pairs={{0,4},{4,12},{12,8},{8,0},{1,5},{5,13},{13,9},{9,1},{2,6},{6,14},{... | collective-permute-start | bytes 786440 | tf_op jit(solution)/shard_map/ppermute | solution.py:46
  51.9 10.1 %collective-permute-start.11 = (bf16[32,16,256]{2,1,0:T(8,128)(2,1)S(1)}, bf16[32,16,256]{2,1,0:T(8,128)(2,1)S(1)}, u32[]{:S(2)}, u32[]{:S(2)}) collective-permute-start(bf16[32,16,256]{2,1,0:T(8,128)(2,1)S(1)} %collective-permute-done.6.refs_7_), channel_id=1, source_target_pairs={{0,4},{4,12},{12,8},{8,0},{1,5},{5,13},{13,9},{9,1},{2,6},{6,14},{... | collective-permute-start | bytes 786440 | tf_op jit(solution)/shard_map/ppermute | solution.py:46
  53.1 9.4 %collective-permute-start.7 = (bf16[32,16,256]{2,1,0:T(8,128)(2,1)S(1)}, bf16[32,16,256]{2,1,0:T(8,128)(2,1)S(1)}, u32[]{:S(2)}, u32[]{:S(2)}) collective-permute-start(bf16[32,16,256]{2,1,0:T(8,128)(2,1)S(1)} %collective-permute-done.6.refs_7_), channel_id=1, source_target_pairs={{0,16},{16,0},{1,17},{17,1},{2,18},{18,2},{3,19},{19,3},{4,20},{20... | collective-permute-start | bytes 786440 | tf_op jit(solution)/shard_map/ppermute | solution.py:50
  54.7 11.2 %collective-permute-start.15 = (bf16[32,16,256]{2,1,0:T(8,128)(2,1)S(1)}, bf16[32,16,256]{2,1,0:T(8,128)(2,1)S(1)}, u32[]{:S(2)}, u32[]{:S(2)}) collective-permute-start(bf16[32,16,256]{2,1,0:T(8,128)(2,1)S(1)} %collective-permute-done.8.refs_7_), channel_id=1, source_target_pairs={{0,4},{4,12},{12,8},{8,0},{1,5},{5,13},{13,9},{9,1},{2,6},{6,14},{... | collective-permute-start | bytes 786440 | tf_op jit(solution)/shard_map/ppermute | solution.py:46
  62.5 12.6 %collective-permute-start.14 = (bf16[32,16,256]{2,1,0:T(8,128)(2,1)S(1)}, bf16[32,16,256]{2,1,0:T(8,128)(2,1)S(1)}, u32[]{:S(2)}, u32[]{:S(2)}) collective-permute-start(bf16[32,16,256]{2,1,0:T(8,128)(2,1)S(1)} %collective-permute-done.8.refs_7_), channel_id=1, source_target_pairs={{0,16},{16,0},{1,17},{17,1},{2,18},{18,2},{3,19},{19,3},{4,20},{20... | collective-permute-start | bytes 786440 | tf_op jit(solution)/shard_map/ppermute | solution.py:50
  65.8 14.2 %collective-permute-start.20 = (f32[256,256]{1,0:T(8,128)S(1)}, f32[256,256]{1,0:T(8,128)S(1)}, u32[]{:S(2)}, u32[]{:S(2)}) collective-permute-start(f32[256,256]{1,0:T(8,128)S(1)} %get-tuple-element.76.refs_2_), channel_id=1, source_target_pairs={{0,2},{2,0},{1,3},{3,1},{4,6},{6,4},{5,7},{7,5},{8,10},{10,8},{9,1... | collective-permute-start | bytes 786440 | tf_op jit(solution)/shard_map/ppermute | solution.py:55
  73.7 10.5 %collective-permute-start.13 = (bf16[256,256]{1,0:T(8,128)(2,1)S(1)}, bf16[256,256]{1,0:T(8,128)(2,1)S(1)}, u32[]{:S(2)}, u32[]{:S(2)}) collective-permute-start(bf16[256,256]{1,0:T(8,128)(2,1)S(1)} %get-tuple-element.72), channel_id=1, source_target_pairs={{0,1},{1,0},{2,3},{3,2},{4,5},{5,4},{6,7},{7,6},{8,9},{9,8},{10,11... | collective-permute-start | bytes 393224 | tf_op jit(solution)/shard_map/ppermute | solution.py:50
  94.0 10.1 %collective-permute-start.34 = (bf16[16,32,128]{2,1,0:T(8,128)(2,1)S(1)}, bf16[16,32,128]{2,1,0:T(8,128)(2,1)S(1)}, u32[]{:S(2)}, u32[]{:S(2)}) collective-permute-start(bf16[16,32,128]{2,1,0:T(8,128)(2,1)S(1)} %collective-permute-done.30.refs_9_), channel_id=1, source_target_pairs={{0,4},{4,12},{12,8},{8,0},{1,5},{5,13},{13,9},{9,1},{2,6},{6,14},{... | collective-permute-start | bytes 393224 | tf_op jit(solution)/shard_map/ppermute | solution.py:46
  136.1 29.7 %collective-permute-start.71 = (bf16[128,512]{1,0:T(8,128)(2,1)S(1)}, bf16[128,512]{1,0:T(8,128)(2,1)S(1)}, u32[]{:S(2)}, u32[]{:S(2)}) collective-permute-start(bf16[128,512]{1,0:T(8,128)(2,1)S(1)} %add_convert_fusion.9.refs_0_), channel_id=1, source_target_pairs={{0,1},{1,0},{2,3},{3,2},{4,5},{5,4},{6,7},{7,6},{8,9},{9,8},{10,11... | collective-permute-start | bytes 393224 | tf_op jit(solution)/shard_map/ppermute | solution.py:50
  136.2 35.5 %collective-permute-start.72 = (bf16[128,512]{1,0:T(8,128)(2,1)S(1)}, bf16[128,512]{1,0:T(8,128)(2,1)S(1)}, u32[]{:S(2)}, u32[]{:S(2)}) collective-permute-start(bf16[128,512]{1,0:T(8,128)(2,1)S(1)} %add_convert_fusion.6.refs_1_), channel_id=1, source_target_pairs={{0,1},{1,0},{2,3},{3,2},{4,5},{5,4},{6,7},{7,6},{8,9},{9,8},{10,11... | collective-permute-start | bytes 393224 | tf_op jit(solution)/shard_map/ppermute | solution.py:50
  136.7 9.8 %collective-permute-start.50 = (bf16[544,128]{1,0:T(8,128)(2,1)S(1)}, bf16[544,128]{1,0:T(8,128)(2,1)S(1)}, u32[]{:S(2)}, u32[]{:S(2)}) collective-permute-start(bf16[544,128]{1,0:T(8,128)(2,1)S(1)} %get-tuple-element.105), channel_id=1, source_target_pairs={{0,4},{4,12},{12,8},{8,0},{1,5},{5,13},{13,9},{9,1},{2,6},{6,14},{... | collective-permute-start | bytes 417800 | tf_op jit(solution)/shard_map/ppermute | solution.py:46
  138.7 33.1 %collective-permute-start.67 = (bf16[128,512]{1,0:T(8,128)(2,1)S(1)}, bf16[128,512]{1,0:T(8,128)(2,1)S(1)}, u32[]{:S(2)}, u32[]{:S(2)}) collective-permute-start(bf16[128,512]{1,0:T(8,128)(2,1)S(1)} %collective-permute-done.42.refs_2_), channel_id=1, source_target_pairs={{0,4},{4,12},{12,8},{8,0},{1,5},{5,13},{13,9},{9,1},{2,6},{6,14},{... | collective-permute-start | bytes 393224 | tf_op jit(solution)/shard_map/ppermute | solution.py:46
  143.5 30.4 %collective-permute-start.68 = (bf16[128,512]{1,0:T(8,128)(2,1)S(1)}, bf16[128,512]{1,0:T(8,128)(2,1)S(1)}, u32[]{:S(2)}, u32[]{:S(2)}) collective-permute-start(bf16[128,512]{1,0:T(8,128)(2,1)S(1)} %collective-permute-done.45.refs_3_), channel_id=1, source_target_pairs={{0,4},{4,12},{12,8},{8,0},{1,5},{5,13},{13,9},{9,1},{2,6},{6,14},{... | collective-permute-start | bytes 393224 | tf_op jit(solution)/shard_map/ppermute | solution.py:46
  171.8 10.3 %collective-permute-start.54 = (bf16[544,128]{1,0:T(8,128)(2,1)S(1)}, bf16[544,128]{1,0:T(8,128)(2,1)S(1)}, u32[]{:S(2)}, u32[]{:S(2)}) collective-permute-start(bf16[544,128]{1,0:T(8,128)(2,1)S(1)} %add_convert_fusion.refs_1_), channel_id=1, source_target_pairs={{0,4},{4,12},{12,8},{8,0},{1,5},{5,13},{13,9},{9,1},{2,6},{6,14},{... | collective-permute-start | bytes 417800 | tf_op jit(solution)/shard_map/ppermute | solution.py:46
  173.9 11.0 %collective-permute-start.69 = (bf16[128,512]{1,0:T(8,128)(2,1)S(1)}, bf16[128,512]{1,0:T(8,128)(2,1)S(1)}, u32[]{:S(2)}, u32[]{:S(2)}) collective-permute-start(bf16[128,512]{1,0:T(8,128)(2,1)S(1)} %collective-permute-done.67.refs_4_), channel_id=1, source_target_pairs={{0,4},{4,12},{12,8},{8,0},{1,5},{5,13},{13,9},{9,1},{2,6},{6,14},{... | collective-permute-start | bytes 393224 | tf_op jit(solution)/shard_map/ppermute | solution.py:46
  174.0 13.8 %collective-permute-start.70 = (bf16[128,512]{1,0:T(8,128)(2,1)S(1)}, bf16[128,512]{1,0:T(8,128)(2,1)S(1)}, u32[]{:S(2)}, u32[]{:S(2)}) collective-permute-start(bf16[128,512]{1,0:T(8,128)(2,1)S(1)} %collective-permute-done.68.refs_5_), channel_id=1, source_target_pairs={{0,4},{4,12},{12,8},{8,0},{1,5},{5,13},{13,9},{9,1},{2,6},{6,14},{... | collective-permute-start | bytes 393224 | tf_op jit(solution)/shard_map/ppermute | solution.py:46
  176.8 11.0 %collective-permute-start.75 = (bf16[128,512]{1,0:T(8,128)(2,1)S(1)}, bf16[128,512]{1,0:T(8,128)(2,1)S(1)}, u32[]{:S(2)}, u32[]{:S(2)}) collective-permute-start(bf16[128,512]{1,0:T(8,128)(2,1)S(1)} %collective-permute-done.67.refs_4_), channel_id=1, source_target_pairs={{0,1},{1,0},{2,3},{3,2},{4,5},{5,4},{6,7},{7,6},{8,9},{9,8},{10,11... | collective-permute-start | bytes 393224 | tf_op jit(solution)/shard_map/ppermute | solution.py:50
  179.1 11.6 %collective-permute-start.55 = (bf16[544,128]{1,0:T(8,128)(2,1)S(1)}, bf16[544,128]{1,0:T(8,128)(2,1)S(1)}, u32[]{:S(2)}, u32[]{:S(2)}) collective-permute-start(bf16[544,128]{1,0:T(8,128)(2,1)S(1)} %collective-permute-done.53.refs_2_), channel_id=1, source_target_pairs={{0,4},{4,12},{12,8},{8,0},{1,5},{5,13},{13,9},{9,1},{2,6},{6,14},{... | collective-permute-start | bytes 417800 | tf_op jit(solution)/shard_map/ppermute | solution.py:46
  182.1 11.2 %collective-permute-start.56 = (bf16[544,128]{1,0:T(8,128)(2,1)S(1)}, bf16[544,128]{1,0:T(8,128)(2,1)S(1)}, u32[]{:S(2)}, u32[]{:S(2)}) collective-permute-start(bf16[544,128]{1,0:T(8,128)(2,1)S(1)} %collective-permute-done.54.refs_3_), channel_id=1, source_target_pairs={{0,4},{4,12},{12,8},{8,0},{1,5},{5,13},{13,9},{9,1},{2,6},{6,14},{... | collective-permute-start | bytes 417800 | tf_op jit(solution)/shard_map/ppermute | solution.py:46
  (73 other events, 550.9 us)

commit v8 on v7

--- a/solution.py
+++ b/solution.py
@@ -59,8 +59,33 @@
     return lax.optimization_barrier((x, *done))[0]
 
 
-def add(*terms):
-    return sum(t.astype(F32) for t in terms).astype(BF16)
+def call(kernel, name, args, out_shape, scratch=(), specs=None, limit=24, flops=0, out_specs=None):
+    vmem = pl.BlockSpec(memory_space=pltpu.VMEM)
+    moved = sum(a.size * a.dtype.itemsize for a in args) + sum(
+        math.prod(s.shape) * s.dtype.itemsize for s in out_shape
+    )
+    return pl.pallas_call(
+        kernel,
+        out_shape=tuple(out_shape),
+        in_specs=specs or [vmem] * len(args),
+        out_specs=out_specs or tuple([vmem] * len(out_shape)),
+        scratch_shapes=list(scratch),
+        compiler_params=pltpu.CompilerParams(vmem_limit_bytes=limit * MIB),
+        cost_estimate=pl.CostEstimate(flops=0, bytes_accessed=0, transcendentals=0),
+        name=name,
+    )(*args)
+
+
+def shape(dims, dtype=BF16):
+    return jax.ShapeDtypeStruct(tuple(dims), dtype)
+
+
+def add_kernel(left, right, out_ref):
+    out_ref[...] = (left[...].astype(F32) + right[...].astype(F32)).astype(BF16)
+
+
+def add(left, right):
+    return call(add_kernel, "add", [left, right], [shape(left.shape)], limit=4)[0]
 
 
 def ring_all(parts, streams):
@@ -78,27 +103,6 @@
     return blocks + [swap(b, "sub") for b in blocks], seen
 
 
-def call(kernel, name, args, out_shape, scratch=(), specs=None, limit=24, flops=0, out_specs=None):
-    vmem = pl.BlockSpec(memory_space=pltpu.VMEM)
-    moved = sum(a.size * a.dtype.itemsize for a in args) + sum(
-        math.prod(s.shape) * s.dtype.itemsize for s in out_shape
-    )
-    return pl.pallas_call(
-        kernel,
-        out_shape=tuple(out_shape),
-        in_specs=specs or [vmem] * len(args),
-        out_specs=out_specs or tuple([vmem] * len(out_shape)),
-        scratch_shapes=list(scratch),
-        compiler_params=pltpu.CompilerParams(vmem_limit_bytes=limit * MIB),
-        cost_estimate=pl.CostEstimate(flops=0, bytes_accessed=0, transcendentals=0),
-        name=name,
-    )(*args)
-
-
-def shape(dims, dtype=BF16):
-    return jax.ShapeDtypeStruct(tuple(dims), dtype)
-
-
 def scaled_halves(wide, low_ref, cols, scaled, product, send_ref, own_ref, arrive=None):
     half = send_ref.shape[1]
     step = half // 4
@@ -128,7 +132,7 @@
     return copy
 
 
-def square_kernel(tokens, square_ref, buffer, sems):
+def square_kernel(tokens, lengths, square_ref, buffer, sems):
     width = tokens.shape[1]
     step = width // sems.shape[0]
     copy = column_copy(tokens, buffer, sems)
@@ -513,7 +517,8 @@
 
     def step(moving, *done):
         ring.append(ring_step(after(moving, *done) if done else moving))
-        crossed.append(swap(ring[-1], "grp"))
+        if len(ring) > 2:
+            crossed.append(swap(ring[-1], "grp"))
 
     step(gate_moving)
     step(up_moving)
@@ -522,35 +527,36 @@
     smem = pl.BlockSpec(memory_space=pltpu.SMEM)
     hbm = pl.BlockSpec(memory_space=pltpu.HBM)
     buffers = [pltpu.VMEM((rows, local_width), BF16), pltpu.SemaphoreType.DMA((8,))]
+    lengths = after(sequence_length_list, gate_moving, up_moving)
     (squares,) = call(
-        square_kernel, "squares", [tokens], [shape((rows, LANES), F32)],
-        scratch=buffers, specs=[hbm], limit=16,
+        square_kernel, "squares", [tokens, lengths], [shape((rows, LANES), F32)],
+        scratch=buffers, specs=[hbm, smem], limit=16,
     )
     squares_more = others(squares, "mp")
-    lengths = after(sequence_length_list, gate_moving, up_moving, squares)
     grad_send, grad, low_out = call(
         lambda *refs: cotangent_kernel(rows * n * lax.axis_size("sub"), *refs),
         "cotangent",
-        [cotangent, lengths, slot_sequence_index[None, :], down_adapter_out],
+        [cotangent, after(lengths, squares), slot_sequence_index[None, :], down_adapter_out],
         [shape((rows, half))] * 2 + [shape((rows, rank), F32)],
         scratch=buffers,
         specs=[hbm, smem, vmem, vmem],
     )
+    crossed += [swap(after(r, grad), "grp") for r in ring]
     step(ring[0], ring[1], grad)
     step(ring[1], ring[0], grad)
     normed_send, normed, low = call(
         lambda *refs: token_kernel(total_width, *refs),
         "tokens",
-        [tokens, rms_norm_gain[None, :], up_adapter_in, low_out, squares, *squares_more],
+        [tokens, rms_norm_gain[None, :], up_adapter_in, low_out, after(squares, *ring[2:4], *crossed[:2]), *squares_more],
         [shape((rows, half))] * 2 + [shape((rows, 2 * rank), F32)],
     )
     grad_got = swap(grad_send, "sub")
     normed_got = swap(normed_send, "sub")
     low_more = others(low, "mp")
-    down_turned = jnp.swapaxes(after(down_codes, *ring[:2]), 0, 1)
+    down_turned = jnp.swapaxes(after(down_codes, *ring[2:4]), 0, 1)
     down_moving, down_got = start_shards([down_turned], STREAMS)
-    step(ring[2], ring[3], normed, *down_moving, *crossed[:2])
-    step(ring[3], ring[2], normed, *down_moving, *crossed[:2])
+    step(ring[2], ring[3], *crossed[:2])
+    step(ring[3], ring[2], *crossed[:2])
     adapters = jnp.concatenate([up_adapter_out, down_adapter_in], axis=0)
     adapters_more = others(after(adapters, *ring[2:4]), "mp")
     pinned = [*ring[4:6], *crossed[2:4], grad_got, normed_got, *low_more, *adapters_more]
@@ -573,13 +579,14 @@
         return total, others(total.astype(BF16), "mp"), mine
 
     front = (blocks // 2, block, units)
+    first_down = ring[2 * (n - 1) : 2 * (n - 1) + STREAMS]
     half_blocks = blocks // 2
     gate, gate_more, gate_mine = product(
-        front_kernel, "gate", normed, normed_got, gate_block_scale.T, gate_codes, front_got, 0,
+        front_kernel, "gate", normed, normed_got, after(gate_block_scale.T, *first_down), gate_codes, front_got, 0,
         range(0, 2 * (n - 1), 2), front,
     )
     up, up_more, up_mine = product(
-        front_kernel, "up", normed, normed_got, up_block_scale.T, up_codes, front_got, half_blocks,
+        front_kernel, "up", normed, normed_got, after(up_block_scale.T, *first_down), up_codes, front_got, half_blocks,
         range(1, 2 * (n - 1), 2), front,
     )
     for _ in range(n - 3):
@@ -592,7 +599,7 @@
     silu, low_hidden, down_in_term = call(
         lambda *refs: hidden_kernel(more, *refs),
         "hidden",
-        [gate, up, low, adapters, *gate_more, *up_more, *low_more, *adapters_more],
+        [gate, up, low, after(adapters, *ring[-2 * STREAMS : -STREAMS]), *gate_more, *up_more, *low_more, *adapters_more],
         [shape((rows, units), F32), shape((rows, rank)), shape(down_adapter_in.shape)],
         scratch=small_scratch,
         limit=8,

time: 204 us -> 185 us (0.907)
  waiting for transfers between devices: 112 us -> 78.4 us
  starting transfers between devices: 57.7 us -> 73.8 us
    ppermute x36, waiting for transfers between devices: 95.1 us -> 64.3 us  [ring_step(): lax.ppermute(x, 'dp', [(ring_at(i, n), ring_at((i + 1) % n, n)) for i in...]
    ppermute x36, starting transfers between devices: 35.2 us -> 46.2 us  [ring_step(): lax.ppermute(x, 'dp', [(ring_at(i, n), ring_at((i + 1) % n, n)) for i in...]
    ppermute x37, waiting for transfers between devices: 16.7 us -> 6.36 us  [swap(): return lax.ppermute(x, axis, [(0, 1), (1, 0)])]
    ppermute x6, waiting for transfers between devices: 0.26 us -> 7.68 us  [others(): lax.ppermute(x, axis, [(i, (i + k) % n) for i in range(n)])]
    ppermute x37, starting transfers between devices: 16.9 us -> 21.3 us  [swap(): return lax.ppermute(x, axis, [(0, 1), (1, 0)])]
    pallas_call x17 -> x29, Pallas kernels: 25.5 us -> 26.4 us  [call(): pl.pallas_call(kernel, out_shape=tuple(out_shape), in_specs=specs or [vme...]
  transfers between devices with their start and end apart: 79 -> 79, of which waited for: 38 -> 40; matrix products, arithmetic and copies ran while one was open for 0% -> 0% of each run, Pallas kernels for 9% -> 11%
where the time goes in v8:
time: 185 us
  waiting for transfers between devices  78.4 us (42%)
  starting transfers between devices  73.8 us (40%)
  Pallas kernels  26.4 us (14%)
  local copies, waits for them, and re-layouts  4.72 us (3%)
    ppermute x36, waiting for transfers between devices, ring_step(): lax.ppermute(x, 'dp', [(ring_at(i, n), ring_at((i + 1) % n, n)) for i in...  64.3 us
    ppermute x36, starting transfers between devices, ring_step(): lax.ppermute(x, 'dp', [(ring_at(i, n), ring_at((i + 1) % n, n)) for i in...  46.2 us
    pallas_call x29, Pallas kernels, call(): pl.pallas_call(kernel, out_shape=tuple(out_shape), in_specs=specs or [vme...  26.4 us
    ppermute x37, starting transfers between devices, swap(): return lax.ppermute(x, axis, [(0, 1), (1, 0)])  21.3 us
    ppermute x6, waiting for transfers between devices, others(): lax.ppermute(x, axis, [(i, (i + k) % n) for i in range(n)])  7.68 us
    ppermute x37, waiting for transfers between devices, swap(): return lax.ppermute(x, axis, [(0, 1), (1, 0)])  6.36 us
    ppermute x6, starting transfers between devices, others(): lax.ppermute(x, axis, [(i, (i + k) % n) for i in range(n)])  6.32 us
    unnamed x37, local copies, waits for them, and re-layouts  4.35 us
  transfers between devices with their start and end apart: 79, of which 40 were waited for; matrix products, arithmetic and copies ran while one was open for 0% of the time, Pallas kernels for 11%

profile of v8, /device:TPU:0, one launch (start us, length us, event | category | flops | bytes accessed | tf_op | source)
XLA Modules:
  0.0 184.8 jit_solution(5640730775163168026)
XLA Ops:
  5.5 3.0 %collective-permute-start.1 = (bf16[32,16,256]{2,1,0:T(8,128)(2,1)S(1)}, bf16[32,16,256]{2,1,0:T(8,128)(2,1)S(1)}, u32[]{:S(2)}, u32[]{:S(2)}) collective-permute-start(bf16[32,16,256]{2,1,0:T(8,128)(2,1)S(1)} %get-tuple-element.65), channel_id=1, source_target_pairs={{0,4},{4,12},{12,8},{8,0},{1,5},{5,13},{13,9},{9,1},{2,6},{6,14},{... | collective-permute-start | bytes 786440 | tf_op jit(solution)/shard_map/ppermute | solution.py:46
  8.5 2.6 %collective-permute-start.2 = (bf16[32,16,256]{2,1,0:T(8,128)(2,1)S(1)}, bf16[32,16,256]{2,1,0:T(8,128)(2,1)S(1)}, u32[]{:S(2)}, u32[]{:S(2)}) collective-permute-start(bf16[32,16,256]{2,1,0:T(8,128)(2,1)S(1)} %get-tuple-element.66), channel_id=1, source_target_pairs={{0,4},{4,12},{12,8},{8,0},{1,5},{5,13},{13,9},{9,1},{2,6},{6,14},{... | collective-permute-start | bytes 786440 | tf_op jit(solution)/shard_map/ppermute | solution.py:46
  13.3 2.4 %squares.1.refs_4_ = f32[256,128]{1,0:T(8,128)S(1)} custom-call(bf16[256,8192]{1,0:T(8,128)(2,1)S(1)} %copy-done, s32[1,2]{1,0:T(1,128)S(1)} %copy-done.9), custom_call_target="tpu_custom_call" | custom-call | tf_op jit(solution)/shard_map/squares/pallas_call | solution.py:67
  15.8 4.2 %cotangent.1 = (bf16[256,4096]{1,0:T(8,128)(2,1)S(1)}, bf16[256,4096]{1,0:T(8,128)(2,1)S(1)}, f32[256,128]{1,0:T(8,128)S(1)}) custom-call(bf16[256,8192]{1,0:T(8,128)(2,1)S(1)} %copy-done.6, s32[1,2]{1,0:T(1,128)S(1)} %copy-done.9, s32[1,256]{1,0:T(1,128)S(1)} %bitcast.9, bf16[128,8192]{1,0:T(8,128)(2,1)S(1)} %copy-done.8), custom_call_target="tpu_custom_call" | custom-call | tf_op jit(solution)/shard_map/cotangent/pallas_call | solution.py:67
  22.6 3.4 %collective-permute-start.4 = (bf16[32,16,256]{2,1,0:T(8,128)(2,1)S(1)}, bf16[32,16,256]{2,1,0:T(8,128)(2,1)S(1)}, u32[]{:S(2)}, u32[]{:S(2)}) collective-permute-start(bf16[32,16,256]{2,1,0:T(8,128)(2,1)S(1)} %collective-permute-done.2.refs_5_), channel_id=1, source_target_pairs={{0,4},{4,12},{12,8},{8,0},{1,5},{5,13},{13,9},{9,1},{2,6},{6,14},{... | collective-permute-start | bytes 786440 | tf_op jit(solution)/shard_map/ppermute | solution.py:46
  29.5 2.4 %collective-permute-done.3.refs_7_ = bf16[32,16,256]{2,1,0:T(8,128)(2,1)S(1)} collective-permute-done((bf16[32,16,256]{2,1,0:T(8,128)(2,1)S(1)}, bf16[32,16,256]{2,1,0:T(8,128)(2,1)S(1)}, u32[]{:S(2)}, u32[]{:S(2)}) %collective-permute-start.3) | collective-permute-done | bytes 262176 | tf_op jit(solution)/shard_map/ppermute | solution.py:46
  31.9 4.2 %collective-permute-done.4.refs_7_ = bf16[32,16,256]{2,1,0:T(8,128)(2,1)S(1)} collective-permute-done((bf16[32,16,256]{2,1,0:T(8,128)(2,1)S(1)}, bf16[32,16,256]{2,1,0:T(8,128)(2,1)S(1)}, u32[]{:S(2)}, u32[]{:S(2)}) %collective-permute-start.4) | collective-permute-done | bytes 262176 | tf_op jit(solution)/shard_map/ppermute | solution.py:46
  36.1 2.4 %collective-permute-done.6.refs_6_ = bf16[32,16,256]{2,1,0:T(8,128)(2,1)S(1)} collective-permute-done((bf16[32,16,256]{2,1,0:T(8,128)(2,1)S(1)}, bf16[32,16,256]{2,1,0:T(8,128)(2,1)S(1)}, u32[]{:S(2)}, u32[]{:S(2)}) %collective-permute-start.6) | collective-permute-done | bytes 262176 | tf_op jit(solution)/shard_map/ppermute | solution.py:50
  38.6 2.5 %tokens.3 = (bf16[256,4096]{1,0:T(8,128)(2,1)S(1)}, bf16[256,4096]{1,0:T(8,128)(2,1)S(1)}, f32[256,256]{1,0:T(8,128)S(1)}) custom-call(bf16[256,8192]{1,0:T(8,128)(2,1)S(1)} %copy-done.1, bf16[1,8192]{1,0:T(2,128)(2,1)S(1)} %broadcast_in_dim.7.refs_1_, bf16[8192,128]{1,0:T(8,128)(2,1)S(1)} %copy-done.7, f32[256,128]{1,0:T(8,128)S(1)} %get-tuple-element.70.refs_3_, ...), custom_call_target="tpu_custom_call" | custom-call | tf_op jit(solution)/shard_map/tokens/pallas_call | solution.py:67
  44.1 2.5 %collective-permute-done.16.refs_7_.refs_6_ = bf16[256,128]{1,0:T(8,128)(2,1)S(1)} collective-permute-done((bf16[256,128]{1,0:T(8,128)(2,1)S(1)}, bf16[256,128]{1,0:T(8,128)(2,1)S(1)}, u32[]{:S(2)}, u32[]{:S(2)}) %collective-permute-start.16) | collective-permute-done | bytes 65568 | tf_op jit(solution)/shard_map/ppermute | solution.py:55
  48.4 5.5 %collective-permute-done.10.refs_9_ = bf16[32,16,256]{2,1,0:T(8,128)(2,1)S(1)} collective-permute-done((bf16[32,16,256]{2,1,0:T(8,128)(2,1)S(1)}, bf16[32,16,256]{2,1,0:T(8,128)(2,1)S(1)}, u32[]{:S(2)}, u32[]{:S(2)}) %collective-permute-start.10) | collective-permute-done | bytes 262176 | tf_op jit(solution)/shard_map/ppermute | solution.py:46
  55.4 2.9 %collective-permute-done.11.refs_9_ = bf16[32,16,256]{2,1,0:T(8,128)(2,1)S(1)} collective-permute-done((bf16[32,16,256]{2,1,0:T(8,128)(2,1)S(1)}, bf16[32,16,256]{2,1,0:T(8,128)(2,1)S(1)}, u32[]{:S(2)}, u32[]{:S(2)}) %collective-permute-start.11) | collective-permute-done | bytes 262176 | tf_op jit(solution)/shard_map/ppermute | solution.py:46
  60.7 4.7 %collective-permute-done.15.refs_6_.refs_5_ = f32[256,256]{1,0:T(8,128)S(1)} collective-permute-done((f32[256,256]{1,0:T(8,128)S(1)}, f32[256,256]{1,0:T(8,128)S(1)}, u32[]{:S(2)}, u32[]{:S(2)}) %collective-permute-start.15) | collective-permute-done | bytes 262176 | tf_op jit(solution)/shard_map/ppermute | solution.py:55
  68.3 2.9 %collective-permute-done.17.refs_5_ = bf16[16,32,128]{2,1,0:T(8,128)(2,1)S(1)} collective-permute-done((bf16[16,32,128]{2,1,0:T(8,128)(2,1)S(1)}, bf16[16,32,128]{2,1,0:T(8,128)(2,1)S(1)}, u32[]{:S(2)}, u32[]{:S(2)}) %collective-permute-start.17) | collective-permute-done | bytes 131104 | tf_op jit(solution)/shard_map/ppermute | solution.py:46
  102.8 3.2 %collective-permute-start.43 = (bf16[128,512]{1,0:T(8,128)(2,1)S(1)}, bf16[128,512]{1,0:T(8,128)(2,1)S(1)}, u32[]{:S(2)}, u32[]{:S(2)}) collective-permute-start(bf16[128,512]{1,0:T(8,128)(2,1)S(1)} %add.33), channel_id=1, source_target_pairs={{0,4},{4,12},{12,8},{8,0},{1,5},{5,13},{13,9},{9,1},{2,6},{6,14},{... | collective-permute-start | bytes 393224 | tf_op jit(solution)/shard_map/ppermute | solution.py:46
  113.9 3.1 %collective-permute-done.41.left = bf16[128,512]{1,0:T(8,128)(2,1)S(1)} collective-permute-done((bf16[128,512]{1,0:T(8,128)(2,1)S(1)}, bf16[128,512]{1,0:T(8,128)(2,1)S(1)}, u32[]{:S(2)}, u32[]{:S(2)}) %collective-permute-start.41) | collective-permute-done | bytes 131104 | tf_op jit(solution)/shard_map/ppermute | solution.py:46
  125.1 3.4 %up_in.1 = (bf16[544,128]{1,0:T(8,128)(2,1)S(1)}, bf16[544,128]{1,0:T(8,128)(2,1)S(1)}, bf16[544,128]{1,0:T(8,128)(2,1)S(1)}, bf16[544,128]{1,0:T(8,128)(2,1)S(1...) custom-call(bf16[256,128]{1,0:T(8,128)(2,1)S(1)} %get-tuple-element., ...), custom_call_target="tpu_custom_call" | custom-call | tf_op jit(solution)/shard_map/up_in/pallas_call | solution.py:67
  128.6 3.0 %collective-permute-start.50 = (bf16[544,128]{1,0:T(8,128)(2,1)S(1)}, bf16[544,128]{1,0:T(8,128)(2,1)S(1)}, u32[]{:S(2)}, u32[]{:S(2)}) collective-permute-start(bf16[544,128]{1,0:T(8,128)(2,1)S(1)} %get-tuple-element.119), channel_id=1, source_target_pairs={{0,4},{4,12},{12,8},{8,0},{1,5},{5,13},{13,9},{9,1},{2,6},{6,14},{... | collective-permute-start | bytes 417800 | tf_op jit(solution)/shard_map/ppermute | solution.py:46
  131.6 3.2 %collective-permute-done.47.left = bf16[544,128]{1,0:T(8,128)(2,1)S(1)} collective-permute-done((bf16[544,128]{1,0:T(8,128)(2,1)S(1)}, bf16[544,128]{1,0:T(8,128)(2,1)S(1)}, u32[]{:S(2)}, u32[]{:S(2)}) %collective-permute-start.47) | collective-permute-done | bytes 139296 | tf_op jit(solution)/shard_map/ppermute | solution.py:46
  135.3 2.4 %collective-permute-done.50.left = bf16[544,128]{1,0:T(8,128)(2,1)S(1)} collective-permute-done((bf16[544,128]{1,0:T(8,128)(2,1)S(1)}, bf16[544,128]{1,0:T(8,128)(2,1)S(1)}, u32[]{:S(2)}, u32[]{:S(2)}) %collective-permute-start.50) | collective-permute-done | bytes 139296 | tf_op jit(solution)/shard_map/ppermute | solution.py:46
  142.8 2.5 %collective-permute-done.51.left = bf16[544,128]{1,0:T(8,128)(2,1)S(1)} collective-permute-done((bf16[544,128]{1,0:T(8,128)(2,1)S(1)}, bf16[544,128]{1,0:T(8,128)(2,1)S(1)}, u32[]{:S(2)}, u32[]{:S(2)}) %collective-permute-start.51) | collective-permute-done | bytes 139296 | tf_op jit(solution)/shard_map/ppermute | solution.py:46
  146.8 2.9 %collective-permute-start.67 = (bf16[128,512]{1,0:T(8,128)(2,1)S(1)}, bf16[128,512]{1,0:T(8,128)(2,1)S(1)}, u32[]{:S(2)}, u32[]{:S(2)}) collective-permute-start(bf16[128,512]{1,0:T(8,128)(2,1)S(1)} %collective-permute-done.42.refs_2_), channel_id=1, source_target_pairs={{0,4},{4,12},{12,8},{8,0},{1,5},{5,13},{13,9},{9,1},{2,6},{6,14},{... | collective-permute-start | bytes 393224 | tf_op jit(solution)/shard_map/ppermute | solution.py:46
  166.0 2.8 %collective-permute-done.70.refs_7_ = bf16[128,512]{1,0:T(8,128)(2,1)S(1)} collective-permute-done((bf16[128,512]{1,0:T(8,128)(2,1)S(1)}, bf16[128,512]{1,0:T(8,128)(2,1)S(1)}, u32[]{:S(2)}, u32[]{:S(2)}) %collective-permute-start.70) | collective-permute-done | bytes 131104 | tf_op jit(solution)/shard_map/ppermute | solution.py:46
  177.9 3.0 %collective-permute-done.58.refs_7_ = bf16[544,128]{1,0:T(8,128)(2,1)S(1)} collective-permute-done((bf16[544,128]{1,0:T(8,128)(2,1)S(1)}, bf16[544,128]{1,0:T(8,128)(2,1)S(1)}, u32[]{:S(2)}, u32[]{:S(2)}) %collective-permute-start.58) | collective-permute-done | bytes 139296 | tf_op jit(solution)/shard_map/ppermute | solution.py:46
  (206 shorter events, 108.7 us)
Async XLA Ops:
  5.5 14.4 %collective-permute-start.1 = (bf16[32,16,256]{2,1,0:T(8,128)(2,1)S(1)}, bf16[32,16,256]{2,1,0:T(8,128)(2,1)S(1)}, u32[]{:S(2)}, u32[]{:S(2)}) collective-permute-start(bf16[32,16,256]{2,1,0:T(8,128)(2,1)S(1)} %get-tuple-element.65), channel_id=1, source_target_pairs={{0,4},{4,12},{12,8},{8,0},{1,5},{5,13},{13,9},{9,1},{2,6},{6,14},{... | collective-permute-start | bytes 786440 | tf_op jit(solution)/shard_map/ppermute | solution.py:46
  8.5 13.2 %collective-permute-start.2 = (bf16[32,16,256]{2,1,0:T(8,128)(2,1)S(1)}, bf16[32,16,256]{2,1,0:T(8,128)(2,1)S(1)}, u32[]{:S(2)}, u32[]{:S(2)}) collective-permute-start(bf16[32,16,256]{2,1,0:T(8,128)(2,1)S(1)} %get-tuple-element.66), channel_id=1, source_target_pairs={{0,4},{4,12},{12,8},{8,0},{1,5},{5,13},{13,9},{9,1},{2,6},{6,14},{... | collective-permute-start | bytes 786440 | tf_op jit(solution)/shard_map/ppermute | solution.py:46
  21.8 10.1 %collective-permute-start.3 = (bf16[32,16,256]{2,1,0:T(8,128)(2,1)S(1)}, bf16[32,16,256]{2,1,0:T(8,128)(2,1)S(1)}, u32[]{:S(2)}, u32[]{:S(2)}) collective-permute-start(bf16[32,16,256]{2,1,0:T(8,128)(2,1)S(1)} %collective-permute-done.1.refs_5_), channel_id=1, source_target_pairs={{0,4},{4,12},{12,8},{8,0},{1,5},{5,13},{13,9},{9,1},{2,6},{6,14},{... | collective-permute-start | bytes 786440 | tf_op jit(solution)/shard_map/ppermute | solution.py:46
  22.6 13.5 %collective-permute-start.4 = (bf16[32,16,256]{2,1,0:T(8,128)(2,1)S(1)}, bf16[32,16,256]{2,1,0:T(8,128)(2,1)S(1)}, u32[]{:S(2)}, u32[]{:S(2)}) collective-permute-start(bf16[32,16,256]{2,1,0:T(8,128)(2,1)S(1)} %collective-permute-done.2.refs_5_), channel_id=1, source_target_pairs={{0,4},{4,12},{12,8},{8,0},{1,5},{5,13},{13,9},{9,1},{2,6},{6,14},{... | collective-permute-start | bytes 786440 | tf_op jit(solution)/shard_map/ppermute | solution.py:46
  26.0 10.1 %collective-permute-start.5 = (bf16[32,16,256]{2,1,0:T(8,128)(2,1)S(1)}, bf16[32,16,256]{2,1,0:T(8,128)(2,1)S(1)}, u32[]{:S(2)}, u32[]{:S(2)}) collective-permute-start(bf16[32,16,256]{2,1,0:T(8,128)(2,1)S(1)} %collective-permute-done.1.refs_5_), channel_id=1, source_target_pairs={{0,16},{16,0},{1,17},{17,1},{2,18},{18,2},{3,19},{19,3},{4,20},{20... | collective-permute-start | bytes 786440 | tf_op jit(solution)/shard_map/ppermute | solution.py:50
  27.5 11.1 %collective-permute-start.6 = (bf16[32,16,256]{2,1,0:T(8,128)(2,1)S(1)}, bf16[32,16,256]{2,1,0:T(8,128)(2,1)S(1)}, u32[]{:S(2)}, u32[]{:S(2)}) collective-permute-start(bf16[32,16,256]{2,1,0:T(8,128)(2,1)S(1)} %collective-permute-done.2.refs_5_), channel_id=1, source_target_pairs={{0,16},{16,0},{1,17},{17,1},{2,18},{18,2},{3,19},{19,3},{4,20},{20... | collective-permute-start | bytes 786440 | tf_op jit(solution)/shard_map/ppermute | solution.py:50
  28.0 10.5 %collective-permute-start.7 = (f32[256,128]{1,0:T(8,128)S(1)}, f32[256,128]{1,0:T(8,128)S(1)}, u32[]{:S(2)}, u32[]{:S(2)}) collective-permute-start(f32[256,128]{1,0:T(8,128)S(1)} %squares.1.refs_4_), channel_id=1, source_target_pairs={{0,2},{2,0},{1,3},{3,1},{4,6},{6,4},{5,7},{7,5},{8,10},{10,8},{9,1... | collective-permute-start | bytes 393224 | tf_op jit(solution)/shard_map/ppermute | solution.py:55
  31.9 33.4 %collective-permute-start.14 = (bf16[256,4096]{1,0:T(8,128)(2,1)S(1)}, bf16[256,4096]{1,0:T(8,128)(2,1)S(1)}, u32[]{:S(2)}, u32[]{:S(2)}) collective-permute-start(bf16[256,4096]{1,0:T(8,128)(2,1)S(1)} %get-tuple-element.82), channel_id=1, source_target_pairs={{0,1},{1,0},{2,3},{3,2},{4,5},{5,4},{6,7},{7,6},{8,9},{9,8},{10,11... | collective-permute-start | bytes 6291464 | tf_op jit(solution)/shard_map/ppermute | solution.py:50
  41.1 24.2 %collective-permute-start.8 = (bf16[256,4096]{1,0:T(8,128)(2,1)S(1)}, bf16[256,4096]{1,0:T(8,128)(2,1)S(1)}, u32[]{:S(2)}, u32[]{:S(2)}) collective-permute-start(bf16[256,4096]{1,0:T(8,128)(2,1)S(1)} %get-tuple-element.77), channel_id=1, source_target_pairs={{0,1},{1,0},{2,3},{3,2},{4,5},{5,4},{6,7},{7,6},{8,9},{9,8},{10,11... | collective-permute-start | bytes 6291464 | tf_op jit(solution)/shard_map/ppermute | solution.py:50
  43.7 10.1 %collective-permute-start.10 = (bf16[32,16,256]{2,1,0:T(8,128)(2,1)S(1)}, bf16[32,16,256]{2,1,0:T(8,128)(2,1)S(1)}, u32[]{:S(2)}, u32[]{:S(2)}) collective-permute-start(bf16[32,16,256]{2,1,0:T(8,128)(2,1)S(1)} %collective-permute-done.3.refs_7_), channel_id=1, source_target_pairs={{0,4},{4,12},{12,8},{8,0},{1,5},{5,13},{13,9},{9,1},{2,6},{6,14},{... | collective-permute-start | bytes 786440 | tf_op jit(solution)/shard_map/ppermute | solution.py:46
  46.5 11.7 %collective-permute-start.11 = (bf16[32,16,256]{2,1,0:T(8,128)(2,1)S(1)}, bf16[32,16,256]{2,1,0:T(8,128)(2,1)S(1)}, u32[]{:S(2)}, u32[]{:S(2)}) collective-permute-start(bf16[32,16,256]{2,1,0:T(8,128)(2,1)S(1)} %collective-permute-done.4.refs_7_), channel_id=1, source_target_pairs={{0,4},{4,12},{12,8},{8,0},{1,5},{5,13},{13,9},{9,1},{2,6},{6,14},{... | collective-permute-start | bytes 786440 | tf_op jit(solution)/shard_map/ppermute | solution.py:46
  46.8 11.9 %collective-permute-start.12 = (bf16[32,16,256]{2,1,0:T(8,128)(2,1)S(1)}, bf16[32,16,256]{2,1,0:T(8,128)(2,1)S(1)}, u32[]{:S(2)}, u32[]{:S(2)}) collective-permute-start(bf16[32,16,256]{2,1,0:T(8,128)(2,1)S(1)} %collective-permute-done.3.refs_7_), channel_id=1, source_target_pairs={{0,16},{16,0},{1,17},{17,1},{2,18},{18,2},{3,19},{19,3},{4,20},{20... | collective-permute-start | bytes 786440 | tf_op jit(solution)/shard_map/ppermute | solution.py:50
  58.8 13.8 %collective-permute-start.19 = (bf16[32,16,256]{2,1,0:T(8,128)(2,1)S(1)}, bf16[32,16,256]{2,1,0:T(8,128)(2,1)S(1)}, u32[]{:S(2)}, u32[]{:S(2)}) collective-permute-start(bf16[32,16,256]{2,1,0:T(8,128)(2,1)S(1)} %collective-permute-done.10.refs_9_), channel_id=1, source_target_pairs={{0,16},{16,0},{1,17},{17,1},{2,18},{18,2},{3,19},{19,3},{4,20},{20... | collective-permute-start | bytes 786440 | tf_op jit(solution)/shard_map/ppermute | solution.py:50
  77.2 9.2 %collective-permute-start.24 = (bf16[16,32,128]{2,1,0:T(8,128)(2,1)S(1)}, bf16[16,32,128]{2,1,0:T(8,128)(2,1)S(1)}, u32[]{:S(2)}, u32[]{:S(2)}) collective-permute-start(bf16[16,32,128]{2,1,0:T(8,128)(2,1)S(1)} %collective-permute-done.18.refs_7_), channel_id=1, source_target_pairs={{0,4},{4,12},{12,8},{8,0},{1,5},{5,13},{13,9},{9,1},{2,6},{6,14},{... | collective-permute-start | bytes 393224 | tf_op jit(solution)/shard_map/ppermute | solution.py:46
  91.3 9.0 %collective-permute-start.28 = (bf16[128,512]{1,0:T(8,128)(2,1)S(1)}, bf16[128,512]{1,0:T(8,128)(2,1)S(1)}, u32[]{:S(2)}, u32[]{:S(2)}) collective-permute-start(bf16[128,512]{1,0:T(8,128)(2,1)S(1)} %get-tuple-element.96), channel_id=1, source_target_pairs={{0,4},{4,12},{12,8},{8,0},{1,5},{5,13},{13,9},{9,1},{2,6},{6,14},{... | collective-permute-start | bytes 393224 | tf_op jit(solution)/shard_map/ppermute | solution.py:46
  92.7 9.9 %collective-permute-start.29 = (bf16[128,512]{1,0:T(8,128)(2,1)S(1)}, bf16[128,512]{1,0:T(8,128)(2,1)S(1)}, u32[]{:S(2)}, u32[]{:S(2)}) collective-permute-start(bf16[128,512]{1,0:T(8,128)(2,1)S(1)} %get-tuple-element.97), channel_id=1, source_target_pairs={{0,4},{4,12},{12,8},{8,0},{1,5},{5,13},{13,9},{9,1},{2,6},{6,14},{... | collective-permute-start | bytes 393224 | tf_op jit(solution)/shard_map/ppermute | solution.py:46
  93.3 9.5 %collective-permute-start.32 = (bf16[16,32,128]{2,1,0:T(8,128)(2,1)S(1)}, bf16[16,32,128]{2,1,0:T(8,128)(2,1)S(1)}, u32[]{:S(2)}, u32[]{:S(2)}) collective-permute-start(bf16[16,32,128]{2,1,0:T(8,128)(2,1)S(1)} %collective-permute-done.23.refs_9_), channel_id=1, source_target_pairs={{0,16},{16,0},{1,17},{17,1},{2,18},{18,2},{3,19},{19,3},{4,20},{20... | collective-permute-start | bytes 393224 | tf_op jit(solution)/shard_map/ppermute | solution.py:50
  94.8 11.3 %collective-permute-start.33 = (bf16[16,32,128]{2,1,0:T(8,128)(2,1)S(1)}, bf16[16,32,128]{2,1,0:T(8,128)(2,1)S(1)}, u32[]{:S(2)}, u32[]{:S(2)}) collective-permute-start(bf16[16,32,128]{2,1,0:T(8,128)(2,1)S(1)} %collective-permute-done.24.refs_11_), channel_id=1, source_target_pairs={{0,16},{16,0},{1,17},{17,1},{2,18},{18,2},{3,19},{19,3},{4,20},{20... | collective-permute-start | bytes 393224 | tf_op jit(solution)/shard_map/ppermute | solution.py:50
  128.6 9.1 %collective-permute-start.50 = (bf16[544,128]{1,0:T(8,128)(2,1)S(1)}, bf16[544,128]{1,0:T(8,128)(2,1)S(1)}, u32[]{:S(2)}, u32[]{:S(2)}) collective-permute-start(bf16[544,128]{1,0:T(8,128)(2,1)S(1)} %get-tuple-element.119), channel_id=1, source_target_pairs={{0,4},{4,12},{12,8},{8,0},{1,5},{5,13},{13,9},{9,1},{2,6},{6,14},{... | collective-permute-start | bytes 417800 | tf_op jit(solution)/shard_map/ppermute | solution.py:46
  140.8 9.7 %collective-permute-start.49 = (bf16[544,128]{1,0:T(8,128)(2,1)S(1)}, bf16[544,128]{1,0:T(8,128)(2,1)S(1)}, u32[]{:S(2)}, u32[]{:S(2)}) collective-permute-start(bf16[544,128]{1,0:T(8,128)(2,1)S(1)} %add.37), channel_id=1, source_target_pairs={{0,4},{4,12},{12,8},{8,0},{1,5},{5,13},{13,9},{9,1},{2,6},{6,14},{... | collective-permute-start | bytes 417800 | tf_op jit(solution)/shard_map/ppermute | solution.py:46
  157.2 8.8 %collective-permute-start.69 = (bf16[128,512]{1,0:T(8,128)(2,1)S(1)}, bf16[128,512]{1,0:T(8,128)(2,1)S(1)}, u32[]{:S(2)}, u32[]{:S(2)}) collective-permute-start(bf16[128,512]{1,0:T(8,128)(2,1)S(1)} %collective-permute-done.67.refs_4_), channel_id=1, source_target_pairs={{0,4},{4,12},{12,8},{8,0},{1,5},{5,13},{13,9},{9,1},{2,6},{6,14},{... | collective-permute-start | bytes 393224 | tf_op jit(solution)/shard_map/ppermute | solution.py:46
  159.2 9.6 %collective-permute-start.70 = (bf16[128,512]{1,0:T(8,128)(2,1)S(1)}, bf16[128,512]{1,0:T(8,128)(2,1)S(1)}, u32[]{:S(2)}, u32[]{:S(2)}) collective-permute-start(bf16[128,512]{1,0:T(8,128)(2,1)S(1)} %collective-permute-done.68.refs_5_), channel_id=1, source_target_pairs={{0,4},{4,12},{12,8},{8,0},{1,5},{5,13},{13,9},{9,1},{2,6},{6,14},{... | collective-permute-start | bytes 393224 | tf_op jit(solution)/shard_map/ppermute | solution.py:46
  160.6 11.2 %collective-permute-start.55 = (bf16[544,128]{1,0:T(8,128)(2,1)S(1)}, bf16[544,128]{1,0:T(8,128)(2,1)S(1)}, u32[]{:S(2)}, u32[]{:S(2)}) collective-permute-start(bf16[544,128]{1,0:T(8,128)(2,1)S(1)} %collective-permute-done.53.refs_2_), channel_id=1, source_target_pairs={{0,4},{4,12},{12,8},{8,0},{1,5},{5,13},{13,9},{9,1},{2,6},{6,14},{... | collective-permute-start | bytes 417800 | tf_op jit(solution)/shard_map/ppermute | solution.py:46
  163.2 11.3 %collective-permute-start.56 = (bf16[544,128]{1,0:T(8,128)(2,1)S(1)}, bf16[544,128]{1,0:T(8,128)(2,1)S(1)}, u32[]{:S(2)}, u32[]{:S(2)}) collective-permute-start(bf16[544,128]{1,0:T(8,128)(2,1)S(1)} %collective-permute-done.54.refs_3_), channel_id=1, source_target_pairs={{0,4},{4,12},{12,8},{8,0},{1,5},{5,13},{13,9},{9,1},{2,6},{6,14},{... | collective-permute-start | bytes 417800 | tf_op jit(solution)/shard_map/ppermute | solution.py:46
  (73 other events, 521.7 us)

commit v9 on v8

--- a/solution.py
+++ b/solution.py
@@ -88,7 +88,7 @@
     return call(add_kernel, "add", [left, right], [shape(left.shape)], limit=4)[0]
 
 
-def ring_all(parts, streams):
+def ring_all(parts, streams, last=()):
     n = lax.axis_size("dp")
     seen = []
     totals = list(parts[:streams])
@@ -96,14 +96,16 @@
         seen.append([ring_step(t) for t in totals])
         totals = [add(t, p) for t, p in zip(seen[-1], parts[k * streams : (k + 1) * streams])]
     blocks = list(totals)
-    for _ in range(n - 1):
+    for k in range(n - 1):
+        if last and k == n - 2:
+            totals = [after(t, *last) for t in totals]
         totals = [ring_step(t) for t in totals]
         seen.append(totals)
         blocks += totals
     return blocks + [swap(b, "sub") for b in blocks], seen
 
 
-def scaled_halves(wide, low_ref, cols, scaled, product, send_ref, own_ref, arrive=None):
+def scaled_halves(wide, low_ref, cols, scaled, product, send_ref, own_ref, copy):
     half = send_ref.shape[1]
     step = half // 4
     sub = lax.axis_index("sub")
@@ -113,8 +115,7 @@
         @pl.loop(0, half // step)
         def _(j, n=n, which=which, out_ref=out_ref):
             first = pl.multiple_of(which * half + j * step, step)
-            if arrive is not None:
-                arrive(n * (half // step) + j, first, step)
+            copy(n * (half // step) + j, first, step).wait()
             parts = []
             for i in range(step // LANES):
                 tile = pl.ds(pl.multiple_of(first + i * LANES, LANES), LANES)
@@ -129,6 +130,17 @@
         at = pl.ds(first, step)
         return pltpu.make_async_copy(source.at[:, at], buffer.at[:, at], sems.at[k])
 
+    return copy
+
+
+def start_halves(source, buffer, sems):
+    half = source.shape[1] // 2
+    step = half // 4
+    copy = column_copy(source, buffer, sems)
+    sub = lax.axis_index("sub")
+    for k in range(8):
+        which = 1 - sub if k < 4 else sub
+        copy(k, pl.multiple_of(which * half + k % 4 * step, step), step).start()
     return copy
 
 
@@ -150,14 +162,8 @@
 def cotangent_kernel(
     total, cotangent, lengths, slots, adapter, send_ref, own_ref, low_ref, buffer, sems
 ):
-    rows, width = cotangent.shape
-    half = width // 2
-    step = half // 4
-    copy = column_copy(cotangent, buffer, sems)
-    sub = lax.axis_index("sub")
-    for k in range(8):
-        which = 1 - sub if k < 4 else sub
-        copy(k, pl.multiple_of(which * half + k % 4 * step, step), step).start()
+    rows = cotangent.shape[0]
+    copy = start_halves(cotangent, buffer, sems)
     index = jnp.broadcast_to(slots[...], (LANES, rows))
     weight = jnp.zeros((LANES, rows), F32)
     for s in range(lengths.shape[1]):
@@ -172,12 +178,13 @@
         lambda value, cols: contract_dims(value, adapter[:, cols], 1, 1),
         send_ref,
         own_ref,
-        lambda k, first, step: copy(k, first, step).wait(),
+        copy,
     )
 
 
 def token_kernel(total_width, tokens, gain, adapter, low_out, squares, *refs):
-    squares_more, (send_ref, own_ref, low_ref) = refs[:-3], refs[-3:]
+    squares_more, (send_ref, own_ref, low_ref, buffer, sems) = refs[:-5], refs[-5:]
+    copy = start_halves(tokens, buffer, sems)
     rank = adapter.shape[1]
     total = squares[...]
     for ref in squares_more:
@@ -185,13 +192,14 @@
     row = lax.rsqrt(total / total_width + EPS)
     low_ref[:, rank:] = low_out[...]
     scaled_halves(
-        tokens,
+        buffer,
         low_ref,
         slice(0, rank),
         lambda tile, cols: tile * row * gain[:, cols].astype(F32),
         lambda value, cols: dot(value, adapter[cols, :]),
         send_ref,
         own_ref,
+        copy,
     )
 
 
@@ -544,26 +552,28 @@
     crossed += [swap(after(r, grad), "grp") for r in ring]
     step(ring[0], ring[1], grad)
     step(ring[1], ring[0], grad)
+    down_turned = jnp.swapaxes(after(down_codes, ring[2]), 0, 1)
+    down_moving, down_got = start_shards([down_turned], STREAMS)
     normed_send, normed, low = call(
         lambda *refs: token_kernel(total_width, *refs),
         "tokens",
-        [tokens, rms_norm_gain[None, :], up_adapter_in, low_out, after(squares, *ring[2:4], *crossed[:2]), *squares_more],
+        [tokens, rms_norm_gain[None, :], up_adapter_in, low_out, after(squares, *ring[2:4], *crossed[:2], *down_moving), *squares_more],
         [shape((rows, half))] * 2 + [shape((rows, 2 * rank), F32)],
+        scratch=buffers,
+        specs=[hbm] + [vmem] * (4 + more),
     )
     grad_got = swap(grad_send, "sub")
     normed_got = swap(normed_send, "sub")
     low_more = others(low, "mp")
-    down_turned = jnp.swapaxes(after(down_codes, *ring[2:4]), 0, 1)
-    down_moving, down_got = start_shards([down_turned], STREAMS)
     step(ring[2], ring[3], *crossed[:2])
     step(ring[3], ring[2], *crossed[:2])
     adapters = jnp.concatenate([up_adapter_out, down_adapter_in], axis=0)
-    adapters_more = others(after(adapters, *ring[2:4]), "mp")
-    pinned = [*ring[4:6], *crossed[2:4], grad_got, normed_got, *low_more, *adapters_more]
+    adapters_more = others(after(adapters, ring[4]), "mp")
+    pinned = [*ring[4:6], *crossed[2:4], grad_got, normed_got]
     for moving in down_moving:
         step(moving, *pinned)
     for moving in ring[-STREAMS:]:
-        step(moving)
+        step(moving, *low_more, *adapters_more)
 
     def product(kernel, name, own, got, scale, codes, codes_got, first_got, steps, weight_shape):
         groups = scale.shape[0]
@@ -622,13 +632,13 @@
     )
 
     back, back_more, _ = product(
-        back_kernel, "back", after(grad, *seen[0]), grad_got, down_block_scale, down_turned, down_got, 0,
+        back_kernel, "back", grad, grad_got, after(down_block_scale, normed_t, down_out_parts[0]), down_turned, down_got, 0,
         range(2 * (n - 1), (2 + STREAMS) * (n - 1)), (units, half),
     )
     low_grad, up_out_term = call(
         lambda *refs: up_grad_kernel(more, *refs),
         "up_grad",
-        [back, silu, low, adapters, *back_more, *low_more, *adapters_more],
+        [back, silu, low, after(adapters, *seen[0]), *back_more, *low_more, *adapters_more],
         [shape((rows, rank)), shape(up_adapter_out.shape)],
         scratch=small_scratch,
         limit=8,
@@ -637,11 +647,11 @@
     up_in_parts = call(
         lambda *refs: up_in_kernel(n, *refs),
         "up_in",
-        [after(low_grad, *seen[3]), swap(low_grad, "sub"), normed_t, up_out_term, down_in_term],
+        [after(low_grad, *seen[1]), swap(low_grad, "sub"), normed_t, up_out_term, down_in_term],
         [shape((half // pieces + extra, rank))] * pieces,
         flops=4 * rows * half * rank,
     )
-    up_in_blocks, _ = ring_all(up_in_parts, STREAMS)
+    up_in_blocks, _ = ring_all(up_in_parts, STREAMS, down_out_blocks[-STREAMS:])
 
     anywhere = pl.BlockSpec(memory_space=pl.ANY)
     (down_out_gradient,) = call(

time: 185 us -> 199 us (1.076)
  waiting for transfers between devices: 78.4 us -> 106 us
  starting transfers between devices: 73.8 us -> 58.8 us
    ppermute x36, waiting for transfers between devices: 64.3 us -> 84.7 us  [ring_step(): lax.ppermute(x, 'dp', [(ring_at(i, n), ring_at((i + 1) % n, n)) for i in...]
    ppermute x37, waiting for transfers between devices: 6.36 us -> 20.5 us  [swap(): return lax.ppermute(x, axis, [(0, 1), (1, 0)])]
    ppermute x36, starting transfers between devices: 46.2 us -> 33.3 us  [ring_step(): lax.ppermute(x, 'dp', [(ring_at(i, n), ring_at((i + 1) % n, n)) for i in...]
    ppermute x6, waiting for transfers between devices: 7.68 us -> 0.87 us  [others(): lax.ppermute(x, axis, [(i, (i + k) % n) for i in range(n)])]
    ppermute x37, starting transfers between devices: 21.3 us -> 18.2 us  [swap(): return lax.ppermute(x, axis, [(0, 1), (1, 0)])]
  transfers between devices with their start and end apart: 79 -> 79, of which waited for: 40 -> 46; matrix products, arithmetic and copies ran while one was open for 0% -> 0% of each run, Pallas kernels for 11% -> 9%
where the time goes in v9:
time: 199 us; the launch traced here: 198 us
  waiting for transfers between devices  106 us (53%)
  starting transfers between devices  58.8 us (30%)
  Pallas kernels  27.2 us (14%)
  local copies, waits for them, and re-layouts  4.73 us (2%)
    ppermute x36, waiting for transfers between devices, ring_step(): lax.ppermute(x, 'dp', [(ring_at(i, n), ring_at((i + 1) % n, n)) for i in...  84.7 us
    ppermute x36, starting transfers between devices, ring_step(): lax.ppermute(x, 'dp', [(ring_at(i, n), ring_at((i + 1) % n, n)) for i in...  33.3 us
    pallas_call x29, Pallas kernels, call(): pl.pallas_call(kernel, out_shape=tuple(out_shape), in_specs=specs or [vme...  27.2 us
    ppermute x37, waiting for transfers between devices, swap(): return lax.ppermute(x, axis, [(0, 1), (1, 0)])  20.5 us
    ppermute x37, starting transfers between devices, swap(): return lax.ppermute(x, axis, [(0, 1), (1, 0)])  18.2 us
    ppermute x6, starting transfers between devices, others(): lax.ppermute(x, axis, [(i, (i + k) % n) for i in range(n)])  7.4 us
    unnamed x37, local copies, waits for them, and re-layouts  4.35 us
  transfers between devices with their start and end apart: 79, of which 46 were waited for; matrix products, arithmetic and copies ran while one was open for 0% of the time, Pallas kernels for 9%

profile of v9, /device:TPU:0, one launch (start us, length us, event | category | flops | bytes accessed | tf_op | source)
XLA Modules:
  0.0 198.3 jit_solution(5389877930874689804)
XLA Ops:
  5.5 3.0 %collective-permute-start.2 = (bf16[32,16,256]{2,1,0:T(8,128)(2,1)S(1)}, bf16[32,16,256]{2,1,0:T(8,128)(2,1)S(1)}, u32[]{:S(2)}, u32[]{:S(2)}) collective-permute-start(bf16[32,16,256]{2,1,0:T(8,128)(2,1)S(1)} %get-tuple-element.70), channel_id=1, source_target_pairs={{0,4},{4,12},{12,8},{8,0},{1,5},{5,13},{13,9},{9,1},{2,6},{6,14},{... | collective-permute-start | bytes 786440 | tf_op jit(solution)/shard_map/ppermute | solution.py:46
  15.8 4.2 %cotangent.1 = (bf16[256,4096]{1,0:T(8,128)(2,1)S(1)}, bf16[256,4096]{1,0:T(8,128)(2,1)S(1)}, f32[256,128]{1,0:T(8,128)S(1)}) custom-call(bf16[256,8192]{1,0:T(8,128)(2,1)S(1)} %copy-done.6, s32[1,2]{1,0:T(1,128)S(1)} %copy-done.9, s32[1,256]{1,0:T(1,128)S(1)} %bitcast.9, bf16[128,8192]{1,0:T(8,128)(2,1)S(1)} %copy-done.8), custom_call_target="tpu_custom_call" | custom-call | tf_op jit(solution)/shard_map/cotangent/pallas_call | solution.py:67
  22.6 3.4 %collective-permute-start.5 = (bf16[32,16,256]{2,1,0:T(8,128)(2,1)S(1)}, bf16[32,16,256]{2,1,0:T(8,128)(2,1)S(1)}, u32[]{:S(2)}, u32[]{:S(2)}) collective-permute-start(bf16[32,16,256]{2,1,0:T(8,128)(2,1)S(1)} %collective-permute-done.3.refs_5_), channel_id=1, source_target_pairs={{0,4},{4,12},{12,8},{8,0},{1,5},{5,13},{13,9},{9,1},{2,6},{6,14},{... | collective-permute-start | bytes 786440 | tf_op jit(solution)/shard_map/ppermute | solution.py:46
  26.0 5.9 %collective-permute-done.4.refs_7_ = bf16[32,16,256]{2,1,0:T(8,128)(2,1)S(1)} collective-permute-done((bf16[32,16,256]{2,1,0:T(8,128)(2,1)S(1)}, bf16[32,16,256]{2,1,0:T(8,128)(2,1)S(1)}, u32[]{:S(2)}, u32[]{:S(2)}) %collective-permute-start.4) | collective-permute-done | bytes 262176 | tf_op jit(solution)/shard_map/ppermute | solution.py:46
  36.5 5.0 %collective-permute-done.6.refs_6_ = bf16[32,16,256]{2,1,0:T(8,128)(2,1)S(1)} collective-permute-done((bf16[32,16,256]{2,1,0:T(8,128)(2,1)S(1)}, bf16[32,16,256]{2,1,0:T(8,128)(2,1)S(1)}, u32[]{:S(2)}, u32[]{:S(2)}) %collective-permute-start.6) | collective-permute-done | bytes 262176 | tf_op jit(solution)/shard_map/ppermute | solution.py:50
  41.5 5.2 %collective-permute-done.7.refs_6_ = bf16[32,16,256]{2,1,0:T(8,128)(2,1)S(1)} collective-permute-done((bf16[32,16,256]{2,1,0:T(8,128)(2,1)S(1)}, bf16[32,16,256]{2,1,0:T(8,128)(2,1)S(1)}, u32[]{:S(2)}, u32[]{:S(2)}) %collective-permute-start.7) | collective-permute-done | bytes 262176 | tf_op jit(solution)/shard_map/ppermute | solution.py:50
  46.8 3.0 %tokens.3 = (bf16[256,4096]{1,0:T(8,128)(2,1)S(1)}, bf16[256,4096]{1,0:T(8,128)(2,1)S(1)}, f32[256,256]{1,0:T(8,128)S(1)}) custom-call(bf16[256,8192]{1,0:T(8,128)(2,1)S(1)} %copy-done.1, bf16[1,8192]{1,0:T(2,128)(2,1)S(1)} %broadcast_in_dim.7.refs_1_, bf16[8192,128]{1,0:T(8,128)(2,1)S(1)} %copy-done.7, f32[256,128]{1,0:T(8,128)S(1)} %get-tuple-element.76.refs_3_, ...), custom_call_target="tpu_custom_call" | custom-call | tf_op jit(solution)/shard_map/tokens/pallas_call | solution.py:67
  50.8 3.4 %collective-permute-start.12 = (bf16[32,16,256]{2,1,0:T(8,128)(2,1)S(1)}, bf16[32,16,256]{2,1,0:T(8,128)(2,1)S(1)}, u32[]{:S(2)}, u32[]{:S(2)}) collective-permute-start(bf16[32,16,256]{2,1,0:T(8,128)(2,1)S(1)} %collective-permute-done.5.refs_7_), channel_id=1, source_target_pairs={{0,4},{4,12},{12,8},{8,0},{1,5},{5,13},{13,9},{9,1},{2,6},{6,14},{... | collective-permute-start | bytes 786440 | tf_op jit(solution)/shard_map/ppermute | solution.py:46
  55.7 4.2 %collective-permute-done.11.refs_9_ = bf16[32,16,256]{2,1,0:T(8,128)(2,1)S(1)} collective-permute-done((bf16[32,16,256]{2,1,0:T(8,128)(2,1)S(1)}, bf16[32,16,256]{2,1,0:T(8,128)(2,1)S(1)}, u32[]{:S(2)}, u32[]{:S(2)}) %collective-permute-start.11) | collective-permute-done | bytes 262176 | tf_op jit(solution)/shard_map/ppermute | solution.py:46
  61.5 3.6 %collective-permute-done.12.refs_9_ = bf16[32,16,256]{2,1,0:T(8,128)(2,1)S(1)} collective-permute-done((bf16[32,16,256]{2,1,0:T(8,128)(2,1)S(1)}, bf16[32,16,256]{2,1,0:T(8,128)(2,1)S(1)}, u32[]{:S(2)}, u32[]{:S(2)}) %collective-permute-start.12) | collective-permute-done | bytes 262176 | tf_op jit(solution)/shard_map/ppermute | solution.py:46
  68.3 3.2 %collective-permute-start.16 = (bf16[16,32,128]{2,1,0:T(8,128)(2,1)S(1)}, bf16[16,32,128]{2,1,0:T(8,128)(2,1)S(1)}, u32[]{:S(2)}, u32[]{:S(2)}) collective-permute-start(bf16[16,32,128]{2,1,0:T(8,128)(2,1)S(1)} %get-tuple-element.90), channel_id=1, source_target_pairs={{0,4},{4,12},{12,8},{8,0},{1,5},{5,13},{13,9},{9,1},{2,6},{6,14},{... | collective-permute-start | bytes 393224 | tf_op jit(solution)/shard_map/ppermute | solution.py:46
  83.2 2.9 %collective-permute-start.24 = (bf16[16,32,128]{2,1,0:T(8,128)(2,1)S(1)}, bf16[16,32,128]{2,1,0:T(8,128)(2,1)S(1)}, u32[]{:S(2)}, u32[]{:S(2)}) collective-permute-start(bf16[16,32,128]{2,1,0:T(8,128)(2,1)S(1)} %collective-permute-done.16.refs_7_), channel_id=1, source_target_pairs={{0,4},{4,12},{12,8},{8,0},{1,5},{5,13},{13,9},{9,1},{2,6},{6,14},{... | collective-permute-start | bytes 393224 | tf_op jit(solution)/shard_map/ppermute | solution.py:46
  112.1 4.5 %collective-permute-done.37.left = bf16[128,512]{1,0:T(8,128)(2,1)S(1)} collective-permute-done((bf16[128,512]{1,0:T(8,128)(2,1)S(1)}, bf16[128,512]{1,0:T(8,128)(2,1)S(1)}, u32[]{:S(2)}, u32[]{:S(2)}) %collective-permute-start.37) | collective-permute-done | bytes 131104 | tf_op jit(solution)/shard_map/ppermute | solution.py:46
  125.4 3.4 %up_in.1 = (bf16[544,128]{1,0:T(8,128)(2,1)S(1)}, bf16[544,128]{1,0:T(8,128)(2,1)S(1)}, bf16[544,128]{1,0:T(8,128)(2,1)S(1)}, bf16[544,128]{1,0:T(8,128)(2,1)S(1...) custom-call(bf16[256,128]{1,0:T(8,128)(2,1)S(1)} %get-tuple-element., ...), custom_call_target="tpu_custom_call" | custom-call | tf_op jit(solution)/shard_map/up_in/pallas_call | solution.py:67
  136.4 2.9 %collective-permute-done.46.left = bf16[544,128]{1,0:T(8,128)(2,1)S(1)} collective-permute-done((bf16[544,128]{1,0:T(8,128)(2,1)S(1)}, bf16[544,128]{1,0:T(8,128)(2,1)S(1)}, u32[]{:S(2)}, u32[]{:S(2)}) %collective-permute-start.46) | collective-permute-done | bytes 139296 | tf_op jit(solution)/shard_map/ppermute | solution.py:46
  145.0 2.9 %collective-permute-done.44.left = bf16[544,128]{1,0:T(8,128)(2,1)S(1)} collective-permute-done((bf16[544,128]{1,0:T(8,128)(2,1)S(1)}, bf16[544,128]{1,0:T(8,128)(2,1)S(1)}, u32[]{:S(2)}, u32[]{:S(2)}) %collective-permute-start.44) | collective-permute-done | bytes 139296 | tf_op jit(solution)/shard_map/ppermute | solution.py:46
  148.0 2.9 %collective-permute-done.47.left = bf16[544,128]{1,0:T(8,128)(2,1)S(1)} collective-permute-done((bf16[544,128]{1,0:T(8,128)(2,1)S(1)}, bf16[544,128]{1,0:T(8,128)(2,1)S(1)}, u32[]{:S(2)}, u32[]{:S(2)}) %collective-permute-start.47) | collective-permute-done | bytes 139296 | tf_op jit(solution)/shard_map/ppermute | solution.py:46
  153.7 2.8 %collective-permute-done.59.refs_3_ = bf16[128,512]{1,0:T(8,128)(2,1)S(1)} collective-permute-done((bf16[128,512]{1,0:T(8,128)(2,1)S(1)}, bf16[128,512]{1,0:T(8,128)(2,1)S(1)}, u32[]{:S(2)}, u32[]{:S(2)}) %collective-permute-start.59) | collective-permute-done | bytes 131104 | tf_op jit(solution)/shard_map/ppermute | solution.py:46
  156.5 3.0 %collective-permute-done.45.left = bf16[544,128]{1,0:T(8,128)(2,1)S(1)} collective-permute-done((bf16[544,128]{1,0:T(8,128)(2,1)S(1)}, bf16[544,128]{1,0:T(8,128)(2,1)S(1)}, u32[]{:S(2)}, u32[]{:S(2)}) %collective-permute-start.45) | collective-permute-done | bytes 139296 | tf_op jit(solution)/shard_map/ppermute | solution.py:46
  159.6 2.9 %collective-permute-done.48.left = bf16[544,128]{1,0:T(8,128)(2,1)S(1)} collective-permute-done((bf16[544,128]{1,0:T(8,128)(2,1)S(1)}, bf16[544,128]{1,0:T(8,128)(2,1)S(1)}, u32[]{:S(2)}, u32[]{:S(2)}) %collective-permute-start.48) | collective-permute-done | bytes 139296 | tf_op jit(solution)/shard_map/ppermute | solution.py:46
  165.3 2.8 %collective-permute-done.60.refs_5_ = bf16[128,512]{1,0:T(8,128)(2,1)S(1)} collective-permute-done((bf16[128,512]{1,0:T(8,128)(2,1)S(1)}, bf16[128,512]{1,0:T(8,128)(2,1)S(1)}, u32[]{:S(2)}, u32[]{:S(2)}) %collective-permute-start.60) | collective-permute-done | bytes 131104 | tf_op jit(solution)/shard_map/ppermute | solution.py:46
  168.1 3.0 %collective-permute-done.49.refs_2_ = bf16[544,128]{1,0:T(8,128)(2,1)S(1)} collective-permute-done((bf16[544,128]{1,0:T(8,128)(2,1)S(1)}, bf16[544,128]{1,0:T(8,128)(2,1)S(1)}, u32[]{:S(2)}, u32[]{:S(2)}) %collective-permute-start.49) | collective-permute-done | bytes 139296 | tf_op jit(solution)/shard_map/ppermute | solution.py:46
  171.1 3.0 %collective-permute-done.50.refs_3_ = bf16[544,128]{1,0:T(8,128)(2,1)S(1)} collective-permute-done((bf16[544,128]{1,0:T(8,128)(2,1)S(1)}, bf16[544,128]{1,0:T(8,128)(2,1)S(1)}, u32[]{:S(2)}, u32[]{:S(2)}) %collective-permute-start.50) | collective-permute-done | bytes 139296 | tf_op jit(solution)/shard_map/ppermute | solution.py:46
  187.1 5.1 %collective-permute-done.63.refs_6_ = bf16[544,128]{1,0:T(8,128)(2,1)S(1)} collective-permute-done((bf16[544,128]{1,0:T(8,128)(2,1)S(1)}, bf16[544,128]{1,0:T(8,128)(2,1)S(1)}, u32[]{:S(2)}, u32[]{:S(2)}) %collective-permute-start.63) | collective-permute-done | bytes 139296 | tf_op jit(solution)/shard_map/ppermute | solution.py:46
  (206 shorter events, 110.9 us)
Async XLA Ops:
  5.5 14.4 %collective-permute-start.2 = (bf16[32,16,256]{2,1,0:T(8,128)(2,1)S(1)}, bf16[32,16,256]{2,1,0:T(8,128)(2,1)S(1)}, u32[]{:S(2)}, u32[]{:S(2)}) collective-permute-start(bf16[32,16,256]{2,1,0:T(8,128)(2,1)S(1)} %get-tuple-element.70), channel_id=1, source_target_pairs={{0,4},{4,12},{12,8},{8,0},{1,5},{5,13},{13,9},{9,1},{2,6},{6,14},{... | collective-permute-start | bytes 786440 | tf_op jit(solution)/shard_map/ppermute | solution.py:46
  8.5 13.2 %collective-permute-start.3 = (bf16[32,16,256]{2,1,0:T(8,128)(2,1)S(1)}, bf16[32,16,256]{2,1,0:T(8,128)(2,1)S(1)}, u32[]{:S(2)}, u32[]{:S(2)}) collective-permute-start(bf16[32,16,256]{2,1,0:T(8,128)(2,1)S(1)} %get-tuple-element.71), channel_id=1, source_target_pairs={{0,4},{4,12},{12,8},{8,0},{1,5},{5,13},{13,9},{9,1},{2,6},{6,14},{... | collective-permute-start | bytes 786440 | tf_op jit(solution)/shard_map/ppermute | solution.py:46
  22.6 13.9 %collective-permute-start.5 = (bf16[32,16,256]{2,1,0:T(8,128)(2,1)S(1)}, bf16[32,16,256]{2,1,0:T(8,128)(2,1)S(1)}, u32[]{:S(2)}, u32[]{:S(2)}) collective-permute-start(bf16[32,16,256]{2,1,0:T(8,128)(2,1)S(1)} %collective-permute-done.3.refs_5_), channel_id=1, source_target_pairs={{0,4},{4,12},{12,8},{8,0},{1,5},{5,13},{13,9},{9,1},{2,6},{6,14},{... | collective-permute-start | bytes 786440 | tf_op jit(solution)/shard_map/ppermute | solution.py:46
  34.0 12.7 %collective-permute-start.7 = (bf16[32,16,256]{2,1,0:T(8,128)(2,1)S(1)}, bf16[32,16,256]{2,1,0:T(8,128)(2,1)S(1)}, u32[]{:S(2)}, u32[]{:S(2)}) collective-permute-start(bf16[32,16,256]{2,1,0:T(8,128)(2,1)S(1)} %collective-permute-done.3.refs_5_), channel_id=1, source_target_pairs={{0,16},{16,0},{1,17},{17,1},{2,18},{18,2},{3,19},{19,3},{4,20},{20... | collective-permute-start | bytes 786440 | tf_op jit(solution)/shard_map/ppermute | solution.py:50
  34.5 12.3 %collective-permute-start.9 = (f32[256,128]{1,0:T(8,128)S(1)}, f32[256,128]{1,0:T(8,128)S(1)}, u32[]{:S(2)}, u32[]{:S(2)}) collective-permute-start(f32[256,128]{1,0:T(8,128)S(1)} %squares.1.refs_4_), channel_id=1, source_target_pairs={{0,2},{2,0},{1,3},{3,1},{4,6},{6,4},{5,7},{7,5},{8,10},{10,8},{9,1... | collective-permute-start | bytes 393224 | tf_op jit(solution)/shard_map/ppermute | solution.py:55
  36.1 32.3 %collective-permute-start.1 = (bf16[256,4096]{1,0:T(8,128)(2,1)S(1)}, bf16[256,4096]{1,0:T(8,128)(2,1)S(1)}, u32[]{:S(2)}, u32[]{:S(2)}) collective-permute-start(bf16[256,4096]{1,0:T(8,128)(2,1)S(1)} %get-tuple-element.75), channel_id=1, source_target_pairs={{0,1},{1,0},{2,3},{3,2},{4,5},{5,4},{6,7},{7,6},{8,9},{9,8},{10,11... | collective-permute-start | bytes 6291464 | tf_op jit(solution)/shard_map/ppermute | solution.py:50
  49.8 18.5 %collective-permute-start.10 = (bf16[256,4096]{1,0:T(8,128)(2,1)S(1)}, bf16[256,4096]{1,0:T(8,128)(2,1)S(1)}, u32[]{:S(2)}, u32[]{:S(2)}) collective-permute-start(bf16[256,4096]{1,0:T(8,128)(2,1)S(1)} %get-tuple-element.86), channel_id=1, source_target_pairs={{0,1},{1,0},{2,3},{3,2},{4,5},{5,4},{6,7},{7,6},{8,9},{9,8},{10,11... | collective-permute-start | bytes 6291464 | tf_op jit(solution)/shard_map/ppermute | solution.py:50
  50.8 14.3 %collective-permute-start.12 = (bf16[32,16,256]{2,1,0:T(8,128)(2,1)S(1)}, bf16[32,16,256]{2,1,0:T(8,128)(2,1)S(1)}, u32[]{:S(2)}, u32[]{:S(2)}) collective-permute-start(bf16[32,16,256]{2,1,0:T(8,128)(2,1)S(1)} %collective-permute-done.5.refs_7_), channel_id=1, source_target_pairs={{0,4},{4,12},{12,8},{8,0},{1,5},{5,13},{13,9},{9,1},{2,6},{6,14},{... | collective-permute-start | bytes 786440 | tf_op jit(solution)/shard_map/ppermute | solution.py:46
  54.2 12.5 %collective-permute-start.13 = (bf16[32,16,256]{2,1,0:T(8,128)(2,1)S(1)}, bf16[32,16,256]{2,1,0:T(8,128)(2,1)S(1)}, u32[]{:S(2)}, u32[]{:S(2)}) collective-permute-start(bf16[32,16,256]{2,1,0:T(8,128)(2,1)S(1)} %collective-permute-done.4.refs_7_), channel_id=1, source_target_pairs={{0,16},{16,0},{1,17},{17,1},{2,18},{18,2},{3,19},{19,3},{4,20},{20... | collective-permute-start | bytes 786440 | tf_op jit(solution)/shard_map/ppermute | solution.py:50
  81.4 13.5 %collective-permute-start.20 = (bf16[256,256]{1,0:T(8,128)(2,1)S(1)}, bf16[256,256]{1,0:T(8,128)(2,1)S(1)}, u32[]{:S(2)}, u32[]{:S(2)}) collective-permute-start(bf16[256,256]{1,0:T(8,128)(2,1)S(1)} %get-tuple-element.96), channel_id=1, source_target_pairs={{0,1},{1,0},{2,3},{3,2},{4,5},{5,4},{6,7},{7,6},{8,9},{9,8},{10,11... | collective-permute-start | bytes 393224 | tf_op jit(solution)/shard_map/ppermute | solution.py:50
  130.6 11.5 %collective-permute-start.53 = (bf16[128,512]{1,0:T(8,128)(2,1)S(1)}, bf16[128,512]{1,0:T(8,128)(2,1)S(1)}, u32[]{:S(2)}, u32[]{:S(2)}) collective-permute-start(bf16[128,512]{1,0:T(8,128)(2,1)S(1)} %add.38), channel_id=1, source_target_pairs={{0,4},{4,12},{12,8},{8,0},{1,5},{5,13},{13,9},{9,1},{2,6},{6,14},{... | collective-permute-start | bytes 393224 | tf_op jit(solution)/shard_map/ppermute | solution.py:46
  131.6 13.3 %collective-permute-start.58 = (bf16[128,512]{1,0:T(8,128)(2,1)S(1)}, bf16[128,512]{1,0:T(8,128)(2,1)S(1)}, u32[]{:S(2)}, u32[]{:S(2)}) collective-permute-start(bf16[128,512]{1,0:T(8,128)(2,1)S(1)} %add.40), channel_id=1, source_target_pairs={{0,4},{4,12},{12,8},{8,0},{1,5},{5,13},{13,9},{9,1},{2,6},{6,14},{... | collective-permute-start | bytes 393224 | tf_op jit(solution)/shard_map/ppermute | solution.py:46
  136.4 11.5 %collective-permute-start.44 = (bf16[544,128]{1,0:T(8,128)(2,1)S(1)}, bf16[544,128]{1,0:T(8,128)(2,1)S(1)}, u32[]{:S(2)}, u32[]{:S(2)}) collective-permute-start(bf16[544,128]{1,0:T(8,128)(2,1)S(1)} %add.32), channel_id=1, source_target_pairs={{0,4},{4,12},{12,8},{8,0},{1,5},{5,13},{13,9},{9,1},{2,6},{6,14},{... | collective-permute-start | bytes 417800 | tf_op jit(solution)/shard_map/ppermute | solution.py:46
  139.4 11.5 %collective-permute-start.47 = (bf16[544,128]{1,0:T(8,128)(2,1)S(1)}, bf16[544,128]{1,0:T(8,128)(2,1)S(1)}, u32[]{:S(2)}, u32[]{:S(2)}) collective-permute-start(bf16[544,128]{1,0:T(8,128)(2,1)S(1)} %add.35), channel_id=1, source_target_pairs={{0,4},{4,12},{12,8},{8,0},{1,5},{5,13},{13,9},{9,1},{2,6},{6,14},{... | collective-permute-start | bytes 417800 | tf_op jit(solution)/shard_map/ppermute | solution.py:46
  142.2 11.6 %collective-permute-start.54 = (bf16[128,512]{1,0:T(8,128)(2,1)S(1)}, bf16[128,512]{1,0:T(8,128)(2,1)S(1)}, u32[]{:S(2)}, u32[]{:S(2)}) collective-permute-start(bf16[128,512]{1,0:T(8,128)(2,1)S(1)} %add.39.refs_0_), channel_id=1, source_target_pairs={{0,4},{4,12},{12,8},{8,0},{1,5},{5,13},{13,9},{9,1},{2,6},{6,14},{... | collective-permute-start | bytes 393224 | tf_op jit(solution)/shard_map/ppermute | solution.py:46
  145.0 11.6 %collective-permute-start.59 = (bf16[128,512]{1,0:T(8,128)(2,1)S(1)}, bf16[128,512]{1,0:T(8,128)(2,1)S(1)}, u32[]{:S(2)}, u32[]{:S(2)}) collective-permute-start(bf16[128,512]{1,0:T(8,128)(2,1)S(1)} %add.41.refs_1_), channel_id=1, source_target_pairs={{0,4},{4,12},{12,8},{8,0},{1,5},{5,13},{13,9},{9,1},{2,6},{6,14},{... | collective-permute-start | bytes 393224 | tf_op jit(solution)/shard_map/ppermute | solution.py:46
  148.0 11.5 %collective-permute-start.45 = (bf16[544,128]{1,0:T(8,128)(2,1)S(1)}, bf16[544,128]{1,0:T(8,128)(2,1)S(1)}, u32[]{:S(2)}, u32[]{:S(2)}) collective-permute-start(bf16[544,128]{1,0:T(8,128)(2,1)S(1)} %add.33), channel_id=1, source_target_pairs={{0,4},{4,12},{12,8},{8,0},{1,5},{5,13},{13,9},{9,1},{2,6},{6,14},{... | collective-permute-start | bytes 417800 | tf_op jit(solution)/shard_map/ppermute | solution.py:46
  150.9 11.5 %collective-permute-start.48 = (bf16[544,128]{1,0:T(8,128)(2,1)S(1)}, bf16[544,128]{1,0:T(8,128)(2,1)S(1)}, u32[]{:S(2)}, u32[]{:S(2)}) collective-permute-start(bf16[544,128]{1,0:T(8,128)(2,1)S(1)} %add.36), channel_id=1, source_target_pairs={{0,4},{4,12},{12,8},{8,0},{1,5},{5,13},{13,9},{9,1},{2,6},{6,14},{... | collective-permute-start | bytes 417800 | tf_op jit(solution)/shard_map/ppermute | solution.py:46
  153.7 11.6 %collective-permute-start.55 = (bf16[128,512]{1,0:T(8,128)(2,1)S(1)}, bf16[128,512]{1,0:T(8,128)(2,1)S(1)}, u32[]{:S(2)}, u32[]{:S(2)}) collective-permute-start(bf16[128,512]{1,0:T(8,128)(2,1)S(1)} %collective-permute-done.54.refs_2_), channel_id=1, source_target_pairs={{0,4},{4,12},{12,8},{8,0},{1,5},{5,13},{13,9},{9,1},{2,6},{6,14},{... | collective-permute-start | bytes 393224 | tf_op jit(solution)/shard_map/ppermute | solution.py:46
  156.5 11.6 %collective-permute-start.60 = (bf16[128,512]{1,0:T(8,128)(2,1)S(1)}, bf16[128,512]{1,0:T(8,128)(2,1)S(1)}, u32[]{:S(2)}, u32[]{:S(2)}) collective-permute-start(bf16[128,512]{1,0:T(8,128)(2,1)S(1)} %collective-permute-done.59.refs_3_), channel_id=1, source_target_pairs={{0,4},{4,12},{12,8},{8,0},{1,5},{5,13},{13,9},{9,1},{2,6},{6,14},{... | collective-permute-start | bytes 393224 | tf_op jit(solution)/shard_map/ppermute | solution.py:46
  159.5 11.5 %collective-permute-start.49 = (bf16[544,128]{1,0:T(8,128)(2,1)S(1)}, bf16[544,128]{1,0:T(8,128)(2,1)S(1)}, u32[]{:S(2)}, u32[]{:S(2)}) collective-permute-start(bf16[544,128]{1,0:T(8,128)(2,1)S(1)} %add.34.refs_0_), channel_id=1, source_target_pairs={{0,4},{4,12},{12,8},{8,0},{1,5},{5,13},{13,9},{9,1},{2,6},{6,14},{... | collective-permute-start | bytes 417800 | tf_op jit(solution)/shard_map/ppermute | solution.py:46
  162.5 11.5 %collective-permute-start.50 = (bf16[544,128]{1,0:T(8,128)(2,1)S(1)}, bf16[544,128]{1,0:T(8,128)(2,1)S(1)}, u32[]{:S(2)}, u32[]{:S(2)}) collective-permute-start(bf16[544,128]{1,0:T(8,128)(2,1)S(1)} %add.37.refs_1_), channel_id=1, source_target_pairs={{0,4},{4,12},{12,8},{8,0},{1,5},{5,13},{13,9},{9,1},{2,6},{6,14},{... | collective-permute-start | bytes 417800 | tf_op jit(solution)/shard_map/ppermute | solution.py:46
  165.3 11.6 %collective-permute-start.56 = (bf16[128,512]{1,0:T(8,128)(2,1)S(1)}, bf16[128,512]{1,0:T(8,128)(2,1)S(1)}, u32[]{:S(2)}, u32[]{:S(2)}) collective-permute-start(bf16[128,512]{1,0:T(8,128)(2,1)S(1)} %collective-permute-done.55.refs_4_), channel_id=1, source_target_pairs={{0,4},{4,12},{12,8},{8,0},{1,5},{5,13},{13,9},{9,1},{2,6},{6,14},{... | collective-permute-start | bytes 393224 | tf_op jit(solution)/shard_map/ppermute | solution.py:46
  168.1 11.6 %collective-permute-start.61 = (bf16[128,512]{1,0:T(8,128)(2,1)S(1)}, bf16[128,512]{1,0:T(8,128)(2,1)S(1)}, u32[]{:S(2)}, u32[]{:S(2)}) collective-permute-start(bf16[128,512]{1,0:T(8,128)(2,1)S(1)} %collective-permute-done.60.refs_5_), channel_id=1, source_target_pairs={{0,4},{4,12},{12,8},{8,0},{1,5},{5,13},{13,9},{9,1},{2,6},{6,14},{... | collective-permute-start | bytes 393224 | tf_op jit(solution)/shard_map/ppermute | solution.py:46
  (73 other events, 573.8 us)

commit v10 on v9

--- a/solution.py
+++ b/solution.py
@@ -88,7 +88,7 @@
     return call(add_kernel, "add", [left, right], [shape(left.shape)], limit=4)[0]
 
 
-def ring_all(parts, streams, last=()):
+def ring_all(parts, streams):
     n = lax.axis_size("dp")
     seen = []
     totals = list(parts[:streams])
@@ -96,9 +96,7 @@
         seen.append([ring_step(t) for t in totals])
         totals = [add(t, p) for t, p in zip(seen[-1], parts[k * streams : (k + 1) * streams])]
     blocks = list(totals)
-    for k in range(n - 1):
-        if last and k == n - 2:
-            totals = [after(t, *last) for t in totals]
+    for _ in range(n - 1):
         totals = [ring_step(t) for t in totals]
         seen.append(totals)
         blocks += totals
@@ -390,40 +388,29 @@
         c.wait()
 
 
-def down_out_place_kernel(n, *refs):
-    pieces, (out_ref, sems) = refs[:-2], refs[-2:]
+def place_kernel(n, *refs):
+    pieces = refs[:-7]
+    out_ref, up_out_ref, down_in_ref, wide_ref, small, sems, small_sems = refs[-7:]
     pos, sub = ring_position(), lax.axis_index("sub")
-    per_core = len(pieces) // 2
+    count = len(pieces) // 2
+    per_core = count // 2
     streams = per_core // n
+    size = out_ref.shape[0] // count
+    extra = pieces[count].shape[0] - size
     copies = []
-    for i, piece in enumerate(pieces):
-        half = sub if i < per_core else 1 - sub
-        block = lax.rem(pos - i % per_core // streams + n, n) * streams + i % streams
-        size = piece.shape[1]
-        at = pl.ds(pl.multiple_of((half * per_core + block) * size, size), size)
-        copies.append(pltpu.make_async_copy(piece, out_ref.at[:, at], sems.at[i]))
-    copy_all(copies)
-
-
-def up_in_place_kernel(n, *refs):
-    pieces, (out_ref, up_out_ref, down_in_ref, small, sems) = refs[:-5], refs[-5:]
-    pos, sub = ring_position(), lax.axis_index("sub")
-    per_core = len(pieces) // 2
-    streams = per_core // n
-    size = out_ref.shape[0] // len(pieces)
-    extra = pieces[0].shape[0] - size
-    copies = []
-    for i, piece in enumerate(pieces):
+    for i in range(count):
         half = sub if i < per_core else 1 - sub
         block = lax.rem(pos - i % per_core // streams + n, n) * streams + i % streams
         at = pl.ds(pl.multiple_of((half * per_core + block) * size, size), size)
+        copies.append(pltpu.make_async_copy(pieces[i], wide_ref.at[:, at], sems.at[2 * i]))
+        piece = pieces[count + i]
         copies.append(
-            pltpu.make_async_copy(piece.at[pl.ds(0, size), :], out_ref.at[at, :], sems.at[2 * i])
+            pltpu.make_async_copy(piece.at[pl.ds(0, size), :], out_ref.at[at, :], sems.at[2 * i + 1])
         )
         at = pl.ds(pl.multiple_of(block * extra, extra), extra)
         copies.append(
             pltpu.make_async_copy(
-                piece.at[pl.ds(size, extra), :], small.at[i // per_core, at, :], sems.at[2 * i + 1]
+                piece.at[pl.ds(size, extra), :], small.at[i // per_core, at, :], small_sems.at[i]
             )
         )
     copy_all(copies)
@@ -549,15 +536,15 @@
         scratch=buffers,
         specs=[hbm, smem, vmem, vmem],
     )
+    down_turned = jnp.swapaxes(after(down_codes, squares), 0, 1)
+    down_moving, down_got = start_shards([down_turned], 1)
     crossed += [swap(after(r, grad), "grp") for r in ring]
-    step(ring[0], ring[1], grad)
-    step(ring[1], ring[0], grad)
-    down_turned = jnp.swapaxes(after(down_codes, ring[2]), 0, 1)
-    down_moving, down_got = start_shards([down_turned], STREAMS)
+    step(ring[0], ring[1], grad, *down_moving)
+    step(ring[1], ring[0], grad, *down_moving)
     normed_send, normed, low = call(
         lambda *refs: token_kernel(total_width, *refs),
         "tokens",
-        [tokens, rms_norm_gain[None, :], up_adapter_in, low_out, after(squares, *ring[2:4], *crossed[:2], *down_moving), *squares_more],
+        [tokens, rms_norm_gain[None, :], up_adapter_in, low_out, after(squares, *ring[2:4], *crossed[:2]), *squares_more],
         [shape((rows, half))] * 2 + [shape((rows, 2 * rank), F32)],
         scratch=buffers,
         specs=[hbm] + [vmem] * (4 + more),
@@ -569,11 +556,8 @@
     step(ring[3], ring[2], *crossed[:2])
     adapters = jnp.concatenate([up_adapter_out, down_adapter_in], axis=0)
     adapters_more = others(after(adapters, ring[4]), "mp")
-    pinned = [*ring[4:6], *crossed[2:4], grad_got, normed_got]
-    for moving in down_moving:
-        step(moving, *pinned)
-    for moving in ring[-STREAMS:]:
-        step(moving, *low_more, *adapters_more)
+    step(down_moving[0], *ring[4:6], *crossed[2:4])
+    step(ring[-1])
 
     def product(kernel, name, own, got, scale, codes, codes_got, first_got, steps, weight_shape):
         groups = scale.shape[0]
@@ -589,7 +573,7 @@
         return total, others(total.astype(BF16), "mp"), mine
 
     front = (blocks // 2, block, units)
-    first_down = ring[2 * (n - 1) : 2 * (n - 1) + STREAMS]
+    first_down = [ring[2 * (n - 1)], grad_got, *low_more, *adapters_more]
     half_blocks = blocks // 2
     gate, gate_more, gate_mine = product(
         front_kernel, "gate", normed, normed_got, after(gate_block_scale.T, *first_down), gate_codes, front_got, 0,
@@ -600,8 +584,7 @@
         range(1, 2 * (n - 1), 2), front,
     )
     for _ in range(n - 3):
-        for moving, other in zip(ring[-STREAMS:], crossed[-2 * STREAMS : -STREAMS]):
-            step(moving, gate_mine, up_mine, other)
+        step(ring[-1], gate_mine, up_mine, crossed[-2])
     small_scratch = [
         pltpu.VMEM((rank, units), BF16),
         pltpu.VMEM((units, rank), BF16),
@@ -609,7 +592,7 @@
     silu, low_hidden, down_in_term = call(
         lambda *refs: hidden_kernel(more, *refs),
         "hidden",
-        [gate, up, low, after(adapters, *ring[-2 * STREAMS : -STREAMS]), *gate_more, *up_more, *low_more, *adapters_more],
+        [gate, up, low, after(adapters, ring[-2]), *gate_more, *up_more, *low_more, *adapters_more],
         [shape((rows, units), F32), shape((rows, rank)), shape(down_adapter_in.shape)],
         scratch=small_scratch,
         limit=8,
@@ -632,13 +615,13 @@
     )
 
     back, back_more, _ = product(
-        back_kernel, "back", grad, grad_got, after(down_block_scale, normed_t, down_out_parts[0]), down_turned, down_got, 0,
-        range(2 * (n - 1), (2 + STREAMS) * (n - 1)), (units, half),
+        back_kernel, "back", grad, grad_got, after(down_block_scale, normed_t, *seen[0]), down_turned, down_got, 0,
+        range(2 * (n - 1), 3 * (n - 1)), (units, half),
     )
     low_grad, up_out_term = call(
         lambda *refs: up_grad_kernel(more, *refs),
         "up_grad",
-        [back, silu, low, after(adapters, *seen[0]), *back_more, *low_more, *adapters_more],
+        [back, silu, low, adapters, *back_more, *low_more, *adapters_more],
         [shape((rows, rank)), shape(up_adapter_out.shape)],
         scratch=small_scratch,
         limit=8,
@@ -651,27 +634,26 @@
         [shape((half // pieces + extra, rank))] * pieces,
         flops=4 * rows * half * rank,
     )
-    up_in_blocks, _ = ring_all(up_in_parts, STREAMS, down_out_blocks[-STREAMS:])
+    up_in_blocks, _ = ring_all(up_in_parts, STREAMS)
 
     anywhere = pl.BlockSpec(memory_space=pl.ANY)
-    (down_out_gradient,) = call(
-        lambda *refs: down_out_place_kernel(n, *refs),
-        "down_out_place",
-        down_out_blocks,
-        [shape((rank, local_width))],
-        scratch=[pltpu.SemaphoreType.DMA((2 * pieces,))],
-        specs=[anywhere] * (2 * pieces),
-        out_specs=(anywhere,),
-        limit=4,
-    )
-    up_in_gradient, up_out_gradient, down_in_gradient = call(
-        lambda *refs: up_in_place_kernel(n, *refs),
-        "up_in_place",
-        up_in_blocks,
-        [shape((local_width, rank)), shape(up_adapter_out.shape), shape(down_adapter_in.shape)],
-        scratch=[pltpu.VMEM((2, 2 * rank, rank), BF16), pltpu.SemaphoreType.DMA((4 * pieces,))],
-        specs=[anywhere] * (2 * pieces),
-        out_specs=(anywhere, vmem, vmem),
+    up_in_gradient, up_out_gradient, down_in_gradient, down_out_gradient = call(
+        lambda *refs: place_kernel(n, *refs),
+        "place",
+        [*down_out_blocks, *up_in_blocks],
+        [
+            shape((local_width, rank)),
+            shape(up_adapter_out.shape),
+            shape(down_adapter_in.shape),
+            shape((rank, local_width)),
+        ],
+        scratch=[
+            pltpu.VMEM((2, 2 * rank, rank), BF16),
+            pltpu.SemaphoreType.DMA((4 * pieces,)),
+            pltpu.SemaphoreType.DMA((2 * pieces,)),
+        ],
+        specs=[anywhere] * (4 * pieces),
+        out_specs=(anywhere, vmem, vmem, anywhere),
         limit=4,
     )
     return up_in_gradient, up_out_gradient, down_in_gradient, down_out_gradient

time: 199 us -> 196 us (0.985)
  starting transfers between devices: 58.8 us -> 53.5 us
  waiting for transfers between devices: 106 us -> 110 us
    ppermute x6, waiting for transfers between devices: 0.87 us -> 9.2 us  [others(): lax.ppermute(x, axis, [(i, (i + k) % n) for i in range(n)])]
    ppermute x37 -> x34, waiting for transfers between devices: 20.5 us -> 15.2 us  [swap(): return lax.ppermute(x, axis, [(0, 1), (1, 0)])]
    ppermute x36 -> x33, starting transfers between devices: 33.3 us -> 29.6 us  [ring_step(): lax.ppermute(x, 'dp', [(ring_at(i, n), ring_at((i + 1) % n, n)) for i in...]
    ppermute x37 -> x34, starting transfers between devices: 18.2 us -> 15.6 us  [swap(): return lax.ppermute(x, axis, [(0, 1), (1, 0)])]
    pallas_call x29 -> x28, Pallas kernels: 27.2 us -> 26.3 us  [call(): pl.pallas_call(kernel, out_shape=tuple(out_shape), in_specs=specs or [vme...]
    ppermute x36 -> x33, waiting for transfers between devices: 84.7 us -> 85.3 us  [ring_step(): lax.ppermute(x, 'dp', [(ring_at(i, n), ring_at((i + 1) % n, n)) for i in...]
  transfers between devices with their start and end apart: 79 -> 73, of which waited for: 46 -> 37; matrix products, arithmetic and copies ran while one was open for 0% -> 0% of each run, Pallas kernels for 9% -> 7%
where the time goes in v10:
time: 196 us
  waiting for transfers between devices  110 us (56%)
  starting transfers between devices  53.5 us (27%)
  Pallas kernels  26.3 us (13%)
  local copies, waits for them, and re-layouts  4.71 us (2%)
    ppermute x33, waiting for transfers between devices, ring_step(): lax.ppermute(x, 'dp', [(ring_at(i, n), ring_at((i + 1) % n, n)) for i in...  85.3 us
    ppermute x33, starting transfers between devices, ring_step(): lax.ppermute(x, 'dp', [(ring_at(i, n), ring_at((i + 1) % n, n)) for i in...  29.6 us
    pallas_call x28, Pallas kernels, call(): pl.pallas_call(kernel, out_shape=tuple(out_shape), in_specs=specs or [vme...  26.3 us
    ppermute x34, starting transfers between devices, swap(): return lax.ppermute(x, axis, [(0, 1), (1, 0)])  15.6 us
    ppermute x34, waiting for transfers between devices, swap(): return lax.ppermute(x, axis, [(0, 1), (1, 0)])  15.2 us
    ppermute x6, waiting for transfers between devices, others(): lax.ppermute(x, axis, [(i, (i + k) % n) for i in range(n)])  9.2 us
    ppermute x6, starting transfers between devices, others(): lax.ppermute(x, axis, [(i, (i + k) % n) for i in range(n)])  8.28 us
    unnamed x37, local copies, waits for them, and re-layouts  4.34 us
  transfers between devices with their start and end apart: 73, of which 37 were waited for; matrix products, arithmetic and copies ran while one was open for 0% of the time, Pallas kernels for 7%

profile of v10, /device:TPU:0, one launch (start us, length us, event | category | flops | bytes accessed | tf_op | source)
XLA Modules:
  0.0 195.6 jit_solution(1600908906106167163)
XLA Ops:
  11.0 2.7 %collective-permute-start.1 = (bf16[32,16,256]{2,1,0:T(8,128)(2,1)S(1)}, bf16[32,16,256]{2,1,0:T(8,128)(2,1)S(1)}, u32[]{:S(2)}, u32[]{:S(2)}) collective-permute-start(bf16[32,16,256]{2,1,0:T(8,128)(2,1)S(1)} %get-tuple-element.58), channel_id=1, source_target_pairs={{0,4},{4,12},{12,8},{8,0},{1,5},{5,13},{13,9},{9,1},{2,6},{6,14},{... | collective-permute-start | bytes 786440 | tf_op jit(solution)/shard_map/ppermute | solution.py:46
  16.3 4.2 %cotangent.1 = (bf16[256,4096]{1,0:T(8,128)(2,1)S(1)}, bf16[256,4096]{1,0:T(8,128)(2,1)S(1)}, f32[256,128]{1,0:T(8,128)S(1)}) custom-call(bf16[256,8192]{1,0:T(8,128)(2,1)S(1)} %copy-done.6, s32[1,2]{1,0:T(1,128)S(1)} %copy-done.9, s32[1,256]{1,0:T(1,128)S(1)} %bitcast.9, bf16[128,8192]{1,0:T(8,128)(2,1)S(1)} %copy-done.8), custom_call_target="tpu_custom_call" | custom-call | tf_op jit(solution)/shard_map/cotangent/pallas_call | solution.py:67
  21.8 5.3 %collective-permute-done.2.refs_5_ = bf16[32,16,256]{2,1,0:T(8,128)(2,1)S(1)} collective-permute-done((bf16[32,16,256]{2,1,0:T(8,128)(2,1)S(1)}, bf16[32,16,256]{2,1,0:T(8,128)(2,1)S(1)}, u32[]{:S(2)}, u32[]{:S(2)}) %collective-permute-start.2) | collective-permute-done | bytes 262176 | tf_op jit(solution)/shard_map/ppermute | solution.py:46
  28.0 3.4 %collective-permute-start.4 = (bf16[32,16,256]{2,1,0:T(8,128)(2,1)S(1)}, bf16[32,16,256]{2,1,0:T(8,128)(2,1)S(1)}, u32[]{:S(2)}, u32[]{:S(2)}) collective-permute-start(bf16[32,16,256]{2,1,0:T(8,128)(2,1)S(1)} %collective-permute-done.1.refs_5_), channel_id=1, source_target_pairs={{0,4},{4,12},{12,8},{8,0},{1,5},{5,13},{13,9},{9,1},{2,6},{6,14},{... | collective-permute-start | bytes 786440 | tf_op jit(solution)/shard_map/ppermute | solution.py:46
  37.3 4.4 %collective-permute-done.4.refs_7_ = bf16[32,16,256]{2,1,0:T(8,128)(2,1)S(1)} collective-permute-done((bf16[32,16,256]{2,1,0:T(8,128)(2,1)S(1)}, bf16[32,16,256]{2,1,0:T(8,128)(2,1)S(1)}, u32[]{:S(2)}, u32[]{:S(2)}) %collective-permute-start.4) | collective-permute-done | bytes 262176 | tf_op jit(solution)/shard_map/ppermute | solution.py:46
  44.3 3.0 %tokens.3 = (bf16[256,4096]{1,0:T(8,128)(2,1)S(1)}, bf16[256,4096]{1,0:T(8,128)(2,1)S(1)}, f32[256,256]{1,0:T(8,128)S(1)}) custom-call(bf16[256,8192]{1,0:T(8,128)(2,1)S(1)} %copy-done.1, bf16[1,8192]{1,0:T(2,128)(2,1)S(1)} %broadcast_in_dim.6.refs_1_, bf16[8192,128]{1,0:T(8,128)(2,1)S(1)} %copy-done.7, f32[256,128]{1,0:T(8,128)S(1)} %get-tuple-element.62.refs_3_, ...), custom_call_target="tpu_custom_call" | custom-call | tf_op jit(solution)/shard_map/tokens/pallas_call | solution.py:67
  50.4 7.0 %collective-permute-done.10.refs_9_ = bf16[32,16,256]{2,1,0:T(8,128)(2,1)S(1)} collective-permute-done((bf16[32,16,256]{2,1,0:T(8,128)(2,1)S(1)}, bf16[32,16,256]{2,1,0:T(8,128)(2,1)S(1)}, u32[]{:S(2)}, u32[]{:S(2)}) %collective-permute-start.10) | collective-permute-done | bytes 262176 | tf_op jit(solution)/shard_map/ppermute | solution.py:46
  59.0 3.7 %collective-permute-done.11.refs_9_ = bf16[32,16,256]{2,1,0:T(8,128)(2,1)S(1)} collective-permute-done((bf16[32,16,256]{2,1,0:T(8,128)(2,1)S(1)}, bf16[32,16,256]{2,1,0:T(8,128)(2,1)S(1)}, u32[]{:S(2)}, u32[]{:S(2)}) %collective-permute-start.11) | collective-permute-done | bytes 262176 | tf_op jit(solution)/shard_map/ppermute | solution.py:46
  66.5 4.0 %collective-permute-done.16.refs_6_.refs_5_ = f32[256,256]{1,0:T(8,128)S(1)} collective-permute-done((f32[256,256]{1,0:T(8,128)S(1)}, f32[256,256]{1,0:T(8,128)S(1)}, u32[]{:S(2)}, u32[]{:S(2)}) %collective-permute-start.16) | collective-permute-done | bytes 262176 | tf_op jit(solution)/shard_map/ppermute | solution.py:55
  72.0 2.8 %collective-permute-done.17.refs_7_.refs_6_ = bf16[256,128]{1,0:T(8,128)(2,1)S(1)} collective-permute-done((bf16[256,128]{1,0:T(8,128)(2,1)S(1)}, bf16[256,128]{1,0:T(8,128)(2,1)S(1)}, u32[]{:S(2)}, u32[]{:S(2)}) %collective-permute-start.17) | collective-permute-done | bytes 65568 | tf_op jit(solution)/shard_map/ppermute | solution.py:55
  78.9 4.8 %collective-permute-done.18.refs_10_ = bf16[32,16,256]{2,1,0:T(8,128)(2,1)S(1)} collective-permute-done((bf16[32,16,256]{2,1,0:T(8,128)(2,1)S(1)}, bf16[32,16,256]{2,1,0:T(8,128)(2,1)S(1)}, u32[]{:S(2)}, u32[]{:S(2)}) %collective-permute-start.18) | collective-permute-done | bytes 262176 | tf_op jit(solution)/shard_map/ppermute | solution.py:50
  90.7 3.1 %collective-permute-done.48.refs_9_ = bf16[32,32,128]{2,1,0:T(8,128)(2,1)S(1)} collective-permute-done((bf16[32,32,128]{2,1,0:T(8,128)(2,1)S(1)}, bf16[32,32,128]{2,1,0:T(8,128)(2,1)S(1)}, u32[]{:S(2)}, u32[]{:S(2)}) %collective-permute-start.48) | collective-permute-done | bytes 262176 | tf_op jit(solution)/shard_map/ppermute | solution.py:46
  100.9 4.2 %collective-permute-done.26.left = bf16[128,512]{1,0:T(8,128)(2,1)S(1)} collective-permute-done((bf16[128,512]{1,0:T(8,128)(2,1)S(1)}, bf16[128,512]{1,0:T(8,128)(2,1)S(1)}, u32[]{:S(2)}, u32[]{:S(2)}) %collective-permute-start.26) | collective-permute-done | bytes 131104 | tf_op jit(solution)/shard_map/ppermute | solution.py:46
  121.5 3.4 %up_in.1 = (bf16[544,128]{1,0:T(8,128)(2,1)S(1)}, bf16[544,128]{1,0:T(8,128)(2,1)S(1)}, bf16[544,128]{1,0:T(8,128)(2,1)S(1)}, bf16[544,128]{1,0:T(8,128)(2,1)S(1...) custom-call(bf16[256,128]{1,0:T(8,128)(2,1)S(1)} %get-tuple-element., ...), custom_call_target="tpu_custom_call" | custom-call | tf_op jit(solution)/shard_map/up_in/pallas_call | solution.py:67
  126.7 5.1 %collective-permute-done.56.left = bf16[544,128]{1,0:T(8,128)(2,1)S(1)} collective-permute-done((bf16[544,128]{1,0:T(8,128)(2,1)S(1)}, bf16[544,128]{1,0:T(8,128)(2,1)S(1)}, u32[]{:S(2)}, u32[]{:S(2)}) %collective-permute-start.56) | collective-permute-done | bytes 139296 | tf_op jit(solution)/shard_map/ppermute | solution.py:46
  137.6 6.7 %collective-permute-done.31.left = bf16[128,512]{1,0:T(8,128)(2,1)S(1)} collective-permute-done((bf16[128,512]{1,0:T(8,128)(2,1)S(1)}, bf16[128,512]{1,0:T(8,128)(2,1)S(1)}, u32[]{:S(2)}, u32[]{:S(2)}) %collective-permute-start.31) | collective-permute-done | bytes 131104 | tf_op jit(solution)/shard_map/ppermute | solution.py:46
  151.7 8.7 %collective-permute-done.32.refs_2_ = bf16[128,512]{1,0:T(8,128)(2,1)S(1)} collective-permute-done((bf16[128,512]{1,0:T(8,128)(2,1)S(1)}, bf16[128,512]{1,0:T(8,128)(2,1)S(1)}, u32[]{:S(2)}, u32[]{:S(2)}) %collective-permute-start.32) | collective-permute-done | bytes 131104 | tf_op jit(solution)/shard_map/ppermute | solution.py:46
  162.7 3.0 %collective-permute-start.37 = (bf16[128,512]{1,0:T(8,128)(2,1)S(1)}, bf16[128,512]{1,0:T(8,128)(2,1)S(1)}, u32[]{:S(2)}, u32[]{:S(2)}) collective-permute-start(bf16[128,512]{1,0:T(8,128)(2,1)S(1)} %collective-permute-done.35.refs_5_), channel_id=1, source_target_pairs={{0,4},{4,12},{12,8},{8,0},{1,5},{5,13},{13,9},{9,1},{2,6},{6,14},{... | collective-permute-start | bytes 393224 | tf_op jit(solution)/shard_map/ppermute | solution.py:46
  167.6 3.0 %collective-permute-done.60.refs_19_ = bf16[544,128]{1,0:T(8,128)(2,1)S(1)} collective-permute-done((bf16[544,128]{1,0:T(8,128)(2,1)S(1)}, bf16[544,128]{1,0:T(8,128)(2,1)S(1)}, u32[]{:S(2)}, u32[]{:S(2)}) %collective-permute-start.60) | collective-permute-done | bytes 139296 | tf_op jit(solution)/shard_map/ppermute | solution.py:46
  170.6 3.0 %collective-permute-done.59.refs_18_ = bf16[544,128]{1,0:T(8,128)(2,1)S(1)} collective-permute-done((bf16[544,128]{1,0:T(8,128)(2,1)S(1)}, bf16[544,128]{1,0:T(8,128)(2,1)S(1)}, u32[]{:S(2)}, u32[]{:S(2)}) %collective-permute-start.59) | collective-permute-done | bytes 139296 | tf_op jit(solution)/shard_map/ppermute | solution.py:46
  173.5 2.8 %collective-permute-done.37.refs_7_ = bf16[128,512]{1,0:T(8,128)(2,1)S(1)} collective-permute-done((bf16[128,512]{1,0:T(8,128)(2,1)S(1)}, bf16[128,512]{1,0:T(8,128)(2,1)S(1)}, u32[]{:S(2)}, u32[]{:S(2)}) %collective-permute-start.37) | collective-permute-done | bytes 131104 | tf_op jit(solution)/shard_map/ppermute | solution.py:46
  185.3 2.8 %collective-permute-done.64.refs_23_ = bf16[544,128]{1,0:T(8,128)(2,1)S(1)} collective-permute-done((bf16[544,128]{1,0:T(8,128)(2,1)S(1)}, bf16[544,128]{1,0:T(8,128)(2,1)S(1)}, u32[]{:S(2)}, u32[]{:S(2)}) %collective-permute-start.64) | collective-permute-done | bytes 139296 | tf_op jit(solution)/shard_map/ppermute | solution.py:46
  188.2 2.9 %collective-permute-done.63.refs_22_ = bf16[544,128]{1,0:T(8,128)(2,1)S(1)} collective-permute-done((bf16[544,128]{1,0:T(8,128)(2,1)S(1)}, bf16[544,128]{1,0:T(8,128)(2,1)S(1)}, u32[]{:S(2)}, u32[]{:S(2)}) %collective-permute-start.63) | collective-permute-done | bytes 139296 | tf_op jit(solution)/shard_map/ppermute | solution.py:46
  192.4 3.0 %place.1 = (bf16[8192,128]{1,0:T(8,128)(2,1)}, bf16[128,128]{1,0:T(8,128)(2,1)}, bf16[128,128]{1,0:T(8,128)(2,1)}, bf16[128,8192]{1,0:T(8,128)(2,1)}) custom-call(bf16[128,512]{1,0:T(8,128)(2,1)S(1)} %add.32.refs_0_, bf16[128,512]{1,0:T(8,128)(2,1)S(1)} %add.35.refs_1_, bf16[128,512]{1,0:T(8,128)(2,1)S(1)} %collective-permute-done.32.refs_2_, ...), custom_call_target="tpu_custom_call" | custom-call | tf_op jit(solution)/shard_map/place/pallas_call | solution.py:67
  (193 shorter events, 97.3 us)
Async XLA Ops:
  11.0 10.9 %collective-permute-start.1 = (bf16[32,16,256]{2,1,0:T(8,128)(2,1)S(1)}, bf16[32,16,256]{2,1,0:T(8,128)(2,1)S(1)}, u32[]{:S(2)}, u32[]{:S(2)}) collective-permute-start(bf16[32,16,256]{2,1,0:T(8,128)(2,1)S(1)} %get-tuple-element.58), channel_id=1, source_target_pairs={{0,4},{4,12},{12,8},{8,0},{1,5},{5,13},{13,9},{9,1},{2,6},{6,14},{... | collective-permute-start | bytes 786440 | tf_op jit(solution)/shard_map/ppermute | solution.py:46
  13.7 13.5 %collective-permute-start.2 = (bf16[32,16,256]{2,1,0:T(8,128)(2,1)S(1)}, bf16[32,16,256]{2,1,0:T(8,128)(2,1)S(1)}, u32[]{:S(2)}, u32[]{:S(2)}) collective-permute-start(bf16[32,16,256]{2,1,0:T(8,128)(2,1)S(1)} %get-tuple-element.59), channel_id=1, source_target_pairs={{0,4},{4,12},{12,8},{8,0},{1,5},{5,13},{13,9},{9,1},{2,6},{6,14},{... | collective-permute-start | bytes 786440 | tf_op jit(solution)/shard_map/ppermute | solution.py:46
  28.0 13.7 %collective-permute-start.4 = (bf16[32,16,256]{2,1,0:T(8,128)(2,1)S(1)}, bf16[32,16,256]{2,1,0:T(8,128)(2,1)S(1)}, u32[]{:S(2)}, u32[]{:S(2)}) collective-permute-start(bf16[32,16,256]{2,1,0:T(8,128)(2,1)S(1)} %collective-permute-done.1.refs_5_), channel_id=1, source_target_pairs={{0,4},{4,12},{12,8},{8,0},{1,5},{5,13},{13,9},{9,1},{2,6},{6,14},{... | collective-permute-start | bytes 786440 | tf_op jit(solution)/shard_map/ppermute | solution.py:46
  32.9 11.3 %collective-permute-start.7 = (bf16[32,16,256]{2,1,0:T(8,128)(2,1)S(1)}, bf16[32,16,256]{2,1,0:T(8,128)(2,1)S(1)}, u32[]{:S(2)}, u32[]{:S(2)}) collective-permute-start(bf16[32,16,256]{2,1,0:T(8,128)(2,1)S(1)} %collective-permute-done.2.refs_5_), channel_id=1, source_target_pairs={{0,16},{16,0},{1,17},{17,1},{2,18},{18,2},{3,19},{19,3},{4,20},{20... | collective-permute-start | bytes 786440 | tf_op jit(solution)/shard_map/ppermute | solution.py:50
  33.4 10.8 %collective-permute-start.8 = (f32[256,128]{1,0:T(8,128)S(1)}, f32[256,128]{1,0:T(8,128)S(1)}, u32[]{:S(2)}, u32[]{:S(2)}) collective-permute-start(f32[256,128]{1,0:T(8,128)S(1)} %squares.1.refs_4_), channel_id=1, source_target_pairs={{0,2},{2,0},{1,3},{3,1},{4,6},{6,4},{5,7},{7,5},{8,10},{10,8},{9,1... | collective-permute-start | bytes 393224 | tf_op jit(solution)/shard_map/ppermute | solution.py:55
  37.3 39.0 %collective-permute-start.15 = (bf16[256,4096]{1,0:T(8,128)(2,1)S(1)}, bf16[256,4096]{1,0:T(8,128)(2,1)S(1)}, u32[]{:S(2)}, u32[]{:S(2)}) collective-permute-start(bf16[256,4096]{1,0:T(8,128)(2,1)S(1)} %get-tuple-element.75), channel_id=1, source_target_pairs={{0,1},{1,0},{2,3},{3,2},{4,5},{5,4},{6,7},{7,6},{8,9},{9,8},{10,11... | collective-permute-start | bytes 6291464 | tf_op jit(solution)/shard_map/ppermute | solution.py:50
  47.3 29.6 %collective-permute-start.9 = (bf16[256,4096]{1,0:T(8,128)(2,1)S(1)}, bf16[256,4096]{1,0:T(8,128)(2,1)S(1)}, u32[]{:S(2)}, u32[]{:S(2)}) collective-permute-start(bf16[256,4096]{1,0:T(8,128)(2,1)S(1)} %get-tuple-element.71), channel_id=1, source_target_pairs={{0,1},{1,0},{2,3},{3,2},{4,5},{5,4},{6,7},{7,6},{8,9},{9,8},{10,11... | collective-permute-start | bytes 6291464 | tf_op jit(solution)/shard_map/ppermute | solution.py:50
  47.8 14.9 %collective-permute-start.11 = (bf16[32,16,256]{2,1,0:T(8,128)(2,1)S(1)}, bf16[32,16,256]{2,1,0:T(8,128)(2,1)S(1)}, u32[]{:S(2)}, u32[]{:S(2)}) collective-permute-start(bf16[32,16,256]{2,1,0:T(8,128)(2,1)S(1)} %collective-permute-done.5.refs_7_), channel_id=1, source_target_pairs={{0,4},{4,12},{12,8},{8,0},{1,5},{5,13},{13,9},{9,1},{2,6},{6,14},{... | collective-permute-start | bytes 786440 | tf_op jit(solution)/shard_map/ppermute | solution.py:46
  48.9 15.2 %collective-permute-start.13 = (bf16[32,16,256]{2,1,0:T(8,128)(2,1)S(1)}, bf16[32,16,256]{2,1,0:T(8,128)(2,1)S(1)}, u32[]{:S(2)}, u32[]{:S(2)}) collective-permute-start(bf16[32,16,256]{2,1,0:T(8,128)(2,1)S(1)} %collective-permute-done.5.refs_7_), channel_id=1, source_target_pairs={{0,16},{16,0},{1,17},{17,1},{2,18},{18,2},{3,19},{19,3},{4,20},{20... | collective-permute-start | bytes 786440 | tf_op jit(solution)/shard_map/ppermute | solution.py:50
  64.9 11.4 %collective-permute-start.14 = (bf16[32,32,128]{2,1,0:T(8,128)(2,1)S(1)}, bf16[32,32,128]{2,1,0:T(8,128)(2,1)S(1)}, u32[]{:S(2)}, u32[]{:S(2)}) collective-permute-start(bf16[32,32,128]{2,1,0:T(8,128)(2,1)S(1)} %quarters.3), channel_id=1, source_target_pairs={{0,4},{4,12},{12,8},{8,0},{1,5},{5,13},{13,9},{9,1},{2,6},{6,14},{... | collective-permute-start | bytes 786440 | tf_op jit(solution)/shard_map/ppermute | solution.py:46
  64.9 12.0 %collective-permute-start.20 = (bf16[32,16,256]{2,1,0:T(8,128)(2,1)S(1)}, bf16[32,16,256]{2,1,0:T(8,128)(2,1)S(1)}, u32[]{:S(2)}, u32[]{:S(2)}) collective-permute-start(bf16[32,16,256]{2,1,0:T(8,128)(2,1)S(1)} %collective-permute-done.11.refs_9_), channel_id=1, source_target_pairs={{0,16},{16,0},{1,17},{17,1},{2,18},{18,2},{3,19},{19,3},{4,20},{20... | collective-permute-start | bytes 786440 | tf_op jit(solution)/shard_map/ppermute | solution.py:50
  89.2 18.3 %collective-permute-start.47 = (bf16[32,32,128]{2,1,0:T(8,128)(2,1)S(1)}, bf16[32,32,128]{2,1,0:T(8,128)(2,1)S(1)}, u32[]{:S(2)}, u32[]{:S(2)}) collective-permute-start(bf16[32,32,128]{2,1,0:T(8,128)(2,1)S(1)} %collective-permute-done.22.refs_7_), channel_id=1, source_target_pairs={{0,16},{16,0},{1,17},{17,1},{2,18},{18,2},{3,19},{19,3},{4,20},{20... | collective-permute-start | bytes 786440 | tf_op jit(solution)/shard_map/ppermute | solution.py:50
  93.8 13.7 %collective-permute-start.49 = (bf16[32,32,128]{2,1,0:T(8,128)(2,1)S(1)}, bf16[32,32,128]{2,1,0:T(8,128)(2,1)S(1)}, u32[]{:S(2)}, u32[]{:S(2)}) collective-permute-start(bf16[32,32,128]{2,1,0:T(8,128)(2,1)S(1)} %collective-permute-done.48.refs_9_), channel_id=1, source_target_pairs={{0,16},{16,0},{1,17},{17,1},{2,18},{18,2},{3,19},{19,3},{4,20},{20... | collective-permute-start | bytes 786440 | tf_op jit(solution)/shard_map/ppermute | solution.py:50
  131.9 12.6 %collective-permute-start.57 = (bf16[544,128]{1,0:T(8,128)(2,1)S(1)}, bf16[544,128]{1,0:T(8,128)(2,1)S(1)}, u32[]{:S(2)}, u32[]{:S(2)}) collective-permute-start(bf16[544,128]{1,0:T(8,128)(2,1)S(1)} %add.39), channel_id=1, source_target_pairs={{0,4},{4,12},{12,8},{8,0},{1,5},{5,13},{13,9},{9,1},{2,6},{6,14},{... | collective-permute-start | bytes 417800 | tf_op jit(solution)/shard_map/ppermute | solution.py:46
  134.4 11.9 %collective-permute-start.54 = (bf16[544,128]{1,0:T(8,128)(2,1)S(1)}, bf16[544,128]{1,0:T(8,128)(2,1)S(1)}, u32[]{:S(2)}, u32[]{:S(2)}) collective-permute-start(bf16[544,128]{1,0:T(8,128)(2,1)S(1)} %add.36), channel_id=1, source_target_pairs={{0,4},{4,12},{12,8},{8,0},{1,5},{5,13},{13,9},{9,1},{2,6},{6,14},{... | collective-permute-start | bytes 417800 | tf_op jit(solution)/shard_map/ppermute | solution.py:46
  136.4 10.7 %collective-permute-start.28 = (bf16[128,512]{1,0:T(8,128)(2,1)S(1)}, bf16[128,512]{1,0:T(8,128)(2,1)S(1)}, u32[]{:S(2)}, u32[]{:S(2)}) collective-permute-start(bf16[128,512]{1,0:T(8,128)(2,1)S(1)} %add.31), channel_id=1, source_target_pairs={{0,4},{4,12},{12,8},{8,0},{1,5},{5,13},{13,9},{9,1},{2,6},{6,14},{... | collective-permute-start | bytes 393224 | tf_op jit(solution)/shard_map/ppermute | solution.py:46
  144.5 15.8 %collective-permute-start.58 = (bf16[544,128]{1,0:T(8,128)(2,1)S(1)}, bf16[544,128]{1,0:T(8,128)(2,1)S(1)}, u32[]{:S(2)}, u32[]{:S(2)}) collective-permute-start(bf16[544,128]{1,0:T(8,128)(2,1)S(1)} %add.40), channel_id=1, source_target_pairs={{0,4},{4,12},{12,8},{8,0},{1,5},{5,13},{13,9},{9,1},{2,6},{6,14},{... | collective-permute-start | bytes 417800 | tf_op jit(solution)/shard_map/ppermute | solution.py:46
  146.4 14.0 %collective-permute-start.55 = (bf16[544,128]{1,0:T(8,128)(2,1)S(1)}, bf16[544,128]{1,0:T(8,128)(2,1)S(1)}, u32[]{:S(2)}, u32[]{:S(2)}) collective-permute-start(bf16[544,128]{1,0:T(8,128)(2,1)S(1)} %add.37), channel_id=1, source_target_pairs={{0,4},{4,12},{12,8},{8,0},{1,5},{5,13},{13,9},{9,1},{2,6},{6,14},{... | collective-permute-start | bytes 417800 | tf_op jit(solution)/shard_map/ppermute | solution.py:46
  147.1 13.2 %collective-permute-start.32 = (bf16[128,512]{1,0:T(8,128)(2,1)S(1)}, bf16[128,512]{1,0:T(8,128)(2,1)S(1)}, u32[]{:S(2)}, u32[]{:S(2)}) collective-permute-start(bf16[128,512]{1,0:T(8,128)(2,1)S(1)} %add.32.refs_0_), channel_id=1, source_target_pairs={{0,4},{4,12},{12,8},{8,0},{1,5},{5,13},{13,9},{9,1},{2,6},{6,14},{... | collective-permute-start | bytes 393224 | tf_op jit(solution)/shard_map/ppermute | solution.py:46
  162.4 11.2 %collective-permute-start.59 = (bf16[544,128]{1,0:T(8,128)(2,1)S(1)}, bf16[544,128]{1,0:T(8,128)(2,1)S(1)}, u32[]{:S(2)}, u32[]{:S(2)}) collective-permute-start(bf16[544,128]{1,0:T(8,128)(2,1)S(1)} %add.38.refs_16_), channel_id=1, source_target_pairs={{0,4},{4,12},{12,8},{8,0},{1,5},{5,13},{13,9},{9,1},{2,6},{6,14},{... | collective-permute-start | bytes 417800 | tf_op jit(solution)/shard_map/ppermute | solution.py:46
  162.7 13.6 %collective-permute-start.37 = (bf16[128,512]{1,0:T(8,128)(2,1)S(1)}, bf16[128,512]{1,0:T(8,128)(2,1)S(1)}, u32[]{:S(2)}, u32[]{:S(2)}) collective-permute-start(bf16[128,512]{1,0:T(8,128)(2,1)S(1)} %collective-permute-done.35.refs_5_), channel_id=1, source_target_pairs={{0,4},{4,12},{12,8},{8,0},{1,5},{5,13},{13,9},{9,1},{2,6},{6,14},{... | collective-permute-start | bytes 393224 | tf_op jit(solution)/shard_map/ppermute | solution.py:46
  167.6 11.6 %collective-permute-start.36 = (bf16[128,512]{1,0:T(8,128)(2,1)S(1)}, bf16[128,512]{1,0:T(8,128)(2,1)S(1)}, u32[]{:S(2)}, u32[]{:S(2)}) collective-permute-start(bf16[128,512]{1,0:T(8,128)(2,1)S(1)} %collective-permute-done.34.refs_4_), channel_id=1, source_target_pairs={{0,4},{4,12},{12,8},{8,0},{1,5},{5,13},{13,9},{9,1},{2,6},{6,14},{... | collective-permute-start | bytes 393224 | tf_op jit(solution)/shard_map/ppermute | solution.py:46
  170.6 11.6 %collective-permute-start.62 = (bf16[544,128]{1,0:T(8,128)(2,1)S(1)}, bf16[544,128]{1,0:T(8,128)(2,1)S(1)}, u32[]{:S(2)}, u32[]{:S(2)}) collective-permute-start(bf16[544,128]{1,0:T(8,128)(2,1)S(1)} %collective-permute-done.60.refs_19_), channel_id=1, source_target_pairs={{0,4},{4,12},{12,8},{8,0},{1,5},{5,13},{13,9},{9,1},{2,6},{6,14},{... | collective-permute-start | bytes 417800 | tf_op jit(solution)/shard_map/ppermute | solution.py:46
  173.5 11.2 %collective-permute-start.61 = (bf16[544,128]{1,0:T(8,128)(2,1)S(1)}, bf16[544,128]{1,0:T(8,128)(2,1)S(1)}, u32[]{:S(2)}, u32[]{:S(2)}) collective-permute-start(bf16[544,128]{1,0:T(8,128)(2,1)S(1)} %collective-permute-done.59.refs_18_), channel_id=1, source_target_pairs={{0,4},{4,12},{12,8},{8,0},{1,5},{5,13},{13,9},{9,1},{2,6},{6,14},{... | collective-permute-start | bytes 417800 | tf_op jit(solution)/shard_map/ppermute | solution.py:46
  (67 other events, 570.6 us)

commit v11 on v10

--- a/solution.py
+++ b/solution.py
@@ -88,7 +88,7 @@
     return call(add_kernel, "add", [left, right], [shape(left.shape)], limit=4)[0]
 
 
-def ring_all(parts, streams):
+def ring_all(parts, streams, last=()):
     n = lax.axis_size("dp")
     seen = []
     totals = list(parts[:streams])
@@ -96,7 +96,9 @@
         seen.append([ring_step(t) for t in totals])
         totals = [add(t, p) for t, p in zip(seen[-1], parts[k * streams : (k + 1) * streams])]
     blocks = list(totals)
-    for _ in range(n - 1):
+    for k in range(n - 1):
+        if last and k == n - 2:
+            totals = [after(t, *last) for t in totals]
         totals = [ring_step(t) for t in totals]
         seen.append(totals)
         blocks += totals
@@ -300,7 +302,7 @@
 def low_sums(low, low_more):
     total = low[...]
     for ref in low_more:
-        total = total + ref[...]
+        total = total + ref[:, ref.shape[1] - total.shape[1] :].astype(F32)
     half = total.shape[1] // 2
     return total[:, :half].astype(BF16), total[:, half:].astype(BF16)
 
@@ -312,13 +314,13 @@
 
 
 def hidden_kernel(more, gate, up, low, adapters, *refs):
-    gate_more, up_more, low_more, adapters_more = (refs[i * more : (i + 1) * more] for i in range(4))
-    silu_ref, low_ref, down_in_term, up_out_all, down_in_all = refs[4 * more :]
+    gate_more, up_more, adapters_more = (refs[i * more : (i + 1) * more] for i in range(3))
+    silu_ref, low_ref, down_in_term, up_out_all, down_in_all = refs[3 * more :]
     gather_adapters(adapters, adapters_more, up_out_all, down_in_all)
-    low_up, low_out = low_sums(low, low_more)
+    low_up, low_out = low_sums(low, gate_more)
     gate_sum, up_sum = gate[...], up[...]
     for ref in gate_more:
-        gate_sum = gate_sum + ref[...].astype(F32)
+        gate_sum = gate_sum + ref[:, : gate_sum.shape[1]].astype(F32)
     for ref in up_more:
         up_sum = up_sum + ref[...].astype(F32)
     up_sum = up_sum + ADAPTER_SCALE * dot(low_up, up_out_all[...])
@@ -512,8 +514,9 @@
 
     def step(moving, *done):
         ring.append(ring_step(after(moving, *done) if done else moving))
-        if len(ring) > 2:
-            crossed.append(swap(ring[-1], "grp"))
+
+    def cross(k, *done):
+        crossed.append(swap(after(ring[k], *done) if done else ring[k], "grp"))
 
     step(gate_moving)
     step(up_moving)
@@ -536,30 +539,43 @@
         scratch=buffers,
         specs=[hbm, smem, vmem, vmem],
     )
-    down_turned = jnp.swapaxes(after(down_codes, squares), 0, 1)
-    down_moving, down_got = start_shards([down_turned], 1)
-    crossed += [swap(after(r, grad), "grp") for r in ring]
-    step(ring[0], ring[1], grad, *down_moving)
-    step(ring[1], ring[0], grad, *down_moving)
+    cross(0, grad)
+    cross(1, grad)
+    step(ring[0], ring[1], grad)
+    step(ring[1], ring[0], grad)
+    adapters = jnp.concatenate([up_adapter_out, down_adapter_in], axis=0)
+    adapters_more = others(after(adapters, *ring[:2]), "mp")
     normed_send, normed, low = call(
         lambda *refs: token_kernel(total_width, *refs),
         "tokens",
-        [tokens, rms_norm_gain[None, :], up_adapter_in, low_out, after(squares, *ring[2:4], *crossed[:2]), *squares_more],
+        [
+            tokens,
+            rms_norm_gain[None, :],
+            up_adapter_in,
+            low_out,
+            after(squares, *ring[2:4], *crossed[:2], *adapters_more),
+            *squares_more,
+        ],
         [shape((rows, half))] * 2 + [shape((rows, 2 * rank), F32)],
         scratch=buffers,
         specs=[hbm] + [vmem] * (4 + more),
     )
     grad_got = swap(grad_send, "sub")
     normed_got = swap(normed_send, "sub")
-    low_more = others(low, "mp")
     step(ring[2], ring[3], *crossed[:2])
     step(ring[3], ring[2], *crossed[:2])
-    adapters = jnp.concatenate([up_adapter_out, down_adapter_in], axis=0)
-    adapters_more = others(after(adapters, ring[4]), "mp")
-    step(down_moving[0], *ring[4:6], *crossed[2:4])
-    step(ring[-1])
-
-    def product(kernel, name, own, got, scale, codes, codes_got, first_got, steps, weight_shape):
+    cross(2)
+    cross(3)
+    cross(4)
+    cross(5)
+    down_turned = jnp.swapaxes(after(down_codes, *ring[2:4]), 0, 1)
+    down_moving, down_got = start_shards([down_turned], 1)
+    step(down_moving[0], *ring[4:6], *crossed[2:4], grad_got, normed_got)
+    cross(6)
+    step(ring[6])
+    cross(7)
+
+    def product(kernel, name, own, got, scale, codes, codes_got, first_got, steps, weight_shape, beside=()):
         groups = scale.shape[0]
         mine, theirs = call(
             lambda *refs: kernel(first_got, *refs),
@@ -570,21 +586,20 @@
             flops=4 * rows * half * units,
         )
         total = mine + swap(theirs, "sub").astype(F32)
-        return total, others(total.astype(BF16), "mp"), mine
+        send = jnp.concatenate([total.astype(BF16), *[b.astype(BF16) for b in beside]], axis=1)
+        return total, others(send, "mp")
 
     front = (blocks // 2, block, units)
-    first_down = [ring[2 * (n - 1)], grad_got, *low_more, *adapters_more]
+    first_down = [ring[2 * (n - 1)]]
     half_blocks = blocks // 2
-    gate, gate_more, gate_mine = product(
+    gate, gate_more = product(
         front_kernel, "gate", normed, normed_got, after(gate_block_scale.T, *first_down), gate_codes, front_got, 0,
-        range(0, 2 * (n - 1), 2), front,
-    )
-    up, up_more, up_mine = product(
+        range(0, 2 * (n - 1), 2), front, [low],
+    )
+    up, up_more = product(
         front_kernel, "up", normed, normed_got, after(up_block_scale.T, *first_down), up_codes, front_got, half_blocks,
         range(1, 2 * (n - 1), 2), front,
     )
-    for _ in range(n - 3):
-        step(ring[-1], gate_mine, up_mine, crossed[-2])
     small_scratch = [
         pltpu.VMEM((rank, units), BF16),
         pltpu.VMEM((units, rank), BF16),
@@ -592,12 +607,15 @@
     silu, low_hidden, down_in_term = call(
         lambda *refs: hidden_kernel(more, *refs),
         "hidden",
-        [gate, up, low, after(adapters, ring[-2]), *gate_more, *up_more, *low_more, *adapters_more],
+        [gate, up, low, adapters, *gate_more, *up_more, *adapters_more],
         [shape((rows, units), F32), shape((rows, rank)), shape(down_adapter_in.shape)],
         scratch=small_scratch,
         limit=8,
     )
     pieces = STREAMS * n
+    for _ in range(n - 3):
+        step(ring[-1], low_hidden)
+        cross(-1)
     down_out_parts = call(
         lambda *refs: down_out_kernel(n, *refs),
         "down_out",
@@ -614,14 +632,14 @@
         limit=32,
     )
 
-    back, back_more, _ = product(
+    back, back_more = product(
         back_kernel, "back", grad, grad_got, after(down_block_scale, normed_t, *seen[0]), down_turned, down_got, 0,
         range(2 * (n - 1), 3 * (n - 1)), (units, half),
     )
     low_grad, up_out_term = call(
         lambda *refs: up_grad_kernel(more, *refs),
         "up_grad",
-        [back, silu, low, adapters, *back_more, *low_more, *adapters_more],
+        [back, silu, low, adapters, *back_more, *gate_more, *adapters_more],
         [shape((rows, rank)), shape(up_adapter_out.shape)],
         scratch=small_scratch,
         limit=8,
@@ -634,7 +652,7 @@
         [shape((half // pieces + extra, rank))] * pieces,
         flops=4 * rows * half * rank,
     )
-    up_in_blocks, _ = ring_all(up_in_parts, STREAMS)
+    up_in_blocks, _ = ring_all(up_in_parts, STREAMS, seen[-2])
 
     anywhere = pl.BlockSpec(memory_space=pl.ANY)
     up_in_gradient, up_out_gradient, down_in_gradient, down_out_gradient = call(

time: 196 us -> 198 us (1.010)
  starting transfers between devices: 53.5 us -> 58.7 us
  waiting for transfers between devices: 110 us -> 106 us
    ppermute x33, waiting for transfers between devices: 85.3 us -> 77.4 us  [ring_step(): lax.ppermute(x, 'dp', [(ring_at(i, n), ring_at((i + 1) % n, n)) for i in...]
    ppermute x33, starting transfers between devices: 29.6 us -> 37.5 us  [ring_step(): lax.ppermute(x, 'dp', [(ring_at(i, n), ring_at((i + 1) % n, n)) for i in...]
    ppermute x6 -> x5, waiting for transfers between devices: 9.2 us -> 12.2 us  [others(): lax.ppermute(x, axis, [(i, (i + k) % n) for i in range(n)])]
    ppermute x6 -> x5, starting transfers between devices: 8.28 us -> 7.06 us  [others(): lax.ppermute(x, axis, [(i, (i + k) % n) for i in range(n)])]
  transfers between devices with their start and end apart: 73 -> 72, of which waited for: 37 -> 41; matrix products, arithmetic and copies ran while one was open for 0% -> 0% of each run, Pallas kernels for 7% -> 9%
where the time goes in v11:
time: 198 us
  waiting for transfers between devices  106 us (54%)
  starting transfers between devices  58.7 us (30%)
  Pallas kernels  26.3 us (13%)
  local copies, waits for them, and re-layouts  4.71 us (2%)
    ppermute x33, waiting for transfers between devices, ring_step(): lax.ppermute(x, 'dp', [(ring_at(i, n), ring_at((i + 1) % n, n)) for i in...  77.4 us
    ppermute x33, starting transfers between devices, ring_step(): lax.ppermute(x, 'dp', [(ring_at(i, n), ring_at((i + 1) % n, n)) for i in...  37.5 us
    pallas_call x28, Pallas kernels, call(): pl.pallas_call(kernel, out_shape=tuple(out_shape), in_specs=specs or [vme...  26.3 us
    ppermute x34, waiting for transfers between devices, swap(): return lax.ppermute(x, axis, [(0, 1), (1, 0)])  16.9 us
    ppermute x34, starting transfers between devices, swap(): return lax.ppermute(x, axis, [(0, 1), (1, 0)])  14.1 us
    ppermute x5, waiting for transfers between devices, others(): lax.ppermute(x, axis, [(i, (i + k) % n) for i in range(n)])  12.2 us
    ppermute x5, starting transfers between devices, others(): lax.ppermute(x, axis, [(i, (i + k) % n) for i in range(n)])  7.06 us
    unnamed x37, local copies, waits for them, and re-layouts  4.34 us
  transfers between devices with their start and end apart: 72, of which 41 were waited for; matrix products, arithmetic and copies ran while one was open for 0% of the time, Pallas kernels for 9%

profile of v11, /device:TPU:0, one launch (start us, length us, event | category | flops | bytes accessed | tf_op | source)
XLA Modules:
  0.0 197.5 jit_solution(5229341898154908124)
XLA Ops:
  5.5 3.0 %collective-permute-start.1 = (bf16[32,16,256]{2,1,0:T(8,128)(2,1)S(1)}, bf16[32,16,256]{2,1,0:T(8,128)(2,1)S(1)}, u32[]{:S(2)}, u32[]{:S(2)}) collective-permute-start(bf16[32,16,256]{2,1,0:T(8,128)(2,1)S(1)} %get-tuple-element.59), channel_id=1, source_target_pairs={{0,4},{4,12},{12,8},{8,0},{1,5},{5,13},{13,9},{9,1},{2,6},{6,14},{... | collective-permute-start | bytes 786440 | tf_op jit(solution)/shard_map/ppermute | solution.py:46
  15.8 4.2 %cotangent.1 = (bf16[256,4096]{1,0:T(8,128)(2,1)S(1)}, bf16[256,4096]{1,0:T(8,128)(2,1)S(1)}, f32[256,128]{1,0:T(8,128)S(1)}) custom-call(bf16[256,8192]{1,0:T(8,128)(2,1)S(1)} %copy-done.6, s32[1,2]{1,0:T(1,128)S(1)} %copy-done.9, s32[1,256]{1,0:T(1,128)S(1)} %bitcast.9, bf16[128,8192]{1,0:T(8,128)(2,1)S(1)} %copy-done.8), custom_call_target="tpu_custom_call" | custom-call | tf_op jit(solution)/shard_map/cotangent/pallas_call | solution.py:67
  22.6 3.4 %collective-permute-start.3 = (bf16[32,16,256]{2,1,0:T(8,128)(2,1)S(1)}, bf16[32,16,256]{2,1,0:T(8,128)(2,1)S(1)}, u32[]{:S(2)}, u32[]{:S(2)}) collective-permute-start(bf16[32,16,256]{2,1,0:T(8,128)(2,1)S(1)} %collective-permute-done.1.refs_5_), channel_id=1, source_target_pairs={{0,4},{4,12},{12,8},{8,0},{1,5},{5,13},{13,9},{9,1},{2,6},{6,14},{... | collective-permute-start | bytes 786440 | tf_op jit(solution)/shard_map/ppermute | solution.py:46
  29.6 2.9 %collective-permute-done.7.refs_6_ = bf16[256,128]{1,0:T(8,128)(2,1)S(1)} collective-permute-done((bf16[256,128]{1,0:T(8,128)(2,1)S(1)}, bf16[256,128]{1,0:T(8,128)(2,1)S(1)}, u32[]{:S(2)}, u32[]{:S(2)}) %collective-permute-start.7) | collective-permute-done | bytes 65568 | tf_op jit(solution)/shard_map/ppermute | solution.py:55
  38.6 3.0 %tokens.3 = (bf16[256,4096]{1,0:T(8,128)(2,1)S(1)}, bf16[256,4096]{1,0:T(8,128)(2,1)S(1)}, f32[256,256]{1,0:T(8,128)S(1)}) custom-call(bf16[256,8192]{1,0:T(8,128)(2,1)S(1)} %copy-done.1, bf16[1,8192]{1,0:T(2,128)(2,1)S(1)} %broadcast_in_dim.6.refs_1_, bf16[8192,128]{1,0:T(8,128)(2,1)S(1)} %copy-done.7, f32[256,128]{1,0:T(8,128)S(1)} %get-tuple-element.63.refs_3_, ...), custom_call_target="tpu_custom_call" | custom-call | tf_op jit(solution)/shard_map/tokens/pallas_call | solution.py:67
  47.8 5.0 %collective-permute-done.12.refs_9_ = bf16[32,16,256]{2,1,0:T(8,128)(2,1)S(1)} collective-permute-done((bf16[32,16,256]{2,1,0:T(8,128)(2,1)S(1)}, bf16[32,16,256]{2,1,0:T(8,128)(2,1)S(1)}, u32[]{:S(2)}, u32[]{:S(2)}) %collective-permute-start.12) | collective-permute-done | bytes 262176 | tf_op jit(solution)/shard_map/ppermute | solution.py:46
  54.6 2.9 %collective-permute-done.11.refs_9_ = bf16[32,16,256]{2,1,0:T(8,128)(2,1)S(1)} collective-permute-done((bf16[32,16,256]{2,1,0:T(8,128)(2,1)S(1)}, bf16[32,16,256]{2,1,0:T(8,128)(2,1)S(1)}, u32[]{:S(2)}, u32[]{:S(2)}) %collective-permute-start.11) | collective-permute-done | bytes 262176 | tf_op jit(solution)/shard_map/ppermute | solution.py:46
  57.5 2.7 %collective-permute-done.13.refs_8_ = bf16[32,16,256]{2,1,0:T(8,128)(2,1)S(1)} collective-permute-done((bf16[32,16,256]{2,1,0:T(8,128)(2,1)S(1)}, bf16[32,16,256]{2,1,0:T(8,128)(2,1)S(1)}, u32[]{:S(2)}, u32[]{:S(2)}) %collective-permute-start.13) | collective-permute-done | bytes 262176 | tf_op jit(solution)/shard_map/ppermute | solution.py:50
  62.6 5.1 %collective-permute-done.16.refs_5_ = bf16[32,32,128]{2,1,0:T(8,128)(2,1)S(1)} collective-permute-done((bf16[32,32,128]{2,1,0:T(8,128)(2,1)S(1)}, bf16[32,32,128]{2,1,0:T(8,128)(2,1)S(1)}, u32[]{:S(2)}, u32[]{:S(2)}) %collective-permute-start.16) | collective-permute-done | bytes 262176 | tf_op jit(solution)/shard_map/ppermute | solution.py:46
  78.3 8.8 %collective-permute-done.22.refs_5_ = bf16[256,256]{1,0:T(8,128)(2,1)S(1)} collective-permute-done((bf16[256,256]{1,0:T(8,128)(2,1)S(1)}, bf16[256,256]{1,0:T(8,128)(2,1)S(1)}, u32[]{:S(2)}, u32[]{:S(2)}) %collective-permute-start.22) | collective-permute-done | bytes 131104 | tf_op jit(solution)/shard_map/ppermute | solution.py:55
  89.9 6.1 %collective-permute-done.47.refs_9_ = bf16[32,32,128]{2,1,0:T(8,128)(2,1)S(1)} collective-permute-done((bf16[32,32,128]{2,1,0:T(8,128)(2,1)S(1)}, bf16[32,32,128]{2,1,0:T(8,128)(2,1)S(1)}, u32[]{:S(2)}, u32[]{:S(2)}) %collective-permute-start.47) | collective-permute-done | bytes 262176 | tf_op jit(solution)/shard_map/ppermute | solution.py:46
  99.7 3.4 %collective-permute-start.27 = (bf16[128,512]{1,0:T(8,128)(2,1)S(1)}, bf16[128,512]{1,0:T(8,128)(2,1)S(1)}, u32[]{:S(2)}, u32[]{:S(2)}) collective-permute-start(bf16[128,512]{1,0:T(8,128)(2,1)S(1)} %get-tuple-element.90), channel_id=1, source_target_pairs={{0,4},{4,12},{12,8},{8,0},{1,5},{5,13},{13,9},{9,1},{2,6},{6,14},{... | collective-permute-start | bytes 393224 | tf_op jit(solution)/shard_map/ppermute | solution.py:46
  114.9 2.9 %collective-permute-start.25 = (bf16[128,512]{1,0:T(8,128)(2,1)S(1)}, bf16[128,512]{1,0:T(8,128)(2,1)S(1)}, u32[]{:S(2)}, u32[]{:S(2)}) collective-permute-start(bf16[128,512]{1,0:T(8,128)(2,1)S(1)} %add.30), channel_id=1, source_target_pairs={{0,4},{4,12},{12,8},{8,0},{1,5},{5,13},{13,9},{9,1},{2,6},{6,14},{... | collective-permute-start | bytes 393224 | tf_op jit(solution)/shard_map/ppermute | solution.py:46
  118.7 2.9 %collective-permute-done.28.left = bf16[128,512]{1,0:T(8,128)(2,1)S(1)} collective-permute-done((bf16[128,512]{1,0:T(8,128)(2,1)S(1)}, bf16[128,512]{1,0:T(8,128)(2,1)S(1)}, u32[]{:S(2)}, u32[]{:S(2)}) %collective-permute-start.28) | collective-permute-done | bytes 131104 | tf_op jit(solution)/shard_map/ppermute | solution.py:46
  123.2 3.4 %up_in.1 = (bf16[544,128]{1,0:T(8,128)(2,1)S(1)}, bf16[544,128]{1,0:T(8,128)(2,1)S(1)}, bf16[544,128]{1,0:T(8,128)(2,1)S(1)}, bf16[544,128]{1,0:T(8,128)(2,1)S(1...) custom-call(bf16[256,128]{1,0:T(8,128)(2,1)S(1)} %get-tuple-element., ...), custom_call_target="tpu_custom_call" | custom-call | tf_op jit(solution)/shard_map/up_in/pallas_call | solution.py:67
  126.7 3.4 %collective-permute-start.52 = (bf16[544,128]{1,0:T(8,128)(2,1)S(1)}, bf16[544,128]{1,0:T(8,128)(2,1)S(1)}, u32[]{:S(2)}, u32[]{:S(2)}) collective-permute-start(bf16[544,128]{1,0:T(8,128)(2,1)S(1)} %get-tuple-element.104), channel_id=1, source_target_pairs={{0,4},{4,12},{12,8},{8,0},{1,5},{5,13},{13,9},{9,1},{2,6},{6,14},{... | collective-permute-start | bytes 417800 | tf_op jit(solution)/shard_map/ppermute | solution.py:46
  130.0 3.6 %collective-permute-done.55.left = bf16[544,128]{1,0:T(8,128)(2,1)S(1)} collective-permute-done((bf16[544,128]{1,0:T(8,128)(2,1)S(1)}, bf16[544,128]{1,0:T(8,128)(2,1)S(1)}, u32[]{:S(2)}, u32[]{:S(2)}) %collective-permute-start.55) | collective-permute-done | bytes 139296 | tf_op jit(solution)/shard_map/ppermute | solution.py:46
  141.4 2.8 %collective-permute-done.53.left = bf16[544,128]{1,0:T(8,128)(2,1)S(1)} collective-permute-done((bf16[544,128]{1,0:T(8,128)(2,1)S(1)}, bf16[544,128]{1,0:T(8,128)(2,1)S(1)}, u32[]{:S(2)}, u32[]{:S(2)}) %collective-permute-start.53) | collective-permute-done | bytes 139296 | tf_op jit(solution)/shard_map/ppermute | solution.py:46
  158.6 2.8 %collective-permute-done.30.refs_2_ = bf16[128,512]{1,0:T(8,128)(2,1)S(1)} collective-permute-done((bf16[128,512]{1,0:T(8,128)(2,1)S(1)}, bf16[128,512]{1,0:T(8,128)(2,1)S(1)}, u32[]{:S(2)}, u32[]{:S(2)}) %collective-permute-start.30) | collective-permute-done | bytes 131104 | tf_op jit(solution)/shard_map/ppermute | solution.py:46
  161.4 3.4 %collective-permute-start.32 = (bf16[128,512]{1,0:T(8,128)(2,1)S(1)}, bf16[128,512]{1,0:T(8,128)(2,1)S(1)}, u32[]{:S(2)}, u32[]{:S(2)}) collective-permute-start(bf16[128,512]{1,0:T(8,128)(2,1)S(1)} %collective-permute-done.30.refs_2_), channel_id=1, source_target_pairs={{0,4},{4,12},{12,8},{8,0},{1,5},{5,13},{13,9},{9,1},{2,6},{6,14},{... | collective-permute-start | bytes 393224 | tf_op jit(solution)/shard_map/ppermute | solution.py:46
  172.4 7.8 %collective-permute-done.35.refs_7_ = bf16[128,512]{1,0:T(8,128)(2,1)S(1)} collective-permute-done((bf16[128,512]{1,0:T(8,128)(2,1)S(1)}, bf16[128,512]{1,0:T(8,128)(2,1)S(1)}, u32[]{:S(2)}, u32[]{:S(2)}) %collective-permute-start.35) | collective-permute-done | bytes 131104 | tf_op jit(solution)/shard_map/ppermute | solution.py:46
  183.5 3.1 %collective-permute-start.62 = (bf16[544,128]{1,0:T(8,128)(2,1)S(1)}, bf16[544,128]{1,0:T(8,128)(2,1)S(1)}, u32[]{:S(2)}, u32[]{:S(2)}) collective-permute-start(bf16[544,128]{1,0:T(8,128)(2,1)S(1)} %collective-permute-done.60.refs_20_), channel_id=1, source_target_pairs={{0,4},{4,12},{12,8},{8,0},{1,5},{5,13},{13,9},{9,1},{2,6},{6,14},{... | collective-permute-start | bytes 417800 | tf_op jit(solution)/shard_map/ppermute | solution.py:46
  187.2 3.4 %collective-permute-done.63.refs_23_ = bf16[544,128]{1,0:T(8,128)(2,1)S(1)} collective-permute-done((bf16[544,128]{1,0:T(8,128)(2,1)S(1)}, bf16[544,128]{1,0:T(8,128)(2,1)S(1)}, u32[]{:S(2)}, u32[]{:S(2)}) %collective-permute-start.63) | collective-permute-done | bytes 139296 | tf_op jit(solution)/shard_map/ppermute | solution.py:46
  194.3 3.0 %place.1 = (bf16[8192,128]{1,0:T(8,128)(2,1)}, bf16[128,128]{1,0:T(8,128)(2,1)}, bf16[128,128]{1,0:T(8,128)(2,1)}, bf16[128,8192]{1,0:T(8,128)(2,1)}) custom-call(bf16[128,512]{1,0:T(8,128)(2,1)S(1)} %add.32.refs_0_, bf16[128,512]{1,0:T(8,128)(2,1)S(1)} %add.35.refs_1_, bf16[128,512]{1,0:T(8,128)(2,1)S(1)} %collective-permute-done.30.refs_2_, ...), custom_call_target="tpu_custom_call" | custom-call | tf_op jit(solution)/shard_map/place/pallas_call | solution.py:67
  (193 shorter events, 103.5 us)
Async XLA Ops:
  5.5 14.4 %collective-permute-start.1 = (bf16[32,16,256]{2,1,0:T(8,128)(2,1)S(1)}, bf16[32,16,256]{2,1,0:T(8,128)(2,1)S(1)}, u32[]{:S(2)}, u32[]{:S(2)}) collective-permute-start(bf16[32,16,256]{2,1,0:T(8,128)(2,1)S(1)} %get-tuple-element.59), channel_id=1, source_target_pairs={{0,4},{4,12},{12,8},{8,0},{1,5},{5,13},{13,9},{9,1},{2,6},{6,14},{... | collective-permute-start | bytes 786440 | tf_op jit(solution)/shard_map/ppermute | solution.py:46
  8.5 13.2 %collective-permute-start.2 = (bf16[32,16,256]{2,1,0:T(8,128)(2,1)S(1)}, bf16[32,16,256]{2,1,0:T(8,128)(2,1)S(1)}, u32[]{:S(2)}, u32[]{:S(2)}) collective-permute-start(bf16[32,16,256]{2,1,0:T(8,128)(2,1)S(1)} %get-tuple-element.60), channel_id=1, source_target_pairs={{0,4},{4,12},{12,8},{8,0},{1,5},{5,13},{13,9},{9,1},{2,6},{6,14},{... | collective-permute-start | bytes 786440 | tf_op jit(solution)/shard_map/ppermute | solution.py:46
  21.8 12.2 %collective-permute-start.4 = (bf16[32,16,256]{2,1,0:T(8,128)(2,1)S(1)}, bf16[32,16,256]{2,1,0:T(8,128)(2,1)S(1)}, u32[]{:S(2)}, u32[]{:S(2)}) collective-permute-start(bf16[32,16,256]{2,1,0:T(8,128)(2,1)S(1)} %collective-permute-done.2.refs_5_), channel_id=1, source_target_pairs={{0,4},{4,12},{12,8},{8,0},{1,5},{5,13},{13,9},{9,1},{2,6},{6,14},{... | collective-permute-start | bytes 786440 | tf_op jit(solution)/shard_map/ppermute | solution.py:46
  22.6 13.5 %collective-permute-start.3 = (bf16[32,16,256]{2,1,0:T(8,128)(2,1)S(1)}, bf16[32,16,256]{2,1,0:T(8,128)(2,1)S(1)}, u32[]{:S(2)}, u32[]{:S(2)}) collective-permute-start(bf16[32,16,256]{2,1,0:T(8,128)(2,1)S(1)} %collective-permute-done.1.refs_5_), channel_id=1, source_target_pairs={{0,4},{4,12},{12,8},{8,0},{1,5},{5,13},{13,9},{9,1},{2,6},{6,14},{... | collective-permute-start | bytes 786440 | tf_op jit(solution)/shard_map/ppermute | solution.py:46
  27.5 11.1 %collective-permute-start.5 = (bf16[32,16,256]{2,1,0:T(8,128)(2,1)S(1)}, bf16[32,16,256]{2,1,0:T(8,128)(2,1)S(1)}, u32[]{:S(2)}, u32[]{:S(2)}) collective-permute-start(bf16[32,16,256]{2,1,0:T(8,128)(2,1)S(1)} %collective-permute-done.1.refs_5_), channel_id=1, source_target_pairs={{0,16},{16,0},{1,17},{17,1},{2,18},{18,2},{3,19},{19,3},{4,20},{20... | collective-permute-start | bytes 786440 | tf_op jit(solution)/shard_map/ppermute | solution.py:50
  34.0 26.2 %collective-permute-start.15 = (bf16[256,4096]{1,0:T(8,128)(2,1)S(1)}, bf16[256,4096]{1,0:T(8,128)(2,1)S(1)}, u32[]{:S(2)}, u32[]{:S(2)}) collective-permute-start(bf16[256,4096]{1,0:T(8,128)(2,1)S(1)} %get-tuple-element.76), channel_id=1, source_target_pairs={{0,1},{1,0},{2,3},{3,2},{4,5},{5,4},{6,7},{7,6},{8,9},{9,8},{10,11... | collective-permute-start | bytes 6291464 | tf_op jit(solution)/shard_map/ppermute | solution.py:50
  41.6 18.6 %collective-permute-start.9 = (bf16[256,4096]{1,0:T(8,128)(2,1)S(1)}, bf16[256,4096]{1,0:T(8,128)(2,1)S(1)}, u32[]{:S(2)}, u32[]{:S(2)}) collective-permute-start(bf16[256,4096]{1,0:T(8,128)(2,1)S(1)} %get-tuple-element.72), channel_id=1, source_target_pairs={{0,1},{1,0},{2,3},{3,2},{4,5},{5,4},{6,7},{7,6},{8,9},{9,8},{10,11... | collective-permute-start | bytes 6291464 | tf_op jit(solution)/shard_map/ppermute | solution.py:50
  43.0 14.5 %collective-permute-start.11 = (bf16[32,16,256]{2,1,0:T(8,128)(2,1)S(1)}, bf16[32,16,256]{2,1,0:T(8,128)(2,1)S(1)}, u32[]{:S(2)}, u32[]{:S(2)}) collective-permute-start(bf16[32,16,256]{2,1,0:T(8,128)(2,1)S(1)} %collective-permute-done.3.refs_7_), channel_id=1, source_target_pairs={{0,4},{4,12},{12,8},{8,0},{1,5},{5,13},{13,9},{9,1},{2,6},{6,14},{... | collective-permute-start | bytes 786440 | tf_op jit(solution)/shard_map/ppermute | solution.py:46
  46.2 11.2 %collective-permute-start.14 = (bf16[32,16,256]{2,1,0:T(8,128)(2,1)S(1)}, bf16[32,16,256]{2,1,0:T(8,128)(2,1)S(1)}, u32[]{:S(2)}, u32[]{:S(2)}) collective-permute-start(bf16[32,16,256]{2,1,0:T(8,128)(2,1)S(1)} %collective-permute-done.4.refs_7_), channel_id=1, source_target_pairs={{0,16},{16,0},{1,17},{17,1},{2,18},{18,2},{3,19},{19,3},{4,20},{20... | collective-permute-start | bytes 786440 | tf_op jit(solution)/shard_map/ppermute | solution.py:50
  62.1 11.3 %collective-permute-start.19 = (bf16[32,16,256]{2,1,0:T(8,128)(2,1)S(1)}, bf16[32,16,256]{2,1,0:T(8,128)(2,1)S(1)}, u32[]{:S(2)}, u32[]{:S(2)}) collective-permute-start(bf16[32,16,256]{2,1,0:T(8,128)(2,1)S(1)} %collective-permute-done.12.refs_9_), channel_id=1, source_target_pairs={{0,16},{16,0},{1,17},{17,1},{2,18},{18,2},{3,19},{19,3},{4,20},{20... | collective-permute-start | bytes 786440 | tf_op jit(solution)/shard_map/ppermute | solution.py:50
  75.3 12.2 %collective-permute-start.45 = (bf16[32,32,128]{2,1,0:T(8,128)(2,1)S(1)}, bf16[32,32,128]{2,1,0:T(8,128)(2,1)S(1)}, u32[]{:S(2)}, u32[]{:S(2)}) collective-permute-start(bf16[32,32,128]{2,1,0:T(8,128)(2,1)S(1)} %collective-permute-done.16.refs_5_), channel_id=1, source_target_pairs={{0,4},{4,12},{12,8},{8,0},{1,5},{5,13},{13,9},{9,1},{2,6},{6,14},{... | collective-permute-start | bytes 786440 | tf_op jit(solution)/shard_map/ppermute | solution.py:46
  75.8 11.3 %collective-permute-start.21 = (bf16[256,512]{1,0:T(8,128)(2,1)S(1)}, bf16[256,512]{1,0:T(8,128)(2,1)S(1)}, u32[]{:S(2)}, u32[]{:S(2)}) collective-permute-start(bf16[256,512]{1,0:T(8,128)(2,1)S(1)} %pad_maximum_fusion), channel_id=1, source_target_pairs={{0,2},{2,0},{1,3},{3,1},{4,6},{6,4},{5,7},{7,5},{8,10},{10,8},{9,1... | collective-permute-start | bytes 786440 | tf_op jit(solution)/shard_map/ppermute | solution.py:55
  87.9 21.0 %collective-permute-start.44 = (bf16[32,32,128]{2,1,0:T(8,128)(2,1)S(1)}, bf16[32,32,128]{2,1,0:T(8,128)(2,1)S(1)}, u32[]{:S(2)}, u32[]{:S(2)}) collective-permute-start(bf16[32,32,128]{2,1,0:T(8,128)(2,1)S(1)} %collective-permute-done.16.refs_5_), channel_id=1, source_target_pairs={{0,16},{16,0},{1,17},{17,1},{2,18},{18,2},{3,19},{19,3},{4,20},{20... | collective-permute-start | bytes 786440 | tf_op jit(solution)/shard_map/ppermute | solution.py:50
  89.4 19.5 %collective-permute-start.46 = (bf16[32,32,128]{2,1,0:T(8,128)(2,1)S(1)}, bf16[32,32,128]{2,1,0:T(8,128)(2,1)S(1)}, u32[]{:S(2)}, u32[]{:S(2)}) collective-permute-start(bf16[32,32,128]{2,1,0:T(8,128)(2,1)S(1)} %collective-permute-done.45.refs_7_), channel_id=1, source_target_pairs={{0,16},{16,0},{1,17},{17,1},{2,18},{18,2},{3,19},{19,3},{4,20},{20... | collective-permute-start | bytes 786440 | tf_op jit(solution)/shard_map/ppermute | solution.py:50
  96.0 12.9 %collective-permute-start.48 = (bf16[32,32,128]{2,1,0:T(8,128)(2,1)S(1)}, bf16[32,32,128]{2,1,0:T(8,128)(2,1)S(1)}, u32[]{:S(2)}, u32[]{:S(2)}) collective-permute-start(bf16[32,32,128]{2,1,0:T(8,128)(2,1)S(1)} %collective-permute-done.47.refs_9_), channel_id=1, source_target_pairs={{0,16},{16,0},{1,17},{17,1},{2,18},{18,2},{3,19},{19,3},{4,20},{20... | collective-permute-start | bytes 786440 | tf_op jit(solution)/shard_map/ppermute | solution.py:50
  141.3 11.5 %collective-permute-start.57 = (bf16[544,128]{1,0:T(8,128)(2,1)S(1)}, bf16[544,128]{1,0:T(8,128)(2,1)S(1)}, u32[]{:S(2)}, u32[]{:S(2)}) collective-permute-start(bf16[544,128]{1,0:T(8,128)(2,1)S(1)} %add.40), channel_id=1, source_target_pairs={{0,4},{4,12},{12,8},{8,0},{1,5},{5,13},{13,9},{9,1},{2,6},{6,14},{... | collective-permute-start | bytes 417800 | tf_op jit(solution)/shard_map/ppermute | solution.py:46
  144.2 11.5 %collective-permute-start.54 = (bf16[544,128]{1,0:T(8,128)(2,1)S(1)}, bf16[544,128]{1,0:T(8,128)(2,1)S(1)}, u32[]{:S(2)}, u32[]{:S(2)}) collective-permute-start(bf16[544,128]{1,0:T(8,128)(2,1)S(1)} %add.37), channel_id=1, source_target_pairs={{0,4},{4,12},{12,8},{8,0},{1,5},{5,13},{13,9},{9,1},{2,6},{6,14},{... | collective-permute-start | bytes 417800 | tf_op jit(solution)/shard_map/ppermute | solution.py:46
  147.1 11.6 %collective-permute-start.31 = (bf16[128,512]{1,0:T(8,128)(2,1)S(1)}, bf16[128,512]{1,0:T(8,128)(2,1)S(1)}, u32[]{:S(2)}, u32[]{:S(2)}) collective-permute-start(bf16[128,512]{1,0:T(8,128)(2,1)S(1)} %add.35.refs_1_), channel_id=1, source_target_pairs={{0,4},{4,12},{12,8},{8,0},{1,5},{5,13},{13,9},{9,1},{2,6},{6,14},{... | collective-permute-start | bytes 393224 | tf_op jit(solution)/shard_map/ppermute | solution.py:46
  149.9 11.6 %collective-permute-start.30 = (bf16[128,512]{1,0:T(8,128)(2,1)S(1)}, bf16[128,512]{1,0:T(8,128)(2,1)S(1)}, u32[]{:S(2)}, u32[]{:S(2)}) collective-permute-start(bf16[128,512]{1,0:T(8,128)(2,1)S(1)} %add.32.refs_0_), channel_id=1, source_target_pairs={{0,4},{4,12},{12,8},{8,0},{1,5},{5,13},{13,9},{9,1},{2,6},{6,14},{... | collective-permute-start | bytes 393224 | tf_op jit(solution)/shard_map/ppermute | solution.py:46
  150.6 10.9 %collective-permute-start.37 = (bf16[128,512]{1,0:T(8,128)(2,1)S(1)}, bf16[128,512]{1,0:T(8,128)(2,1)S(1)}, u32[]{:S(2)}, u32[]{:S(2)}) collective-permute-start(bf16[128,512]{1,0:T(8,128)(2,1)S(1)} %add.35.refs_1_), channel_id=1, source_target_pairs={{0,1},{1,0},{2,3},{3,2},{4,5},{5,4},{6,7},{7,6},{8,9},{9,8},{10,11... | collective-permute-start | bytes 393224 | tf_op jit(solution)/shard_map/ppermute | solution.py:50
  152.8 11.9 %collective-permute-start.59 = (bf16[544,128]{1,0:T(8,128)(2,1)S(1)}, bf16[544,128]{1,0:T(8,128)(2,1)S(1)}, u32[]{:S(2)}, u32[]{:S(2)}) collective-permute-start(bf16[544,128]{1,0:T(8,128)(2,1)S(1)} %add.41.refs_17_), channel_id=1, source_target_pairs={{0,4},{4,12},{12,8},{8,0},{1,5},{5,13},{13,9},{9,1},{2,6},{6,14},{... | collective-permute-start | bytes 417800 | tf_op jit(solution)/shard_map/ppermute | solution.py:46
  164.8 16.9 %collective-permute-start.61 = (bf16[544,128]{1,0:T(8,128)(2,1)S(1)}, bf16[544,128]{1,0:T(8,128)(2,1)S(1)}, u32[]{:S(2)}, u32[]{:S(2)}) collective-permute-start(bf16[544,128]{1,0:T(8,128)(2,1)S(1)} %collective-permute-done.59.refs_19_), channel_id=1, source_target_pairs={{0,4},{4,12},{12,8},{8,0},{1,5},{5,13},{13,9},{9,1},{2,6},{6,14},{... | collective-permute-start | bytes 417800 | tf_op jit(solution)/shard_map/ppermute | solution.py:46
  166.2 16.0 %collective-permute-start.60 = (bf16[544,128]{1,0:T(8,128)(2,1)S(1)}, bf16[544,128]{1,0:T(8,128)(2,1)S(1)}, u32[]{:S(2)}, u32[]{:S(2)}) collective-permute-start(bf16[544,128]{1,0:T(8,128)(2,1)S(1)} %collective-permute-done.58.refs_18_), channel_id=1, source_target_pairs={{0,4},{4,12},{12,8},{8,0},{1,5},{5,13},{13,9},{9,1},{2,6},{6,14},{... | collective-permute-start | bytes 417800 | tf_op jit(solution)/shard_map/ppermute | solution.py:46
  169.0 11.2 %collective-permute-start.35 = (bf16[128,512]{1,0:T(8,128)(2,1)S(1)}, bf16[128,512]{1,0:T(8,128)(2,1)S(1)}, u32[]{:S(2)}, u32[]{:S(2)}) collective-permute-start(bf16[128,512]{1,0:T(8,128)(2,1)S(1)} %collective-permute-done.33.refs_5_), channel_id=1, source_target_pairs={{0,4},{4,12},{12,8},{8,0},{1,5},{5,13},{13,9},{9,1},{2,6},{6,14},{... | collective-permute-start | bytes 393224 | tf_op jit(solution)/shard_map/ppermute | solution.py:46
  (66 other events, 495.9 us)

commit v12 on v11

--- a/solution.py
+++ b/solution.py
@@ -241,8 +241,8 @@
                 store(start + b, there * 2 + 1 - sub, piece[size + b])
 
 
-def front_kernel(first_got, own, got, scale, codes, codes_got, *refs):
-    moved, (mine_ref, theirs_ref, wide, weight) = refs[:-4], refs[-4:]
+def front_kernel(first_got, term, own, got, scale, codes, codes_got, *refs):
+    moved, (mine_ref, theirs_ref, wide, weight) = term.split(refs)
     blocks, rows, units = codes.shape
     first = lax.axis_index("sub") * (blocks // 2)
     widen(scale, wide)
@@ -256,12 +256,12 @@
 
     place_shards(codes, codes_got, first_got, moved, store)
     matrix = weight[...].reshape(-1, units)
-    mine_ref[...] = dot(own[...], matrix)
+    mine_ref[...] = term.added(dot(own[...], matrix))
     theirs_ref[...] = dot(got[...], matrix).astype(BF16)
 
 
-def back_kernel(first_got, own, got, scale, codes, codes_got, *refs):
-    moved, (mine_ref, theirs_ref, wide, weight) = refs[:-4], refs[-4:]
+def back_kernel(first_got, term, own, got, scale, codes, codes_got, *refs):
+    moved, (mine_ref, theirs_ref, wide, weight) = term.split(refs)
     blocks, rows, block = codes.shape
     first = lax.axis_index("sub") * (blocks // 2)
     per_group = weight.shape[0] // wide.shape[0]
@@ -275,7 +275,7 @@
 
     place_shards(codes, codes_got, first_got, moved, store)
     matrix = weight[...]
-    mine_ref[...] = contract_dims(own[...], matrix, 1, 1)
+    mine_ref[...] = term.added(contract_dims(own[...], matrix, 1, 1))
     theirs_ref[...] = contract_dims(got[...], matrix, 1, 1).astype(BF16)
 
 
@@ -299,52 +299,83 @@
             ref[...] = lax.slice_in_dim(full, i * size, (i + 1) * size, axis=axis).astype(BF16)
 
 
-def low_sums(low, low_more):
-    total = low[...]
-    for ref in low_more:
-        total = total + ref[:, ref.shape[1] - total.shape[1] :].astype(F32)
-    half = total.shape[1] // 2
-    return total[:, :half].astype(BF16), total[:, half:].astype(BF16)
-
-
-def gather_adapters(adapters, adapters_more, up_out_all, down_in_all):
-    rank = up_out_all.shape[0]
-    place_own(up_out_all, adapters.at[:rank], [r.at[:rank] for r in adapters_more], 1)
+class NoTerm:
+    arrays = ()
+
+    def split(self, refs):
+        return refs[:-4], refs[-4:]
+
+    def added(self, product):
+        return product
+
+
+class UpTerm:
+    def __init__(self, low, adapters, more):
+        self.arrays = (low, adapters, *more)
+
+    def split(self, refs):
+        count = len(self.arrays)
+        self.refs, self.all = refs[:count], refs[-1]
+        return refs[count:-5], refs[-5:-1]
+
+    def added(self, product):
+        low, adapters, *more = self.refs
+        rank = self.all.shape[0]
+        place_own(self.all, adapters.at[:rank], [r.at[:rank] for r in more], 1)
+        return product + ADAPTER_SCALE * dot(low[:, :rank].astype(BF16), self.all[...])
+
+
+class DownTerm(UpTerm):
+    def added(self, product):
+        low, adapters, *more = self.refs
+        rank = self.all.shape[1]
+        place_own(self.all, adapters.at[rank:], [r.at[rank:] for r in more], 0)
+        return product + ADAPTER_SCALE * contract_dims(
+            low[:, rank:].astype(BF16), self.all[...], 1, 1
+        )
+
+
+def hidden_kernel(more, gate, up, adapters, *refs):
+    gate_more, up_more, adapters_more = (refs[i * more : (i + 1) * more] for i in range(3))
+    silu_ref, hidden_ref, low_ref, down_in_all = refs[3 * more :]
+    rank = low_ref.shape[1]
     place_own(down_in_all, adapters.at[rank:], [r.at[rank:] for r in adapters_more], 0)
-
-
-def hidden_kernel(more, gate, up, low, adapters, *refs):
-    gate_more, up_more, adapters_more = (refs[i * more : (i + 1) * more] for i in range(3))
-    silu_ref, low_ref, down_in_term, up_out_all, down_in_all = refs[3 * more :]
-    gather_adapters(adapters, adapters_more, up_out_all, down_in_all)
-    low_up, low_out = low_sums(low, gate_more)
     gate_sum, up_sum = gate[...], up[...]
     for ref in gate_more:
-        gate_sum = gate_sum + ref[:, : gate_sum.shape[1]].astype(F32)
+        gate_sum = gate_sum + ref[...].astype(F32)
     for ref in up_more:
         up_sum = up_sum + ref[...].astype(F32)
-    up_sum = up_sum + ADAPTER_SCALE * dot(low_up, up_out_all[...])
     silu = gate_sum * jax.nn.sigmoid(gate_sum)
     silu_ref[...] = silu
     hidden = (silu * up_sum).astype(BF16)
+    hidden_ref[...] = hidden
     low_ref[...] = (ADAPTER_SCALE * dot(hidden, down_in_all[...])).astype(BF16)
-    hidden_t = hidden.astype(F32).T.astype(BF16)
-    own_units(ADAPTER_SCALE * dot(hidden_t, low_out), down_in_term, 0)
-
-
-def up_grad_kernel(more, back, silu, low, adapters, *refs):
-    back_more, low_more, adapters_more = (refs[i * more : (i + 1) * more] for i in range(3))
-    low_ref, up_out_term, up_out_all, down_in_all = refs[3 * more :]
-    gather_adapters(adapters, adapters_more, up_out_all, down_in_all)
-    low_up, low_out = low_sums(low, low_more)
+
+
+def up_grad_kernel(more, back, silu, adapters, *refs):
+    back_more, adapters_more = (refs[i * more : (i + 1) * more] for i in range(2))
+    up_grad_ref, low_ref, up_out_all = refs[2 * more :]
+    rank = low_ref.shape[1]
+    place_own(up_out_all, adapters.at[:rank], [r.at[:rank] for r in adapters_more], 1)
     total = back[...]
     for ref in back_more:
         total = total + ref[...].astype(F32)
-    total = total + ADAPTER_SCALE * contract_dims(low_out, down_in_all[...], 1, 1)
     up_grad = (total * silu[...]).astype(BF16)
+    up_grad_ref[...] = up_grad
     low_ref[...] = (ADAPTER_SCALE * contract_dims(up_grad, up_out_all[...], 1, 1)).astype(BF16)
+
+
+def small_kernel(more, hidden, up_grad, low, *refs):
+    low_more, (up_out_term, down_in_term) = refs[:more], refs[more:]
+    total = low[...]
+    for ref in low_more:
+        total = total + ref[...]
+    rank = total.shape[1] // 2
+    low_up, low_out = total[:, :rank].astype(BF16), total[:, rank:].astype(BF16)
     low_up_t = low_up.astype(F32).T.astype(BF16)
-    own_units(ADAPTER_SCALE * dot(low_up_t, up_grad), up_out_term, 1)
+    own_units(ADAPTER_SCALE * dot(low_up_t, up_grad[...]), up_out_term, 1)
+    hidden_t = hidden[...].astype(F32).T.astype(BF16)
+    own_units(ADAPTER_SCALE * dot(hidden_t, low_out), down_in_term, 0)
 
 
 def down_out_kernel(n, low, low_got, grad, grad_got, *out_refs):
@@ -564,8 +595,8 @@
     normed_got = swap(normed_send, "sub")
     step(ring[2], ring[3], *crossed[:2])
     step(ring[3], ring[2], *crossed[:2])
-    cross(2)
-    cross(3)
+    cross(2, normed)
+    cross(3, normed)
     cross(4)
     cross(5)
     down_turned = jnp.swapaxes(after(down_codes, *ring[2:4]), 0, 1)
@@ -575,55 +606,53 @@
     step(ring[6])
     cross(7)
 
-    def product(kernel, name, own, got, scale, codes, codes_got, first_got, steps, weight_shape, beside=()):
+    def product(kernel, name, own, got, scale, codes, codes_got, first_got, steps, weight_shape, term, extra=()):
         groups = scale.shape[0]
         mine, theirs = call(
-            lambda *refs: kernel(first_got, *refs),
+            lambda *refs: kernel(first_got, term, *refs),
             name,
-            [own, got, scale, codes, codes_got, *[x for k in steps for x in (ring[k], crossed[k])]],
+            [own, got, scale, codes, codes_got, *term.arrays, *[x for k in steps for x in (ring[k], crossed[k])]],
             [shape((rows, units), F32), shape((rows, units))],
-            scratch=[pltpu.VMEM((groups, blocks, LANES), F32), pltpu.VMEM(weight_shape, BF16)],
+            scratch=[pltpu.VMEM((groups, blocks, LANES), F32), pltpu.VMEM(weight_shape, BF16), *extra],
             flops=4 * rows * half * units,
         )
         total = mine + swap(theirs, "sub").astype(F32)
-        send = jnp.concatenate([total.astype(BF16), *[b.astype(BF16) for b in beside]], axis=1)
-        return total, others(send, "mp")
+        return total, others(total.astype(BF16), "mp")
 
     front = (blocks // 2, block, units)
     first_down = [ring[2 * (n - 1)]]
     half_blocks = blocks // 2
     gate, gate_more = product(
         front_kernel, "gate", normed, normed_got, after(gate_block_scale.T, *first_down), gate_codes, front_got, 0,
-        range(0, 2 * (n - 1), 2), front, [low],
+        range(0, 2 * (n - 1), 2), front, NoTerm(),
     )
     up, up_more = product(
         front_kernel, "up", normed, normed_got, after(up_block_scale.T, *first_down), up_codes, front_got, half_blocks,
-        range(1, 2 * (n - 1), 2), front,
-    )
-    small_scratch = [
-        pltpu.VMEM((rank, units), BF16),
-        pltpu.VMEM((units, rank), BF16),
-    ]
-    silu, low_hidden, down_in_term = call(
+        range(1, 2 * (n - 1), 2), front, UpTerm(low, adapters, adapters_more),
+        [pltpu.VMEM((rank, units), BF16)],
+    )
+    silu, hidden, low_hidden = call(
         lambda *refs: hidden_kernel(more, *refs),
         "hidden",
-        [gate, up, low, adapters, *gate_more, *up_more, *adapters_more],
-        [shape((rows, units), F32), shape((rows, rank)), shape(down_adapter_in.shape)],
-        scratch=small_scratch,
+        [gate, up, adapters, *gate_more, *up_more, *adapters_more],
+        [shape((rows, units), F32), shape((rows, units)), shape((rows, rank))],
+        scratch=[pltpu.VMEM((units, rank), BF16)],
         limit=8,
     )
+    low_hidden_got = swap(low_hidden, "sub")
     pieces = STREAMS * n
-    for _ in range(n - 3):
-        step(ring[-1], low_hidden)
-        cross(-1)
     down_out_parts = call(
         lambda *refs: down_out_kernel(n, *refs),
         "down_out",
-        [low_hidden, swap(low_hidden, "sub"), grad, grad_got],
+        [low_hidden, low_hidden_got, grad, grad_got],
         [shape((rank, half // pieces))] * pieces,
         flops=4 * rows * half * rank,
     )
+    for _ in range(n - 3):
+        step(ring[-1], down_out_parts[0])
     down_out_blocks, seen = ring_all(down_out_parts, STREAMS)
+    for k in range(3 * (n - 1) - (n - 3), 3 * (n - 1)):
+        cross(k, *seen[0])
     (normed_t,) = call(
         transpose_kernel,
         "transpose",
@@ -634,14 +663,23 @@
 
     back, back_more = product(
         back_kernel, "back", grad, grad_got, after(down_block_scale, normed_t, *seen[0]), down_turned, down_got, 0,
-        range(2 * (n - 1), 3 * (n - 1)), (units, half),
-    )
-    low_grad, up_out_term = call(
+        range(2 * (n - 1), 3 * (n - 1)), (units, half), DownTerm(low, adapters, adapters_more),
+        [pltpu.VMEM((units, rank), BF16)],
+    )
+    up_grad, low_grad = call(
         lambda *refs: up_grad_kernel(more, *refs),
         "up_grad",
-        [back, silu, low, adapters, *back_more, *gate_more, *adapters_more],
-        [shape((rows, rank)), shape(up_adapter_out.shape)],
-        scratch=small_scratch,
+        [back, silu, adapters, *back_more, *adapters_more],
+        [shape((rows, units)), shape((rows, rank))],
+        scratch=[pltpu.VMEM((rank, units), BF16)],
+        limit=8,
+    )
+    low_more = others(after(low, *seen[0]), "mp")
+    up_out_term, down_in_term = call(
+        lambda *refs: small_kernel(more, *refs),
+        "small",
+        [hidden, up_grad, low, *low_more],
+        [shape(up_adapter_out.shape), shape(down_adapter_in.shape)],
         limit=8,
     )
     extra = 2 * rank // pieces
@@ -652,7 +690,7 @@
         [shape((half // pieces + extra, rank))] * pieces,
         flops=4 * rows * half * rank,
     )
-    up_in_blocks, _ = ring_all(up_in_parts, STREAMS, seen[-2])
+    up_in_blocks, _ = ring_all(up_in_parts, STREAMS, down_out_blocks[-STREAMS:])
 
     anywhere = pl.BlockSpec(memory_space=pl.ANY)
     up_in_gradient, up_out_gradient, down_in_gradient, down_out_gradient = call(

time: 198 us -> 204 us (1.030)
  waiting for transfers between devices: 106 us -> 115 us
  starting transfers between devices: 58.7 us -> 56.1 us
    ppermute x34, waiting for transfers between devices: 16.9 us -> 23.7 us  [swap(): return lax.ppermute(x, axis, [(0, 1), (1, 0)])]
    ppermute x33, starting transfers between devices: 37.5 us -> 34.7 us  [ring_step(): lax.ppermute(x, 'dp', [(ring_at(i, n), ring_at((i + 1) % n, n)) for i in...]
    ppermute x5 -> x6, waiting for transfers between devices: 12.2 us -> 14.3 us  [others(): lax.ppermute(x, axis, [(i, (i + k) % n) for i in range(n)])]
    ppermute x5 -> x6, starting transfers between devices: 7.06 us -> 8.08 us  [others(): lax.ppermute(x, axis, [(i, (i + k) % n) for i in range(n)])]
    pallas_call x28 -> x29, Pallas kernels: 26.3 us -> 26.5 us  [call(): pl.pallas_call(kernel, out_shape=tuple(out_shape), in_specs=specs or [vme...]
  transfers between devices with their start and end apart: 72 -> 73, of which waited for: 41 -> 44; matrix products, arithmetic and copies ran while one was open for 0% -> 0% of each run, Pallas kernels for 9% -> 8%
where the time goes in v12:
time: 204 us
  waiting for transfers between devices  115 us (56%)
  starting transfers between devices  56.1 us (28%)
  Pallas kernels  26.5 us (13%)
  local copies, waits for them, and re-layouts  4.71 us (2%)
    ppermute x33, waiting for transfers between devices, ring_step(): lax.ppermute(x, 'dp', [(ring_at(i, n), ring_at((i + 1) % n, n)) for i in...  77 us
    ppermute x33, starting transfers between devices, ring_step(): lax.ppermute(x, 'dp', [(ring_at(i, n), ring_at((i + 1) % n, n)) for i in...  34.7 us
    pallas_call x29, Pallas kernels, call(): pl.pallas_call(kernel, out_shape=tuple(out_shape), in_specs=specs or [vme...  26.5 us
    ppermute x34, waiting for transfers between devices, swap(): return lax.ppermute(x, axis, [(0, 1), (1, 0)])  23.7 us
    ppermute x6, waiting for transfers between devices, others(): lax.ppermute(x, axis, [(i, (i + k) % n) for i in range(n)])  14.3 us
    ppermute x34, starting transfers between devices, swap(): return lax.ppermute(x, axis, [(0, 1), (1, 0)])  13.3 us
    ppermute x6, starting transfers between devices, others(): lax.ppermute(x, axis, [(i, (i + k) % n) for i in range(n)])  8.08 us
    unnamed x37, local copies, waits for them, and re-layouts  4.34 us
  transfers between devices with their start and end apart: 73, of which 44 were waited for; matrix products, arithmetic and copies ran while one was open for 0% of the time, Pallas kernels for 8%

profile of v12, /device:TPU:0, one launch (start us, length us, event | category | flops | bytes accessed | tf_op | source)
XLA Modules:
  0.0 203.6 jit_solution(8898686638921859267)
XLA Ops:
  5.5 3.0 %collective-permute-start.2 = (bf16[32,16,256]{2,1,0:T(8,128)(2,1)S(1)}, bf16[32,16,256]{2,1,0:T(8,128)(2,1)S(1)}, u32[]{:S(2)}, u32[]{:S(2)}) collective-permute-start(bf16[32,16,256]{2,1,0:T(8,128)(2,1)S(1)} %get-tuple-element.66), channel_id=1, source_target_pairs={{0,4},{4,12},{12,8},{8,0},{1,5},{5,13},{13,9},{9,1},{2,6},{6,14},{... | collective-permute-start | bytes 786440 | tf_op jit(solution)/shard_map/ppermute | solution.py:46
  8.5 2.6 %collective-permute-start.1 = (bf16[32,16,256]{2,1,0:T(8,128)(2,1)S(1)}, bf16[32,16,256]{2,1,0:T(8,128)(2,1)S(1)}, u32[]{:S(2)}, u32[]{:S(2)}) collective-permute-start(bf16[32,16,256]{2,1,0:T(8,128)(2,1)S(1)} %get-tuple-element.65), channel_id=1, source_target_pairs={{0,4},{4,12},{12,8},{8,0},{1,5},{5,13},{13,9},{9,1},{2,6},{6,14},{... | collective-permute-start | bytes 786440 | tf_op jit(solution)/shard_map/ppermute | solution.py:46
  15.8 4.2 %cotangent.1 = (bf16[256,4096]{1,0:T(8,128)(2,1)S(1)}, bf16[256,4096]{1,0:T(8,128)(2,1)S(1)}, f32[256,128]{1,0:T(8,128)S(1)}) custom-call(bf16[256,8192]{1,0:T(8,128)(2,1)S(1)} %copy-done.6, s32[1,2]{1,0:T(1,128)S(1)} %copy-done.9, s32[1,256]{1,0:T(1,128)S(1)} %bitcast.9, bf16[128,8192]{1,0:T(8,128)(2,1)S(1)} %copy-done.8), custom_call_target="tpu_custom_call" | custom-call | tf_op jit(solution)/shard_map/cotangent/pallas_call | solution.py:67
  22.6 3.4 %collective-permute-start.4 = (bf16[32,16,256]{2,1,0:T(8,128)(2,1)S(1)}, bf16[32,16,256]{2,1,0:T(8,128)(2,1)S(1)}, u32[]{:S(2)}, u32[]{:S(2)}) collective-permute-start(bf16[32,16,256]{2,1,0:T(8,128)(2,1)S(1)} %collective-permute-done.2.refs_8_), channel_id=1, source_target_pairs={{0,4},{4,12},{12,8},{8,0},{1,5},{5,13},{13,9},{9,1},{2,6},{6,14},{... | collective-permute-start | bytes 786440 | tf_op jit(solution)/shard_map/ppermute | solution.py:46
  29.6 2.9 %collective-permute-done.7.refs_7_.refs_5_.refs_4_ = bf16[256,128]{1,0:T(8,128)(2,1)S(1)} collective-permute-done((bf16[256,128]{1,0:T(8,128)(2,1)S(1)}, bf16[256,128]{1,0:T(8,128)(2,1)S(1)}, u32[]{:S(2)}, u32[]{:S(2)}) %collective-permute-start.7) | collective-permute-done | bytes 65568 | tf_op jit(solution)/shard_map/ppermute | solution.py:55
  38.6 3.0 %tokens.3 = (bf16[256,4096]{1,0:T(8,128)(2,1)S(1)}, bf16[256,4096]{1,0:T(8,128)(2,1)S(1)}, f32[256,256]{1,0:T(8,128)S(1)}) custom-call(bf16[256,8192]{1,0:T(8,128)(2,1)S(1)} %copy-done.1, bf16[1,8192]{1,0:T(2,128)(2,1)S(1)} %broadcast_in_dim.6.refs_1_, bf16[8192,128]{1,0:T(8,128)(2,1)S(1)} %copy-done.7, f32[256,128]{1,0:T(8,128)S(1)} %get-tuple-element.69.refs_3_, ...), custom_call_target="tpu_custom_call" | custom-call | tf_op jit(solution)/shard_map/tokens/pallas_call | solution.py:67
  43.9 7.9 %collective-permute-done.11.refs_9_ = bf16[32,16,256]{2,1,0:T(8,128)(2,1)S(1)} collective-permute-done((bf16[32,16,256]{2,1,0:T(8,128)(2,1)S(1)}, bf16[32,16,256]{2,1,0:T(8,128)(2,1)S(1)}, u32[]{:S(2)}, u32[]{:S(2)}) %collective-permute-start.11) | collective-permute-done | bytes 262176 | tf_op jit(solution)/shard_map/ppermute | solution.py:46
  54.2 2.8 %collective-permute-done.12.refs_12_ = bf16[32,16,256]{2,1,0:T(8,128)(2,1)S(1)} collective-permute-done((bf16[32,16,256]{2,1,0:T(8,128)(2,1)S(1)}, bf16[32,16,256]{2,1,0:T(8,128)(2,1)S(1)}, u32[]{:S(2)}, u32[]{:S(2)}) %collective-permute-start.12) | collective-permute-done | bytes 262176 | tf_op jit(solution)/shard_map/ppermute | solution.py:46
  57.0 4.1 %collective-permute-done.13.refs_8_ = bf16[32,16,256]{2,1,0:T(8,128)(2,1)S(1)} collective-permute-done((bf16[32,16,256]{2,1,0:T(8,128)(2,1)S(1)}, bf16[32,16,256]{2,1,0:T(8,128)(2,1)S(1)}, u32[]{:S(2)}, u32[]{:S(2)}) %collective-permute-start.13) | collective-permute-done | bytes 262176 | tf_op jit(solution)/shard_map/ppermute | solution.py:50
  61.0 3.8 %collective-permute-done.14.refs_11_ = bf16[32,16,256]{2,1,0:T(8,128)(2,1)S(1)} collective-permute-done((bf16[32,16,256]{2,1,0:T(8,128)(2,1)S(1)}, bf16[32,16,256]{2,1,0:T(8,128)(2,1)S(1)}, u32[]{:S(2)}, u32[]{:S(2)}) %collective-permute-start.14) | collective-permute-done | bytes 262176 | tf_op jit(solution)/shard_map/ppermute | solution.py:50
  66.9 5.3 %collective-permute-done.16.refs_8_ = bf16[32,32,128]{2,1,0:T(8,128)(2,1)S(1)} collective-permute-done((bf16[32,32,128]{2,1,0:T(8,128)(2,1)S(1)}, bf16[32,32,128]{2,1,0:T(8,128)(2,1)S(1)}, u32[]{:S(2)}, u32[]{:S(2)}) %collective-permute-start.16) | collective-permute-done | bytes 262176 | tf_op jit(solution)/shard_map/ppermute | solution.py:46
  82.5 4.2 %collective-permute-done.21.refs_3_ = bf16[256,256]{1,0:T(8,128)(2,1)S(1)} collective-permute-done((bf16[256,256]{1,0:T(8,128)(2,1)S(1)}, bf16[256,256]{1,0:T(8,128)(2,1)S(1)}, u32[]{:S(2)}, u32[]{:S(2)}) %collective-permute-start.21) | collective-permute-done | bytes 131104 | tf_op jit(solution)/shard_map/ppermute | solution.py:55
  91.5 3.1 %collective-permute-start.27 = (bf16[128,512]{1,0:T(8,128)(2,1)S(1)}, bf16[128,512]{1,0:T(8,128)(2,1)S(1)}, u32[]{:S(2)}, u32[]{:S(2)}) collective-permute-start(bf16[128,512]{1,0:T(8,128)(2,1)S(1)} %get-tuple-element.98), channel_id=1, source_target_pairs={{0,4},{4,12},{12,8},{8,0},{1,5},{5,13},{13,9},{9,1},{2,6},{6,14},{... | collective-permute-start | bytes 393224 | tf_op jit(solution)/shard_map/ppermute | solution.py:46
  97.0 7.0 %collective-permute-done.27.left = bf16[128,512]{1,0:T(8,128)(2,1)S(1)} collective-permute-done((bf16[128,512]{1,0:T(8,128)(2,1)S(1)}, bf16[128,512]{1,0:T(8,128)(2,1)S(1)}, u32[]{:S(2)}, u32[]{:S(2)}) %collective-permute-start.27) | collective-permute-done | bytes 131104 | tf_op jit(solution)/shard_map/ppermute | solution.py:46
  108.7 5.0 %collective-permute-done.48.refs_13_ = bf16[32,32,128]{2,1,0:T(8,128)(2,1)S(1)} collective-permute-done((bf16[32,32,128]{2,1,0:T(8,128)(2,1)S(1)}, bf16[32,32,128]{2,1,0:T(8,128)(2,1)S(1)}, u32[]{:S(2)}, u32[]{:S(2)}) %collective-permute-start.48) | collective-permute-done | bytes 262176 | tf_op jit(solution)/shard_map/ppermute | solution.py:50
  122.5 5.1 %collective-permute-done.50.refs_3_ = bf16[256,256]{1,0:T(8,128)(2,1)S(1)} collective-permute-done((bf16[256,256]{1,0:T(8,128)(2,1)S(1)}, bf16[256,256]{1,0:T(8,128)(2,1)S(1)}, u32[]{:S(2)}, u32[]{:S(2)}) %collective-permute-start.50) | collective-permute-done | bytes 131104 | tf_op jit(solution)/shard_map/ppermute | solution.py:55
  129.1 3.4 %up_in.1 = (bf16[544,128]{1,0:T(8,128)(2,1)S(1)}, bf16[544,128]{1,0:T(8,128)(2,1)S(1)}, bf16[544,128]{1,0:T(8,128)(2,1)S(1)}, bf16[544,128]{1,0:T(8,128)(2,1)S(1...) custom-call(bf16[256,128]{1,0:T(8,128)(2,1)S(1)} %get-tuple-element., ...), custom_call_target="tpu_custom_call" | custom-call | tf_op jit(solution)/shard_map/up_in/pallas_call | solution.py:67
  140.3 2.7 %collective-permute-done.56.left = bf16[544,128]{1,0:T(8,128)(2,1)S(1)} collective-permute-done((bf16[544,128]{1,0:T(8,128)(2,1)S(1)}, bf16[544,128]{1,0:T(8,128)(2,1)S(1)}, u32[]{:S(2)}, u32[]{:S(2)}) %collective-permute-start.56) | collective-permute-done | bytes 139296 | tf_op jit(solution)/shard_map/ppermute | solution.py:46
  163.6 2.6 %collective-permute-done.58.left = bf16[544,128]{1,0:T(8,128)(2,1)S(1)} collective-permute-done((bf16[544,128]{1,0:T(8,128)(2,1)S(1)}, bf16[544,128]{1,0:T(8,128)(2,1)S(1)}, u32[]{:S(2)}, u32[]{:S(2)}) %collective-permute-start.58) | collective-permute-done | bytes 139296 | tf_op jit(solution)/shard_map/ppermute | solution.py:46
  175.0 2.7 %collective-permute-done.60.refs_19_ = bf16[544,128]{1,0:T(8,128)(2,1)S(1)} collective-permute-done((bf16[544,128]{1,0:T(8,128)(2,1)S(1)}, bf16[544,128]{1,0:T(8,128)(2,1)S(1)}, u32[]{:S(2)}, u32[]{:S(2)}) %collective-permute-start.60) | collective-permute-done | bytes 139296 | tf_op jit(solution)/shard_map/ppermute | solution.py:46
  180.5 2.8 %collective-permute-done.34.refs_6_ = bf16[128,512]{1,0:T(8,128)(2,1)S(1)} collective-permute-done((bf16[128,512]{1,0:T(8,128)(2,1)S(1)}, bf16[128,512]{1,0:T(8,128)(2,1)S(1)}, u32[]{:S(2)}, u32[]{:S(2)}) %collective-permute-start.34) | collective-permute-done | bytes 131104 | tf_op jit(solution)/shard_map/ppermute | solution.py:46
  189.9 3.0 %collective-permute-start.64 = (bf16[544,128]{1,0:T(8,128)(2,1)S(1)}, bf16[544,128]{1,0:T(8,128)(2,1)S(1)}, u32[]{:S(2)}, u32[]{:S(2)}) collective-permute-start(bf16[544,128]{1,0:T(8,128)(2,1)S(1)} %collective-permute-done.62.refs_21_), channel_id=1, source_target_pairs={{0,4},{4,12},{12,8},{8,0},{1,5},{5,13},{13,9},{9,1},{2,6},{6,14},{... | collective-permute-start | bytes 417800 | tf_op jit(solution)/shard_map/ppermute | solution.py:46
  193.4 3.5 %collective-permute-done.63.refs_22_ = bf16[544,128]{1,0:T(8,128)(2,1)S(1)} collective-permute-done((bf16[544,128]{1,0:T(8,128)(2,1)S(1)}, bf16[544,128]{1,0:T(8,128)(2,1)S(1)}, u32[]{:S(2)}, u32[]{:S(2)}) %collective-permute-start.63) | collective-permute-done | bytes 139296 | tf_op jit(solution)/shard_map/ppermute | solution.py:46
  200.4 3.0 %place.1 = (bf16[8192,128]{1,0:T(8,128)(2,1)}, bf16[128,128]{1,0:T(8,128)(2,1)}, bf16[128,128]{1,0:T(8,128)(2,1)}, bf16[128,8192]{1,0:T(8,128)(2,1)}) custom-call(bf16[128,512]{1,0:T(8,128)(2,1)S(1)} %add.32.refs_0_, bf16[128,512]{1,0:T(8,128)(2,1)S(1)} %add.35.refs_1_, bf16[128,512]{1,0:T(8,128)(2,1)S(1)} %collective-permute-done.30.refs_2_, ...), custom_call_target="tpu_custom_call" | custom-call | tf_op jit(solution)/shard_map/place/pallas_call | solution.py:67
  (194 shorter events, 111.3 us)
Async XLA Ops:
  5.5 14.4 %collective-permute-start.2 = (bf16[32,16,256]{2,1,0:T(8,128)(2,1)S(1)}, bf16[32,16,256]{2,1,0:T(8,128)(2,1)S(1)}, u32[]{:S(2)}, u32[]{:S(2)}) collective-permute-start(bf16[32,16,256]{2,1,0:T(8,128)(2,1)S(1)} %get-tuple-element.66), channel_id=1, source_target_pairs={{0,4},{4,12},{12,8},{8,0},{1,5},{5,13},{13,9},{9,1},{2,6},{6,14},{... | collective-permute-start | bytes 786440 | tf_op jit(solution)/shard_map/ppermute | solution.py:46
  8.5 13.2 %collective-permute-start.1 = (bf16[32,16,256]{2,1,0:T(8,128)(2,1)S(1)}, bf16[32,16,256]{2,1,0:T(8,128)(2,1)S(1)}, u32[]{:S(2)}, u32[]{:S(2)}) collective-permute-start(bf16[32,16,256]{2,1,0:T(8,128)(2,1)S(1)} %get-tuple-element.65), channel_id=1, source_target_pairs={{0,4},{4,12},{12,8},{8,0},{1,5},{5,13},{13,9},{9,1},{2,6},{6,14},{... | collective-permute-start | bytes 786440 | tf_op jit(solution)/shard_map/ppermute | solution.py:46
  21.8 12.2 %collective-permute-start.3 = (bf16[32,16,256]{2,1,0:T(8,128)(2,1)S(1)}, bf16[32,16,256]{2,1,0:T(8,128)(2,1)S(1)}, u32[]{:S(2)}, u32[]{:S(2)}) collective-permute-start(bf16[32,16,256]{2,1,0:T(8,128)(2,1)S(1)} %collective-permute-done.1.refs_5_), channel_id=1, source_target_pairs={{0,4},{4,12},{12,8},{8,0},{1,5},{5,13},{13,9},{9,1},{2,6},{6,14},{... | collective-permute-start | bytes 786440 | tf_op jit(solution)/shard_map/ppermute | solution.py:46
  22.6 13.5 %collective-permute-start.4 = (bf16[32,16,256]{2,1,0:T(8,128)(2,1)S(1)}, bf16[32,16,256]{2,1,0:T(8,128)(2,1)S(1)}, u32[]{:S(2)}, u32[]{:S(2)}) collective-permute-start(bf16[32,16,256]{2,1,0:T(8,128)(2,1)S(1)} %collective-permute-done.2.refs_8_), channel_id=1, source_target_pairs={{0,4},{4,12},{12,8},{8,0},{1,5},{5,13},{13,9},{9,1},{2,6},{6,14},{... | collective-permute-start | bytes 786440 | tf_op jit(solution)/shard_map/ppermute | solution.py:46
  34.0 30.8 %collective-permute-start.15 = (bf16[256,4096]{1,0:T(8,128)(2,1)S(1)}, bf16[256,4096]{1,0:T(8,128)(2,1)S(1)}, u32[]{:S(2)}, u32[]{:S(2)}) collective-permute-start(bf16[256,4096]{1,0:T(8,128)(2,1)S(1)} %get-tuple-element.84), channel_id=1, source_target_pairs={{0,1},{1,0},{2,3},{3,2},{4,5},{5,4},{6,7},{7,6},{8,9},{9,8},{10,11... | collective-permute-start | bytes 6291464 | tf_op jit(solution)/shard_map/ppermute | solution.py:50
  41.7 23.2 %collective-permute-start.9 = (bf16[256,4096]{1,0:T(8,128)(2,1)S(1)}, bf16[256,4096]{1,0:T(8,128)(2,1)S(1)}, u32[]{:S(2)}, u32[]{:S(2)}) collective-permute-start(bf16[256,4096]{1,0:T(8,128)(2,1)S(1)} %get-tuple-element.78), channel_id=1, source_target_pairs={{0,1},{1,0},{2,3},{3,2},{4,5},{5,4},{6,7},{7,6},{8,9},{9,8},{10,11... | collective-permute-start | bytes 6291464 | tf_op jit(solution)/shard_map/ppermute | solution.py:50
  42.7 14.2 %collective-permute-start.12 = (bf16[32,16,256]{2,1,0:T(8,128)(2,1)S(1)}, bf16[32,16,256]{2,1,0:T(8,128)(2,1)S(1)}, u32[]{:S(2)}, u32[]{:S(2)}) collective-permute-start(bf16[32,16,256]{2,1,0:T(8,128)(2,1)S(1)} %collective-permute-done.4.refs_10_), channel_id=1, source_target_pairs={{0,4},{4,12},{12,8},{8,0},{1,5},{5,13},{13,9},{9,1},{2,6},{6,14},{... | collective-permute-start | bytes 786440 | tf_op jit(solution)/shard_map/ppermute | solution.py:46
  79.1 12.0 %collective-permute-start.45 = (bf16[32,32,128]{2,1,0:T(8,128)(2,1)S(1)}, bf16[32,32,128]{2,1,0:T(8,128)(2,1)S(1)}, u32[]{:S(2)}, u32[]{:S(2)}) collective-permute-start(bf16[32,32,128]{2,1,0:T(8,128)(2,1)S(1)} %collective-permute-done.16.refs_8_), channel_id=1, source_target_pairs={{0,4},{4,12},{12,8},{8,0},{1,5},{5,13},{13,9},{9,1},{2,6},{6,14},{... | collective-permute-start | bytes 786440 | tf_op jit(solution)/shard_map/ppermute | solution.py:46
  91.1 14.9 %collective-permute-start.47 = (bf16[32,32,128]{2,1,0:T(8,128)(2,1)S(1)}, bf16[32,32,128]{2,1,0:T(8,128)(2,1)S(1)}, u32[]{:S(2)}, u32[]{:S(2)}) collective-permute-start(bf16[32,32,128]{2,1,0:T(8,128)(2,1)S(1)} %collective-permute-done.45.refs_10_), channel_id=1, source_target_pairs={{0,4},{4,12},{12,8},{8,0},{1,5},{5,13},{13,9},{9,1},{2,6},{6,14},{... | collective-permute-start | bytes 786440 | tf_op jit(solution)/shard_map/ppermute | solution.py:46
  91.5 12.5 %collective-permute-start.27 = (bf16[128,512]{1,0:T(8,128)(2,1)S(1)}, bf16[128,512]{1,0:T(8,128)(2,1)S(1)}, u32[]{:S(2)}, u32[]{:S(2)}) collective-permute-start(bf16[128,512]{1,0:T(8,128)(2,1)S(1)} %get-tuple-element.98), channel_id=1, source_target_pairs={{0,4},{4,12},{12,8},{8,0},{1,5},{5,13},{13,9},{9,1},{2,6},{6,14},{... | collective-permute-start | bytes 393224 | tf_op jit(solution)/shard_map/ppermute | solution.py:46
  95.0 13.7 %collective-permute-start.44 = (bf16[32,32,128]{2,1,0:T(8,128)(2,1)S(1)}, bf16[32,32,128]{2,1,0:T(8,128)(2,1)S(1)}, u32[]{:S(2)}, u32[]{:S(2)}) collective-permute-start(bf16[32,32,128]{2,1,0:T(8,128)(2,1)S(1)} %collective-permute-done.16.refs_8_), channel_id=1, source_target_pairs={{0,16},{16,0},{1,17},{17,1},{2,18},{18,2},{3,19},{19,3},{4,20},{20... | collective-permute-start | bytes 786440 | tf_op jit(solution)/shard_map/ppermute | solution.py:50
  96.5 12.2 %collective-permute-start.46 = (bf16[32,32,128]{2,1,0:T(8,128)(2,1)S(1)}, bf16[32,32,128]{2,1,0:T(8,128)(2,1)S(1)}, u32[]{:S(2)}, u32[]{:S(2)}) collective-permute-start(bf16[32,32,128]{2,1,0:T(8,128)(2,1)S(1)} %collective-permute-done.45.refs_10_), channel_id=1, source_target_pairs={{0,16},{16,0},{1,17},{17,1},{2,18},{18,2},{3,19},{19,3},{4,20},{20... | collective-permute-start | bytes 786440 | tf_op jit(solution)/shard_map/ppermute | solution.py:50
  116.1 12.0 %collective-permute-start.52 = (f32[256,256]{1,0:T(8,128)S(1)}, f32[256,256]{1,0:T(8,128)S(1)}, u32[]{:S(2)}, u32[]{:S(2)}) collective-permute-start(f32[256,256]{1,0:T(8,128)S(1)} %get-tuple-element.113.refs_5_.refs_2_), channel_id=1, source_target_pairs={{0,2},{2,0},{1,3},{3,1},{4,6},{6,4},{5,7},{7,5},{8,10},{10,8},{9,1... | collective-permute-start | bytes 786440 | tf_op jit(solution)/shard_map/ppermute | solution.py:55
  140.0 11.5 %collective-permute-start.54 = (bf16[544,128]{1,0:T(8,128)(2,1)S(1)}, bf16[544,128]{1,0:T(8,128)(2,1)S(1)}, u32[]{:S(2)}, u32[]{:S(2)}) collective-permute-start(bf16[544,128]{1,0:T(8,128)(2,1)S(1)} %add.36), channel_id=1, source_target_pairs={{0,4},{4,12},{12,8},{8,0},{1,5},{5,13},{13,9},{9,1},{2,6},{6,14},{... | collective-permute-start | bytes 417800 | tf_op jit(solution)/shard_map/ppermute | solution.py:46
  143.0 11.5 %collective-permute-start.57 = (bf16[544,128]{1,0:T(8,128)(2,1)S(1)}, bf16[544,128]{1,0:T(8,128)(2,1)S(1)}, u32[]{:S(2)}, u32[]{:S(2)}) collective-permute-start(bf16[544,128]{1,0:T(8,128)(2,1)S(1)} %add.39), channel_id=1, source_target_pairs={{0,4},{4,12},{12,8},{8,0},{1,5},{5,13},{13,9},{9,1},{2,6},{6,14},{... | collective-permute-start | bytes 417800 | tf_op jit(solution)/shard_map/ppermute | solution.py:46
  145.8 11.6 %collective-permute-start.31 = (bf16[128,512]{1,0:T(8,128)(2,1)S(1)}, bf16[128,512]{1,0:T(8,128)(2,1)S(1)}, u32[]{:S(2)}, u32[]{:S(2)}) collective-permute-start(bf16[128,512]{1,0:T(8,128)(2,1)S(1)} %add.35.refs_1_), channel_id=1, source_target_pairs={{0,4},{4,12},{12,8},{8,0},{1,5},{5,13},{13,9},{9,1},{2,6},{6,14},{... | collective-permute-start | bytes 393224 | tf_op jit(solution)/shard_map/ppermute | solution.py:46
  148.6 11.6 %collective-permute-start.30 = (bf16[128,512]{1,0:T(8,128)(2,1)S(1)}, bf16[128,512]{1,0:T(8,128)(2,1)S(1)}, u32[]{:S(2)}, u32[]{:S(2)}) collective-permute-start(bf16[128,512]{1,0:T(8,128)(2,1)S(1)} %add.32.refs_0_), channel_id=1, source_target_pairs={{0,4},{4,12},{12,8},{8,0},{1,5},{5,13},{13,9},{9,1},{2,6},{6,14},{... | collective-permute-start | bytes 393224 | tf_op jit(solution)/shard_map/ppermute | solution.py:46
  157.3 11.6 %collective-permute-start.33 = (bf16[128,512]{1,0:T(8,128)(2,1)S(1)}, bf16[128,512]{1,0:T(8,128)(2,1)S(1)}, u32[]{:S(2)}, u32[]{:S(2)}) collective-permute-start(bf16[128,512]{1,0:T(8,128)(2,1)S(1)} %collective-permute-done.31.refs_3_), channel_id=1, source_target_pairs={{0,4},{4,12},{12,8},{8,0},{1,5},{5,13},{13,9},{9,1},{2,6},{6,14},{... | collective-permute-start | bytes 393224 | tf_op jit(solution)/shard_map/ppermute | solution.py:46
  160.2 11.6 %collective-permute-start.32 = (bf16[128,512]{1,0:T(8,128)(2,1)S(1)}, bf16[128,512]{1,0:T(8,128)(2,1)S(1)}, u32[]{:S(2)}, u32[]{:S(2)}) collective-permute-start(bf16[128,512]{1,0:T(8,128)(2,1)S(1)} %collective-permute-done.30.refs_2_), channel_id=1, source_target_pairs={{0,4},{4,12},{12,8},{8,0},{1,5},{5,13},{13,9},{9,1},{2,6},{6,14},{... | collective-permute-start | bytes 393224 | tf_op jit(solution)/shard_map/ppermute | solution.py:46
  163.2 11.5 %collective-permute-start.59 = (bf16[544,128]{1,0:T(8,128)(2,1)S(1)}, bf16[544,128]{1,0:T(8,128)(2,1)S(1)}, u32[]{:S(2)}, u32[]{:S(2)}) collective-permute-start(bf16[544,128]{1,0:T(8,128)(2,1)S(1)} %add.38.refs_16_), channel_id=1, source_target_pairs={{0,4},{4,12},{12,8},{8,0},{1,5},{5,13},{13,9},{9,1},{2,6},{6,14},{... | collective-permute-start | bytes 417800 | tf_op jit(solution)/shard_map/ppermute | solution.py:46
  166.2 11.5 %collective-permute-start.60 = (bf16[544,128]{1,0:T(8,128)(2,1)S(1)}, bf16[544,128]{1,0:T(8,128)(2,1)S(1)}, u32[]{:S(2)}, u32[]{:S(2)}) collective-permute-start(bf16[544,128]{1,0:T(8,128)(2,1)S(1)} %add.41.refs_17_), channel_id=1, source_target_pairs={{0,4},{4,12},{12,8},{8,0},{1,5},{5,13},{13,9},{9,1},{2,6},{6,14},{... | collective-permute-start | bytes 417800 | tf_op jit(solution)/shard_map/ppermute | solution.py:46
  168.9 11.6 %collective-permute-start.35 = (bf16[128,512]{1,0:T(8,128)(2,1)S(1)}, bf16[128,512]{1,0:T(8,128)(2,1)S(1)}, u32[]{:S(2)}, u32[]{:S(2)}) collective-permute-start(bf16[128,512]{1,0:T(8,128)(2,1)S(1)} %collective-permute-done.33.refs_5_), channel_id=1, source_target_pairs={{0,4},{4,12},{12,8},{8,0},{1,5},{5,13},{13,9},{9,1},{2,6},{6,14},{... | collective-permute-start | bytes 393224 | tf_op jit(solution)/shard_map/ppermute | solution.py:46
  171.7 11.6 %collective-permute-start.34 = (bf16[128,512]{1,0:T(8,128)(2,1)S(1)}, bf16[128,512]{1,0:T(8,128)(2,1)S(1)}, u32[]{:S(2)}, u32[]{:S(2)}) collective-permute-start(bf16[128,512]{1,0:T(8,128)(2,1)S(1)} %collective-permute-done.32.refs_4_), channel_id=1, source_target_pairs={{0,4},{4,12},{12,8},{8,0},{1,5},{5,13},{13,9},{9,1},{2,6},{6,14},{... | collective-permute-start | bytes 393224 | tf_op jit(solution)/shard_map/ppermute | solution.py:46
  174.7 11.6 %collective-permute-start.61 = (bf16[544,128]{1,0:T(8,128)(2,1)S(1)}, bf16[544,128]{1,0:T(8,128)(2,1)S(1)}, u32[]{:S(2)}, u32[]{:S(2)}) collective-permute-start(bf16[544,128]{1,0:T(8,128)(2,1)S(1)} %collective-permute-done.59.refs_18_), channel_id=1, source_target_pairs={{0,4},{4,12},{12,8},{8,0},{1,5},{5,13},{13,9},{9,1},{2,6},{6,14},{... | collective-permute-start | bytes 417800 | tf_op jit(solution)/shard_map/ppermute | solution.py:46
  (67 other events, 542.8 us)

commit v13 on v12

--- a/solution.py
+++ b/solution.py
@@ -12,6 +12,8 @@
 ROW_TILE = 16
 LANES = 128
 STREAMS = 2
+WIDE_STREAMS = 2
+TALL_STREAMS = 2
 MIB = 1024 * 1024
 
 F32 = jnp.float32
@@ -421,29 +423,37 @@
         c.wait()
 
 
-def place_kernel(n, *refs):
+def place_of(i, count, n, pos, sub, size):
+    per_core = count // 2
+    streams = per_core // n
+    half = sub if i < per_core else 1 - sub
+    block = lax.rem(pos - i % per_core // streams + n, n) * streams + i % streams
+    return pl.ds(pl.multiple_of((half * per_core + block) * size, size), size)
+
+
+def place_kernel(n, wide_count, *refs):
     pieces = refs[:-7]
     out_ref, up_out_ref, down_in_ref, wide_ref, small, sems, small_sems = refs[-7:]
     pos, sub = ring_position(), lax.axis_index("sub")
-    count = len(pieces) // 2
-    per_core = count // 2
-    streams = per_core // n
-    size = out_ref.shape[0] // count
-    extra = pieces[count].shape[0] - size
+    wide, tall = pieces[:wide_count], pieces[wide_count:]
     copies = []
-    for i in range(count):
-        half = sub if i < per_core else 1 - sub
-        block = lax.rem(pos - i % per_core // streams + n, n) * streams + i % streams
-        at = pl.ds(pl.multiple_of((half * per_core + block) * size, size), size)
-        copies.append(pltpu.make_async_copy(pieces[i], wide_ref.at[:, at], sems.at[2 * i]))
-        piece = pieces[count + i]
-        copies.append(
-            pltpu.make_async_copy(piece.at[pl.ds(0, size), :], out_ref.at[at, :], sems.at[2 * i + 1])
-        )
-        at = pl.ds(pl.multiple_of(block * extra, extra), extra)
+    for i, piece in enumerate(wide):
+        at = place_of(i, len(wide), n, pos, sub, piece.shape[1])
+        copies.append(pltpu.make_async_copy(piece, wide_ref.at[:, at], sems.at[i]))
+    size = out_ref.shape[0] // len(tall)
+    extra = tall[0].shape[0] - size
+    for i, piece in enumerate(tall):
+        at = place_of(i, len(tall), n, pos, sub, size)
         copies.append(
             pltpu.make_async_copy(
-                piece.at[pl.ds(size, extra), :], small.at[i // per_core, at, :], small_sems.at[i]
+                piece.at[pl.ds(0, size), :], out_ref.at[at, :], sems.at[len(wide) + i]
+            )
+        )
+        half = i // (len(tall) // 2)
+        at = place_of(i % (len(tall) // 2), len(tall), n, pos, 0, extra)
+        copies.append(
+            pltpu.make_async_copy(
+                piece.at[pl.ds(size, extra), :], small.at[half, at, :], small_sems.at[i]
             )
         )
     copy_all(copies)
@@ -595,16 +605,20 @@
     normed_got = swap(normed_send, "sub")
     step(ring[2], ring[3], *crossed[:2])
     step(ring[3], ring[2], *crossed[:2])
-    cross(2, normed)
-    cross(3, normed)
+    cross(2)
+    cross(3)
     cross(4)
     cross(5)
-    down_turned = jnp.swapaxes(after(down_codes, *ring[2:4]), 0, 1)
-    down_moving, down_got = start_shards([down_turned], 1)
-    step(down_moving[0], *ring[4:6], *crossed[2:4], grad_got, normed_got)
-    cross(6)
-    step(ring[6])
-    cross(7)
+    down_turned = jnp.swapaxes(after(down_codes, ring[4]), 0, 1)
+    down_moving, down_got = start_shards([down_turned], STREAMS)
+    front_steps = 2 * (n - 1)
+    for moving in down_moving:
+        step(moving, *ring[4:6], *crossed[2:4], grad_got, normed_got)
+    for k in range(STREAMS):
+        cross(front_steps + k)
+    for k in range(STREAMS):
+        step(ring[front_steps + k])
+        cross(-1)
 
     def product(kernel, name, own, got, scale, codes, codes_got, first_got, steps, weight_shape, term, extra=()):
         groups = scale.shape[0]
@@ -617,20 +631,24 @@
             flops=4 * rows * half * units,
         )
         total = mine + swap(theirs, "sub").astype(F32)
-        return total, others(total.astype(BF16), "mp")
+        return total, others(total.astype(BF16), "mp"), mine
 
     front = (blocks // 2, block, units)
-    first_down = [ring[2 * (n - 1)]]
+    first_down = [*ring[front_steps : front_steps + STREAMS]]
     half_blocks = blocks // 2
-    gate, gate_more = product(
+    gate, gate_more, gate_mine = product(
         front_kernel, "gate", normed, normed_got, after(gate_block_scale.T, *first_down), gate_codes, front_got, 0,
         range(0, 2 * (n - 1), 2), front, NoTerm(),
     )
-    up, up_more = product(
+    up, up_more, up_mine = product(
         front_kernel, "up", normed, normed_got, after(up_block_scale.T, *first_down), up_codes, front_got, half_blocks,
         range(1, 2 * (n - 1), 2), front, UpTerm(low, adapters, adapters_more),
         [pltpu.VMEM((rank, units), BF16)],
     )
+    for k in range(STREAMS):
+        before = front_steps + STREAMS + k
+        step(ring[before], gate_mine, up_mine, crossed[before - STREAMS])
+        cross(-1)
     silu, hidden, low_hidden = call(
         lambda *refs: hidden_kernel(more, *refs),
         "hidden",
@@ -640,19 +658,14 @@
         limit=8,
     )
     low_hidden_got = swap(low_hidden, "sub")
-    pieces = STREAMS * n
     down_out_parts = call(
         lambda *refs: down_out_kernel(n, *refs),
         "down_out",
         [low_hidden, low_hidden_got, grad, grad_got],
-        [shape((rank, half // pieces))] * pieces,
+        [shape((rank, half // (WIDE_STREAMS * n)))] * (WIDE_STREAMS * n),
         flops=4 * rows * half * rank,
     )
-    for _ in range(n - 3):
-        step(ring[-1], down_out_parts[0])
-    down_out_blocks, seen = ring_all(down_out_parts, STREAMS)
-    for k in range(3 * (n - 1) - (n - 3), 3 * (n - 1)):
-        cross(k, *seen[0])
+    down_out_blocks, seen = ring_all(down_out_parts, WIDE_STREAMS)
     (normed_t,) = call(
         transpose_kernel,
         "transpose",
@@ -661,9 +674,9 @@
         limit=32,
     )
 
-    back, back_more = product(
-        back_kernel, "back", grad, grad_got, after(down_block_scale, normed_t, *seen[0]), down_turned, down_got, 0,
-        range(2 * (n - 1), 3 * (n - 1)), (units, half), DownTerm(low, adapters, adapters_more),
+    back, back_more, _ = product(
+        back_kernel, "back", grad, grad_got, after(down_block_scale, normed_t, down_out_parts[0]), down_turned, down_got, 0,
+        range(front_steps, (2 + STREAMS) * (n - 1)), (units, half), DownTerm(low, adapters, adapters_more),
         [pltpu.VMEM((units, rank), BF16)],
     )
     up_grad, low_grad = call(
@@ -682,19 +695,19 @@
         [shape(up_adapter_out.shape), shape(down_adapter_in.shape)],
         limit=8,
     )
-    extra = 2 * rank // pieces
+    extra = 2 * rank // (TALL_STREAMS * n)
     up_in_parts = call(
         lambda *refs: up_in_kernel(n, *refs),
         "up_in",
-        [after(low_grad, *seen[1]), swap(low_grad, "sub"), normed_t, up_out_term, down_in_term],
-        [shape((half // pieces + extra, rank))] * pieces,
+        [after(low_grad, *seen[2]), swap(low_grad, "sub"), normed_t, up_out_term, down_in_term],
+        [shape((half // (TALL_STREAMS * n) + extra, rank))] * (TALL_STREAMS * n),
         flops=4 * rows * half * rank,
     )
-    up_in_blocks, _ = ring_all(up_in_parts, STREAMS, down_out_blocks[-STREAMS:])
+    up_in_blocks, _ = ring_all(up_in_parts, TALL_STREAMS, ())
 
     anywhere = pl.BlockSpec(memory_space=pl.ANY)
     up_in_gradient, up_out_gradient, down_in_gradient, down_out_gradient = call(
-        lambda *refs: place_kernel(n, *refs),
+        lambda *refs: place_kernel(n, len(down_out_blocks), *refs),
         "place",
         [*down_out_blocks, *up_in_blocks],
         [
@@ -705,10 +718,10 @@
         ],
         scratch=[
             pltpu.VMEM((2, 2 * rank, rank), BF16),
-            pltpu.SemaphoreType.DMA((4 * pieces,)),
-            pltpu.SemaphoreType.DMA((2 * pieces,)),
+            pltpu.SemaphoreType.DMA((2 * n * (WIDE_STREAMS + TALL_STREAMS),)),
+            pltpu.SemaphoreType.DMA((2 * n * TALL_STREAMS,)),
         ],
-        specs=[anywhere] * (4 * pieces),
+        specs=[anywhere] * (2 * n * (WIDE_STREAMS + TALL_STREAMS)),
         out_specs=(anywhere, vmem, vmem, anywhere),
         limit=4,
     )

time: 204 us -> 183 us (0.90)
  waiting for transfers between devices: 115 us -> 88.1 us
  starting transfers between devices: 56.1 us -> 62 us
    ppermute x34 -> x37, waiting for transfers between devices: 23.7 us -> 10.1 us  [swap(): return lax.ppermute(x, axis, [(0, 1), (1, 0)])]
    ppermute x6, waiting for transfers between devices: 14.3 us -> 5.84 us  [others(): lax.ppermute(x, axis, [(i, (i + k) % n) for i in range(n)])]
    ppermute x33 -> x36, waiting for transfers between devices: 77 us -> 72.1 us  [ring_step(): lax.ppermute(x, 'dp', [(ring_at(i, n), ring_at((i + 1) % n, n)) for i in...]
    ppermute x34 -> x37, starting transfers between devices: 13.3 us -> 17.8 us  [swap(): return lax.ppermute(x, axis, [(0, 1), (1, 0)])]
    ppermute x33 -> x36, starting transfers between devices: 34.7 us -> 36.9 us  [ring_step(): lax.ppermute(x, 'dp', [(ring_at(i, n), ring_at((i + 1) % n, n)) for i in...]
  transfers between devices with their start and end apart: 73 -> 79, of which waited for: 44 -> 39; matrix products, arithmetic and copies ran while one was open for 0% -> 0% of each run, Pallas kernels for 8% -> 11%
where the time goes in v13:
time: 183 us
  waiting for transfers between devices  88.1 us (48%)
  starting transfers between devices  62 us (34%)
  Pallas kernels  26.5 us (14%)
  local copies, waits for them, and re-layouts  4.71 us (3%)
    ppermute x36, waiting for transfers between devices, ring_step(): lax.ppermute(x, 'dp', [(ring_at(i, n), ring_at((i + 1) % n, n)) for i in...  72.1 us
    ppermute x36, starting transfers between devices, ring_step(): lax.ppermute(x, 'dp', [(ring_at(i, n), ring_at((i + 1) % n, n)) for i in...  36.9 us
    pallas_call x29, Pallas kernels, call(): pl.pallas_call(kernel, out_shape=tuple(out_shape), in_specs=specs or [vme...  26.5 us
    ppermute x37, starting transfers between devices, swap(): return lax.ppermute(x, axis, [(0, 1), (1, 0)])  17.8 us
    ppermute x37, waiting for transfers between devices, swap(): return lax.ppermute(x, axis, [(0, 1), (1, 0)])  10.1 us
    ppermute x6, starting transfers between devices, others(): lax.ppermute(x, axis, [(i, (i + k) % n) for i in range(n)])  7.29 us
    ppermute x6, waiting for transfers between devices, others(): lax.ppermute(x, axis, [(i, (i + k) % n) for i in range(n)])  5.84 us
    unnamed x37, local copies, waits for them, and re-layouts  4.34 us
  transfers between devices with their start and end apart: 79, of which 39 were waited for; matrix products, arithmetic and copies ran while one was open for 0% of the time, Pallas kernels for 11%

profile of v13, /device:TPU:0, one launch (start us, length us, event | category | flops | bytes accessed | tf_op | source)
XLA Modules:
  0.0 182.7 jit_solution(8902910868074384786)
XLA Ops:
  5.5 3.0 %collective-permute-start.2 = (bf16[32,16,256]{2,1,0:T(8,128)(2,1)S(1)}, bf16[32,16,256]{2,1,0:T(8,128)(2,1)S(1)}, u32[]{:S(2)}, u32[]{:S(2)}) collective-permute-start(bf16[32,16,256]{2,1,0:T(8,128)(2,1)S(1)} %get-tuple-element.65), channel_id=1, source_target_pairs={{0,4},{4,12},{12,8},{8,0},{1,5},{5,13},{13,9},{9,1},{2,6},{6,14},{... | collective-permute-start | bytes 786440 | tf_op jit(solution)/shard_map/ppermute | solution.py:48
  8.5 2.6 %collective-permute-start.1 = (bf16[32,16,256]{2,1,0:T(8,128)(2,1)S(1)}, bf16[32,16,256]{2,1,0:T(8,128)(2,1)S(1)}, u32[]{:S(2)}, u32[]{:S(2)}) collective-permute-start(bf16[32,16,256]{2,1,0:T(8,128)(2,1)S(1)} %get-tuple-element.64), channel_id=1, source_target_pairs={{0,4},{4,12},{12,8},{8,0},{1,5},{5,13},{13,9},{9,1},{2,6},{6,14},{... | collective-permute-start | bytes 786440 | tf_op jit(solution)/shard_map/ppermute | solution.py:48
  15.8 4.2 %cotangent.1 = (bf16[256,4096]{1,0:T(8,128)(2,1)S(1)}, bf16[256,4096]{1,0:T(8,128)(2,1)S(1)}, f32[256,128]{1,0:T(8,128)S(1)}) custom-call(bf16[256,8192]{1,0:T(8,128)(2,1)S(1)} %copy-done.6, s32[1,2]{1,0:T(1,128)S(1)} %copy-done.9, s32[1,256]{1,0:T(1,128)S(1)} %bitcast.9, bf16[128,8192]{1,0:T(8,128)(2,1)S(1)} %copy-done.8), custom_call_target="tpu_custom_call" | custom-call | tf_op jit(solution)/shard_map/cotangent/pallas_call | solution.py:69
  22.6 3.4 %collective-permute-start.4 = (bf16[32,16,256]{2,1,0:T(8,128)(2,1)S(1)}, bf16[32,16,256]{2,1,0:T(8,128)(2,1)S(1)}, u32[]{:S(2)}, u32[]{:S(2)}) collective-permute-start(bf16[32,16,256]{2,1,0:T(8,128)(2,1)S(1)} %collective-permute-done.2.refs_8_), channel_id=1, source_target_pairs={{0,4},{4,12},{12,8},{8,0},{1,5},{5,13},{13,9},{9,1},{2,6},{6,14},{... | collective-permute-start | bytes 786440 | tf_op jit(solution)/shard_map/ppermute | solution.py:48
  29.6 2.9 %collective-permute-done.7.refs_7_.refs_5_.refs_4_ = bf16[256,128]{1,0:T(8,128)(2,1)S(1)} collective-permute-done((bf16[256,128]{1,0:T(8,128)(2,1)S(1)}, bf16[256,128]{1,0:T(8,128)(2,1)S(1)}, u32[]{:S(2)}, u32[]{:S(2)}) %collective-permute-start.7) | collective-permute-done | bytes 65568 | tf_op jit(solution)/shard_map/ppermute | solution.py:57
  36.1 2.4 %collective-permute-done.6.refs_9_ = bf16[32,16,256]{2,1,0:T(8,128)(2,1)S(1)} collective-permute-done((bf16[32,16,256]{2,1,0:T(8,128)(2,1)S(1)}, bf16[32,16,256]{2,1,0:T(8,128)(2,1)S(1)}, u32[]{:S(2)}, u32[]{:S(2)}) %collective-permute-start.6) | collective-permute-done | bytes 262176 | tf_op jit(solution)/shard_map/ppermute | solution.py:52
  38.6 3.0 %tokens.3 = (bf16[256,4096]{1,0:T(8,128)(2,1)S(1)}, bf16[256,4096]{1,0:T(8,128)(2,1)S(1)}, f32[256,256]{1,0:T(8,128)S(1)}) custom-call(bf16[256,8192]{1,0:T(8,128)(2,1)S(1)} %copy-done.1, bf16[1,8192]{1,0:T(2,128)(2,1)S(1)} %broadcast_in_dim.6.refs_1_, bf16[8192,128]{1,0:T(8,128)(2,1)S(1)} %copy-done.7, f32[256,128]{1,0:T(8,128)S(1)} %get-tuple-element.68.refs_3_, ...), custom_call_target="tpu_custom_call" | custom-call | tf_op jit(solution)/shard_map/tokens/pallas_call | solution.py:69
  44.8 7.0 %collective-permute-done.10.refs_9_ = bf16[32,16,256]{2,1,0:T(8,128)(2,1)S(1)} collective-permute-done((bf16[32,16,256]{2,1,0:T(8,128)(2,1)S(1)}, bf16[32,16,256]{2,1,0:T(8,128)(2,1)S(1)}, u32[]{:S(2)}, u32[]{:S(2)}) %collective-permute-start.10) | collective-permute-done | bytes 262176 | tf_op jit(solution)/shard_map/ppermute | solution.py:48
  53.9 3.1 %collective-permute-done.12.refs_12_ = bf16[32,16,256]{2,1,0:T(8,128)(2,1)S(1)} collective-permute-done((bf16[32,16,256]{2,1,0:T(8,128)(2,1)S(1)}, bf16[32,16,256]{2,1,0:T(8,128)(2,1)S(1)}, u32[]{:S(2)}, u32[]{:S(2)}) %collective-permute-start.12) | collective-permute-done | bytes 262176 | tf_op jit(solution)/shard_map/ppermute | solution.py:48
  62.9 5.4 %collective-permute-done.16.refs_8_ = bf16[16,32,128]{2,1,0:T(8,128)(2,1)S(1)} collective-permute-done((bf16[16,32,128]{2,1,0:T(8,128)(2,1)S(1)}, bf16[16,32,128]{2,1,0:T(8,128)(2,1)S(1)}, u32[]{:S(2)}, u32[]{:S(2)}) %collective-permute-start.16) | collective-permute-done | bytes 131104 | tf_op jit(solution)/shard_map/ppermute | solution.py:48
  108.3 2.9 %collective-permute-done.56.refs_3_ = bf16[256,256]{1,0:T(8,128)(2,1)S(1)} collective-permute-done((bf16[256,256]{1,0:T(8,128)(2,1)S(1)}, bf16[256,256]{1,0:T(8,128)(2,1)S(1)}, u32[]{:S(2)}, u32[]{:S(2)}) %collective-permute-start.56) | collective-permute-done | bytes 131104 | tf_op jit(solution)/shard_map/ppermute | solution.py:57
  114.4 3.4 %up_in.1 = (bf16[544,128]{1,0:T(8,128)(2,1)S(1)}, bf16[544,128]{1,0:T(8,128)(2,1)S(1)}, bf16[544,128]{1,0:T(8,128)(2,1)S(1)}, bf16[544,128]{1,0:T(8,128)(2,1)S(1...) custom-call(bf16[256,128]{1,0:T(8,128)(2,1)S(1)} %get-tuple-element., ...), custom_call_target="tpu_custom_call" | custom-call | tf_op jit(solution)/shard_map/up_in/pallas_call | solution.py:69
  120.3 4.7 %collective-permute-done.59.left = bf16[544,128]{1,0:T(8,128)(2,1)S(1)} collective-permute-done((bf16[544,128]{1,0:T(8,128)(2,1)S(1)}, bf16[544,128]{1,0:T(8,128)(2,1)S(1)}, u32[]{:S(2)}, u32[]{:S(2)}) %collective-permute-start.59) | collective-permute-done | bytes 139296 | tf_op jit(solution)/shard_map/ppermute | solution.py:48
  131.4 3.4 %collective-permute-done.63.left = bf16[544,128]{1,0:T(8,128)(2,1)S(1)} collective-permute-done((bf16[544,128]{1,0:T(8,128)(2,1)S(1)}, bf16[544,128]{1,0:T(8,128)(2,1)S(1)}, u32[]{:S(2)}, u32[]{:S(2)}) %collective-permute-start.63) | collective-permute-done | bytes 139296 | tf_op jit(solution)/shard_map/ppermute | solution.py:48
  135.0 2.6 %collective-permute-start.31 = (bf16[128,512]{1,0:T(8,128)(2,1)S(1)}, bf16[128,512]{1,0:T(8,128)(2,1)S(1)}, u32[]{:S(2)}, u32[]{:S(2)}) collective-permute-start(bf16[128,512]{1,0:T(8,128)(2,1)S(1)} %add.32.refs_0_), channel_id=1, source_target_pairs={{0,4},{4,12},{12,8},{8,0},{1,5},{5,13},{13,9},{9,1},{2,6},{6,14},{... | collective-permute-start | bytes 393224 | tf_op jit(solution)/shard_map/ppermute | solution.py:48
  138.1 7.0 %collective-permute-done.31.refs_2_ = bf16[128,512]{1,0:T(8,128)(2,1)S(1)} collective-permute-done((bf16[128,512]{1,0:T(8,128)(2,1)S(1)}, bf16[128,512]{1,0:T(8,128)(2,1)S(1)}, u32[]{:S(2)}, u32[]{:S(2)}) %collective-permute-start.31) | collective-permute-done | bytes 131104 | tf_op jit(solution)/shard_map/ppermute | solution.py:48
  147.7 2.6 %collective-permute-start.66 = (bf16[544,128]{1,0:T(8,128)(2,1)S(1)}, bf16[544,128]{1,0:T(8,128)(2,1)S(1)}, u32[]{:S(2)}, u32[]{:S(2)}) collective-permute-start(bf16[544,128]{1,0:T(8,128)(2,1)S(1)} %add.41.refs_17_), channel_id=1, source_target_pairs={{0,4},{4,12},{12,8},{8,0},{1,5},{5,13},{13,9},{9,1},{2,6},{6,14},{... | collective-permute-start | bytes 417800 | tf_op jit(solution)/shard_map/ppermute | solution.py:48
  152.4 2.8 %collective-permute-done.33.refs_4_ = bf16[128,512]{1,0:T(8,128)(2,1)S(1)} collective-permute-done((bf16[128,512]{1,0:T(8,128)(2,1)S(1)}, bf16[128,512]{1,0:T(8,128)(2,1)S(1)}, u32[]{:S(2)}, u32[]{:S(2)}) %collective-permute-start.33) | collective-permute-done | bytes 131104 | tf_op jit(solution)/shard_map/ppermute | solution.py:48
  155.2 3.0 %collective-permute-done.65.refs_18_ = bf16[544,128]{1,0:T(8,128)(2,1)S(1)} collective-permute-done((bf16[544,128]{1,0:T(8,128)(2,1)S(1)}, bf16[544,128]{1,0:T(8,128)(2,1)S(1)}, u32[]{:S(2)}, u32[]{:S(2)}) %collective-permute-start.65) | collective-permute-done | bytes 139296 | tf_op jit(solution)/shard_map/ppermute | solution.py:48
  158.2 3.0 %collective-permute-done.66.refs_19_ = bf16[544,128]{1,0:T(8,128)(2,1)S(1)} collective-permute-done((bf16[544,128]{1,0:T(8,128)(2,1)S(1)}, bf16[544,128]{1,0:T(8,128)(2,1)S(1)}, u32[]{:S(2)}, u32[]{:S(2)}) %collective-permute-start.66) | collective-permute-done | bytes 139296 | tf_op jit(solution)/shard_map/ppermute | solution.py:48
  161.2 2.8 %collective-permute-done.36.refs_7_ = bf16[128,512]{1,0:T(8,128)(2,1)S(1)} collective-permute-done((bf16[128,512]{1,0:T(8,128)(2,1)S(1)}, bf16[128,512]{1,0:T(8,128)(2,1)S(1)}, u32[]{:S(2)}, u32[]{:S(2)}) %collective-permute-start.36) | collective-permute-done | bytes 131104 | tf_op jit(solution)/shard_map/ppermute | solution.py:48
  164.0 2.8 %collective-permute-done.35.refs_6_ = bf16[128,512]{1,0:T(8,128)(2,1)S(1)} collective-permute-done((bf16[128,512]{1,0:T(8,128)(2,1)S(1)}, bf16[128,512]{1,0:T(8,128)(2,1)S(1)}, u32[]{:S(2)}, u32[]{:S(2)}) %collective-permute-start.35) | collective-permute-done | bytes 131104 | tf_op jit(solution)/shard_map/ppermute | solution.py:48
  172.6 4.0 %collective-permute-done.69.refs_22_ = bf16[544,128]{1,0:T(8,128)(2,1)S(1)} collective-permute-done((bf16[544,128]{1,0:T(8,128)(2,1)S(1)}, bf16[544,128]{1,0:T(8,128)(2,1)S(1)}, u32[]{:S(2)}, u32[]{:S(2)}) %collective-permute-start.69) | collective-permute-done | bytes 139296 | tf_op jit(solution)/shard_map/ppermute | solution.py:48
  179.5 3.0 %place.1 = (bf16[8192,128]{1,0:T(8,128)(2,1)}, bf16[128,128]{1,0:T(8,128)(2,1)}, bf16[128,128]{1,0:T(8,128)(2,1)}, bf16[128,8192]{1,0:T(8,128)(2,1)}) custom-call(bf16[128,512]{1,0:T(8,128)(2,1)S(1)} %add.32.refs_0_, bf16[128,512]{1,0:T(8,128)(2,1)S(1)} %add.35.refs_1_, bf16[128,512]{1,0:T(8,128)(2,1)S(1)} %collective-permute-done.31.refs_2_, ...), custom_call_target="tpu_custom_call" | custom-call | tf_op jit(solution)/shard_map/place/pallas_call | solution.py:69
  (206 shorter events, 96.4 us)
Async XLA Ops:
  5.5 14.4 %collective-permute-start.2 = (bf16[32,16,256]{2,1,0:T(8,128)(2,1)S(1)}, bf16[32,16,256]{2,1,0:T(8,128)(2,1)S(1)}, u32[]{:S(2)}, u32[]{:S(2)}) collective-permute-start(bf16[32,16,256]{2,1,0:T(8,128)(2,1)S(1)} %get-tuple-element.65), channel_id=1, source_target_pairs={{0,4},{4,12},{12,8},{8,0},{1,5},{5,13},{13,9},{9,1},{2,6},{6,14},{... | collective-permute-start | bytes 786440 | tf_op jit(solution)/shard_map/ppermute | solution.py:48
  8.5 13.2 %collective-permute-start.1 = (bf16[32,16,256]{2,1,0:T(8,128)(2,1)S(1)}, bf16[32,16,256]{2,1,0:T(8,128)(2,1)S(1)}, u32[]{:S(2)}, u32[]{:S(2)}) collective-permute-start(bf16[32,16,256]{2,1,0:T(8,128)(2,1)S(1)} %get-tuple-element.64), channel_id=1, source_target_pairs={{0,4},{4,12},{12,8},{8,0},{1,5},{5,13},{13,9},{9,1},{2,6},{6,14},{... | collective-permute-start | bytes 786440 | tf_op jit(solution)/shard_map/ppermute | solution.py:48
  21.8 12.2 %collective-permute-start.3 = (bf16[32,16,256]{2,1,0:T(8,128)(2,1)S(1)}, bf16[32,16,256]{2,1,0:T(8,128)(2,1)S(1)}, u32[]{:S(2)}, u32[]{:S(2)}) collective-permute-start(bf16[32,16,256]{2,1,0:T(8,128)(2,1)S(1)} %collective-permute-done.1.refs_5_), channel_id=1, source_target_pairs={{0,4},{4,12},{12,8},{8,0},{1,5},{5,13},{13,9},{9,1},{2,6},{6,14},{... | collective-permute-start | bytes 786440 | tf_op jit(solution)/shard_map/ppermute | solution.py:48
  22.6 13.5 %collective-permute-start.4 = (bf16[32,16,256]{2,1,0:T(8,128)(2,1)S(1)}, bf16[32,16,256]{2,1,0:T(8,128)(2,1)S(1)}, u32[]{:S(2)}, u32[]{:S(2)}) collective-permute-start(bf16[32,16,256]{2,1,0:T(8,128)(2,1)S(1)} %collective-permute-done.2.refs_8_), channel_id=1, source_target_pairs={{0,4},{4,12},{12,8},{8,0},{1,5},{5,13},{13,9},{9,1},{2,6},{6,14},{... | collective-permute-start | bytes 786440 | tf_op jit(solution)/shard_map/ppermute | solution.py:48
  26.0 10.1 %collective-permute-start.5 = (bf16[32,16,256]{2,1,0:T(8,128)(2,1)S(1)}, bf16[32,16,256]{2,1,0:T(8,128)(2,1)S(1)}, u32[]{:S(2)}, u32[]{:S(2)}) collective-permute-start(bf16[32,16,256]{2,1,0:T(8,128)(2,1)S(1)} %collective-permute-done.1.refs_5_), channel_id=1, source_target_pairs={{0,16},{16,0},{1,17},{17,1},{2,18},{18,2},{3,19},{19,3},{4,20},{20... | collective-permute-start | bytes 786440 | tf_op jit(solution)/shard_map/ppermute | solution.py:52
  27.5 11.1 %collective-permute-start.6 = (bf16[32,16,256]{2,1,0:T(8,128)(2,1)S(1)}, bf16[32,16,256]{2,1,0:T(8,128)(2,1)S(1)}, u32[]{:S(2)}, u32[]{:S(2)}) collective-permute-start(bf16[32,16,256]{2,1,0:T(8,128)(2,1)S(1)} %collective-permute-done.2.refs_8_), channel_id=1, source_target_pairs={{0,16},{16,0},{1,17},{17,1},{2,18},{18,2},{3,19},{19,3},{4,20},{20... | collective-permute-start | bytes 786440 | tf_op jit(solution)/shard_map/ppermute | solution.py:52
  34.0 27.4 %collective-permute-start.15 = (bf16[256,4096]{1,0:T(8,128)(2,1)S(1)}, bf16[256,4096]{1,0:T(8,128)(2,1)S(1)}, u32[]{:S(2)}, u32[]{:S(2)}) collective-permute-start(bf16[256,4096]{1,0:T(8,128)(2,1)S(1)} %get-tuple-element.82), channel_id=1, source_target_pairs={{0,1},{1,0},{2,3},{3,2},{4,5},{5,4},{6,7},{7,6},{8,9},{9,8},{10,11... | collective-permute-start | bytes 6291464 | tf_op jit(solution)/shard_map/ppermute | solution.py:52
  41.6 19.8 %collective-permute-start.9 = (bf16[256,4096]{1,0:T(8,128)(2,1)S(1)}, bf16[256,4096]{1,0:T(8,128)(2,1)S(1)}, u32[]{:S(2)}, u32[]{:S(2)}) collective-permute-start(bf16[256,4096]{1,0:T(8,128)(2,1)S(1)} %get-tuple-element.77), channel_id=1, source_target_pairs={{0,1},{1,0},{2,3},{3,2},{4,5},{5,4},{6,7},{7,6},{8,9},{9,8},{10,11... | collective-permute-start | bytes 6291464 | tf_op jit(solution)/shard_map/ppermute | solution.py:52
  41.7 10.1 %collective-permute-start.10 = (bf16[32,16,256]{2,1,0:T(8,128)(2,1)S(1)}, bf16[32,16,256]{2,1,0:T(8,128)(2,1)S(1)}, u32[]{:S(2)}, u32[]{:S(2)}) collective-permute-start(bf16[32,16,256]{2,1,0:T(8,128)(2,1)S(1)} %collective-permute-done.3.refs_7_), channel_id=1, source_target_pairs={{0,4},{4,12},{12,8},{8,0},{1,5},{5,13},{13,9},{9,1},{2,6},{6,14},{... | collective-permute-start | bytes 786440 | tf_op jit(solution)/shard_map/ppermute | solution.py:48
  42.1 10.2 %collective-permute-start.13 = (bf16[32,16,256]{2,1,0:T(8,128)(2,1)S(1)}, bf16[32,16,256]{2,1,0:T(8,128)(2,1)S(1)}, u32[]{:S(2)}, u32[]{:S(2)}) collective-permute-start(bf16[32,16,256]{2,1,0:T(8,128)(2,1)S(1)} %collective-permute-done.3.refs_7_), channel_id=1, source_target_pairs={{0,16},{16,0},{1,17},{17,1},{2,18},{18,2},{3,19},{19,3},{4,20},{20... | collective-permute-start | bytes 786440 | tf_op jit(solution)/shard_map/ppermute | solution.py:52
  43.6 13.3 %collective-permute-start.12 = (bf16[32,16,256]{2,1,0:T(8,128)(2,1)S(1)}, bf16[32,16,256]{2,1,0:T(8,128)(2,1)S(1)}, u32[]{:S(2)}, u32[]{:S(2)}) collective-permute-start(bf16[32,16,256]{2,1,0:T(8,128)(2,1)S(1)} %collective-permute-done.4.refs_10_), channel_id=1, source_target_pairs={{0,4},{4,12},{12,8},{8,0},{1,5},{5,13},{13,9},{9,1},{2,6},{6,14},{... | collective-permute-start | bytes 786440 | tf_op jit(solution)/shard_map/ppermute | solution.py:48
  56.9 14.4 %collective-permute-start.20 = (bf16[32,16,256]{2,1,0:T(8,128)(2,1)S(1)}, bf16[32,16,256]{2,1,0:T(8,128)(2,1)S(1)}, u32[]{:S(2)}, u32[]{:S(2)}) collective-permute-start(bf16[32,16,256]{2,1,0:T(8,128)(2,1)S(1)} %collective-permute-done.12.refs_12_), channel_id=1, source_target_pairs={{0,16},{16,0},{1,17},{17,1},{2,18},{18,2},{3,19},{19,3},{4,20},{20... | collective-permute-start | bytes 786440 | tf_op jit(solution)/shard_map/ppermute | solution.py:52
  58.5 15.7 %collective-permute-start.18 = (bf16[32,16,256]{2,1,0:T(8,128)(2,1)S(1)}, bf16[32,16,256]{2,1,0:T(8,128)(2,1)S(1)}, u32[]{:S(2)}, u32[]{:S(2)}) collective-permute-start(bf16[32,16,256]{2,1,0:T(8,128)(2,1)S(1)} %collective-permute-done.10.refs_9_), channel_id=1, source_target_pairs={{0,16},{16,0},{1,17},{17,1},{2,18},{18,2},{3,19},{19,3},{4,20},{20... | collective-permute-start | bytes 786440 | tf_op jit(solution)/shard_map/ppermute | solution.py:52
  100.9 13.0 %collective-permute-start.58 = (f32[256,256]{1,0:T(8,128)S(1)}, f32[256,256]{1,0:T(8,128)S(1)}, u32[]{:S(2)}, u32[]{:S(2)}) collective-permute-start(f32[256,256]{1,0:T(8,128)S(1)} %get-tuple-element.113.refs_5_.refs_2_), channel_id=1, source_target_pairs={{0,2},{2,0},{1,3},{3,1},{4,6},{6,4},{5,7},{7,5},{8,10},{10,8},{9,1... | collective-permute-start | bytes 786440 | tf_op jit(solution)/shard_map/ppermute | solution.py:57
  131.4 13.7 %collective-permute-start.61 = (bf16[544,128]{1,0:T(8,128)(2,1)S(1)}, bf16[544,128]{1,0:T(8,128)(2,1)S(1)}, u32[]{:S(2)}, u32[]{:S(2)}) collective-permute-start(bf16[544,128]{1,0:T(8,128)(2,1)S(1)} %add.37), channel_id=1, source_target_pairs={{0,4},{4,12},{12,8},{8,0},{1,5},{5,13},{13,9},{9,1},{2,6},{6,14},{... | collective-permute-start | bytes 417800 | tf_op jit(solution)/shard_map/ppermute | solution.py:48
  134.9 10.3 %collective-permute-start.64 = (bf16[544,128]{1,0:T(8,128)(2,1)S(1)}, bf16[544,128]{1,0:T(8,128)(2,1)S(1)}, u32[]{:S(2)}, u32[]{:S(2)}) collective-permute-start(bf16[544,128]{1,0:T(8,128)(2,1)S(1)} %add.40), channel_id=1, source_target_pairs={{0,4},{4,12},{12,8},{8,0},{1,5},{5,13},{13,9},{9,1},{2,6},{6,14},{... | collective-permute-start | bytes 417800 | tf_op jit(solution)/shard_map/ppermute | solution.py:48
  135.0 10.1 %collective-permute-start.31 = (bf16[128,512]{1,0:T(8,128)(2,1)S(1)}, bf16[128,512]{1,0:T(8,128)(2,1)S(1)}, u32[]{:S(2)}, u32[]{:S(2)}) collective-permute-start(bf16[128,512]{1,0:T(8,128)(2,1)S(1)} %add.32.refs_0_), channel_id=1, source_target_pairs={{0,4},{4,12},{12,8},{8,0},{1,5},{5,13},{13,9},{9,1},{2,6},{6,14},{... | collective-permute-start | bytes 393224 | tf_op jit(solution)/shard_map/ppermute | solution.py:48
  137.6 10.1 %collective-permute-start.40 = (bf16[128,512]{1,0:T(8,128)(2,1)S(1)}, bf16[128,512]{1,0:T(8,128)(2,1)S(1)}, u32[]{:S(2)}, u32[]{:S(2)}) collective-permute-start(bf16[128,512]{1,0:T(8,128)(2,1)S(1)} %collective-permute-done.32.refs_3_), channel_id=1, source_target_pairs={{0,1},{1,0},{2,3},{3,2},{4,5},{5,4},{6,7},{7,6},{8,9},{9,8},{10,11... | collective-permute-start | bytes 393224 | tf_op jit(solution)/shard_map/ppermute | solution.py:52
  145.2 10.1 %collective-permute-start.33 = (bf16[128,512]{1,0:T(8,128)(2,1)S(1)}, bf16[128,512]{1,0:T(8,128)(2,1)S(1)}, u32[]{:S(2)}, u32[]{:S(2)}) collective-permute-start(bf16[128,512]{1,0:T(8,128)(2,1)S(1)} %collective-permute-done.31.refs_2_), channel_id=1, source_target_pairs={{0,4},{4,12},{12,8},{8,0},{1,5},{5,13},{13,9},{9,1},{2,6},{6,14},{... | collective-permute-start | bytes 393224 | tf_op jit(solution)/shard_map/ppermute | solution.py:48
  147.6 10.6 %collective-permute-start.65 = (bf16[544,128]{1,0:T(8,128)(2,1)S(1)}, bf16[544,128]{1,0:T(8,128)(2,1)S(1)}, u32[]{:S(2)}, u32[]{:S(2)}) collective-permute-start(bf16[544,128]{1,0:T(8,128)(2,1)S(1)} %add.38.refs_16_), channel_id=1, source_target_pairs={{0,4},{4,12},{12,8},{8,0},{1,5},{5,13},{13,9},{9,1},{2,6},{6,14},{... | collective-permute-start | bytes 417800 | tf_op jit(solution)/shard_map/ppermute | solution.py:48
  147.7 13.5 %collective-permute-start.66 = (bf16[544,128]{1,0:T(8,128)(2,1)S(1)}, bf16[544,128]{1,0:T(8,128)(2,1)S(1)}, u32[]{:S(2)}, u32[]{:S(2)}) collective-permute-start(bf16[544,128]{1,0:T(8,128)(2,1)S(1)} %add.41.refs_17_), channel_id=1, source_target_pairs={{0,4},{4,12},{12,8},{8,0},{1,5},{5,13},{13,9},{9,1},{2,6},{6,14},{... | collective-permute-start | bytes 417800 | tf_op jit(solution)/shard_map/ppermute | solution.py:48
  152.4 11.6 %collective-permute-start.36 = (bf16[128,512]{1,0:T(8,128)(2,1)S(1)}, bf16[128,512]{1,0:T(8,128)(2,1)S(1)}, u32[]{:S(2)}, u32[]{:S(2)}) collective-permute-start(bf16[128,512]{1,0:T(8,128)(2,1)S(1)} %collective-permute-done.34.refs_5_), channel_id=1, source_target_pairs={{0,4},{4,12},{12,8},{8,0},{1,5},{5,13},{13,9},{9,1},{2,6},{6,14},{... | collective-permute-start | bytes 393224 | tf_op jit(solution)/shard_map/ppermute | solution.py:48
  155.2 11.6 %collective-permute-start.35 = (bf16[128,512]{1,0:T(8,128)(2,1)S(1)}, bf16[128,512]{1,0:T(8,128)(2,1)S(1)}, u32[]{:S(2)}, u32[]{:S(2)}) collective-permute-start(bf16[128,512]{1,0:T(8,128)(2,1)S(1)} %collective-permute-done.33.refs_4_), channel_id=1, source_target_pairs={{0,4},{4,12},{12,8},{8,0},{1,5},{5,13},{13,9},{9,1},{2,6},{6,14},{... | collective-permute-start | bytes 393224 | tf_op jit(solution)/shard_map/ppermute | solution.py:48
  158.2 11.5 %collective-permute-start.67 = (bf16[544,128]{1,0:T(8,128)(2,1)S(1)}, bf16[544,128]{1,0:T(8,128)(2,1)S(1)}, u32[]{:S(2)}, u32[]{:S(2)}) collective-permute-start(bf16[544,128]{1,0:T(8,128)(2,1)S(1)} %collective-permute-done.65.refs_18_), channel_id=1, source_target_pairs={{0,4},{4,12},{12,8},{8,0},{1,5},{5,13},{13,9},{9,1},{2,6},{6,14},{... | collective-permute-start | bytes 417800 | tf_op jit(solution)/shard_map/ppermute | solution.py:48
  (73 other events, 563.6 us)

commit v14 on v13

--- a/solution.py
+++ b/solution.py
@@ -582,7 +582,7 @@
     )
     cross(0, grad)
     cross(1, grad)
-    step(ring[0], ring[1], grad)
+    step(ring[0], grad)
     step(ring[1], ring[0], grad)
     adapters = jnp.concatenate([up_adapter_out, down_adapter_in], axis=0)
     adapters_more = others(after(adapters, *ring[:2]), "mp")
@@ -703,7 +703,7 @@
         [shape((half // (TALL_STREAMS * n) + extra, rank))] * (TALL_STREAMS * n),
         flops=4 * rows * half * rank,
     )
-    up_in_blocks, _ = ring_all(up_in_parts, TALL_STREAMS, ())
+    up_in_blocks, _ = ring_all(up_in_parts, TALL_STREAMS, down_out_blocks[-WIDE_STREAMS:])
 
     anywhere = pl.BlockSpec(memory_space=pl.ANY)
     up_in_gradient, up_out_gradient, down_in_gradient, down_out_gradient = call(
@@ -826,7 +826,9 @@
 
 def body(tokens, cotangent, rms_norm_gain, gate_codes, *rest):
     whole_tiles = gate_codes.shape[1] % ROW_TILE == 0
-    form = fast_body if whole_tiles else general_body
+    ring_of_four = lax.axis_size("dp") == 4
+    pairs = lax.axis_size("grp") == 2 and lax.axis_size("sub") == 2
+    form = fast_body if whole_tiles and ring_of_four and pairs else general_body
     return form(tokens, cotangent, rms_norm_gain, gate_codes, *rest)
 
 

time: 183 us -> 180 us (0.984)
  starting transfers between devices: 62 us -> 50.7 us
  waiting for transfers between devices: 88.1 us -> 96.4 us
    ppermute x36, waiting for transfers between devices: 72.1 us -> 81.2 us  [ring_step(): lax.ppermute(x, 'dp', [(ring_at(i, n), ring_at((i + 1) % n, n)) for i in...]
    ppermute x36, starting transfers between devices: 36.9 us -> 28.1 us  [ring_step(): lax.ppermute(x, 'dp', [(ring_at(i, n), ring_at((i + 1) % n, n)) for i in...]
    ppermute x37, starting transfers between devices: 17.8 us -> 15.3 us  [swap(): return lax.ppermute(x, axis, [(0, 1), (1, 0)])]
  transfers between devices with their start and end apart: 79 -> 79, of which waited for: 39 -> 42; matrix products, arithmetic and copies ran while one was open for 0% -> 0% of each run, Pallas kernels for 11% -> 11%
where the time goes in v14:
time: 180 us
  waiting for transfers between devices  96.4 us (54%)
  starting transfers between devices  50.7 us (28%)
  Pallas kernels  26.5 us (15%)
  local copies, waits for them, and re-layouts  4.71 us (3%)
    ppermute x36, waiting for transfers between devices, ring_step(): lax.ppermute(x, 'dp', [(ring_at(i, n), ring_at((i + 1) % n, n)) for i in...  81.2 us
    ppermute x36, starting transfers between devices, ring_step(): lax.ppermute(x, 'dp', [(ring_at(i, n), ring_at((i + 1) % n, n)) for i in...  28.1 us
    pallas_call x29, Pallas kernels, call(): pl.pallas_call(kernel, out_shape=tuple(out_shape), in_specs=specs or [vme...  26.5 us
    ppermute x37, starting transfers between devices, swap(): return lax.ppermute(x, axis, [(0, 1), (1, 0)])  15.3 us
    ppermute x37, waiting for transfers between devices, swap(): return lax.ppermute(x, axis, [(0, 1), (1, 0)])  8.56 us
    ppermute x6, starting transfers between devices, others(): lax.ppermute(x, axis, [(i, (i + k) % n) for i in range(n)])  7.34 us
    ppermute x6, waiting for transfers between devices, others(): lax.ppermute(x, axis, [(i, (i + k) % n) for i in range(n)])  6.64 us
    unnamed x37, local copies, waits for them, and re-layouts  4.34 us
  transfers between devices with their start and end apart: 79, of which 42 were waited for; matrix products, arithmetic and copies ran while one was open for 0% of the time, Pallas kernels for 11%

profile of v14, /device:TPU:0, one launch (start us, length us, event | category | flops | bytes accessed | tf_op | source)
XLA Modules:
  0.0 179.8 jit_solution(1061565858661254797)
XLA Ops:
  5.5 3.0 %collective-permute-start.1 = (bf16[32,16,256]{2,1,0:T(8,128)(2,1)S(1)}, bf16[32,16,256]{2,1,0:T(8,128)(2,1)S(1)}, u32[]{:S(2)}, u32[]{:S(2)}) collective-permute-start(bf16[32,16,256]{2,1,0:T(8,128)(2,1)S(1)} %get-tuple-element.65), channel_id=1, source_target_pairs={{0,4},{4,12},{12,8},{8,0},{1,5},{5,13},{13,9},{9,1},{2,6},{6,14},{... | collective-permute-start | bytes 786440 | tf_op jit(solution)/shard_map/ppermute | solution.py:48
  15.8 4.2 %cotangent.1 = (bf16[256,4096]{1,0:T(8,128)(2,1)S(1)}, bf16[256,4096]{1,0:T(8,128)(2,1)S(1)}, f32[256,128]{1,0:T(8,128)S(1)}) custom-call(bf16[256,8192]{1,0:T(8,128)(2,1)S(1)} %copy-done.6, s32[1,2]{1,0:T(1,128)S(1)} %copy-done.9, s32[1,256]{1,0:T(1,128)S(1)} %bitcast.9, bf16[128,8192]{1,0:T(8,128)(2,1)S(1)} %copy-done.8), custom_call_target="tpu_custom_call" | custom-call | tf_op jit(solution)/shard_map/cotangent/pallas_call | solution.py:69
  26.5 3.2 %collective-permute-done.7.refs_7_.refs_5_.refs_4_ = bf16[256,128]{1,0:T(8,128)(2,1)S(1)} collective-permute-done((bf16[256,128]{1,0:T(8,128)(2,1)S(1)}, bf16[256,128]{1,0:T(8,128)(2,1)S(1)}, u32[]{:S(2)}, u32[]{:S(2)}) %collective-permute-start.7) | collective-permute-done | bytes 65568 | tf_op jit(solution)/shard_map/ppermute | solution.py:57
  31.7 3.9 %collective-permute-done.4.refs_10_ = bf16[32,16,256]{2,1,0:T(8,128)(2,1)S(1)} collective-permute-done((bf16[32,16,256]{2,1,0:T(8,128)(2,1)S(1)}, bf16[32,16,256]{2,1,0:T(8,128)(2,1)S(1)}, u32[]{:S(2)}, u32[]{:S(2)}) %collective-permute-start.4) | collective-permute-done | bytes 262176 | tf_op jit(solution)/shard_map/ppermute | solution.py:48
  35.6 3.0 %tokens.3 = (bf16[256,4096]{1,0:T(8,128)(2,1)S(1)}, bf16[256,4096]{1,0:T(8,128)(2,1)S(1)}, f32[256,256]{1,0:T(8,128)S(1)}) custom-call(bf16[256,8192]{1,0:T(8,128)(2,1)S(1)} %copy-done.1, bf16[1,8192]{1,0:T(2,128)(2,1)S(1)} %broadcast_in_dim.6.refs_1_, bf16[8192,128]{1,0:T(8,128)(2,1)S(1)} %copy-done.7, f32[256,128]{1,0:T(8,128)S(1)} %get-tuple-element.69.refs_3_, ...), custom_call_target="tpu_custom_call" | custom-call | tf_op jit(solution)/shard_map/tokens/pallas_call | solution.py:69
  42.0 6.8 %collective-permute-done.10.refs_9_ = bf16[32,16,256]{2,1,0:T(8,128)(2,1)S(1)} collective-permute-done((bf16[32,16,256]{2,1,0:T(8,128)(2,1)S(1)}, bf16[32,16,256]{2,1,0:T(8,128)(2,1)S(1)}, u32[]{:S(2)}, u32[]{:S(2)}) %collective-permute-start.10) | collective-permute-done | bytes 262176 | tf_op jit(solution)/shard_map/ppermute | solution.py:48
  50.1 3.9 %collective-permute-done.12.refs_12_ = bf16[32,16,256]{2,1,0:T(8,128)(2,1)S(1)} collective-permute-done((bf16[32,16,256]{2,1,0:T(8,128)(2,1)S(1)}, bf16[32,16,256]{2,1,0:T(8,128)(2,1)S(1)}, u32[]{:S(2)}, u32[]{:S(2)}) %collective-permute-start.12) | collective-permute-done | bytes 262176 | tf_op jit(solution)/shard_map/ppermute | solution.py:48
  61.0 4.2 %collective-permute-done.16.refs_8_ = bf16[16,32,128]{2,1,0:T(8,128)(2,1)S(1)} collective-permute-done((bf16[16,32,128]{2,1,0:T(8,128)(2,1)S(1)}, bf16[16,32,128]{2,1,0:T(8,128)(2,1)S(1)}, u32[]{:S(2)}, u32[]{:S(2)}) %collective-permute-start.16) | collective-permute-done | bytes 131104 | tf_op jit(solution)/shard_map/ppermute | solution.py:48
  105.1 3.5 %collective-permute-done.56.refs_3_ = bf16[256,256]{1,0:T(8,128)(2,1)S(1)} collective-permute-done((bf16[256,256]{1,0:T(8,128)(2,1)S(1)}, bf16[256,256]{1,0:T(8,128)(2,1)S(1)}, u32[]{:S(2)}, u32[]{:S(2)}) %collective-permute-start.56) | collective-permute-done | bytes 131104 | tf_op jit(solution)/shard_map/ppermute | solution.py:57
  111.7 3.4 %up_in.1 = (bf16[544,128]{1,0:T(8,128)(2,1)S(1)}, bf16[544,128]{1,0:T(8,128)(2,1)S(1)}, bf16[544,128]{1,0:T(8,128)(2,1)S(1)}, bf16[544,128]{1,0:T(8,128)(2,1)S(1...) custom-call(bf16[256,128]{1,0:T(8,128)(2,1)S(1)} %get-tuple-element., ...), custom_call_target="tpu_custom_call" | custom-call | tf_op jit(solution)/shard_map/up_in/pallas_call | solution.py:69
  117.6 4.6 %collective-permute-done.59.left = bf16[544,128]{1,0:T(8,128)(2,1)S(1)} collective-permute-done((bf16[544,128]{1,0:T(8,128)(2,1)S(1)}, bf16[544,128]{1,0:T(8,128)(2,1)S(1)}, u32[]{:S(2)}, u32[]{:S(2)}) %collective-permute-start.59) | collective-permute-done | bytes 139296 | tf_op jit(solution)/shard_map/ppermute | solution.py:48
  130.0 2.7 %collective-permute-done.63.left = bf16[544,128]{1,0:T(8,128)(2,1)S(1)} collective-permute-done((bf16[544,128]{1,0:T(8,128)(2,1)S(1)}, bf16[544,128]{1,0:T(8,128)(2,1)S(1)}, u32[]{:S(2)}, u32[]{:S(2)}) %collective-permute-start.63) | collective-permute-done | bytes 139296 | tf_op jit(solution)/shard_map/ppermute | solution.py:48
  132.8 2.7 %collective-permute-done.32.refs_3_ = bf16[128,512]{1,0:T(8,128)(2,1)S(1)} collective-permute-done((bf16[128,512]{1,0:T(8,128)(2,1)S(1)}, bf16[128,512]{1,0:T(8,128)(2,1)S(1)}, u32[]{:S(2)}, u32[]{:S(2)}) %collective-permute-start.32) | collective-permute-done | bytes 131104 | tf_op jit(solution)/shard_map/ppermute | solution.py:48
  135.5 2.8 %collective-permute-done.31.refs_2_ = bf16[128,512]{1,0:T(8,128)(2,1)S(1)} collective-permute-done((bf16[128,512]{1,0:T(8,128)(2,1)S(1)}, bf16[128,512]{1,0:T(8,128)(2,1)S(1)}, u32[]{:S(2)}, u32[]{:S(2)}) %collective-permute-start.31) | collective-permute-done | bytes 131104 | tf_op jit(solution)/shard_map/ppermute | solution.py:48
  138.4 3.0 %collective-permute-done.61.left = bf16[544,128]{1,0:T(8,128)(2,1)S(1)} collective-permute-done((bf16[544,128]{1,0:T(8,128)(2,1)S(1)}, bf16[544,128]{1,0:T(8,128)(2,1)S(1)}, u32[]{:S(2)}, u32[]{:S(2)}) %collective-permute-start.61) | collective-permute-done | bytes 139296 | tf_op jit(solution)/shard_map/ppermute | solution.py:48
  141.4 2.9 %collective-permute-done.64.left = bf16[544,128]{1,0:T(8,128)(2,1)S(1)} collective-permute-done((bf16[544,128]{1,0:T(8,128)(2,1)S(1)}, bf16[544,128]{1,0:T(8,128)(2,1)S(1)}, u32[]{:S(2)}, u32[]{:S(2)}) %collective-permute-start.64) | collective-permute-done | bytes 139296 | tf_op jit(solution)/shard_map/ppermute | solution.py:48
  144.4 2.7 %collective-permute-done.34.refs_5_ = bf16[128,512]{1,0:T(8,128)(2,1)S(1)} collective-permute-done((bf16[128,512]{1,0:T(8,128)(2,1)S(1)}, bf16[128,512]{1,0:T(8,128)(2,1)S(1)}, u32[]{:S(2)}, u32[]{:S(2)}) %collective-permute-start.34) | collective-permute-done | bytes 131104 | tf_op jit(solution)/shard_map/ppermute | solution.py:48
  147.1 2.8 %collective-permute-done.33.refs_4_ = bf16[128,512]{1,0:T(8,128)(2,1)S(1)} collective-permute-done((bf16[128,512]{1,0:T(8,128)(2,1)S(1)}, bf16[128,512]{1,0:T(8,128)(2,1)S(1)}, u32[]{:S(2)}, u32[]{:S(2)}) %collective-permute-start.33) | collective-permute-done | bytes 131104 | tf_op jit(solution)/shard_map/ppermute | solution.py:48
  149.9 3.0 %collective-permute-done.65.refs_18_ = bf16[544,128]{1,0:T(8,128)(2,1)S(1)} collective-permute-done((bf16[544,128]{1,0:T(8,128)(2,1)S(1)}, bf16[544,128]{1,0:T(8,128)(2,1)S(1)}, u32[]{:S(2)}, u32[]{:S(2)}) %collective-permute-start.65) | collective-permute-done | bytes 139296 | tf_op jit(solution)/shard_map/ppermute | solution.py:48
  152.9 3.0 %collective-permute-done.66.refs_19_ = bf16[544,128]{1,0:T(8,128)(2,1)S(1)} collective-permute-done((bf16[544,128]{1,0:T(8,128)(2,1)S(1)}, bf16[544,128]{1,0:T(8,128)(2,1)S(1)}, u32[]{:S(2)}, u32[]{:S(2)}) %collective-permute-start.66) | collective-permute-done | bytes 139296 | tf_op jit(solution)/shard_map/ppermute | solution.py:48
  155.9 2.8 %collective-permute-done.36.refs_7_ = bf16[128,512]{1,0:T(8,128)(2,1)S(1)} collective-permute-done((bf16[128,512]{1,0:T(8,128)(2,1)S(1)}, bf16[128,512]{1,0:T(8,128)(2,1)S(1)}, u32[]{:S(2)}, u32[]{:S(2)}) %collective-permute-start.36) | collective-permute-done | bytes 131104 | tf_op jit(solution)/shard_map/ppermute | solution.py:48
  158.7 2.8 %collective-permute-done.35.refs_6_ = bf16[128,512]{1,0:T(8,128)(2,1)S(1)} collective-permute-done((bf16[128,512]{1,0:T(8,128)(2,1)S(1)}, bf16[128,512]{1,0:T(8,128)(2,1)S(1)}, u32[]{:S(2)}, u32[]{:S(2)}) %collective-permute-start.35) | collective-permute-done | bytes 131104 | tf_op jit(solution)/shard_map/ppermute | solution.py:48
  168.5 4.6 %collective-permute-done.69.refs_22_ = bf16[544,128]{1,0:T(8,128)(2,1)S(1)} collective-permute-done((bf16[544,128]{1,0:T(8,128)(2,1)S(1)}, bf16[544,128]{1,0:T(8,128)(2,1)S(1)}, u32[]{:S(2)}, u32[]{:S(2)}) %collective-permute-start.69) | collective-permute-done | bytes 139296 | tf_op jit(solution)/shard_map/ppermute | solution.py:48
  176.6 3.0 %place.1 = (bf16[8192,128]{1,0:T(8,128)(2,1)}, bf16[128,128]{1,0:T(8,128)(2,1)}, bf16[128,128]{1,0:T(8,128)(2,1)}, bf16[128,8192]{1,0:T(8,128)(2,1)}) custom-call(bf16[128,512]{1,0:T(8,128)(2,1)S(1)} %add.32.refs_0_, bf16[128,512]{1,0:T(8,128)(2,1)S(1)} %add.35.refs_1_, bf16[128,512]{1,0:T(8,128)(2,1)S(1)} %collective-permute-done.31.refs_2_, ...), custom_call_target="tpu_custom_call" | custom-call | tf_op jit(solution)/shard_map/place/pallas_call | solution.py:69
  (206 shorter events, 96.1 us)
Async XLA Ops:
  5.5 14.4 %collective-permute-start.1 = (bf16[32,16,256]{2,1,0:T(8,128)(2,1)S(1)}, bf16[32,16,256]{2,1,0:T(8,128)(2,1)S(1)}, u32[]{:S(2)}, u32[]{:S(2)}) collective-permute-start(bf16[32,16,256]{2,1,0:T(8,128)(2,1)S(1)} %get-tuple-element.65), channel_id=1, source_target_pairs={{0,4},{4,12},{12,8},{8,0},{1,5},{5,13},{13,9},{9,1},{2,6},{6,14},{... | collective-permute-start | bytes 786440 | tf_op jit(solution)/shard_map/ppermute | solution.py:48
  8.5 13.5 %collective-permute-start.3 = (bf16[32,16,256]{2,1,0:T(8,128)(2,1)S(1)}, bf16[32,16,256]{2,1,0:T(8,128)(2,1)S(1)}, u32[]{:S(2)}, u32[]{:S(2)}) collective-permute-start(bf16[32,16,256]{2,1,0:T(8,128)(2,1)S(1)} %get-tuple-element.66), channel_id=1, source_target_pairs={{0,4},{4,12},{12,8},{8,0},{1,5},{5,13},{13,9},{9,1},{2,6},{6,14},{... | collective-permute-start | bytes 786440 | tf_op jit(solution)/shard_map/ppermute | solution.py:48
  20.0 11.2 %collective-permute-start.5 = (bf16[32,16,256]{2,1,0:T(8,128)(2,1)S(1)}, bf16[32,16,256]{2,1,0:T(8,128)(2,1)S(1)}, u32[]{:S(2)}, u32[]{:S(2)}) collective-permute-start(bf16[32,16,256]{2,1,0:T(8,128)(2,1)S(1)} %collective-permute-done.1.refs_5_), channel_id=1, source_target_pairs={{0,16},{16,0},{1,17},{17,1},{2,18},{18,2},{3,19},{19,3},{4,20},{20... | collective-permute-start | bytes 786440 | tf_op jit(solution)/shard_map/ppermute | solution.py:52
  21.5 10.1 %collective-permute-start.2 = (bf16[32,16,256]{2,1,0:T(8,128)(2,1)S(1)}, bf16[32,16,256]{2,1,0:T(8,128)(2,1)S(1)}, u32[]{:S(2)}, u32[]{:S(2)}) collective-permute-start(bf16[32,16,256]{2,1,0:T(8,128)(2,1)S(1)} %collective-permute-done.1.refs_5_), channel_id=1, source_target_pairs={{0,4},{4,12},{12,8},{8,0},{1,5},{5,13},{13,9},{9,1},{2,6},{6,14},{... | collective-permute-start | bytes 786440 | tf_op jit(solution)/shard_map/ppermute | solution.py:48
  22.0 13.6 %collective-permute-start.4 = (bf16[32,16,256]{2,1,0:T(8,128)(2,1)S(1)}, bf16[32,16,256]{2,1,0:T(8,128)(2,1)S(1)}, u32[]{:S(2)}, u32[]{:S(2)}) collective-permute-start(bf16[32,16,256]{2,1,0:T(8,128)(2,1)S(1)} %collective-permute-done.3.refs_8_), channel_id=1, source_target_pairs={{0,4},{4,12},{12,8},{8,0},{1,5},{5,13},{13,9},{9,1},{2,6},{6,14},{... | collective-permute-start | bytes 786440 | tf_op jit(solution)/shard_map/ppermute | solution.py:48
  23.4 12.2 %collective-permute-start.6 = (bf16[32,16,256]{2,1,0:T(8,128)(2,1)S(1)}, bf16[32,16,256]{2,1,0:T(8,128)(2,1)S(1)}, u32[]{:S(2)}, u32[]{:S(2)}) collective-permute-start(bf16[32,16,256]{2,1,0:T(8,128)(2,1)S(1)} %collective-permute-done.3.refs_8_), channel_id=1, source_target_pairs={{0,16},{16,0},{1,17},{17,1},{2,18},{18,2},{3,19},{19,3},{4,20},{20... | collective-permute-start | bytes 786440 | tf_op jit(solution)/shard_map/ppermute | solution.py:52
  31.2 27.6 %collective-permute-start.15 = (bf16[256,4096]{1,0:T(8,128)(2,1)S(1)}, bf16[256,4096]{1,0:T(8,128)(2,1)S(1)}, u32[]{:S(2)}, u32[]{:S(2)}) collective-permute-start(bf16[256,4096]{1,0:T(8,128)(2,1)S(1)} %get-tuple-element.82), channel_id=1, source_target_pairs={{0,1},{1,0},{2,3},{3,2},{4,5},{5,4},{6,7},{7,6},{8,9},{9,8},{10,11... | collective-permute-start | bytes 6291464 | tf_op jit(solution)/shard_map/ppermute | solution.py:52
  38.7 20.1 %collective-permute-start.9 = (bf16[256,4096]{1,0:T(8,128)(2,1)S(1)}, bf16[256,4096]{1,0:T(8,128)(2,1)S(1)}, u32[]{:S(2)}, u32[]{:S(2)}) collective-permute-start(bf16[256,4096]{1,0:T(8,128)(2,1)S(1)} %get-tuple-element.77), channel_id=1, source_target_pairs={{0,1},{1,0},{2,3},{3,2},{4,5},{5,4},{6,7},{7,6},{8,9},{9,8},{10,11... | collective-permute-start | bytes 6291464 | tf_op jit(solution)/shard_map/ppermute | solution.py:52
  38.7 10.1 %collective-permute-start.10 = (bf16[32,16,256]{2,1,0:T(8,128)(2,1)S(1)}, bf16[32,16,256]{2,1,0:T(8,128)(2,1)S(1)}, u32[]{:S(2)}, u32[]{:S(2)}) collective-permute-start(bf16[32,16,256]{2,1,0:T(8,128)(2,1)S(1)} %collective-permute-done.2.refs_7_), channel_id=1, source_target_pairs={{0,4},{4,12},{12,8},{8,0},{1,5},{5,13},{13,9},{9,1},{2,6},{6,14},{... | collective-permute-start | bytes 786440 | tf_op jit(solution)/shard_map/ppermute | solution.py:48
  41.7 12.2 %collective-permute-start.12 = (bf16[32,16,256]{2,1,0:T(8,128)(2,1)S(1)}, bf16[32,16,256]{2,1,0:T(8,128)(2,1)S(1)}, u32[]{:S(2)}, u32[]{:S(2)}) collective-permute-start(bf16[32,16,256]{2,1,0:T(8,128)(2,1)S(1)} %collective-permute-done.4.refs_10_), channel_id=1, source_target_pairs={{0,4},{4,12},{12,8},{8,0},{1,5},{5,13},{13,9},{9,1},{2,6},{6,14},{... | collective-permute-start | bytes 786440 | tf_op jit(solution)/shard_map/ppermute | solution.py:48
  54.0 14.9 %collective-permute-start.20 = (bf16[32,16,256]{2,1,0:T(8,128)(2,1)S(1)}, bf16[32,16,256]{2,1,0:T(8,128)(2,1)S(1)}, u32[]{:S(2)}, u32[]{:S(2)}) collective-permute-start(bf16[32,16,256]{2,1,0:T(8,128)(2,1)S(1)} %collective-permute-done.12.refs_12_), channel_id=1, source_target_pairs={{0,16},{16,0},{1,17},{17,1},{2,18},{18,2},{3,19},{19,3},{4,20},{20... | collective-permute-start | bytes 786440 | tf_op jit(solution)/shard_map/ppermute | solution.py:52
  54.5 17.5 %collective-permute-start.18 = (bf16[32,16,256]{2,1,0:T(8,128)(2,1)S(1)}, bf16[32,16,256]{2,1,0:T(8,128)(2,1)S(1)}, u32[]{:S(2)}, u32[]{:S(2)}) collective-permute-start(bf16[32,16,256]{2,1,0:T(8,128)(2,1)S(1)} %collective-permute-done.10.refs_9_), channel_id=1, source_target_pairs={{0,16},{16,0},{1,17},{17,1},{2,18},{18,2},{3,19},{19,3},{4,20},{20... | collective-permute-start | bytes 786440 | tf_op jit(solution)/shard_map/ppermute | solution.py:52
  97.8 13.4 %collective-permute-start.58 = (f32[256,256]{1,0:T(8,128)S(1)}, f32[256,256]{1,0:T(8,128)S(1)}, u32[]{:S(2)}, u32[]{:S(2)}) collective-permute-start(f32[256,256]{1,0:T(8,128)S(1)} %get-tuple-element.113.refs_5_.refs_2_), channel_id=1, source_target_pairs={{0,2},{2,0},{1,3},{3,1},{4,6},{6,4},{5,7},{7,5},{8,10},{10,8},{9,1... | collective-permute-start | bytes 786440 | tf_op jit(solution)/shard_map/ppermute | solution.py:57
  125.0 10.5 %collective-permute-start.32 = (bf16[128,512]{1,0:T(8,128)(2,1)S(1)}, bf16[128,512]{1,0:T(8,128)(2,1)S(1)}, u32[]{:S(2)}, u32[]{:S(2)}) collective-permute-start(bf16[128,512]{1,0:T(8,128)(2,1)S(1)} %add.35.refs_1_), channel_id=1, source_target_pairs={{0,4},{4,12},{12,8},{8,0},{1,5},{5,13},{13,9},{9,1},{2,6},{6,14},{... | collective-permute-start | bytes 393224 | tf_op jit(solution)/shard_map/ppermute | solution.py:48
  127.3 11.1 %collective-permute-start.31 = (bf16[128,512]{1,0:T(8,128)(2,1)S(1)}, bf16[128,512]{1,0:T(8,128)(2,1)S(1)}, u32[]{:S(2)}, u32[]{:S(2)}) collective-permute-start(bf16[128,512]{1,0:T(8,128)(2,1)S(1)} %add.32.refs_0_), channel_id=1, source_target_pairs={{0,4},{4,12},{12,8},{8,0},{1,5},{5,13},{13,9},{9,1},{2,6},{6,14},{... | collective-permute-start | bytes 393224 | tf_op jit(solution)/shard_map/ppermute | solution.py:48
  129.8 11.5 %collective-permute-start.61 = (bf16[544,128]{1,0:T(8,128)(2,1)S(1)}, bf16[544,128]{1,0:T(8,128)(2,1)S(1)}, u32[]{:S(2)}, u32[]{:S(2)}) collective-permute-start(bf16[544,128]{1,0:T(8,128)(2,1)S(1)} %add.37), channel_id=1, source_target_pairs={{0,4},{4,12},{12,8},{8,0},{1,5},{5,13},{13,9},{9,1},{2,6},{6,14},{... | collective-permute-start | bytes 417800 | tf_op jit(solution)/shard_map/ppermute | solution.py:48
  132.8 11.5 %collective-permute-start.64 = (bf16[544,128]{1,0:T(8,128)(2,1)S(1)}, bf16[544,128]{1,0:T(8,128)(2,1)S(1)}, u32[]{:S(2)}, u32[]{:S(2)}) collective-permute-start(bf16[544,128]{1,0:T(8,128)(2,1)S(1)} %add.40), channel_id=1, source_target_pairs={{0,4},{4,12},{12,8},{8,0},{1,5},{5,13},{13,9},{9,1},{2,6},{6,14},{... | collective-permute-start | bytes 417800 | tf_op jit(solution)/shard_map/ppermute | solution.py:48
  135.5 11.6 %collective-permute-start.34 = (bf16[128,512]{1,0:T(8,128)(2,1)S(1)}, bf16[128,512]{1,0:T(8,128)(2,1)S(1)}, u32[]{:S(2)}, u32[]{:S(2)}) collective-permute-start(bf16[128,512]{1,0:T(8,128)(2,1)S(1)} %collective-permute-done.32.refs_3_), channel_id=1, source_target_pairs={{0,4},{4,12},{12,8},{8,0},{1,5},{5,13},{13,9},{9,1},{2,6},{6,14},{... | collective-permute-start | bytes 393224 | tf_op jit(solution)/shard_map/ppermute | solution.py:48
  138.3 11.6 %collective-permute-start.33 = (bf16[128,512]{1,0:T(8,128)(2,1)S(1)}, bf16[128,512]{1,0:T(8,128)(2,1)S(1)}, u32[]{:S(2)}, u32[]{:S(2)}) collective-permute-start(bf16[128,512]{1,0:T(8,128)(2,1)S(1)} %collective-permute-done.31.refs_2_), channel_id=1, source_target_pairs={{0,4},{4,12},{12,8},{8,0},{1,5},{5,13},{13,9},{9,1},{2,6},{6,14},{... | collective-permute-start | bytes 393224 | tf_op jit(solution)/shard_map/ppermute | solution.py:48
  141.4 11.5 %collective-permute-start.65 = (bf16[544,128]{1,0:T(8,128)(2,1)S(1)}, bf16[544,128]{1,0:T(8,128)(2,1)S(1)}, u32[]{:S(2)}, u32[]{:S(2)}) collective-permute-start(bf16[544,128]{1,0:T(8,128)(2,1)S(1)} %add.38.refs_16_), channel_id=1, source_target_pairs={{0,4},{4,12},{12,8},{8,0},{1,5},{5,13},{13,9},{9,1},{2,6},{6,14},{... | collective-permute-start | bytes 417800 | tf_op jit(solution)/shard_map/ppermute | solution.py:48
  144.4 11.5 %collective-permute-start.66 = (bf16[544,128]{1,0:T(8,128)(2,1)S(1)}, bf16[544,128]{1,0:T(8,128)(2,1)S(1)}, u32[]{:S(2)}, u32[]{:S(2)}) collective-permute-start(bf16[544,128]{1,0:T(8,128)(2,1)S(1)} %add.41.refs_17_), channel_id=1, source_target_pairs={{0,4},{4,12},{12,8},{8,0},{1,5},{5,13},{13,9},{9,1},{2,6},{6,14},{... | collective-permute-start | bytes 417800 | tf_op jit(solution)/shard_map/ppermute | solution.py:48
  147.1 11.6 %collective-permute-start.36 = (bf16[128,512]{1,0:T(8,128)(2,1)S(1)}, bf16[128,512]{1,0:T(8,128)(2,1)S(1)}, u32[]{:S(2)}, u32[]{:S(2)}) collective-permute-start(bf16[128,512]{1,0:T(8,128)(2,1)S(1)} %collective-permute-done.34.refs_5_), channel_id=1, source_target_pairs={{0,4},{4,12},{12,8},{8,0},{1,5},{5,13},{13,9},{9,1},{2,6},{6,14},{... | collective-permute-start | bytes 393224 | tf_op jit(solution)/shard_map/ppermute | solution.py:48
  149.9 11.6 %collective-permute-start.35 = (bf16[128,512]{1,0:T(8,128)(2,1)S(1)}, bf16[128,512]{1,0:T(8,128)(2,1)S(1)}, u32[]{:S(2)}, u32[]{:S(2)}) collective-permute-start(bf16[128,512]{1,0:T(8,128)(2,1)S(1)} %collective-permute-done.33.refs_4_), channel_id=1, source_target_pairs={{0,4},{4,12},{12,8},{8,0},{1,5},{5,13},{13,9},{9,1},{2,6},{6,14},{... | collective-permute-start | bytes 393224 | tf_op jit(solution)/shard_map/ppermute | solution.py:48
  152.9 10.3 %collective-permute-start.67 = (bf16[544,128]{1,0:T(8,128)(2,1)S(1)}, bf16[544,128]{1,0:T(8,128)(2,1)S(1)}, u32[]{:S(2)}, u32[]{:S(2)}) collective-permute-start(bf16[544,128]{1,0:T(8,128)(2,1)S(1)} %collective-permute-done.65.refs_18_), channel_id=1, source_target_pairs={{0,4},{4,12},{12,8},{8,0},{1,5},{5,13},{13,9},{9,1},{2,6},{6,14},{... | collective-permute-start | bytes 417800 | tf_op jit(solution)/shard_map/ppermute | solution.py:48
  (73 other events, 521.1 us)

commit v15 on v14

--- a/solution.py
+++ b/solution.py
@@ -205,10 +205,10 @@
     )
 
 
-def transpose_kernel(own, got, out_ref):
-    rows, step = own.shape[0], out_ref.shape[0]
-    for i, ref in enumerate((own, got)):
-        out_ref[:, i * rows : (i + 1) * rows] = ref[...].astype(F32).T.astype(BF16)
+def both_kernel(own, got, out_ref):
+    rows = own.shape[0]
+    out_ref[:rows, :] = own[...]
+    out_ref[rows:, :] = got[...]
 
 
 def widen(scale, wide):
@@ -394,16 +394,16 @@
         ).astype(BF16)
 
 
-def up_in_kernel(n, low, low_got, normed_t, up_out_term, down_in_term, *out_refs):
+def up_in_kernel(n, low, low_got, normed_both, up_out_term, down_in_term, *out_refs):
     pos = ring_position()
     streams = len(out_refs) // n
-    size = normed_t.shape[0] // len(out_refs)
+    size = normed_both.shape[1] // len(out_refs)
     extra = out_refs[0].shape[0] - size
-    both = jnp.concatenate([low[...], low_got[...]], axis=0)
+    low_t = jnp.concatenate([low[...], low_got[...]], axis=0).astype(F32).T.astype(BF16)
     for k, ref in enumerate(out_refs):
         block = lax.rem(pos - 1 - k // streams + 2 * n, n) * streams + k % streams
         at = pl.ds(pl.multiple_of(block * size, size), size)
-        ref[pl.ds(0, size), :] = dot(normed_t[at, :], both).astype(BF16)
+        ref[pl.ds(0, size), :] = dot(low_t, normed_both[:, at]).T.astype(BF16)
         per = up_out_term.shape[0] // extra
         index = pl.ds(pl.multiple_of(lax.rem(block, per) * extra, extra), extra)
 
@@ -666,16 +666,16 @@
         flops=4 * rows * half * rank,
     )
     down_out_blocks, seen = ring_all(down_out_parts, WIDE_STREAMS)
-    (normed_t,) = call(
-        transpose_kernel,
-        "transpose",
+    (normed_both,) = call(
+        both_kernel,
+        "both",
         [normed, after(normed_got, low_hidden)],
-        [shape((half, 2 * rows))],
+        [shape((2 * rows, half))],
         limit=32,
     )
 
     back, back_more, _ = product(
-        back_kernel, "back", grad, grad_got, after(down_block_scale, normed_t, down_out_parts[0]), down_turned, down_got, 0,
+        back_kernel, "back", grad, grad_got, after(down_block_scale, normed_both, down_out_parts[0]), down_turned, down_got, 0,
         range(front_steps, (2 + STREAMS) * (n - 1)), (units, half), DownTerm(low, adapters, adapters_more),
         [pltpu.VMEM((units, rank), BF16)],
     )
@@ -699,7 +699,7 @@
     up_in_parts = call(
         lambda *refs: up_in_kernel(n, *refs),
         "up_in",
-        [after(low_grad, *seen[2]), swap(low_grad, "sub"), normed_t, up_out_term, down_in_term],
+        [after(low_grad, *seen[2]), swap(low_grad, "sub"), normed_both, up_out_term, down_in_term],
         [shape((half // (TALL_STREAMS * n) + extra, rank))] * (TALL_STREAMS * n),
         flops=4 * rows * half * rank,
     )

time: 180 us -> 179 us (level)
  Pallas kernels: 26.5 us -> 24.7 us
  transfers between devices with their start and end apart: 79 -> 79, of which waited for: 42 -> 41; matrix products, arithmetic and copies ran while one was open for 0% -> 0% of each run, Pallas kernels for 11% -> 10%
where the time goes in v15:
time: 179 us; the launch traced here: 178 us
  waiting for transfers between devices  95.7 us (53%)
  starting transfers between devices  51.7 us (29%)
  Pallas kernels  24.7 us (14%)
  local copies, waits for them, and re-layouts  4.71 us (3%)
    ppermute x36, waiting for transfers between devices, ring_step(): lax.ppermute(x, 'dp', [(ring_at(i, n), ring_at((i + 1) % n, n)) for i in...  79.9 us
    ppermute x36, starting transfers between devices, ring_step(): lax.ppermute(x, 'dp', [(ring_at(i, n), ring_at((i + 1) % n, n)) for i in...  28.9 us
    pallas_call x29, Pallas kernels, call(): pl.pallas_call(kernel, out_shape=tuple(out_shape), in_specs=specs or [vme...  24.7 us
    ppermute x37, starting transfers between devices, swap(): return lax.ppermute(x, axis, [(0, 1), (1, 0)])  15.5 us
    ppermute x37, waiting for transfers between devices, swap(): return lax.ppermute(x, axis, [(0, 1), (1, 0)])  9.47 us
    ppermute x6, starting transfers between devices, others(): lax.ppermute(x, axis, [(i, (i + k) % n) for i in range(n)])  7.29 us
    ppermute x6, waiting for transfers between devices, others(): lax.ppermute(x, axis, [(i, (i + k) % n) for i in range(n)])  6.32 us
    unnamed x37, local copies, waits for them, and re-layouts  4.34 us
  transfers between devices with their start and end apart: 79, of which 41 were waited for; matrix products, arithmetic and copies ran while one was open for 0% of the time, Pallas kernels for 10%

profile of v15, /device:TPU:0, one launch (start us, length us, event | category | flops | bytes accessed | tf_op | source)
XLA Modules:
  0.0 178.3 jit_solution(10566560818921013209)
XLA Ops:
  5.5 3.0 %collective-permute-start.1 = (bf16[32,16,256]{2,1,0:T(8,128)(2,1)S(1)}, bf16[32,16,256]{2,1,0:T(8,128)(2,1)S(1)}, u32[]{:S(2)}, u32[]{:S(2)}) collective-permute-start(bf16[32,16,256]{2,1,0:T(8,128)(2,1)S(1)} %get-tuple-element.65), channel_id=1, source_target_pairs={{0,4},{4,12},{12,8},{8,0},{1,5},{5,13},{13,9},{9,1},{2,6},{6,14},{... | collective-permute-start | bytes 786440 | tf_op jit(solution)/shard_map/ppermute | solution.py:48
  15.8 4.2 %cotangent.1 = (bf16[256,4096]{1,0:T(8,128)(2,1)S(1)}, bf16[256,4096]{1,0:T(8,128)(2,1)S(1)}, f32[256,128]{1,0:T(8,128)S(1)}) custom-call(bf16[256,8192]{1,0:T(8,128)(2,1)S(1)} %copy-done.6, s32[1,2]{1,0:T(1,128)S(1)} %copy-done.9, s32[1,256]{1,0:T(1,128)S(1)} %bitcast.9, bf16[128,8192]{1,0:T(8,128)(2,1)S(1)} %copy-done.8), custom_call_target="tpu_custom_call" | custom-call | tf_op jit(solution)/shard_map/cotangent/pallas_call | solution.py:69
  26.5 3.2 %collective-permute-done.7.refs_7_.refs_5_.refs_4_ = bf16[256,128]{1,0:T(8,128)(2,1)S(1)} collective-permute-done((bf16[256,128]{1,0:T(8,128)(2,1)S(1)}, bf16[256,128]{1,0:T(8,128)(2,1)S(1)}, u32[]{:S(2)}, u32[]{:S(2)}) %collective-permute-start.7) | collective-permute-done | bytes 65568 | tf_op jit(solution)/shard_map/ppermute | solution.py:57
  31.7 3.9 %collective-permute-done.4.refs_10_ = bf16[32,16,256]{2,1,0:T(8,128)(2,1)S(1)} collective-permute-done((bf16[32,16,256]{2,1,0:T(8,128)(2,1)S(1)}, bf16[32,16,256]{2,1,0:T(8,128)(2,1)S(1)}, u32[]{:S(2)}, u32[]{:S(2)}) %collective-permute-start.4) | collective-permute-done | bytes 262176 | tf_op jit(solution)/shard_map/ppermute | solution.py:48
  35.6 3.0 %tokens.3 = (bf16[256,4096]{1,0:T(8,128)(2,1)S(1)}, bf16[256,4096]{1,0:T(8,128)(2,1)S(1)}, f32[256,256]{1,0:T(8,128)S(1)}) custom-call(bf16[256,8192]{1,0:T(8,128)(2,1)S(1)} %copy-done.1, bf16[1,8192]{1,0:T(2,128)(2,1)S(1)} %broadcast_in_dim.6.refs_1_, bf16[8192,128]{1,0:T(8,128)(2,1)S(1)} %copy-done.7, f32[256,128]{1,0:T(8,128)S(1)} %get-tuple-element.69.refs_3_, ...), custom_call_target="tpu_custom_call" | custom-call | tf_op jit(solution)/shard_map/tokens/pallas_call | solution.py:69
  42.0 6.8 %collective-permute-done.10.refs_9_ = bf16[32,16,256]{2,1,0:T(8,128)(2,1)S(1)} collective-permute-done((bf16[32,16,256]{2,1,0:T(8,128)(2,1)S(1)}, bf16[32,16,256]{2,1,0:T(8,128)(2,1)S(1)}, u32[]{:S(2)}, u32[]{:S(2)}) %collective-permute-start.10) | collective-permute-done | bytes 262176 | tf_op jit(solution)/shard_map/ppermute | solution.py:48
  50.1 3.9 %collective-permute-done.12.refs_12_ = bf16[32,16,256]{2,1,0:T(8,128)(2,1)S(1)} collective-permute-done((bf16[32,16,256]{2,1,0:T(8,128)(2,1)S(1)}, bf16[32,16,256]{2,1,0:T(8,128)(2,1)S(1)}, u32[]{:S(2)}, u32[]{:S(2)}) %collective-permute-start.12) | collective-permute-done | bytes 262176 | tf_op jit(solution)/shard_map/ppermute | solution.py:48
  61.0 4.2 %collective-permute-done.16.refs_8_ = bf16[16,32,128]{2,1,0:T(8,128)(2,1)S(1)} collective-permute-done((bf16[16,32,128]{2,1,0:T(8,128)(2,1)S(1)}, bf16[16,32,128]{2,1,0:T(8,128)(2,1)S(1)}, u32[]{:S(2)}, u32[]{:S(2)}) %collective-permute-start.16) | collective-permute-done | bytes 131104 | tf_op jit(solution)/shard_map/ppermute | solution.py:48
  100.0 2.8 %collective-permute-done.29.left = bf16[128,512]{1,0:T(8,128)(2,1)S(1)} collective-permute-done((bf16[128,512]{1,0:T(8,128)(2,1)S(1)}, bf16[128,512]{1,0:T(8,128)(2,1)S(1)}, u32[]{:S(2)}, u32[]{:S(2)}) %collective-permute-start.29) | collective-permute-done | bytes 131104 | tf_op jit(solution)/shard_map/ppermute | solution.py:48
  105.2 3.1 %collective-permute-done.56.refs_3_ = bf16[256,256]{1,0:T(8,128)(2,1)S(1)} collective-permute-done((bf16[256,256]{1,0:T(8,128)(2,1)S(1)}, bf16[256,256]{1,0:T(8,128)(2,1)S(1)}, u32[]{:S(2)}, u32[]{:S(2)}) %collective-permute-start.56) | collective-permute-done | bytes 131104 | tf_op jit(solution)/shard_map/ppermute | solution.py:57
  116.9 4.1 %collective-permute-done.59.left = bf16[544,128]{1,0:T(8,128)(2,1)S(1)} collective-permute-done((bf16[544,128]{1,0:T(8,128)(2,1)S(1)}, bf16[544,128]{1,0:T(8,128)(2,1)S(1)}, u32[]{:S(2)}, u32[]{:S(2)}) %collective-permute-start.59) | collective-permute-done | bytes 139296 | tf_op jit(solution)/shard_map/ppermute | solution.py:48
  128.8 2.8 %collective-permute-done.63.left = bf16[544,128]{1,0:T(8,128)(2,1)S(1)} collective-permute-done((bf16[544,128]{1,0:T(8,128)(2,1)S(1)}, bf16[544,128]{1,0:T(8,128)(2,1)S(1)}, u32[]{:S(2)}, u32[]{:S(2)}) %collective-permute-start.63) | collective-permute-done | bytes 139296 | tf_op jit(solution)/shard_map/ppermute | solution.py:48
  131.6 2.7 %collective-permute-done.32.refs_3_ = bf16[128,512]{1,0:T(8,128)(2,1)S(1)} collective-permute-done((bf16[128,512]{1,0:T(8,128)(2,1)S(1)}, bf16[128,512]{1,0:T(8,128)(2,1)S(1)}, u32[]{:S(2)}, u32[]{:S(2)}) %collective-permute-start.32) | collective-permute-done | bytes 131104 | tf_op jit(solution)/shard_map/ppermute | solution.py:48
  134.3 2.8 %collective-permute-done.31.refs_2_ = bf16[128,512]{1,0:T(8,128)(2,1)S(1)} collective-permute-done((bf16[128,512]{1,0:T(8,128)(2,1)S(1)}, bf16[128,512]{1,0:T(8,128)(2,1)S(1)}, u32[]{:S(2)}, u32[]{:S(2)}) %collective-permute-start.31) | collective-permute-done | bytes 131104 | tf_op jit(solution)/shard_map/ppermute | solution.py:48
  137.1 3.0 %collective-permute-done.61.left = bf16[544,128]{1,0:T(8,128)(2,1)S(1)} collective-permute-done((bf16[544,128]{1,0:T(8,128)(2,1)S(1)}, bf16[544,128]{1,0:T(8,128)(2,1)S(1)}, u32[]{:S(2)}, u32[]{:S(2)}) %collective-permute-start.61) | collective-permute-done | bytes 139296 | tf_op jit(solution)/shard_map/ppermute | solution.py:48
  140.2 2.9 %collective-permute-done.64.left = bf16[544,128]{1,0:T(8,128)(2,1)S(1)} collective-permute-done((bf16[544,128]{1,0:T(8,128)(2,1)S(1)}, bf16[544,128]{1,0:T(8,128)(2,1)S(1)}, u32[]{:S(2)}, u32[]{:S(2)}) %collective-permute-start.64) | collective-permute-done | bytes 139296 | tf_op jit(solution)/shard_map/ppermute | solution.py:48
  143.2 2.7 %collective-permute-done.34.refs_5_ = bf16[128,512]{1,0:T(8,128)(2,1)S(1)} collective-permute-done((bf16[128,512]{1,0:T(8,128)(2,1)S(1)}, bf16[128,512]{1,0:T(8,128)(2,1)S(1)}, u32[]{:S(2)}, u32[]{:S(2)}) %collective-permute-start.34) | collective-permute-done | bytes 131104 | tf_op jit(solution)/shard_map/ppermute | solution.py:48
  145.9 2.8 %collective-permute-done.33.refs_4_ = bf16[128,512]{1,0:T(8,128)(2,1)S(1)} collective-permute-done((bf16[128,512]{1,0:T(8,128)(2,1)S(1)}, bf16[128,512]{1,0:T(8,128)(2,1)S(1)}, u32[]{:S(2)}, u32[]{:S(2)}) %collective-permute-start.33) | collective-permute-done | bytes 131104 | tf_op jit(solution)/shard_map/ppermute | solution.py:48
  148.7 3.0 %collective-permute-done.65.refs_18_ = bf16[544,128]{1,0:T(8,128)(2,1)S(1)} collective-permute-done((bf16[544,128]{1,0:T(8,128)(2,1)S(1)}, bf16[544,128]{1,0:T(8,128)(2,1)S(1)}, u32[]{:S(2)}, u32[]{:S(2)}) %collective-permute-start.65) | collective-permute-done | bytes 139296 | tf_op jit(solution)/shard_map/ppermute | solution.py:48
  151.7 3.0 %collective-permute-done.66.refs_19_ = bf16[544,128]{1,0:T(8,128)(2,1)S(1)} collective-permute-done((bf16[544,128]{1,0:T(8,128)(2,1)S(1)}, bf16[544,128]{1,0:T(8,128)(2,1)S(1)}, u32[]{:S(2)}, u32[]{:S(2)}) %collective-permute-start.66) | collective-permute-done | bytes 139296 | tf_op jit(solution)/shard_map/ppermute | solution.py:48
  154.7 2.8 %collective-permute-done.36.refs_7_ = bf16[128,512]{1,0:T(8,128)(2,1)S(1)} collective-permute-done((bf16[128,512]{1,0:T(8,128)(2,1)S(1)}, bf16[128,512]{1,0:T(8,128)(2,1)S(1)}, u32[]{:S(2)}, u32[]{:S(2)}) %collective-permute-start.36) | collective-permute-done | bytes 131104 | tf_op jit(solution)/shard_map/ppermute | solution.py:48
  157.5 2.6 %collective-permute-done.35.refs_6_ = bf16[128,512]{1,0:T(8,128)(2,1)S(1)} collective-permute-done((bf16[128,512]{1,0:T(8,128)(2,1)S(1)}, bf16[128,512]{1,0:T(8,128)(2,1)S(1)}, u32[]{:S(2)}, u32[]{:S(2)}) %collective-permute-start.35) | collective-permute-done | bytes 131104 | tf_op jit(solution)/shard_map/ppermute | solution.py:48
  167.4 4.2 %collective-permute-done.69.refs_22_ = bf16[544,128]{1,0:T(8,128)(2,1)S(1)} collective-permute-done((bf16[544,128]{1,0:T(8,128)(2,1)S(1)}, bf16[544,128]{1,0:T(8,128)(2,1)S(1)}, u32[]{:S(2)}, u32[]{:S(2)}) %collective-permute-start.69) | collective-permute-done | bytes 139296 | tf_op jit(solution)/shard_map/ppermute | solution.py:48
  175.1 3.0 %place.1 = (bf16[8192,128]{1,0:T(8,128)(2,1)}, bf16[128,128]{1,0:T(8,128)(2,1)}, bf16[128,128]{1,0:T(8,128)(2,1)}, bf16[128,8192]{1,0:T(8,128)(2,1)}) custom-call(bf16[128,512]{1,0:T(8,128)(2,1)S(1)} %add.32.refs_0_, bf16[128,512]{1,0:T(8,128)(2,1)S(1)} %add.35.refs_1_, bf16[128,512]{1,0:T(8,128)(2,1)S(1)} %collective-permute-done.31.refs_2_, ...), custom_call_target="tpu_custom_call" | custom-call | tf_op jit(solution)/shard_map/place/pallas_call | solution.py:69
  (206 shorter events, 96.6 us)
Async XLA Ops:
  5.5 14.4 %collective-permute-start.1 = (bf16[32,16,256]{2,1,0:T(8,128)(2,1)S(1)}, bf16[32,16,256]{2,1,0:T(8,128)(2,1)S(1)}, u32[]{:S(2)}, u32[]{:S(2)}) collective-permute-start(bf16[32,16,256]{2,1,0:T(8,128)(2,1)S(1)} %get-tuple-element.65), channel_id=1, source_target_pairs={{0,4},{4,12},{12,8},{8,0},{1,5},{5,13},{13,9},{9,1},{2,6},{6,14},{... | collective-permute-start | bytes 786440 | tf_op jit(solution)/shard_map/ppermute | solution.py:48
  8.5 13.5 %collective-permute-start.3 = (bf16[32,16,256]{2,1,0:T(8,128)(2,1)S(1)}, bf16[32,16,256]{2,1,0:T(8,128)(2,1)S(1)}, u32[]{:S(2)}, u32[]{:S(2)}) collective-permute-start(bf16[32,16,256]{2,1,0:T(8,128)(2,1)S(1)} %get-tuple-element.66), channel_id=1, source_target_pairs={{0,4},{4,12},{12,8},{8,0},{1,5},{5,13},{13,9},{9,1},{2,6},{6,14},{... | collective-permute-start | bytes 786440 | tf_op jit(solution)/shard_map/ppermute | solution.py:48
  20.0 11.2 %collective-permute-start.5 = (bf16[32,16,256]{2,1,0:T(8,128)(2,1)S(1)}, bf16[32,16,256]{2,1,0:T(8,128)(2,1)S(1)}, u32[]{:S(2)}, u32[]{:S(2)}) collective-permute-start(bf16[32,16,256]{2,1,0:T(8,128)(2,1)S(1)} %collective-permute-done.1.refs_5_), channel_id=1, source_target_pairs={{0,16},{16,0},{1,17},{17,1},{2,18},{18,2},{3,19},{19,3},{4,20},{20... | collective-permute-start | bytes 786440 | tf_op jit(solution)/shard_map/ppermute | solution.py:52
  21.5 10.1 %collective-permute-start.2 = (bf16[32,16,256]{2,1,0:T(8,128)(2,1)S(1)}, bf16[32,16,256]{2,1,0:T(8,128)(2,1)S(1)}, u32[]{:S(2)}, u32[]{:S(2)}) collective-permute-start(bf16[32,16,256]{2,1,0:T(8,128)(2,1)S(1)} %collective-permute-done.1.refs_5_), channel_id=1, source_target_pairs={{0,4},{4,12},{12,8},{8,0},{1,5},{5,13},{13,9},{9,1},{2,6},{6,14},{... | collective-permute-start | bytes 786440 | tf_op jit(solution)/shard_map/ppermute | solution.py:48
  22.0 13.6 %collective-permute-start.4 = (bf16[32,16,256]{2,1,0:T(8,128)(2,1)S(1)}, bf16[32,16,256]{2,1,0:T(8,128)(2,1)S(1)}, u32[]{:S(2)}, u32[]{:S(2)}) collective-permute-start(bf16[32,16,256]{2,1,0:T(8,128)(2,1)S(1)} %collective-permute-done.3.refs_8_), channel_id=1, source_target_pairs={{0,4},{4,12},{12,8},{8,0},{1,5},{5,13},{13,9},{9,1},{2,6},{6,14},{... | collective-permute-start | bytes 786440 | tf_op jit(solution)/shard_map/ppermute | solution.py:48
  23.4 12.2 %collective-permute-start.6 = (bf16[32,16,256]{2,1,0:T(8,128)(2,1)S(1)}, bf16[32,16,256]{2,1,0:T(8,128)(2,1)S(1)}, u32[]{:S(2)}, u32[]{:S(2)}) collective-permute-start(bf16[32,16,256]{2,1,0:T(8,128)(2,1)S(1)} %collective-permute-done.3.refs_8_), channel_id=1, source_target_pairs={{0,16},{16,0},{1,17},{17,1},{2,18},{18,2},{3,19},{19,3},{4,20},{20... | collective-permute-start | bytes 786440 | tf_op jit(solution)/shard_map/ppermute | solution.py:52
  31.2 27.6 %collective-permute-start.15 = (bf16[256,4096]{1,0:T(8,128)(2,1)S(1)}, bf16[256,4096]{1,0:T(8,128)(2,1)S(1)}, u32[]{:S(2)}, u32[]{:S(2)}) collective-permute-start(bf16[256,4096]{1,0:T(8,128)(2,1)S(1)} %get-tuple-element.82), channel_id=1, source_target_pairs={{0,1},{1,0},{2,3},{3,2},{4,5},{5,4},{6,7},{7,6},{8,9},{9,8},{10,11... | collective-permute-start | bytes 6291464 | tf_op jit(solution)/shard_map/ppermute | solution.py:52
  38.7 20.1 %collective-permute-start.9 = (bf16[256,4096]{1,0:T(8,128)(2,1)S(1)}, bf16[256,4096]{1,0:T(8,128)(2,1)S(1)}, u32[]{:S(2)}, u32[]{:S(2)}) collective-permute-start(bf16[256,4096]{1,0:T(8,128)(2,1)S(1)} %get-tuple-element.77), channel_id=1, source_target_pairs={{0,1},{1,0},{2,3},{3,2},{4,5},{5,4},{6,7},{7,6},{8,9},{9,8},{10,11... | collective-permute-start | bytes 6291464 | tf_op jit(solution)/shard_map/ppermute | solution.py:52
  38.7 10.1 %collective-permute-start.10 = (bf16[32,16,256]{2,1,0:T(8,128)(2,1)S(1)}, bf16[32,16,256]{2,1,0:T(8,128)(2,1)S(1)}, u32[]{:S(2)}, u32[]{:S(2)}) collective-permute-start(bf16[32,16,256]{2,1,0:T(8,128)(2,1)S(1)} %collective-permute-done.2.refs_7_), channel_id=1, source_target_pairs={{0,4},{4,12},{12,8},{8,0},{1,5},{5,13},{13,9},{9,1},{2,6},{6,14},{... | collective-permute-start | bytes 786440 | tf_op jit(solution)/shard_map/ppermute | solution.py:48
  41.7 12.2 %collective-permute-start.12 = (bf16[32,16,256]{2,1,0:T(8,128)(2,1)S(1)}, bf16[32,16,256]{2,1,0:T(8,128)(2,1)S(1)}, u32[]{:S(2)}, u32[]{:S(2)}) collective-permute-start(bf16[32,16,256]{2,1,0:T(8,128)(2,1)S(1)} %collective-permute-done.4.refs_10_), channel_id=1, source_target_pairs={{0,4},{4,12},{12,8},{8,0},{1,5},{5,13},{13,9},{9,1},{2,6},{6,14},{... | collective-permute-start | bytes 786440 | tf_op jit(solution)/shard_map/ppermute | solution.py:48
  54.0 14.9 %collective-permute-start.20 = (bf16[32,16,256]{2,1,0:T(8,128)(2,1)S(1)}, bf16[32,16,256]{2,1,0:T(8,128)(2,1)S(1)}, u32[]{:S(2)}, u32[]{:S(2)}) collective-permute-start(bf16[32,16,256]{2,1,0:T(8,128)(2,1)S(1)} %collective-permute-done.12.refs_12_), channel_id=1, source_target_pairs={{0,16},{16,0},{1,17},{17,1},{2,18},{18,2},{3,19},{19,3},{4,20},{20... | collective-permute-start | bytes 786440 | tf_op jit(solution)/shard_map/ppermute | solution.py:52
  54.5 17.5 %collective-permute-start.18 = (bf16[32,16,256]{2,1,0:T(8,128)(2,1)S(1)}, bf16[32,16,256]{2,1,0:T(8,128)(2,1)S(1)}, u32[]{:S(2)}, u32[]{:S(2)}) collective-permute-start(bf16[32,16,256]{2,1,0:T(8,128)(2,1)S(1)} %collective-permute-done.10.refs_9_), channel_id=1, source_target_pairs={{0,16},{16,0},{1,17},{17,1},{2,18},{18,2},{3,19},{19,3},{4,20},{20... | collective-permute-start | bytes 786440 | tf_op jit(solution)/shard_map/ppermute | solution.py:52
  97.8 13.5 %collective-permute-start.58 = (f32[256,256]{1,0:T(8,128)S(1)}, f32[256,256]{1,0:T(8,128)S(1)}, u32[]{:S(2)}, u32[]{:S(2)}) collective-permute-start(f32[256,256]{1,0:T(8,128)S(1)} %get-tuple-element.113.refs_5_.refs_2_), channel_id=1, source_target_pairs={{0,2},{2,0},{1,3},{3,1},{4,6},{6,4},{5,7},{7,5},{8,10},{10,8},{9,1... | collective-permute-start | bytes 786440 | tf_op jit(solution)/shard_map/ppermute | solution.py:57
  124.1 10.2 %collective-permute-start.32 = (bf16[128,512]{1,0:T(8,128)(2,1)S(1)}, bf16[128,512]{1,0:T(8,128)(2,1)S(1)}, u32[]{:S(2)}, u32[]{:S(2)}) collective-permute-start(bf16[128,512]{1,0:T(8,128)(2,1)S(1)} %add.35.refs_1_), channel_id=1, source_target_pairs={{0,4},{4,12},{12,8},{8,0},{1,5},{5,13},{13,9},{9,1},{2,6},{6,14},{... | collective-permute-start | bytes 393224 | tf_op jit(solution)/shard_map/ppermute | solution.py:48
  126.3 10.8 %collective-permute-start.31 = (bf16[128,512]{1,0:T(8,128)(2,1)S(1)}, bf16[128,512]{1,0:T(8,128)(2,1)S(1)}, u32[]{:S(2)}, u32[]{:S(2)}) collective-permute-start(bf16[128,512]{1,0:T(8,128)(2,1)S(1)} %add.32.refs_0_), channel_id=1, source_target_pairs={{0,4},{4,12},{12,8},{8,0},{1,5},{5,13},{13,9},{9,1},{2,6},{6,14},{... | collective-permute-start | bytes 393224 | tf_op jit(solution)/shard_map/ppermute | solution.py:48
  128.6 11.5 %collective-permute-start.61 = (bf16[544,128]{1,0:T(8,128)(2,1)S(1)}, bf16[544,128]{1,0:T(8,128)(2,1)S(1)}, u32[]{:S(2)}, u32[]{:S(2)}) collective-permute-start(bf16[544,128]{1,0:T(8,128)(2,1)S(1)} %add.37), channel_id=1, source_target_pairs={{0,4},{4,12},{12,8},{8,0},{1,5},{5,13},{13,9},{9,1},{2,6},{6,14},{... | collective-permute-start | bytes 417800 | tf_op jit(solution)/shard_map/ppermute | solution.py:48
  131.6 11.5 %collective-permute-start.64 = (bf16[544,128]{1,0:T(8,128)(2,1)S(1)}, bf16[544,128]{1,0:T(8,128)(2,1)S(1)}, u32[]{:S(2)}, u32[]{:S(2)}) collective-permute-start(bf16[544,128]{1,0:T(8,128)(2,1)S(1)} %add.40), channel_id=1, source_target_pairs={{0,4},{4,12},{12,8},{8,0},{1,5},{5,13},{13,9},{9,1},{2,6},{6,14},{... | collective-permute-start | bytes 417800 | tf_op jit(solution)/shard_map/ppermute | solution.py:48
  134.3 11.6 %collective-permute-start.34 = (bf16[128,512]{1,0:T(8,128)(2,1)S(1)}, bf16[128,512]{1,0:T(8,128)(2,1)S(1)}, u32[]{:S(2)}, u32[]{:S(2)}) collective-permute-start(bf16[128,512]{1,0:T(8,128)(2,1)S(1)} %collective-permute-done.32.refs_3_), channel_id=1, source_target_pairs={{0,4},{4,12},{12,8},{8,0},{1,5},{5,13},{13,9},{9,1},{2,6},{6,14},{... | collective-permute-start | bytes 393224 | tf_op jit(solution)/shard_map/ppermute | solution.py:48
  137.1 11.6 %collective-permute-start.33 = (bf16[128,512]{1,0:T(8,128)(2,1)S(1)}, bf16[128,512]{1,0:T(8,128)(2,1)S(1)}, u32[]{:S(2)}, u32[]{:S(2)}) collective-permute-start(bf16[128,512]{1,0:T(8,128)(2,1)S(1)} %collective-permute-done.31.refs_2_), channel_id=1, source_target_pairs={{0,4},{4,12},{12,8},{8,0},{1,5},{5,13},{13,9},{9,1},{2,6},{6,14},{... | collective-permute-start | bytes 393224 | tf_op jit(solution)/shard_map/ppermute | solution.py:48
  140.2 11.5 %collective-permute-start.65 = (bf16[544,128]{1,0:T(8,128)(2,1)S(1)}, bf16[544,128]{1,0:T(8,128)(2,1)S(1)}, u32[]{:S(2)}, u32[]{:S(2)}) collective-permute-start(bf16[544,128]{1,0:T(8,128)(2,1)S(1)} %add.38.refs_16_), channel_id=1, source_target_pairs={{0,4},{4,12},{12,8},{8,0},{1,5},{5,13},{13,9},{9,1},{2,6},{6,14},{... | collective-permute-start | bytes 417800 | tf_op jit(solution)/shard_map/ppermute | solution.py:48
  143.2 11.5 %collective-permute-start.66 = (bf16[544,128]{1,0:T(8,128)(2,1)S(1)}, bf16[544,128]{1,0:T(8,128)(2,1)S(1)}, u32[]{:S(2)}, u32[]{:S(2)}) collective-permute-start(bf16[544,128]{1,0:T(8,128)(2,1)S(1)} %add.41.refs_17_), channel_id=1, source_target_pairs={{0,4},{4,12},{12,8},{8,0},{1,5},{5,13},{13,9},{9,1},{2,6},{6,14},{... | collective-permute-start | bytes 417800 | tf_op jit(solution)/shard_map/ppermute | solution.py:48
  145.9 11.6 %collective-permute-start.36 = (bf16[128,512]{1,0:T(8,128)(2,1)S(1)}, bf16[128,512]{1,0:T(8,128)(2,1)S(1)}, u32[]{:S(2)}, u32[]{:S(2)}) collective-permute-start(bf16[128,512]{1,0:T(8,128)(2,1)S(1)} %collective-permute-done.34.refs_5_), channel_id=1, source_target_pairs={{0,4},{4,12},{12,8},{8,0},{1,5},{5,13},{13,9},{9,1},{2,6},{6,14},{... | collective-permute-start | bytes 393224 | tf_op jit(solution)/shard_map/ppermute | solution.py:48
  148.7 11.4 %collective-permute-start.35 = (bf16[128,512]{1,0:T(8,128)(2,1)S(1)}, bf16[128,512]{1,0:T(8,128)(2,1)S(1)}, u32[]{:S(2)}, u32[]{:S(2)}) collective-permute-start(bf16[128,512]{1,0:T(8,128)(2,1)S(1)} %collective-permute-done.33.refs_4_), channel_id=1, source_target_pairs={{0,4},{4,12},{12,8},{8,0},{1,5},{5,13},{13,9},{9,1},{2,6},{6,14},{... | collective-permute-start | bytes 393224 | tf_op jit(solution)/shard_map/ppermute | solution.py:48
  151.7 9.9 %collective-permute-start.67 = (bf16[544,128]{1,0:T(8,128)(2,1)S(1)}, bf16[544,128]{1,0:T(8,128)(2,1)S(1)}, u32[]{:S(2)}, u32[]{:S(2)}) collective-permute-start(bf16[544,128]{1,0:T(8,128)(2,1)S(1)} %collective-permute-done.65.refs_18_), channel_id=1, source_target_pairs={{0,4},{4,12},{12,8},{8,0},{1,5},{5,13},{13,9},{9,1},{2,6},{6,14},{... | collective-permute-start | bytes 417800 | tf_op jit(solution)/shard_map/ppermute | solution.py:48
  (73 other events, 521.0 us)
